TPU v7x, 32 devices: a whole 2x2x4 slice. The times are simulated.
32 devices in a mesh: row: 4 (over z), col: 8 (over y, x, core).
Axes of the slice: x: 2, y: 2, z: 4, core: 2. Of those that a mesh axis runs over, the one named last changes fastest.
Arguments:
- stored_blocks: float32 [4, 8, 2, 14, 256, 256], P('row', 'col'), may hold values from -0.0390625 to 0.0390625
- onsite: float32 [4, 8, 2, 256], P('row', 'col'), may hold values from 0.05 to 0.95
- bond_mask: int32 [4, 8, 2, 13], P('row', 'col'), may hold values 0 or 1
Outputs:
- purified: float32 [4, 8, 2, 14, 256, 256], P('row', 'col')
All inputs are finite; a program needn't handle non-finite values. No bound on the sum of `bond_mask` on one device may be relied on, other than what follows from the above.
Results may differ from a plain program's by a relative error of at most 0.00024.
Values sent between devices are 32-bit elements; how exact they have to be, the bound alone decides.
No kernel may reach another device: no remote copies, remote signals or barrier semaphores. Data moves between devices by JAX's collectives and lax.ppermute only.
A program may use at most 448 MiB of HBM per device.

v0:
```python
import jax
import jax.numpy as jnp
import numpy as np
from jax import lax
from jax.sharding import PartitionSpec as P


def passed_along(shard, axis, by):
    peers = lax.axis_size(axis)
    return lax.ppermute(shard, axis, [(i, (i + by) % peers) for i in range(peers)])


def offset_list():
    return [
        (step_x, step_y, step_z)
        for step_x in (-1, 0, 1)
        for step_y in (-1, 0, 1)
        for step_z in (-1, 0, 1)
        if (step_x, step_y, step_z) > (0, 0, 0)
    ]


def slot_number(offset):
    return offset_list().index(offset) + 1


def needed(side_x, side_y):
    chosen = [0]
    for position, offset in enumerate(offset_list()):
        if abs(side_x + offset[0]) <= 1 and abs(side_y + offset[1]) <= 1:
            chosen.append(position + 1)
    return chosen


def select_slots(blocks_in, slot_list, wanted):
    return jnp.concatenate(
        [
            blocks_in[:, slot_list.index(slot_id) : slot_list.index(slot_id) + 1]
            for slot_id in wanted
        ],
        axis=1,
    )


def first_slots(toward):
    merged = set()
    for across in (-1, 0, 1):
        merged.update(needed(toward, across))
    return sorted(merged)


def second_payload(held_data, toward):
    pieces = []
    layout = []
    for across in (-1, 0, 1):
        source = (across, 0)
        target = (across, toward)
        wanted = needed(target[0], target[1])
        blocks_in, slot_list = held_data[source]
        pieces.append(select_slots(blocks_in, slot_list, wanted))
        layout.append((target, wanted))
    return (jnp.concatenate(pieces, axis=1), layout)


def unpack(received, layout, lookup):
    cursor = 0
    for target, wanted in layout:
        lookup[target] = (received[:, cursor : cursor + len(wanted)], wanted)
        cursor += len(wanted)


def build_local(stored_blocks, onsite, bond_mask):
    blocks_here = stored_blocks[0, 0]
    layers = blocks_here.shape[0]
    block_size = blocks_here.shape[-1]
    leading = blocks_here[:, 0]
    identity = jnp.eye(block_size, dtype=jnp.float32)
    diagonal = (
        0.5 * (leading + jnp.swapaxes(leading, 1, 2)) + identity[None] * onsite[0, 0][:, None, :]
    )
    inside = np.array(
        [
            [1.0 if 0 <= layer_id + offset[2] < layers else 0.0 for offset in offset_list()]
            for layer_id in range(layers)
        ],
        np.float32,
    )
    keep_mask = bond_mask[0, 0].astype(jnp.float32) * inside
    others = blocks_here[:, 1:] * keep_mask[:, :, None, None]
    return (jnp.concatenate([diagonal[:, None], others], axis=1), keep_mask)


def fetch_block(lookup, cell_at, slot_id):
    blocks_in, slot_list = lookup[cell_at[0], cell_at[1]]
    return blocks_in[cell_at[2], slot_list.index(slot_id)]


def block_at(lookup, cell_at, offset, layers):
    if not 0 <= cell_at[2] < layers:
        return None
    if offset == (0, 0, 0):
        return (fetch_block(lookup, cell_at, 0), False)
    if offset > (0, 0, 0):
        if not 0 <= cell_at[2] + offset[2] < layers:
            return None
        return (fetch_block(lookup, cell_at, slot_number(offset)), False)
    source = (cell_at[0] + offset[0], cell_at[1] + offset[1], cell_at[2] + offset[2])
    if not 0 <= source[2] < layers:
        return None
    return (fetch_block(lookup, source, slot_number((-offset[0], -offset[1], -offset[2]))), True)


def oriented(term):
    block, flipped = term
    return jnp.swapaxes(block, 0, 1) if flipped else block


def square_all(lookup, layers, block_size):
    zero_block = jnp.zeros((block_size, block_size), jnp.float32)
    all_offsets = [
        (step_x, step_y, step_z)
        for step_x in (-1, 0, 1)
        for step_y in (-1, 0, 1)
        for step_z in (-1, 0, 1)
    ]
    results = []
    for target_offset in [(0, 0, 0)] + offset_list():
        middles = []
        for middle in all_offsets:
            remainder = (
                target_offset[0] - middle[0],
                target_offset[1] - middle[1],
                target_offset[2] - middle[2],
            )
            if max(abs(remainder[0]), abs(remainder[1]), abs(remainder[2])) <= 1:
                middles.append((middle, remainder))
        left_levels = []
        right_levels = []
        for layer_id in range(layers):
            left_parts = []
            right_parts = []
            for middle, remainder in middles:
                left_term = block_at(lookup, (0, 0, layer_id), middle, layers)
                right_term = block_at(
                    lookup, (middle[0], middle[1], layer_id + middle[2]), remainder, layers
                )
                if left_term is None or right_term is None:
                    left_parts.append(zero_block)
                    right_parts.append(zero_block)
                else:
                    left_parts.append(oriented(left_term))
                    right_parts.append(oriented(right_term))
            left_levels.append(jnp.concatenate(left_parts, axis=1))
            right_levels.append(jnp.concatenate(right_parts, axis=0))
        left_stack = jnp.stack(left_levels, axis=0)
        right_stack = jnp.stack(right_levels, axis=0)
        results.append(
            jnp.einsum(
                "lak,lkc->lac",
                left_stack,
                right_stack,
                precision=lax.Precision.HIGHEST,
                preferred_element_type=jnp.float32,
            )
        )
    return jnp.stack(results, axis=1)


def shards(stored_blocks, onsite, bond_mask):
    layers = stored_blocks.shape[2]
    block_size = stored_blocks.shape[-1]
    local_blocks, keep_mask = build_local(stored_blocks, onsite, bond_mask)
    own_slots = list(range(local_blocks.shape[1]))
    lookup = {(0, 0): (local_blocks, own_slots)}
    plus_slots = first_slots(1)
    minus_slots = first_slots(-1)
    lookup[1, 0] = (
        passed_along(select_slots(local_blocks, own_slots, plus_slots), "row", -1),
        plus_slots,
    )
    lookup[-1, 0] = (
        passed_along(select_slots(local_blocks, own_slots, minus_slots), "row", 1),
        minus_slots,
    )
    held_data = dict(lookup)
    payload, layout = second_payload(held_data, 1)
    unpack(passed_along(payload, "col", -1), layout, lookup)
    payload, layout = second_payload(held_data, -1)
    unpack(passed_along(payload, "col", 1), layout, lookup)
    diag_now = local_blocks[:, 0]
    trace_one = jnp.sum(jnp.trace(diag_now, axis1=1, axis2=2))
    squared = square_all(lookup, layers, block_size)
    diag_trace = jnp.sum(jnp.trace(squared[:, 0], axis1=1, axis2=2))
    trace_one, trace_two = lax.psum((trace_one, diag_trace), ("row", "col"))
    cell_count = lax.axis_size("row") * lax.axis_size("col") * layers
    target_fill = float(cell_count * block_size // 2)
    steering = jax.nn.sigmoid(
        (jnp.abs(trace_two - target_fill) - jnp.abs(2.0 * trace_one - trace_two - target_fill))
        / block_size
    )
    full_keep = jnp.concatenate([jnp.ones((layers, 1), jnp.float32), keep_mask], axis=1)
    result = full_keep[:, :, None, None] * (squared + 2.0 * steering * (local_blocks - squared))
    return result[None, None]


def solution(mesh):
    in_specs = (
        P("row", "col", None, None, None, None),
        P("row", "col", None, None),
        P("row", "col", None, None),
    )
    out_specs = P("row", "col", None, None, None, None)
    return jax.shard_map(shards, mesh=mesh, in_specs=in_specs, out_specs=out_specs, check_vma=False)
```

profile of v0, /device:TPU:0, one launch (start us, length us, event | category | flops | bytes accessed | tf_op | source)
XLA Modules:
  0.0 943.7 jit_solution(10323093666217821158)
XLA Ops:
  0.0 8.4 copy.5
  8.4 6.4 slice.329
  15.9 7.6 copy.7
  23.8 3.9 broadcast_multiply_fusion
  33.2 160.0 %collective-permute-done = f32[2,14,256,256]{3,2,1,0:T(8,128)S(1)} collective-permute-done((f32[2,14,256,256]{3,2,1,0:T(8,128)S(1)}, f32[2,14,256,256]{3,2,1,0:T(8,128)S(1)}, u32[]{:S(2)}, u32[]{:S(2)}) %collective-permute-start) | collective-permute-done | bytes 7340064 | tf_op jit(solution)/shard_map/ppermute | solution.py:10
  206.1 3.4 slice_dynamic-update-slice_fusion
  209.5 52.0 %collective-permute-done.1 = f32[2,5,256,256]{3,2,1,0:T(8,128)S(1)} collective-permute-done((f32[2,5,256,256]{3,2,1,0:T(8,128)S(1)}, f32[2,5,256,256]{3,2,1,0:T(8,128)S(1)}, u32[]{:S(2)}, u32[]{:S(2)}) %collective-permute-start.1) | collective-permute-done | bytes 2621472 | tf_op jit(solution)/shard_map/ppermute | solution.py:10
  263.4 15.2 %copy.8 = f32[2,27,256,256]{2,3,1,0:T(8,128)} copy(f32[2,27,256,256]{3,2,1,0:T(8,128)} %constant_dynamic-update-slice_fusion) | data formatting | bytes 28311552 | tf_op jit(solution)/shard_map/concatenate | solution.py:62
  279.6 3.1 collective-permute-start.3
  282.8 4.1 slice_bitcast_fusion.37
  339.4 6.6 fusion.213
  374.8 111.7 %collective-permute-done.3 = f32[2,18,256,256]{3,2,1,0:T(8,128)} collective-permute-done((f32[2,18,256,256]{3,2,1,0:T(8,128)}, f32[2,18,256,256]{3,2,1,0:T(8,128)}, u32[]{:S(2)}, u32[]{:S(2)}) %collective-permute-start.3) | collective-permute-done | bytes 9437216 | tf_op jit(solution)/shard_map/ppermute | solution.py:10
  486.5 3.9 slice_bitcast_fusion.2
  536.0 4.0 slice_bitcast_fusion.10
  633.1 3.5 constant_dynamic-update-slice_fusion.547
  714.3 15.9 %constant_dynamic-update-slice_fusion.551 = (f32[1,1,2,14,256,256]{5,4,3,2,1,0:T(8,128)}, f32[2,256,256]{2,1,0:T(8,128)S(1)}) fusion(f32[1,6912,256]{2,1,0:T(8,128)} %bitcast.78, f32[1,6912,256]{2,1,0:T(8,128)S(1)} %bitcast.993, f32[1,256,6912]{2,1,0:T(8,128)S(1)} %bitcast.994, f32[1,256,6912]{2,1,0:T(8,128)S(1)} %bitcast.990), kind=kOutput, calls=%fused_computation.651 | convolution fusion | flops 10878713856 | bytes 29360128 | tf_op jit(solution)/shard_map/lak,lkc->lac/dot_general | solution.py:158
  731.1 40.2 %all-reduce.19 = (f32[]{:T(128)}, f32[]{:T(128)}) all-reduce(f32[]{:T(128)} %get-tuple-element.6, f32[]{:T(128)} %get-tuple-element.5), channel_id=1, replica_groups=mesh['row'=4,'col'=8] {'row','col'}, use_global_device_ids=true, to_apply=%region_1.2 | all-reduce | flops 2 | bytes 16 | tf_op jit(solution)/shard_map/psum | solution.py:194
  821.7 3.4 constant_dynamic-update-slice_fusion.525
  832.5 13.4 %fusion.70 = f32[1,1,2,14,256,256]{5,4,3,2,1,0:T(8,128)S(1)} fusion(f32[1,1,2,14,256,256]{5,4,3,2,1,0:T(8,128)S(1)} %bitcast.976, f32[1,4608,256]{1,2,0:T(8,128)S(1)} %bitcast.977, f32[256,4608]{1,0:T(8,128)} %get-tuple-element.186), kind=kOutput, calls=%fused_computation.75 | convolution fusion | flops 3623878656 | bytes 9961472 | tf_op jit(solution)/shard_map/lak,lkc->lac/dot_general | solution.py:158
  845.8 8.0 fusion.160
  853.8 16.7 %fusion.150 = f32[1,1,2,14,256,256]{5,4,3,2,1,0:T(8,128)S(1)} fusion(f32[1,1,2,14,256,256]{5,4,3,2,1,0:T(8,128)S(1)} %fusion.160, f32[1,4608,256]{2,1,0:T(8,128)} %bitcast.142, f32[1,4608,256]{2,1,0:T(8,128)} %bitcast.128, f32[1,256,4608]{2,1,0:T(8,128)} %bitcast.122, f32[1,256,4608]{2,1,0:T(8,128)} %bitcast.121), kind=kOutput, calls=%fused_computation.91 | convolution fusion | flops 7252475904 | bytes 19398656 | tf_op jit(solution)/shard_map/lak,lkc->lac/dot_general | solution.py:158
  870.6 7.2 fusion.170
  877.8 4.5 fusion.80
  882.3 8.2 fusion.130
  890.6 4.6 fusion.90
  895.2 4.0 fusion.180
  899.3 11.6 %fusion.140 = f32[1,1,2,14,256,256]{5,4,3,2,1,0:T(8,128)S(1)} fusion(f32[1,1,2,14,256,256]{5,4,3,2,1,0:T(8,128)S(1)} %fusion.180, f32[1,4608,256]{1,2,0:T(8,128)S(1)} %bitcast.981, f32[1,4608,256]{1,2,0:T(8,128)S(1)} %bitcast.978, f32[1,256,4608]{2,1,0:T(8,128)S(1)} %bitcast.984, f32[1,256,4608]{2,1,0:T(8,128)} %bitcast.197), kind=kOutput, calls=%fused_computation.89 | convolution fusion | flops 7252475904 | bytes 19398656 | tf_op jit(solution)/shard_map/lak,lkc->lac/dot_general | solution.py:158
  910.9 7.1 fusion.190
  918.0 4.9 fusion.100
  922.9 11.8 %fusion.120 = f32[1,1,2,14,256,256]{5,4,3,2,1,0:T(8,128)S(1)} fusion(f32[1,1,2,14,256,256]{5,4,3,2,1,0:T(8,128)S(1)} %fusion.100, f32[1,3072,256]{2,1,0:T(8,128)} %bitcast.227, f32[1,3072,256]{2,1,0:T(8,128)} %bitcast.225, f32[1,256,3072]{2,1,0:T(8,128)} %bitcast.224, f32[1,256,3072]{2,1,0:T(8,128)} %bitcast.223), kind=kOutput, calls=%fused_computation.85 | convolution fusion | flops 4834983936 | bytes 13107200 | tf_op jit(solution)/shard_map/lak,lkc->lac/dot_general | solution.py:158
  934.7 5.1 fusion.110
  939.8 3.7 fusion.25
  (553 shorter events, 375.6 us)
Async XLA Ops:
  27.8 178.3 %copy-start = (f32[2,13,256,256]{3,2,1,0:T(8,128)}, f32[2,13,256,256]{3,2,1,0:T(8,128)S(1)}, u32[]{:S(2)}) copy-start(f32[2,13,256,256]{3,2,1,0:T(8,128)S(1)} %broadcast_multiply_fusion) | copy-start | bytes 20447236
  30.1 163.1 %collective-permute-start = (f32[2,14,256,256]{3,2,1,0:T(8,128)S(1)}, f32[2,14,256,256]{3,2,1,0:T(8,128)S(1)}, u32[]{:S(2)}, u32[]{:S(2)}) collective-permute-start(f32[2,14,256,256]{3,2,1,0:T(8,128)S(1)} %pad_maximum_fusion), channel_id=1, source_target_pairs={{0,8},{8,16},{16,24},{24,0},{1,9},{9,17},{17,25},{25,1},{2,10},{10... | collective-permute-start | bytes 22020104 | tf_op jit(solution)/shard_map/ppermute | solution.py:10
  203.5 58.1 %collective-permute-start.1 = (f32[2,5,256,256]{3,2,1,0:T(8,128)S(1)}, f32[2,5,256,256]{3,2,1,0:T(8,128)S(1)}, u32[]{:S(2)}, u32[]{:S(2)}) collective-permute-start(f32[2,5,256,256]{3,2,1,0:T(8,128)S(1)} %pad_maximum_fusion.1), channel_id=1, source_target_pairs={{0,24},{8,0},{16,8},{24,16},{1,25},{9,1},{17,9},{25,17},{2,26},{10... | collective-permute-start | bytes 7864328 | tf_op jit(solution)/shard_map/ppermute | solution.py:10
  278.6 257.4 %collective-permute-start.2 = (f32[2,27,256,256]{2,3,1,0:T(8,128)}, f32[2,27,256,256]{2,3,1,0:T(8,128)}, u32[]{:S(2)}, u32[]{:S(2)}) collective-permute-start(f32[2,27,256,256]{2,3,1,0:T(8,128)} %copy.8), channel_id=1, source_target_pairs={{0,1},{1,2},{2,3},{3,4},{4,5},{5,6},{6,7},{7,0},{8,9},{9,10},{10,1... | collective-permute-start | bytes 42467336 | tf_op jit(solution)/shard_map/ppermute | solution.py:10
  279.6 206.8 %collective-permute-start.3 = (f32[2,18,256,256]{3,2,1,0:T(8,128)}, f32[2,18,256,256]{3,2,1,0:T(8,128)}, u32[]{:S(2)}, u32[]{:S(2)}) collective-permute-start(f32[2,18,256,256]{3,2,1,0:T(8,128)} %constant_dynamic-update-slice_fusion.3), channel_id=1, source_target_pairs={{0,7},{1,0},{2,1},{3,2},{4,3},{5,4},{6,5},{7,6},{8,15},{9,8},{10,9... | collective-permute-start | bytes 28311560 | tf_op jit(solution)/shard_map/ppermute | solution.py:10
  350.2 24.6 %copy-start.28 = (f32[256,256]{1,0:T(8,128)}, f32[256,256]{1,0:T(8,128)S(1)}, u32[]{:S(2)}) copy-start(f32[256,256]{1,0:T(8,128)S(1)} %copy.16) | copy-start | bytes 786436
  630.7 13.3 %copy-start.1 = (f32[256,3072]{1,0:T(8,128)}, f32[256,3072]{1,0:T(8,128)S(1)}, u32[]{:S(2)}) copy-start(f32[256,3072]{1,0:T(8,128)S(1)} %get-tuple-element.180) | copy-start | bytes 9437188
  630.7 14.2 %copy-start.10 = (f32[256,4608]{1,0:T(8,128)}, f32[256,4608]{1,0:T(8,128)S(1)}, u32[]{:S(2)}) copy-start(f32[256,4608]{1,0:T(8,128)S(1)} %get-tuple-element.181) | copy-start | bytes 14155780
  630.7 14.2 %copy-start.72 = (f32[256,6912]{1,0:T(8,128)}, f32[256,6912]{1,0:T(8,128)S(1)}, u32[]{:S(2)}) copy-start(f32[256,6912]{1,0:T(8,128)S(1)} %get-tuple-element.178) | copy-start | bytes 21233668
  672.8 36.3 %copy-start.73 = (f32[256,6912]{1,0:T(8,128)S(1)}, f32[256,6912]{1,0:T(8,128)}, u32[]{:S(2)}) copy-start(f32[256,6912]{1,0:T(8,128)} %copy-done.72) | copy-start | bytes 21233668
  674.3 24.2 %slice-start.10 = ((s8[7077888]{0:T(1024)(128)(4,1)}), s8[4194304]{0:T(1024)(128)(4,1)S(1)}, s32[]{:S(2)}) async-start(s8[7077888]{0:T(1024)(128)(4,1)} %bitcast.991), calls=%async_computation.10 | async-start | bytes 8388608
  681.8 16.7 %copy-start.21 = (f32[256,256]{1,0:T(8,128)S(1)}, f32[256,256]{1,0:T(8,128)}, u32[]{:S(2)}) copy-start(f32[256,256]{1,0:T(8,128)} %copy.26) | copy-start | bytes 786436
  684.2 14.3 %copy-start.69 = (f32[256,256]{0,1:T(8,128)S(1)}, f32[256,256]{0,1:T(8,128)}, u32[]{:S(2)}) copy-start(f32[256,256]{0,1:T(8,128)} %copy.28) | copy-start | bytes 786436
  684.2 14.3 %slice-start.11 = ((s8[7077888]{0:T(1024)(128)(4,1)}), s8[2883584]{0:T(1024)(128)(4,1)S(1)}, s32[]{:S(2)}) async-start(s8[7077888]{0:T(1024)(128)(4,1)} %bitcast.991), calls=%async_computation.11 | async-start | bytes 5767168
  684.2 14.4 %copy-start.68 = (f32[256,256]{0,1:T(8,128)S(1)}, f32[256,256]{0,1:T(8,128)}, u32[]{:S(2)}) copy-start(f32[256,256]{0,1:T(8,128)} %copy.29) | copy-start | bytes 786436
  686.7 12.0 %copy-start.67 = (f32[256,256]{0,1:T(8,128)S(1)}, f32[256,256]{0,1:T(8,128)}, u32[]{:S(2)}) copy-start(f32[256,256]{0,1:T(8,128)} %copy.30) | copy-start | bytes 786436
  686.7 12.1 %copy-start.66 = (f32[256,256]{0,1:T(8,128)S(1)}, f32[256,256]{0,1:T(8,128)}, u32[]{:S(2)}) copy-start(f32[256,256]{0,1:T(8,128)} %copy.31) | copy-start | bytes 786436
  773.1 12.0 %copy-start.19 = (f32[256,256]{0,1:T(8,128)S(1)}, f32[256,256]{0,1:T(8,128)}, u32[]{:S(2)}) copy-start(f32[256,256]{0,1:T(8,128)} %copy.33) | copy-start | bytes 786436
  773.1 12.0 %copy-start.16 = (f32[256,256]{0,1:T(8,128)S(1)}, f32[256,256]{0,1:T(8,128)}, u32[]{:S(2)}) copy-start(f32[256,256]{0,1:T(8,128)} %copy.67) | copy-start | bytes 786436
  773.1 12.1 %copy-start.14 = (f32[1,1,256,256]{2,3,1,0:T(8,128)S(1)}, f32[1,1,256,256]{2,3,1,0:T(8,128)}, u32[]{:S(2)}) copy-start(f32[1,1,256,256]{2,3,1,0:T(8,128)} %copy.184) | copy-start | bytes 786436
  794.3 12.1 %copy-start.43 = (f32[1,1,256,256]{2,3,1,0:T(8,128)S(1)}, f32[1,1,256,256]{2,3,1,0:T(8,128)}, u32[]{:S(2)}) copy-start(f32[1,1,256,256]{2,3,1,0:T(8,128)} %copy.178) | copy-start | bytes 786436
  810.4 22.0 %slice-start.4 = ((s8[7340032]{0:T(1024)(128)(4,1)}), s8[4194304]{0:T(1024)(128)(4,1)S(1)}, s32[]{:S(2)}) async-start(s8[7340032]{0:T(1024)(128)(4,1)} %bitcast.975), calls=%async_computation.4 | async-start | bytes 8388608
  811.6 16.8 %copy-start.49 = (f32[256,256]{0,1:T(8,128)S(1)}, f32[256,256]{0,1:T(8,128)}, u32[]{:S(2)}) copy-start(f32[256,256]{0,1:T(8,128)} %copy.68) | copy-start | bytes 786436
  812.8 16.4 %copy-start.50 = (f32[256,256]{0,1:T(8,128)S(1)}, f32[256,256]{0,1:T(8,128)}, u32[]{:S(2)}) copy-start(f32[256,256]{0,1:T(8,128)} %copy.69) | copy-start | bytes 786436
  813.8 16.1 %copy-start.40 = (f32[256,256]{0,1:T(8,128)S(1)}, f32[256,256]{0,1:T(8,128)}, u32[]{:S(2)}) copy-start(f32[256,256]{0,1:T(8,128)} %copy.157) | copy-start | bytes 786436
  815.8 14.9 %copy-start.42 = (f32[1,1,256,256]{2,3,1,0:T(8,128)S(1)}, f32[1,1,256,256]{2,3,1,0:T(8,128)}, u32[]{:S(2)}) copy-start(f32[1,1,256,256]{2,3,1,0:T(8,128)} %copy.181) | copy-start | bytes 786436
  816.8 14.7 %copy-start.41 = (f32[1,1,256,256]{2,3,1,0:T(8,128)S(1)}, f32[1,1,256,256]{2,3,1,0:T(8,128)}, u32[]{:S(2)}) copy-start(f32[1,1,256,256]{2,3,1,0:T(8,128)} %copy.182) | copy-start | bytes 786436
  820.1 12.3 %slice-start.5 = ((s8[7340032]{0:T(1024)(128)(4,1)}), s8[3145728]{0:T(1024)(128)(4,1)S(1)}, s32[]{:S(2)}) async-start(s8[7340032]{0:T(1024)(128)(4,1)} %bitcast.975), calls=%async_computation.5 | async-start | bytes 6291456
  820.1 12.3 %copy-start.22 = (f32[3072,256]{0,1:T(8,128)}, f32[3072,256]{0,1:T(8,128)S(1)}, u32[]{:S(2)}) copy-start(f32[3072,256]{0,1:T(8,128)S(1)} %get-tuple-element.324) | copy-start | bytes 9437188
  820.2 12.2 %copy-start.9 = (f32[4608,256]{0,1:T(8,128)}, f32[4608,256]{0,1:T(8,128)S(1)}, u32[]{:S(2)}) copy-start(f32[4608,256]{0,1:T(8,128)S(1)} %constant_dynamic-update-slice_fusion.429) | copy-start | bytes 14155780
  922.9 16.9 %slice-start.2 = ((s8[6815744]{0:T(1024)(128)(4,1)}), s8[4194304]{0:T(1024)(128)(4,1)S(1)}, s32[]{:S(2)}) async-start(s8[6815744]{0:T(1024)(128)(4,1)} %bitcast.972), calls=%async_computation.2 | async-start | bytes 8388608
  922.9 16.9 %slice-start.3 = ((s8[6815744]{0:T(1024)(128)(4,1)}), s8[2621440]{0:T(1024)(128)(4,1)S(1)}, s32[]{:S(2)}) async-start(s8[6815744]{0:T(1024)(128)(4,1)} %bitcast.972), calls=%async_computation.3 | async-start | bytes 5242880
  (61 other events, 395.6 us)
where the time goes:
time: 952 us; the launch traced here: 944 us
  local copies, waits for them, and re-layouts  427 us (45%)
  waiting for transfers between devices  324 us (34%)
  matrix products  123 us (13%)
  blocking collectives  40.2 us (4%)
  other arithmetic  17.7 us (2%)
    ppermute x4, waiting for transfers between devices, passed_along(): lax.ppermute(shard, axis, [(i, (i + by) % peers) for i in range(peers)])  324 us
    unnamed x459, local copies, waits for them, and re-layouts  267 us
    dot_general x14, matrix products, square_all(): jnp.einsum('lak,lkc->lac', left_stack, right_stack, precision=lax.Precisi...  123 us
    squeeze x41, local copies, waits for them, and re-layouts, fetch_block(): return blocks_in[cell_at[2], slot_list.index(slot_id)]  77.1 us
    psum x1, blocking collectives, shards(): trace_one, trace_two = lax.psum((trace_one, diag_trace), ('row', 'col'))  40.2 us
    transpose x16, local copies, waits for them, and re-layouts, oriented(): return jnp.swapaxes(block, 0, 1) if flipped else block  27.1 us
  transfers between devices with their start and end apart: 4, of which 3 were waited for; matrix products, arithmetic and copies ran while one was open for 16% of the time, Pallas kernels for 0%

commit v1 on v0

v1 whole, which is shorter than its diff:
```python
import functools

import jax
import jax.numpy as jnp
from jax import lax
from jax.experimental import pallas as pl
from jax.experimental.pallas import tpu as pltpu
from jax.sharding import PartitionSpec as P


F32 = jnp.float32
BF16 = jnp.bfloat16
NN = ((1,), (0,))
NT = ((1,), (1,))
TN = ((0,), (0,))
IN_PLANE = {"C": (0, 0), "N": (0, 1), "S": (1, -1), "E": (1, 0), "D": (1, 1)}


def offset_list():
    steps = (-1, 0, 1)
    return [(i, j, k) for i in steps for j in steps for k in steps if (i, j, k) > (0, 0, 0)]


def slot_number(offset):
    return offset_list().index(offset) + 1


def panel_blocks(name, layers):
    side = IN_PLANE[name]
    found = []
    for low in range(layers):
        for high in range(layers):
            step = high - low
            if abs(step) <= 1 and (*side, step) > (0, 0, 0):
                found.append((low, high, slot_number((*side, step))))
    return found


def sym_rows(layers, size):
    return (layers * (layers - 1) // 2 + (layers + 1) // 2) * size + 8 * (layers // 2)


def rows_cols(size):
    return (
        lax.broadcasted_iota(jnp.int32, (size, size), 0),
        lax.broadcasted_iota(jnp.int32, (size, size), 1),
    )


def put_sym(ref, get, layers, size):
    row, col = rows_cols(size)
    at = 0
    for a in range(layers):
        for b in range(a + 1, layers):
            ref[at : at + size, :] = get(a, b)
            at += size
    marks = []
    for a in range(0, layers, 2):
        block = get(a, a)
        if a + 1 < layers:
            other = get(a + 1, a + 1)
            marks.append(jnp.sum(jnp.where(row == col, other, 0.0), axis=0, keepdims=True))
            block = jnp.where(row <= col, block, other)
        ref[at : at + size, :] = block
        at += size
    for mark in marks:
        ref[at : at + 8, :] = jnp.broadcast_to(mark, (8, size))
        at += 8


def take_sym(packed, layers, size):
    row, col = rows_cols(size)
    blocks = {}
    at = 0
    for a in range(layers):
        for b in range(a + 1, layers):
            blocks[a, b] = packed[at : at + size, :]
            at += size
    marks_at = at + (layers + 1) // 2 * size
    for a in range(0, layers, 2):
        block = packed[at : at + size, :]
        at += size
        if a + 1 < layers:
            flipped = block.T
            mark = packed[marks_at : marks_at + 1, :]
            marks_at += 8
            blocks[a, a] = jnp.where(row <= col, block, flipped)
            blocks[a + 1, a + 1] = jnp.where(row == col, mark, jnp.where(row < col, flipped, block))
        else:
            blocks[a, a] = block
    return blocks


def whole_sym(blocks, layers):
    rows = []
    for a in range(layers):
        rows.append(
            jnp.concatenate(
                [blocks[a, b] if a <= b else blocks[b, a].T for b in range(layers)], axis=1
            )
        )
    return jnp.concatenate(rows, axis=0)


def split(value):
    high = value.astype(BF16)
    return high, (value - high.astype(F32)).astype(BF16)


def dot3(a, b, dims):
    go = functools.partial(lax.dot_general, dimension_numbers=(dims, ((), ())), preferred_element_type=F32)
    return go(a[0], b[0]) + (go(a[0], b[1]) + go(a[1], b[0]))


def cut(pair, at, size):
    return tuple(part[at : at + size, :] for part in pair)


def sym_product(pair, layers, size, dims):
    blocks = {}
    for a in range(layers):
        if dims == NT:
            left = tuple(part[a * size : (a + 1) * size, :] for part in pair)
            right = tuple(part[a * size :, :] for part in pair)
        else:
            left = tuple(part[:, a * size : (a + 1) * size] for part in pair)
            right = tuple(part[:, a * size :] for part in pair)
        strip = dot3(left, right, dims)
        for b in range(a, layers):
            blocks[a, b] = strip[:, (b - a) * size : (b - a + 1) * size]
    return blocks


def kept(mask_ref, layer, slot):
    return mask_ref[layer, slot - 1] > 0


def load_panel(out_ref, held, first, name, layers, size, mask_ref, flip=False):
    blocks = panel_blocks(name, layers)
    if layers > 2 or name == "C":
        out_ref[...] = jnp.zeros(out_ref.shape, F32)
    for k, (low, high, slot) in enumerate(blocks):
        value = jnp.where(kept(mask_ref, low, slot), held[first + k], 0.0)
        if flip:
            low, high, value = high, low, value.T
        out_ref[low * size : (low + 1) * size, high * size : (high + 1) * size] = value
    return len(blocks)


def start_loads(stored_ref, held, sems, wanted):
    copies = [
        pltpu.make_async_copy(stored_ref.at[low, slot], held.at[k], sems.at[k])
        for k, (low, slot) in enumerate(wanted)
    ]
    for copy in copies:
        copy.start()
    return copies


def pack_t_wanted(layers):
    return (
        [(low, slot) for low, _, slot in panel_blocks("N", layers)]
        + [(layer, 0) for layer in range(layers)]
        + [(low, slot) for low, _, slot in panel_blocks("C", layers)]
    )


def pack_t_body(layers, size, mask_ref, stored_ref, onsite_ref, n_ref, packed_ref, c_ref, held, sems):
    for copy in start_loads(stored_ref, held, sems, pack_t_wanted(layers)):
        copy.wait()
    at = load_panel(n_ref, held, 0, "N", layers, size, mask_ref)
    row, col = rows_cols(size)
    c_ref[...] = jnp.zeros(c_ref.shape, F32)
    for layer in range(layers):
        block = held[at + layer]
        block = 0.5 * (block + block.T) + jnp.where(row == col, onsite_ref[layer : layer + 1, :], 0.0)
        c_ref[layer * size : (layer + 1) * size, layer * size : (layer + 1) * size] = block
    at += layers
    for k, (low, high, slot) in enumerate(panel_blocks("C", layers)):
        block = jnp.where(kept(mask_ref, low, slot), held[at + k], 0.0)
        c_ref[low * size : (low + 1) * size, high * size : (high + 1) * size] = block
        c_ref[high * size : (high + 1) * size, low * size : (low + 1) * size] = block.T
    put_sym(
        packed_ref,
        lambda a, b: c_ref[a * size : (a + 1) * size, b * size : (b + 1) * size],
        layers,
        size,
    )


def pack_e_wanted(layers):
    return [(low, slot) for name in "SED" for low, _, slot in panel_blocks(name, layers)]


def pack_e_body(layers, size, mask_ref, stored_ref, st_ref, e_ref, d_ref, held, sems):
    for copy in start_loads(stored_ref, held, sems, pack_e_wanted(layers)):
        copy.wait()
    at = load_panel(st_ref, held, 0, "S", layers, size, mask_ref, flip=True)
    at += load_panel(e_ref, held, at, "E", layers, size, mask_ref)
    load_panel(d_ref, held, at, "D", layers, size, mask_ref)


def up_body(layers, size, n_ref, d_ref, gc_ref, yc_ref):
    for panel, out_ref in ((d_ref, gc_ref), (n_ref, yc_ref)):
        blocks = sym_product(split(panel[...]), layers, size, TN)
        put_sym(out_ref, lambda a, b: blocks[a, b], layers, size)


def local_g_body(layers, size, n_ref, e_ref, d_ref, gc_ref, gn_ref, rs_ref, re_ref):
    n, e, d = split(n_ref[...]), split(e_ref[...]), split(d_ref[...])
    blocks = sym_product(e, layers, size, TN)
    put_sym(gc_ref, lambda a, b: blocks[a, b], layers, size)
    gn_ref[...] = dot3(e, d, TN)
    rs_ref[...] = dot3(n, e, TN)
    re_ref[...] = dot3(n, d, TN)


def local_y_body(
    layers, size, c_ref, n_ref, st_ref, e_ref, d_ref, yc_ref, yn_ref, ys_ref, ye_ref, yd_ref, sums_ref
):
    row, col = rows_cols(c_ref.shape[0])
    c_now = c_ref[...]
    trace = jnp.sum(jnp.where(row == col, c_now, 0.0))
    squares = jnp.sum(c_now * c_now)
    for ref in (n_ref, st_ref, e_ref, d_ref):
        value = ref[...]
        squares = squares + 2.0 * jnp.sum(value * value)
    line = lax.broadcasted_iota(jnp.int32, sums_ref.shape, 0)
    sums_ref[...] = jnp.where(line == 0, trace, squares)
    c, n, st, e, d = (split(ref[...]) for ref in (c_ref, n_ref, st_ref, e_ref, d_ref))
    yn_ref[...] = dot3(c, n, NN)
    ys_ref[...] = dot3(c, st, NT)
    ye_ref[...] = dot3(c, e, NN)
    yd_ref[...] = dot3(c, d, NN)
    terms = [
        sym_product(pair, layers, size, dims)
        for pair, dims in ((c, NT), (n, NT), (st, TN), (e, NT), (d, NT))
    ]
    put_sym(yc_ref, lambda a, b: sum(term[a, b] for term in terms), layers, size)


def g_body(layers, size, gc0_ref, gn0_ref, stu_ref, eu_ref, up_ref, gc_ref, gn_ref):
    stu, eu = split(stu_ref[...]), split(eu_ref[...])
    blocks = sym_product(stu, layers, size, NT)
    put_sym(gc_ref, lambda a, b: blocks[a, b], layers, size)
    gc_ref[...] += gc0_ref[...] + up_ref[...]
    gn_ref[...] = gn0_ref[...] + dot3(stu, eu, NN)


def r_body(layers, size, rs0_ref, re0_ref, stu_ref, eu_ref, cx_ref, nx_ref, rs_ref, re_ref):
    su, eu, nx = split(stu_ref[...].T), split(eu_ref[...]), split(nx_ref[...])
    cx = split(whole_sym(take_sym(cx_ref, layers, size), layers))
    rs_ref[...] = rs0_ref[...] + dot3(su, cx, NN) + dot3(eu, nx, NT)
    re_ref[...] = re0_ref[...] + dot3(su, nx, NN)


def middle_body(
    layers, size, n_ref, e_ref, d_ref, stu_ref, eu_ref, cu_ref, cx_ref, nx_ref, yn0_ref, ye0_ref, yd0_ref,
    yn_ref, ye_ref, yd_ref,
):
    n, e, d = split(n_ref[...]), split(e_ref[...]), split(d_ref[...])
    stu, eu, nx = split(stu_ref[...]), split(eu_ref[...]), split(nx_ref[...])
    cu = split(whole_sym(take_sym(cu_ref, layers, size), layers))
    yn_ref[...] = yn0_ref[...] + dot3(n, cu, NN) + dot3(e, stu, NN) + dot3(d, eu, NT)
    cx = split(whole_sym(take_sym(cx_ref, layers, size), layers))
    ye_ref[...] = ye0_ref[...] + dot3(n, stu, NT) + dot3(e, cx, NN) + dot3(d, nx, NT)
    yd_ref[...] = yd0_ref[...] + dot3(n, eu, NN) + dot3(e, nx, NN)


def last_body(
    layers, size, mask_ref, h_ref, c_ref, n_ref, st_ref, e_ref, d_ref,
    yc_ref, yn_ref, ys_ref, ye_ref, yd_ref, cxu_ref, ycu_ref, gc_ref, gn_ref, rs_ref, re_ref, out_ref,
):
    twice = 2.0 * h_ref[0]
    slots = out_ref.shape[1]

    def mixed(y, a):
        return y + twice * (a - y)

    c_blocks = take_sym(yc_ref[...] + ycu_ref[...] + gc_ref[...], layers, size)
    done = set()
    for layer in range(layers):
        here = slice(layer * size, (layer + 1) * size)
        out_ref[layer, 0] = mixed(c_blocks[layer, layer], c_ref[here, here])
        done.add((layer, 0))
    for low, high, slot in panel_blocks("C", layers):
        a = c_ref[low * size : (low + 1) * size, high * size : (high + 1) * size]
        out_ref[low, slot] = jnp.where(kept(mask_ref, low, slot), mixed(c_blocks[low, high], a), 0.0)
        done.add((low, slot))
    cxu = split(whole_sym(take_sym(cxu_ref, layers, size), layers))
    yd_ref[...] += dot3(split(d_ref[...]), cxu, NN)
    for name, a_ref, terms in (
        ("N", n_ref, (yn_ref, gn_ref)),
        ("S", st_ref, (ys_ref, rs_ref)),
        ("E", e_ref, (ye_ref, re_ref)),
        ("D", d_ref, (yd_ref,)),
    ):
        for low, high, slot in panel_blocks(name, layers):
            rows, cols = slice(low * size, (low + 1) * size), slice(high * size, (high + 1) * size)
            y = sum(ref[rows, cols] for ref in terms)
            a = a_ref[cols, rows].T if name == "S" else a_ref[rows, cols]
            out_ref[low, slot] = jnp.where(kept(mask_ref, low, slot), mixed(y, a), 0.0)
            done.add((low, slot))
    for layer in range(layers):
        for slot in range(slots):
            if (layer, slot) not in done:
                out_ref[layer, slot] = jnp.zeros((size, size), F32)


def call(body, layers, size, outs, spaces, products, scratch=(), limit=40):
    n = layers * size
    return pl.pallas_call(
        functools.partial(body, layers, size),
        out_shape=[jax.ShapeDtypeStruct(shape, F32) for shape in outs],
        in_specs=[pl.BlockSpec(memory_space=space) for space in spaces],
        out_specs=[pl.BlockSpec(memory_space=pltpu.VMEM)] * len(outs),
        scratch_shapes=list(scratch),
        compiler_params=pltpu.CompilerParams(vmem_limit_bytes=limit << 20),
        cost_estimate=pl.CostEstimate(
            flops=int(products * 6 * n**3), bytes_accessed=4 * n * n * (len(outs) + len(spaces)), transcendentals=0
        ),
    )


def passed_along(value, axis, by):
    peers = lax.axis_size(axis)
    return lax.ppermute(value, axis, [(i, (i + by) % peers) for i in range(peers)])


def summed(value, axis):
    peers = lax.axis_size(axis)
    if peers & (peers - 1):
        return value + sum(passed_along(value, axis, by) for by in range(1, peers))
    by = 1
    while by < peers:
        value = value + passed_along(value, axis, by)
        by *= 2
    return value


def shards(stored_blocks, onsite, bond_mask):
    stored, onsite, mask = stored_blocks[0, 0], onsite[0, 0], bond_mask[0, 0]
    layers, slots, size = stored.shape[:3]
    n = layers * size
    panel, packed = (n, n), (sym_rows(layers, size), size)
    vmem, smem, anywhere = pltpu.VMEM, pltpu.SMEM, pl.ANY

    def loads(count):
        return [pltpu.VMEM((count, size, size), F32), pltpu.SemaphoreType.DMA((count,))]

    go = functools.partial(call, layers=layers, size=size)
    N, Cp, C = go(
        pack_t_body, outs=[panel, packed, panel], spaces=[smem, anywhere, vmem], products=0.1,
        scratch=loads(len(pack_t_wanted(layers))), limit=16,
    )(mask, stored, onsite)
    N_x, Cp_x = passed_along(N, "row", -1), passed_along(Cp, "row", -1)
    St, E, D = go(
        pack_e_body, outs=[panel] * 3, spaces=[smem, anywhere], products=0.1,
        scratch=loads(len(pack_e_wanted(layers))), limit=16,
    )(mask, stored)
    St_u, E_u, Cp_u = (passed_along(value, "col", -1) for value in (St, E, Cp))
    gc_up, yc_up = go(up_body, outs=[packed] * 2, spaces=[vmem] * 2, products=2, limit=16)(N, D)
    gc_up, yc_up = passed_along(gc_up, "col", 1), passed_along(yc_up, "col", 1)
    gc, gn, rs, re = go(local_g_body, outs=[packed, panel, panel, panel], spaces=[vmem] * 3, products=4, limit=24)(N, E, D)
    yc, yn, ys, ye, yd, sums = go(
        local_y_body, outs=[packed] + [panel] * 4 + [(8, 128)], spaces=[vmem] * 5, products=8
    )(C, N, St, E, D)
    sums = summed(summed(sums, "row"), "col")
    gc, gn = go(g_body, outs=[packed, panel], spaces=[vmem] * 5, products=2, limit=24)(gc, gn, St_u, E_u, gc_up)
    gc, gn = passed_along(gc, "row", 1), passed_along(gn, "row", 1)
    Cp_xu = passed_along(Cp_x, "col", -1)
    rs, re = go(r_body, outs=[panel] * 2, spaces=[vmem] * 6, products=3, limit=24)(rs, re, St_u, E_u, Cp_x, N_x)
    rs, re = passed_along(rs, "col", 1), passed_along(re, "col", 1)
    yn, ye, yd = go(middle_body, outs=[panel] * 3, spaces=[vmem] * 11, products=8)(
        N, E, D, St_u, E_u, Cp_u, Cp_x, N_x, yn, ye, yd
    )
    cells = lax.axis_size("row") * lax.axis_size("col") * layers
    target = float(cells * size // 2)
    t1, t2 = sums[0, 0], sums[1, 0]
    steering = jax.nn.sigmoid((jnp.abs(t2 - target) - jnp.abs(2.0 * t1 - t2 - target)) / size)
    (out,) = go(last_body, outs=[(layers, slots, size, size)], spaces=[smem] * 2 + [vmem] * 16, products=1, limit=56)(
        mask, steering[None], C, N, St, E, D, yc, yn, ys, ye, yd, Cp_xu, yc_up, gc, gn, rs, re
    )
    return out[None, None]


def solution(mesh):
    in_specs = (
        P("row", "col", None, None, None, None),
        P("row", "col", None, None),
        P("row", "col", None, None),
    )
    out_specs = P("row", "col", None, None, None, None)
    return jax.shard_map(shards, mesh=mesh, in_specs=in_specs, out_specs=out_specs, check_vma=False)
```

time: 952 us -> 125 us (0.13)
  local copies, waits for them, and re-layouts: 427 us -> 9.19 us
  waiting for transfers between devices: 324 us -> 56.8 us
  matrix products: 123 us -> 0 us
  blocking collectives: 40.2 us -> 0 us
  Pallas kernels: 0 us -> 35.7 us
  other arithmetic: 17.7 us -> 0.02 us
  starting transfers between devices: 8.02 us -> 20.6 us
    ppermute x4 -> x17, waiting for transfers between devices: 324 us -> 56.8 us  [passed_along(): lax.ppermute(value, axis, [(i, (i + by) % peers) for i in range(peers)])]
    unnamed x459 -> x38, local copies, waits for them, and re-layouts: 267 us -> 8.65 us
    dot_general x14 -> x0, matrix products: 123 us -> none  [square_all(): jnp.einsum('lak,lkc->lac', left_stack, right_stack, precision=lax.Precisi...]
    squeeze x43 -> x0, local copies, waits for them, and re-layouts: 78.3 us -> none  [the longest x41 77.1 us: fetch_block(): return blocks_in[cell_at[2], slot_list.index(slot_id)]]
    psum x1 -> x0, blocking collectives: 40.2 us -> none  [shards(): trace_one, trace_two = lax.psum((trace_one, diag_trace), ('row', 'col'))]
    concatenate x25 -> x0, local copies, waits for them, and re-layouts: 38.3 us -> none  [the longest x3 18.1 us: second_payload(): return (jnp.concatenate(pieces, axis=1), layout)]
    pallas_call x0 -> x9, Pallas kernels: none -> 35.7 us  [the longest x1 10.5 us: shards(): go(last_body, outs=[(layers, slots, size, size)], spaces=[smem] * 2 + [vm...]
    transpose x16 -> x0, local copies, waits for them, and re-layouts: 27.1 us -> none  [oriented(): return jnp.swapaxes(block, 0, 1) if flipped else block]
  transfers between devices with their start and end apart: 4 -> 17, of which waited for: 3 -> 8; matrix products, arithmetic and copies ran while one was open for 16% -> 0% of each run, Pallas kernels for 0% -> 19%
where the time goes in v1:
time: 125 us
  waiting for transfers between devices  56.8 us (45%)
  Pallas kernels  35.7 us (29%)
  starting transfers between devices  20.6 us (16%)
  local copies, waits for them, and re-layouts  9.19 us (7%)
  between operations  2.25 us (2%)
    ppermute x17, waiting for transfers between devices, passed_along(): lax.ppermute(value, axis, [(i, (i + by) % peers) for i in range(peers)])  56.8 us
    ppermute x17, starting transfers between devices, passed_along(): lax.ppermute(value, axis, [(i, (i + by) % peers) for i in range(peers)])  20.6 us
    pallas_call x1, Pallas kernels, shards(): go(last_body, outs=[(layers, slots, size, size)], spaces=[smem] * 2 + [vm...  10.5 us
    unnamed x38, local copies, waits for them, and re-layouts  8.65 us
    pallas_call x1, Pallas kernels, shards(): go(middle_body, outs=[panel] * 3, spaces=[vmem] * 11, products=8)  6.84 us
    pallas_call x1, Pallas kernels, shards(): go(local_y_body, outs=[packed] + [panel] * 4 + [(8, 128)], spaces=[vmem]...  6.72 us
    pallas_call x1, Pallas kernels, shards(): go(local_g_body, outs=[packed, panel, panel, panel], spaces=[vmem] * 3, p...  3.28 us
    pallas_call x1, Pallas kernels, shards(): go(r_body, outs=[panel] * 2, spaces=[vmem] * 6, products=3, limit=24)  2.84 us
  transfers between devices with their start and end apart: 17, of which 8 were waited for; matrix products, arithmetic and copies ran while one was open for 0% of the time, Pallas kernels for 19%

profile of v1, /device:TPU:0, one launch (start us, length us, event | category | flops | bytes accessed | tf_op | source)
XLA Modules:
  0.0 124.7 jit_solution(12364742401650476561)
XLA Ops:
  0.0 3.1 %copy-done = f32[1,1,2,14,256,256]{5,4,3,2,1,0:T(8,128)S(1)} copy-done((f32[1,1,2,14,256,256]{5,4,3,2,1,0:T(8,128)S(1)}, f32[1,1,2,14,256,256]{5,4,3,2,1,0:T(8,128)}, u32[]{:S(2)}) %copy-start) | copy-done | bytes 7340056
  3.1 0.7 copy-done.11
  3.8 1.4 %shard_map.38 = (f32[512,512]{1,0:T(8,128)S(1)}, f32[512,512]{1,0:T(8,128)S(1)}, f32[512,512]{1,0:T(8,128)S(1)}) custom-call(s32[2,13]{1,0:T(2,128)S(1)} %bitcast.8, f32[2,14,256,256]{3,2,1,0:T(8,128)S(1)} %bitcast.5), custom_call_target="tpu_custom_call" | custom-call | flops 80530640 | bytes 5242880 | tf_op jit(solution)/shard_map/pallas_call | solution.py:357
  5.2 3.4 %collective-permute-start.6 = (f32[512,512]{1,0:T(8,128)S(1)}, f32[512,512]{1,0:T(8,128)S(1)}, u32[]{:S(2)}, u32[]{:S(2)}) collective-permute-start(f32[512,512]{1,0:T(8,128)S(1)} %get-tuple-element.33.e_ref), channel_id=1, source_target_pairs={{0,7},{1,0},{2,1},{3,2},{4,3},{5,4},{6,5},{7,6},{8,15},{9,8},{10,9... | collective-permute-start | bytes 3145736 | tf_op jit(solution)/shard_map/ppermute | solution.py:327
  8.6 1.1 shard_map.37
  9.7 3.7 %collective-permute-start.9 = (f32[512,512]{1,0:T(8,128)S(1)}, f32[512,512]{1,0:T(8,128)S(1)}, u32[]{:S(2)}, u32[]{:S(2)}) collective-permute-start(f32[512,512]{1,0:T(8,128)S(1)} %get-tuple-element.31.n_ref), channel_id=1, source_target_pairs={{0,24},{8,0},{16,8},{24,16},{1,25},{9,1},{17,9},{25,17},{2,26},{10... | collective-permute-start | bytes 3145736 | tf_op jit(solution)/shard_map/ppermute | solution.py:327
  14.2 6.7 %shard_map.39 = (f32[520,256]{1,0:T(8,128)S(1)}, f32[512,512]{1,0:T(8,128)S(1)}, f32[512,512]{1,0:T(8,128)S(1)}, f32[512,512]{1,0:T(8,128)S(1)}, f32[512,512]{1,0:T(8,128)S(1)}, /*index=5*/f32[8,128]{1,0:T(8,128)S(1)}) custom-call(f32[512,512]{1,0:T(8,128)S(1)} %get-tuple-element.30.c_ref, f32[512,512]{1,0:T(8,128)S(1)} %get-tuple-element.31.n_ref, ...), custom_call_target="tpu_custom_call" | custom-call | flops 6442450944 | bytes 11534336 | tf_op jit(solution)/shard_map/pallas_call | solution.py:365
  21.0 1.6 %collective-permute-start = (f32[8,128]{1,0:T(8,128)S(1)}, f32[8,128]{1,0:T(8,128)S(1)}, u32[]{:S(2)}, u32[]{:S(2)}) collective-permute-start(f32[8,128]{1,0:T(8,128)S(1)} %get-tuple-element.35), channel_id=1, source_target_pairs={{0,8},{8,16},{16,24},{24,0},{1,9},{9,17},{17,25},{25,1},{2,10},{10... | collective-permute-start | bytes 12296 | tf_op jit(solution)/shard_map/ppermute | solution.py:327
  22.6 24.4 %collective-permute-done = f32[8,128]{1,0:T(8,128)S(1)} collective-permute-done((f32[8,128]{1,0:T(8,128)S(1)}, f32[8,128]{1,0:T(8,128)S(1)}, u32[]{:S(2)}, u32[]{:S(2)}) %collective-permute-start) | collective-permute-done | bytes 4128 | tf_op jit(solution)/shard_map/ppermute | solution.py:327
  47.0 4.5 %collective-permute-done.1 = f32[8,128]{1,0:T(8,128)S(1)} collective-permute-done((f32[8,128]{1,0:T(8,128)S(1)}, f32[8,128]{1,0:T(8,128)S(1)}, u32[]{:S(2)}, u32[]{:S(2)}) %collective-permute-start.1) | collective-permute-done | bytes 4128 | tf_op jit(solution)/shard_map/ppermute | solution.py:327
  51.5 3.9 %collective-permute-done.2 = f32[8,128]{1,0:T(8,128)S(1)} collective-permute-done((f32[8,128]{1,0:T(8,128)S(1)}, f32[8,128]{1,0:T(8,128)S(1)}, u32[]{:S(2)}, u32[]{:S(2)}) %collective-permute-start.2) | collective-permute-done | bytes 4128 | tf_op jit(solution)/shard_map/ppermute | solution.py:327
  55.4 0.6 collective-permute-start.3
  56.0 1.4 %shard_map.41 = (f32[520,256]{1,0:T(8,128)S(1)}, f32[520,256]{1,0:T(8,128)S(1)}) custom-call(f32[512,512]{1,0:T(8,128)S(1)} %get-tuple-element.31.n_ref, f32[512,512]{1,0:T(8,128)S(1)} %get-tuple-element.34.d_ref), custom_call_target="tpu_custom_call" | custom-call | flops 1610612736 | bytes 4194304 | tf_op jit(solution)/shard_map/pallas_call | solution.py:362
  57.5 2.5 %collective-permute-done.3 = f32[8,128]{1,0:T(8,128)S(1)} collective-permute-done((f32[8,128]{1,0:T(8,128)S(1)}, f32[8,128]{1,0:T(8,128)S(1)}, u32[]{:S(2)}, u32[]{:S(2)}) %collective-permute-start.3) | collective-permute-done | bytes 4128 | tf_op jit(solution)/shard_map/ppermute | solution.py:327
  59.9 3.3 %shard_map.42 = (f32[520,256]{1,0:T(8,128)S(1)}, f32[512,512]{1,0:T(8,128)S(1)}, f32[512,512]{1,0:T(8,128)S(1)}, f32[512,512]{1,0:T(8,128)S(1)}) custom-call(f32[512,512]{1,0:T(8,128)S(1)} %get-tuple-element.31.n_ref, f32[512,512]{1,0:T(8,128)S(1)} %get-tuple-element.33.e_ref, f32[512,512]{1,0:T(8,128)S(1)} %get-tuple-element.34.d_ref), custom_call_target="tpu_custom_call" | custom-call | flops 3221225472 | bytes 7340032 | tf_op jit(solution)/shard_map/pallas_call | solution.py:364
  63.3 2.7 %collective-permute-start.7 = (f32[520,256]{1,0:T(8,128)S(1)}, f32[520,256]{1,0:T(8,128)S(1)}, u32[]{:S(2)}, u32[]{:S(2)}) collective-permute-start(f32[520,256]{1,0:T(8,128)S(1)} %get-tuple-element.37), channel_id=1, source_target_pairs={{0,7},{1,0},{2,1},{3,2},{4,3},{5,4},{6,5},{7,6},{8,15},{9,8},{10,9... | collective-permute-start | bytes 1597448 | tf_op jit(solution)/shard_map/ppermute | solution.py:327
  66.0 1.6 %collective-permute-start.4 = (f32[8,128]{1,0:T(8,128)S(1)}, f32[8,128]{1,0:T(8,128)S(1)}, u32[]{:S(2)}, u32[]{:S(2)}) collective-permute-start(f32[8,128]{1,0:T(8,128)S(1)} %add.25), channel_id=1, source_target_pairs={{0,4},{1,5},{2,6},{3,7},{4,0},{5,1},{6,2},{7,3},{8,12},{9,13},{10,... | collective-permute-start | bytes 12296 | tf_op jit(solution)/shard_map/ppermute | solution.py:327
  67.6 2.8 %shard_map.44 = (f32[512,512]{1,0:T(8,128)S(1)}, f32[512,512]{1,0:T(8,128)S(1)}) custom-call(f32[512,512]{1,0:T(8,128)S(1)} %get-tuple-element.51.rs0_ref, f32[512,512]{1,0:T(8,128)S(1)} %get-tuple-element.52.re0_ref, f32[512,512]{1,0:T(8,128)S(1)} %collective-permute-done.5.stu_ref, f32[512,512]{1,0:T(8,128)S(1)} %collective-permute-done.6.eu_ref, ...), custom_call_target="tpu_custom_call" | custom-call | flops 2415919104 | bytes 8388608 | tf_op jit(solution)/shard_map/pallas_call | solution.py:372
  70.5 1.3 %collective-permute-done.12.up_ref = f32[520,256]{1,0:T(8,128)S(1)} collective-permute-done((f32[520,256]{1,0:T(8,128)S(1)}, f32[520,256]{1,0:T(8,128)S(1)}, u32[]{:S(2)}, u32[]{:S(2)}) %collective-permute-start.12) | collective-permute-done | bytes 532512 | tf_op jit(solution)/shard_map/ppermute | solution.py:327
  71.8 1.7 %shard_map.43 = (f32[520,256]{1,0:T(8,128)S(1)}, f32[512,512]{1,0:T(8,128)S(1)}) custom-call(f32[520,256]{1,0:T(8,128)S(1)} %get-tuple-element.46.gc0_ref, f32[512,512]{1,0:T(8,128)S(1)} %get-tuple-element.47.gn0_ref, f32[512,512]{1,0:T(8,128)S(1)} %collective-permute-done.5.stu_ref, f32[512,512]{1,0:T(8,128)S(1)} %collective-permute-done.6.eu_ref, ...), custom_call_target="tpu_custom_call" | custom-call | flops 1610612736 | bytes 7340032 | tf_op jit(solution)/shard_map/pallas_call | solution.py:369
  73.4 1.7 %collective-permute-start.14 = (f32[512,512]{1,0:T(8,128)S(1)}, f32[512,512]{1,0:T(8,128)S(1)}, u32[]{:S(2)}, u32[]{:S(2)}) collective-permute-start(f32[512,512]{1,0:T(8,128)S(1)} %get-tuple-element.50), channel_id=1, source_target_pairs={{0,8},{8,16},{16,24},{24,0},{1,9},{9,17},{17,25},{25,1},{2,10},{10... | collective-permute-start | bytes 3145736 | tf_op jit(solution)/shard_map/ppermute | solution.py:327
  77.7 0.8 collective-permute-done.7.cu_ref
  78.5 3.1 %collective-permute-start.10 = (f32[520,256]{1,0:T(8,128)S(1)}, f32[520,256]{1,0:T(8,128)S(1)}, u32[]{:S(2)}, u32[]{:S(2)}) collective-permute-start(f32[520,256]{1,0:T(8,128)S(1)} %collective-permute-done.8.cx_ref), channel_id=1, source_target_pairs={{0,7},{1,0},{2,1},{3,2},{4,3},{5,4},{6,5},{7,6},{8,15},{9,8},{10,9... | collective-permute-start | bytes 1597448 | tf_op jit(solution)/shard_map/ppermute | solution.py:327
  81.6 1.4 %collective-permute-start.13 = (f32[520,256]{1,0:T(8,128)S(1)}, f32[520,256]{1,0:T(8,128)S(1)}, u32[]{:S(2)}, u32[]{:S(2)}) collective-permute-start(f32[520,256]{1,0:T(8,128)S(1)} %get-tuple-element.49), channel_id=1, source_target_pairs={{0,8},{8,16},{16,24},{24,0},{1,9},{9,17},{17,25},{25,1},{2,10},{10... | collective-permute-start | bytes 1597448 | tf_op jit(solution)/shard_map/ppermute | solution.py:327
  83.0 6.8 %shard_map.40 = (f32[512,512]{1,0:T(8,128)S(1)}, f32[512,512]{1,0:T(8,128)S(1)}, f32[512,512]{1,0:T(8,128)S(1)}) custom-call(f32[512,512]{1,0:T(8,128)S(1)} %get-tuple-element.31.n_ref, f32[512,512]{1,0:T(8,128)S(1)} %get-tuple-element.33.e_ref, f32[512,512]{1,0:T(8,128)S(1)} %get-tuple-element.34.d_ref, f32[512,512]{1,0:T(8,128)S(1)} %collective-permute-done.5.stu_ref, ...), custom_call_target="tpu_custom_call" | custom-call | flops 6442450944 | bytes 14680064 | tf_op jit(solution)/shard_map/pallas_call | solution.py:374
  89.9 1.0 copy-done.7
  90.8 1.1 copy-done.8
  91.9 1.0 copy-done.9
  92.9 1.3 %collective-permute-done.10.cxu_ref = f32[520,256]{1,0:T(8,128)S(1)} collective-permute-done((f32[520,256]{1,0:T(8,128)S(1)}, f32[520,256]{1,0:T(8,128)S(1)}, u32[]{:S(2)}, u32[]{:S(2)}) %collective-permute-start.10) | collective-permute-done | bytes 532512 | tf_op jit(solution)/shard_map/ppermute | solution.py:327
  94.2 18.2 %collective-permute-done.13.gc_ref = f32[520,256]{1,0:T(8,128)S(1)} collective-permute-done((f32[520,256]{1,0:T(8,128)S(1)}, f32[520,256]{1,0:T(8,128)S(1)}, u32[]{:S(2)}, u32[]{:S(2)}) %collective-permute-start.13) | collective-permute-done | bytes 532512 | tf_op jit(solution)/shard_map/ppermute | solution.py:327
  112.4 1.0 copy-done.15
  114.2 10.5 %shard_map.45 = f32[2,14,256,256]{3,2,1,0:T(8,128)} custom-call(s32[2,13]{1,0:T(2,128)} %bitcast.7, f32[1]{0:T(128)} %bitcast.3.h_ref, f32[512,512]{1,0:T(8,128)} %copy-done.5, f32[512,512]{1,0:T(8,128)} %copy-done.4, f32[512,512]{1,0:T(8,128)} %copy-done.1, f32[512,512]{1,0:T(8,128)} %copy-done.2, f32[512,512]{1,0:T(8,128)} %copy-done.3, ...), custom_call_target="tpu_custom_call" | custom-call | flops 805306368 | bytes 19922944 | tf_op jit(solution)/shard_map/pallas_call | solution.py:381
  (55 shorter events, 2.3 us)
Async XLA Ops:
  0.0 8.6 %copy-start.12 = (f32[1,1,2,256]{3,2,1,0:T(2,128)S(1)}, f32[1,1,2,256]{3,2,1,0:T(2,128)}, u32[]{:S(2)}) copy-start(f32[1,1,2,256]{3,2,1,0:T(2,128)} %param.4) | copy-start | bytes 6148
  0.0 3.1 %copy-start = (f32[1,1,2,14,256,256]{5,4,3,2,1,0:T(8,128)S(1)}, f32[1,1,2,14,256,256]{5,4,3,2,1,0:T(8,128)}, u32[]{:S(2)}) copy-start(f32[1,1,2,14,256,256]{5,4,3,2,1,0:T(8,128)} %param.3) | copy-start | bytes 22020100
  5.2 15.8 %copy-start.1 = (f32[512,512]{1,0:T(8,128)}, f32[512,512]{1,0:T(8,128)S(1)}, u32[]{:S(2)}) copy-start(f32[512,512]{1,0:T(8,128)S(1)} %get-tuple-element.32.st_ref) | copy-start | bytes 3145732
  5.2 77.8 %copy-start.2 = (f32[512,512]{1,0:T(8,128)}, f32[512,512]{1,0:T(8,128)S(1)}, u32[]{:S(2)}) copy-start(f32[512,512]{1,0:T(8,128)S(1)} %get-tuple-element.33.e_ref) | copy-start | bytes 3145732
  5.2 77.8 %copy-start.3 = (f32[512,512]{1,0:T(8,128)}, f32[512,512]{1,0:T(8,128)S(1)}, u32[]{:S(2)}) copy-start(f32[512,512]{1,0:T(8,128)S(1)} %get-tuple-element.34.d_ref) | copy-start | bytes 3145732
  5.2 60.8 %collective-permute-start.6 = (f32[512,512]{1,0:T(8,128)S(1)}, f32[512,512]{1,0:T(8,128)S(1)}, u32[]{:S(2)}, u32[]{:S(2)}) collective-permute-start(f32[512,512]{1,0:T(8,128)S(1)} %get-tuple-element.33.e_ref), channel_id=1, source_target_pairs={{0,7},{1,0},{2,1},{3,2},{4,3},{5,4},{6,5},{7,6},{8,15},{9,8},{10,9... | collective-permute-start | bytes 3145736 | tf_op jit(solution)/shard_map/ppermute | solution.py:327
  9.7 11.3 %copy-start.5 = (f32[512,512]{1,0:T(8,128)}, f32[512,512]{1,0:T(8,128)S(1)}, u32[]{:S(2)}) copy-start(f32[512,512]{1,0:T(8,128)S(1)} %get-tuple-element.30.c_ref) | copy-start | bytes 3145732
  9.7 73.3 %copy-start.4 = (f32[512,512]{1,0:T(8,128)}, f32[512,512]{1,0:T(8,128)S(1)}, u32[]{:S(2)}) copy-start(f32[512,512]{1,0:T(8,128)S(1)} %get-tuple-element.31.n_ref) | copy-start | bytes 3145732
  9.7 56.3 %collective-permute-start.9 = (f32[512,512]{1,0:T(8,128)S(1)}, f32[512,512]{1,0:T(8,128)S(1)}, u32[]{:S(2)}, u32[]{:S(2)}) collective-permute-start(f32[512,512]{1,0:T(8,128)S(1)} %get-tuple-element.31.n_ref), channel_id=1, source_target_pairs={{0,24},{8,0},{16,8},{24,16},{1,25},{9,1},{17,9},{25,17},{2,26},{10... | collective-permute-start | bytes 3145736 | tf_op jit(solution)/shard_map/ppermute | solution.py:327
  13.4 54.2 %collective-permute-start.5 = (f32[512,512]{1,0:T(8,128)S(1)}, f32[512,512]{1,0:T(8,128)S(1)}, u32[]{:S(2)}, u32[]{:S(2)}) collective-permute-start(f32[512,512]{1,0:T(8,128)S(1)} %get-tuple-element.32.st_ref), channel_id=1, source_target_pairs={{0,7},{1,0},{2,1},{3,2},{4,3},{5,4},{6,5},{7,6},{8,15},{9,8},{10,9... | collective-permute-start | bytes 3145736 | tf_op jit(solution)/shard_map/ppermute | solution.py:327
  13.8 49.5 %collective-permute-start.8 = (f32[520,256]{1,0:T(8,128)S(1)}, f32[520,256]{1,0:T(8,128)S(1)}, u32[]{:S(2)}, u32[]{:S(2)}) collective-permute-start(f32[520,256]{1,0:T(8,128)S(1)} %get-tuple-element.37), channel_id=1, source_target_pairs={{0,24},{8,0},{16,8},{24,16},{1,25},{9,1},{17,9},{25,17},{2,26},{10... | collective-permute-start | bytes 1597448 | tf_op jit(solution)/shard_map/ppermute | solution.py:327
  21.0 42.3 %copy-start.6 = (f32[512,512]{1,0:T(8,128)}, f32[512,512]{1,0:T(8,128)S(1)}, u32[]{:S(2)}) copy-start(f32[512,512]{1,0:T(8,128)S(1)} %get-tuple-element.42.ys_ref) | copy-start | bytes 3145732
  21.0 42.3 %copy-start.10 = (f32[520,256]{1,0:T(8,128)}, f32[520,256]{1,0:T(8,128)S(1)}, u32[]{:S(2)}) copy-start(f32[520,256]{1,0:T(8,128)S(1)} %get-tuple-element.36.yc_ref) | copy-start | bytes 1597444
  21.0 26.0 %collective-permute-start = (f32[8,128]{1,0:T(8,128)S(1)}, f32[8,128]{1,0:T(8,128)S(1)}, u32[]{:S(2)}, u32[]{:S(2)}) collective-permute-start(f32[8,128]{1,0:T(8,128)S(1)} %get-tuple-element.35), channel_id=1, source_target_pairs={{0,8},{8,16},{16,24},{24,0},{1,9},{9,17},{17,25},{25,1},{2,10},{10... | collective-permute-start | bytes 12296 | tf_op jit(solution)/shard_map/ppermute | solution.py:327
  47.0 4.5 %collective-permute-start.1 = (f32[8,128]{1,0:T(8,128)S(1)}, f32[8,128]{1,0:T(8,128)S(1)}, u32[]{:S(2)}, u32[]{:S(2)}) collective-permute-start(f32[8,128]{1,0:T(8,128)S(1)} %add.22), channel_id=1, source_target_pairs={{0,16},{8,24},{16,0},{24,8},{1,17},{9,25},{17,1},{25,9},{2,18},{10... | collective-permute-start | bytes 12296 | tf_op jit(solution)/shard_map/ppermute | solution.py:327
  51.5 3.9 %collective-permute-start.2 = (f32[8,128]{1,0:T(8,128)S(1)}, f32[8,128]{1,0:T(8,128)S(1)}, u32[]{:S(2)}, u32[]{:S(2)}) collective-permute-start(f32[8,128]{1,0:T(8,128)S(1)} %add.23), channel_id=1, source_target_pairs={{0,1},{1,2},{2,3},{3,4},{4,5},{5,6},{6,7},{7,0},{8,9},{9,10},{10,1... | collective-permute-start | bytes 12296 | tf_op jit(solution)/shard_map/ppermute | solution.py:327
  55.4 4.5 %collective-permute-start.3 = (f32[8,128]{1,0:T(8,128)S(1)}, f32[8,128]{1,0:T(8,128)S(1)}, u32[]{:S(2)}, u32[]{:S(2)}) collective-permute-start(f32[8,128]{1,0:T(8,128)S(1)} %add.24), channel_id=1, source_target_pairs={{0,2},{1,3},{2,4},{3,5},{4,6},{5,7},{6,0},{7,1},{8,10},{9,11},{10,... | collective-permute-start | bytes 12296 | tf_op jit(solution)/shard_map/ppermute | solution.py:327
  59.9 11.8 %collective-permute-start.12 = (f32[520,256]{1,0:T(8,128)S(1)}, f32[520,256]{1,0:T(8,128)S(1)}, u32[]{:S(2)}, u32[]{:S(2)}) collective-permute-start(f32[520,256]{1,0:T(8,128)S(1)} %get-tuple-element.48), channel_id=1, source_target_pairs={{0,1},{1,2},{2,3},{3,4},{4,5},{5,6},{6,7},{7,0},{8,9},{9,10},{10,1... | collective-permute-start | bytes 1597448 | tf_op jit(solution)/shard_map/ppermute | solution.py:327
  63.3 15.2 %collective-permute-start.7 = (f32[520,256]{1,0:T(8,128)S(1)}, f32[520,256]{1,0:T(8,128)S(1)}, u32[]{:S(2)}, u32[]{:S(2)}) collective-permute-start(f32[520,256]{1,0:T(8,128)S(1)} %get-tuple-element.37), channel_id=1, source_target_pairs={{0,7},{1,0},{2,1},{3,2},{4,3},{5,4},{6,5},{7,6},{8,15},{9,8},{10,9... | collective-permute-start | bytes 1597448 | tf_op jit(solution)/shard_map/ppermute | solution.py:327
  66.0 15.7 %collective-permute-start.11 = (f32[520,256]{1,0:T(8,128)S(1)}, f32[520,256]{1,0:T(8,128)S(1)}, u32[]{:S(2)}, u32[]{:S(2)}) collective-permute-start(f32[520,256]{1,0:T(8,128)S(1)} %get-tuple-element.45), channel_id=1, source_target_pairs={{0,1},{1,2},{2,3},{3,4},{4,5},{5,6},{6,7},{7,0},{8,9},{9,10},{10,1... | collective-permute-start | bytes 1597448 | tf_op jit(solution)/shard_map/ppermute | solution.py:327
  66.0 7.5 %collective-permute-start.4 = (f32[8,128]{1,0:T(8,128)S(1)}, f32[8,128]{1,0:T(8,128)S(1)}, u32[]{:S(2)}, u32[]{:S(2)}) collective-permute-start(f32[8,128]{1,0:T(8,128)S(1)} %add.25), channel_id=1, source_target_pairs={{0,4},{1,5},{2,6},{3,7},{4,0},{5,1},{6,2},{7,3},{8,12},{9,13},{10,... | collective-permute-start | bytes 12296 | tf_op jit(solution)/shard_map/ppermute | solution.py:327
  70.4 41.9 %collective-permute-start.15 = (f32[512,512]{1,0:T(8,128)S(1)}, f32[512,512]{1,0:T(8,128)S(1)}, u32[]{:S(2)}, u32[]{:S(2)}) collective-permute-start(f32[512,512]{1,0:T(8,128)S(1)} %get-tuple-element.53), channel_id=1, source_target_pairs={{0,1},{1,2},{2,3},{3,4},{4,5},{5,6},{6,7},{7,0},{8,9},{9,10},{10,1... | collective-permute-start | bytes 3145736 | tf_op jit(solution)/shard_map/ppermute | solution.py:327
  71.8 40.6 %collective-permute-start.16 = (f32[512,512]{1,0:T(8,128)S(1)}, f32[512,512]{1,0:T(8,128)S(1)}, u32[]{:S(2)}, u32[]{:S(2)}) collective-permute-start(f32[512,512]{1,0:T(8,128)S(1)} %get-tuple-element.54), channel_id=1, source_target_pairs={{0,1},{1,2},{2,3},{3,4},{4,5},{5,6},{6,7},{7,0},{8,9},{9,10},{10,1... | collective-permute-start | bytes 3145736 | tf_op jit(solution)/shard_map/ppermute | solution.py:327
  73.4 38.9 %collective-permute-start.14 = (f32[512,512]{1,0:T(8,128)S(1)}, f32[512,512]{1,0:T(8,128)S(1)}, u32[]{:S(2)}, u32[]{:S(2)}) collective-permute-start(f32[512,512]{1,0:T(8,128)S(1)} %get-tuple-element.50), channel_id=1, source_target_pairs={{0,8},{8,16},{16,24},{24,0},{1,9},{9,17},{17,25},{25,1},{2,10},{10... | collective-permute-start | bytes 3145736 | tf_op jit(solution)/shard_map/ppermute | solution.py:327
  78.5 15.7 %collective-permute-start.10 = (f32[520,256]{1,0:T(8,128)S(1)}, f32[520,256]{1,0:T(8,128)S(1)}, u32[]{:S(2)}, u32[]{:S(2)}) collective-permute-start(f32[520,256]{1,0:T(8,128)S(1)} %collective-permute-done.8.cx_ref), channel_id=1, source_target_pairs={{0,7},{1,0},{2,1},{3,2},{4,3},{5,4},{6,5},{7,6},{8,15},{9,8},{10,9... | collective-permute-start | bytes 1597448 | tf_op jit(solution)/shard_map/ppermute | solution.py:327
  81.6 8.2 %copy-start.16 = (f32[520,256]{1,0:T(8,128)}, f32[520,256]{1,0:T(8,128)S(1)}, u32[]{:S(2)}) copy-start(f32[520,256]{1,0:T(8,128)S(1)} %collective-permute-done.11.ycu_ref) | copy-start | bytes 1597444
  81.6 30.7 %collective-permute-start.13 = (f32[520,256]{1,0:T(8,128)S(1)}, f32[520,256]{1,0:T(8,128)S(1)}, u32[]{:S(2)}, u32[]{:S(2)}) collective-permute-start(f32[520,256]{1,0:T(8,128)S(1)} %get-tuple-element.49), channel_id=1, source_target_pairs={{0,8},{8,16},{16,24},{24,0},{1,9},{9,17},{17,25},{25,1},{2,10},{10... | collective-permute-start | bytes 1597448 | tf_op jit(solution)/shard_map/ppermute | solution.py:327
  90.8 1.1 copy-start.8
  94.2 19.2 %copy-start.17 = (f32[520,256]{1,0:T(8,128)}, f32[520,256]{1,0:T(8,128)S(1)}, u32[]{:S(2)}) copy-start(f32[520,256]{1,0:T(8,128)S(1)} %collective-permute-done.10.cxu_ref) | copy-start | bytes 1597444
  112.3 1.2 copy-start.18
  112.3 1.5 %copy-start.13 = (f32[512,512]{1,0:T(8,128)}, f32[512,512]{1,0:T(8,128)S(1)}, u32[]{:S(2)}) copy-start(f32[512,512]{1,0:T(8,128)S(1)} %collective-permute-done.15.rs_ref) | copy-start | bytes 3145732
  112.3 1.8 %copy-start.14 = (f32[512,512]{1,0:T(8,128)}, f32[512,512]{1,0:T(8,128)S(1)}, u32[]{:S(2)}) copy-start(f32[512,512]{1,0:T(8,128)S(1)} %collective-permute-done.16.re_ref) | copy-start | bytes 3145732
  (4 other events, 3.7 us)

commit v2 on v1

--- a/solution.py
+++ b/solution.py
@@ -165,7 +165,15 @@
     )
 
 
-def pack_t_body(layers, size, mask_ref, stored_ref, onsite_ref, n_ref, packed_ref, c_ref, held, sems):
+def squares_of(refs):
+    total = 0.0
+    for ref in refs:
+        value = ref[...]
+        total = total + jnp.sum(value * value)
+    return total
+
+
+def pack_t_body(layers, size, mask_ref, stored_ref, onsite_ref, n_ref, packed_ref, c_ref, sums_ref, held, sems):
     for copy in start_loads(stored_ref, held, sems, pack_t_wanted(layers)):
         copy.wait()
     at = load_panel(n_ref, held, 0, "N", layers, size, mask_ref)
@@ -186,24 +194,30 @@
         layers,
         size,
     )
+    row, col = rows_cols(c_ref.shape[0])
+    trace = jnp.sum(jnp.where(row == col, c_ref[...], 0.0))
+    squares = squares_of([c_ref]) + 2.0 * squares_of([n_ref])
+    line = lax.broadcasted_iota(jnp.int32, sums_ref.shape, 0)
+    sums_ref[...] = jnp.where(line == 0, trace, squares)
 
 
 def pack_e_wanted(layers):
     return [(low, slot) for name in "SED" for low, _, slot in panel_blocks(name, layers)]
 
 
-def pack_e_body(layers, size, mask_ref, stored_ref, st_ref, e_ref, d_ref, held, sems):
+def pack_e_body(layers, size, mask_ref, stored_ref, before_ref, st_ref, e_ref, d_ref, sums_ref, held, sems):
     for copy in start_loads(stored_ref, held, sems, pack_e_wanted(layers)):
         copy.wait()
     at = load_panel(st_ref, held, 0, "S", layers, size, mask_ref, flip=True)
     at += load_panel(e_ref, held, at, "E", layers, size, mask_ref)
     load_panel(d_ref, held, at, "D", layers, size, mask_ref)
-
-
-def up_body(layers, size, n_ref, d_ref, gc_ref, yc_ref):
-    for panel, out_ref in ((d_ref, gc_ref), (n_ref, yc_ref)):
-        blocks = sym_product(split(panel[...]), layers, size, TN)
-        put_sym(out_ref, lambda a, b: blocks[a, b], layers, size)
+    line = lax.broadcasted_iota(jnp.int32, sums_ref.shape, 0)
+    sums_ref[...] = before_ref[...] + jnp.where(line == 0, 0.0, 2.0 * squares_of([st_ref, e_ref, d_ref]))
+
+
+def own_sym_body(layers, size, panel_ref, out_ref):
+    blocks = sym_product(split(panel_ref[...]), layers, size, TN)
+    put_sym(out_ref, lambda a, b: blocks[a, b], layers, size)
 
 
 def local_g_body(layers, size, n_ref, e_ref, d_ref, gc_ref, gn_ref, rs_ref, re_ref):
@@ -215,18 +229,7 @@
     re_ref[...] = dot3(n, d, TN)
 
 
-def local_y_body(
-    layers, size, c_ref, n_ref, st_ref, e_ref, d_ref, yc_ref, yn_ref, ys_ref, ye_ref, yd_ref, sums_ref
-):
-    row, col = rows_cols(c_ref.shape[0])
-    c_now = c_ref[...]
-    trace = jnp.sum(jnp.where(row == col, c_now, 0.0))
-    squares = jnp.sum(c_now * c_now)
-    for ref in (n_ref, st_ref, e_ref, d_ref):
-        value = ref[...]
-        squares = squares + 2.0 * jnp.sum(value * value)
-    line = lax.broadcasted_iota(jnp.int32, sums_ref.shape, 0)
-    sums_ref[...] = jnp.where(line == 0, trace, squares)
+def local_y_body(layers, size, c_ref, n_ref, st_ref, e_ref, d_ref, yc_ref, yn_ref, ys_ref, ye_ref, yd_ref):
     c, n, st, e, d = (split(ref[...]) for ref in (c_ref, n_ref, st_ref, e_ref, d_ref))
     yn_ref[...] = dot3(c, n, NN)
     ys_ref[...] = dot3(c, st, NT)
@@ -267,54 +270,97 @@
     yd_ref[...] = yd0_ref[...] + dot3(n, eu, NN) + dot3(e, nx, NN)
 
 
-def last_body(
-    layers, size, mask_ref, h_ref, c_ref, n_ref, st_ref, e_ref, d_ref,
-    yc_ref, yn_ref, ys_ref, ye_ref, yd_ref, cxu_ref, ycu_ref, gc_ref, gn_ref, rs_ref, re_ref, out_ref,
+def mix_body(
+    layers, size, target, mask_ref, c_ref, n_ref, st_ref, e_ref, d_ref, yc_ref, yn_ref, ys_ref, ye_ref, yd_ref,
+    cxu_ref, ycu_ref, *rest,
 ):
-    twice = 2.0 * h_ref[0]
+    *sums_refs, out_ref, pc_ref, pn_ref, ps_ref, pe_ref, scale_ref, held, zero, sems = rest
+    sums = sum(ref[...] for ref in sums_refs)
+    t1, t2 = sums[0:1, :], sums[1:2, :]
+    twice = 2.0 * jax.nn.sigmoid((jnp.abs(t2 - target) - jnp.abs(2.0 * t1 - t2 - target)) / size)
+    scale_ref[...] = jnp.broadcast_to(1.0 - twice, scale_ref.shape)
     slots = out_ref.shape[1]
+    zero[...] = jnp.zeros(zero.shape, F32)
+    written = {(layer, 0) for layer in range(layers)}
+    for name in IN_PLANE:
+        written |= {(low, slot) for low, _, slot in panel_blocks(name, layers)}
+    copies = []
+    for layer in range(layers):
+        for slot in range(slots):
+            if (layer, slot) not in written:
+                copies.append(pltpu.make_async_copy(zero, out_ref.at[layer, slot], sems.at[len(copies)]))
+                copies[-1].start()
 
     def mixed(y, a):
         return y + twice * (a - y)
 
-    c_blocks = take_sym(yc_ref[...] + ycu_ref[...] + gc_ref[...], layers, size)
-    done = set()
+    cxu = split(whole_sym(take_sym(cxu_ref, layers, size), layers))
+    yd = yd_ref[...] + dot3(split(d_ref[...]), cxu, NN)
+    for k, (low, high, slot) in enumerate(panel_blocks("D", layers)):
+        rows, cols = slice(low * size, (low + 1) * size), slice(high * size, (high + 1) * size)
+        held[k] = jnp.where(kept(mask_ref, low, slot), mixed(yd[rows, cols], d_ref[rows, cols]), 0.0)
+        copies.append(pltpu.make_async_copy(held.at[k], out_ref.at[low, slot], sems.at[len(copies)]))
+        copies[-1].start()
+    c_blocks = take_sym(yc_ref[...] + ycu_ref[...], layers, size)
+    put_sym(
+        pc_ref,
+        lambda a, b: mixed(c_blocks[a, b], c_ref[a * size : (a + 1) * size, b * size : (b + 1) * size]),
+        layers,
+        size,
+    )
     for layer in range(layers):
-        here = slice(layer * size, (layer + 1) * size)
-        out_ref[layer, 0] = mixed(c_blocks[layer, layer], c_ref[here, here])
-        done.add((layer, 0))
-    for low, high, slot in panel_blocks("C", layers):
-        a = c_ref[low * size : (low + 1) * size, high * size : (high + 1) * size]
-        out_ref[low, slot] = jnp.where(kept(mask_ref, low, slot), mixed(c_blocks[low, high], a), 0.0)
-        done.add((low, slot))
-    cxu = split(whole_sym(take_sym(cxu_ref, layers, size), layers))
-    yd_ref[...] += dot3(split(d_ref[...]), cxu, NN)
-    for name, a_ref, terms in (
-        ("N", n_ref, (yn_ref, gn_ref)),
-        ("S", st_ref, (ys_ref, rs_ref)),
-        ("E", e_ref, (ye_ref, re_ref)),
-        ("D", d_ref, (yd_ref,)),
-    ):
+        for name, y_ref, a_ref, p_ref in (
+            ("N", yn_ref, n_ref, pn_ref),
+            ("S", ys_ref, st_ref, ps_ref),
+            ("E", ye_ref, e_ref, pe_ref),
+        ):
+            rows = slice(layer * size, (layer + 1) * size)
+            for other in range(layers):
+                cols = slice(other * size, (other + 1) * size)
+                a = a_ref[cols, rows].T if name == "S" else a_ref[rows, cols]
+                p_ref[rows, cols] = mixed(y_ref[rows, cols], a)
+    for copy in copies:
+        copy.wait()
+
+
+def mix_body_for(target, layers, size, *refs):
+    mix_body(layers, size, target, *refs)
+
+
+def side_body(names, layers, size, mask_ref, _, scale_ref, *rest):
+    refs, (out_ref, held, sems) = rest[: 2 * len(names)], rest[2 * len(names) :]
+    scale = scale_ref[0:1, :]
+    copies = []
+
+    def send(value, low, slot):
+        k = len(copies)
+        held[k] = value
+        copies.append(pltpu.make_async_copy(held.at[k], out_ref.at[low, slot], sems.at[k]))
+        copies[-1].start()
+
+    for at, name in enumerate(names):
+        p_ref, late_ref = refs[2 * at], refs[2 * at + 1]
+        if name == "C":
+            blocks = take_sym(p_ref[...] + scale * late_ref[...], layers, size)
+            for layer in range(layers):
+                send(blocks[layer, layer], layer, 0)
         for low, high, slot in panel_blocks(name, layers):
             rows, cols = slice(low * size, (low + 1) * size), slice(high * size, (high + 1) * size)
-            y = sum(ref[rows, cols] for ref in terms)
-            a = a_ref[cols, rows].T if name == "S" else a_ref[rows, cols]
-            out_ref[low, slot] = jnp.where(kept(mask_ref, low, slot), mixed(y, a), 0.0)
-            done.add((low, slot))
-    for layer in range(layers):
-        for slot in range(slots):
-            if (layer, slot) not in done:
-                out_ref[layer, slot] = jnp.zeros((size, size), F32)
-
-
-def call(body, layers, size, outs, spaces, products, scratch=(), limit=40):
+            value = blocks[low, high] if name == "C" else p_ref[rows, cols] + scale * late_ref[rows, cols]
+            send(jnp.where(kept(mask_ref, low, slot), value, 0.0), low, slot)
+    for copy in copies:
+        copy.wait()
+
+
+def call(body, layers, size, outs, spaces, products, scratch=(), limit=40, out_spaces=None, aliases=None):
     n = layers * size
     return pl.pallas_call(
         functools.partial(body, layers, size),
         out_shape=[jax.ShapeDtypeStruct(shape, F32) for shape in outs],
         in_specs=[pl.BlockSpec(memory_space=space) for space in spaces],
-        out_specs=[pl.BlockSpec(memory_space=pltpu.VMEM)] * len(outs),
+        out_specs=[pl.BlockSpec(memory_space=space) for space in out_spaces or [pltpu.VMEM] * len(outs)],
         scratch_shapes=list(scratch),
+        input_output_aliases=aliases or {},
         compiler_params=pltpu.CompilerParams(vmem_limit_bytes=limit << 20),
         cost_estimate=pl.CostEstimate(
             flops=int(products * 6 * n**3), bytes_accessed=4 * n * n * (len(outs) + len(spaces)), transcendentals=0
@@ -327,47 +373,39 @@
     return lax.ppermute(value, axis, [(i, (i + by) % peers) for i in range(peers)])
 
 
-def summed(value, axis):
-    peers = lax.axis_size(axis)
-    if peers & (peers - 1):
-        return value + sum(passed_along(value, axis, by) for by in range(1, peers))
-    by = 1
-    while by < peers:
-        value = value + passed_along(value, axis, by)
-        by *= 2
-    return value
-
-
 def shards(stored_blocks, onsite, bond_mask):
     stored, onsite, mask = stored_blocks[0, 0], onsite[0, 0], bond_mask[0, 0]
     layers, slots, size = stored.shape[:3]
     n = layers * size
-    panel, packed = (n, n), (sym_rows(layers, size), size)
-    vmem, smem, anywhere = pltpu.VMEM, pltpu.SMEM, pl.ANY
-
-    def loads(count):
+    panel, packed, sums = (n, n), (sym_rows(layers, size), size), (8, size)
+    vmem, smem, hbm = pltpu.VMEM, pltpu.SMEM, pltpu.HBM
+
+    def blocks(count):
         return [pltpu.VMEM((count, size, size), F32), pltpu.SemaphoreType.DMA((count,))]
 
     go = functools.partial(call, layers=layers, size=size)
-    N, Cp, C = go(
-        pack_t_body, outs=[panel, packed, panel], spaces=[smem, anywhere, vmem], products=0.1,
-        scratch=loads(len(pack_t_wanted(layers))), limit=16,
+    N, Cp, C, own = go(
+        pack_t_body, outs=[panel, packed, panel, sums], spaces=[smem, hbm, vmem], products=0.1,
+        scratch=blocks(len(pack_t_wanted(layers))), limit=16,
     )(mask, stored, onsite)
     N_x, Cp_x = passed_along(N, "row", -1), passed_along(Cp, "row", -1)
-    St, E, D = go(
-        pack_e_body, outs=[panel] * 3, spaces=[smem, anywhere], products=0.1,
-        scratch=loads(len(pack_e_wanted(layers))), limit=16,
-    )(mask, stored)
-    St_u, E_u, Cp_u = (passed_along(value, "col", -1) for value in (St, E, Cp))
-    gc_up, yc_up = go(up_body, outs=[packed] * 2, spaces=[vmem] * 2, products=2, limit=16)(N, D)
-    gc_up, yc_up = passed_along(gc_up, "col", 1), passed_along(yc_up, "col", 1)
+    St, E, D, own = go(
+        pack_e_body, outs=[panel] * 3 + [sums], spaces=[smem, hbm, vmem], products=0.1,
+        scratch=blocks(len(pack_e_wanted(layers))), limit=16,
+    )(mask, stored, own)
+    St_u, E_u = passed_along(St, "col", -1), passed_along(E, "col", -1)
+    (gc_up,) = go(own_sym_body, outs=[packed], spaces=[vmem], products=1, limit=16)(D)
+    gc_up = passed_along(gc_up, "col", 1)
+    Cp_u = passed_along(Cp, "col", -1)
+    (yc_up,) = go(own_sym_body, outs=[packed], spaces=[vmem], products=1, limit=16)(N)
+    yc_up = passed_along(yc_up, "col", 1)
+    own = own + sum(passed_along(own, "col", by) for by in range(1, lax.axis_size("col")))
     gc, gn, rs, re = go(local_g_body, outs=[packed, panel, panel, panel], spaces=[vmem] * 3, products=4, limit=24)(N, E, D)
-    yc, yn, ys, ye, yd, sums = go(
-        local_y_body, outs=[packed] + [panel] * 4 + [(8, 128)], spaces=[vmem] * 5, products=8
-    )(C, N, St, E, D)
-    sums = summed(summed(sums, "row"), "col")
+    yc, yn, ys, ye, yd = go(local_y_body, outs=[packed] + [panel] * 4, spaces=[vmem] * 5, products=8)(C, N, St, E, D)
     gc, gn = go(g_body, outs=[packed, panel], spaces=[vmem] * 5, products=2, limit=24)(gc, gn, St_u, E_u, gc_up)
-    gc, gn = passed_along(gc, "row", 1), passed_along(gn, "row", 1)
+    gc = passed_along(gc, "row", 1)
+    every = [own] + [passed_along(own, "row", by) for by in range(1, lax.axis_size("row"))]
+    gn = passed_along(gn, "row", 1)
     Cp_xu = passed_along(Cp_x, "col", -1)
     rs, re = go(r_body, outs=[panel] * 2, spaces=[vmem] * 6, products=3, limit=24)(rs, re, St_u, E_u, Cp_x, N_x)
     rs, re = passed_along(rs, "col", 1), passed_along(re, "col", 1)
@@ -375,12 +413,20 @@
         N, E, D, St_u, E_u, Cp_u, Cp_x, N_x, yn, ye, yd
     )
     cells = lax.axis_size("row") * lax.axis_size("col") * layers
-    target = float(cells * size // 2)
-    t1, t2 = sums[0, 0], sums[1, 0]
-    steering = jax.nn.sigmoid((jnp.abs(t2 - target) - jnp.abs(2.0 * t1 - t2 - target)) / size)
-    (out,) = go(last_body, outs=[(layers, slots, size, size)], spaces=[smem] * 2 + [vmem] * 16, products=1, limit=56)(
-        mask, steering[None], C, N, St, E, D, yc, yn, ys, ye, yd, Cp_xu, yc_up, gc, gn, rs, re
-    )
+    stack = (layers, slots, size, size)
+    count = len(panel_blocks("D", layers))
+    out, pc, pn, ps, pe, scale = go(
+        functools.partial(mix_body_for, float(cells * size // 2)),
+        outs=[stack, packed, panel, panel, panel, sums], out_spaces=[hbm] + [vmem] * 5,
+        spaces=[smem] + [vmem] * (12 + len(every)), products=1,
+        scratch=[pltpu.VMEM((count, size, size), F32), pltpu.VMEM((size, size), F32), pltpu.SemaphoreType.DMA((layers * slots,))],
+    )(mask, C, N, St, E, D, yc, yn, ys, ye, yd, Cp_xu, yc_up, *every)
+    for names, terms in ((("S", "E"), (ps, rs, pe, re)), (("C", "N"), (pc, gc, pn, gn))):
+        count = sum(len(panel_blocks(name, layers)) for name in names) + layers * ("C" in names)
+        (out,) = go(
+            functools.partial(side_body, names), outs=[stack], out_spaces=[hbm], spaces=[smem, hbm] + [vmem] * 5,
+            products=0.1, scratch=blocks(count), limit=16, aliases={1: 0},
+        )(mask, out, scale, *terms)
     return out[None, None]
 
 

time: 125 us -> 114 us (0.912)
  waiting for transfers between devices: 56.8 us -> 45.5 us
  starting transfers between devices: 20.6 us -> 23.8 us
  between operations: 2.25 us -> 0.29 us
  local copies, waits for them, and re-layouts: 9.19 us -> 7.27 us
    ppermute x17 -> x22, waiting for transfers between devices: 56.8 us -> 45.5 us  [passed_along(): lax.ppermute(value, axis, [(i, (i + by) % peers) for i in range(peers)])]
    ppermute x17 -> x22, starting transfers between devices: 20.6 us -> 23.8 us  [passed_along(): lax.ppermute(value, axis, [(i, (i + by) % peers) for i in range(peers)])]
    pallas_call x5 -> x8, Pallas kernels: 21.1 us -> 19.7 us  [the longest x1 6.58 us: shards(): go(local_y_body, outs=[packed] + [panel] * 4, spaces=[vmem] * 5, products=8)]
    unnamed x38 -> x18, local copies, waits for them, and re-layouts: 8.65 us -> 7.27 us
  transfers between devices with their start and end apart: 17 -> 22, of which waited for: 8 -> 9; matrix products, arithmetic and copies ran while one was open for 0% -> 0% of each run, Pallas kernels for 19% -> 29%
where the time goes in v2:
time: 114 us; the launch traced here: 113 us
  waiting for transfers between devices  45.5 us (40%)
  Pallas kernels  36.5 us (32%)
  starting transfers between devices  23.8 us (21%)
  local copies, waits for them, and re-layouts  7.27 us (6%)
    ppermute x22, waiting for transfers between devices, passed_along(): lax.ppermute(value, axis, [(i, (i + by) % peers) for i in range(peers)])  45.5 us
    ppermute x22, starting transfers between devices, passed_along(): lax.ppermute(value, axis, [(i, (i + by) % peers) for i in range(peers)])  23.8 us
    unnamed x18, local copies, waits for them, and re-layouts  7.27 us
    pallas_call x1, Pallas kernels, shards(): go(middle_body, outs=[panel] * 3, spaces=[vmem] * 11, products=8)  6.92 us
    pallas_call x1, Pallas kernels, shards(): go(local_y_body, outs=[packed] + [panel] * 4, spaces=[vmem] * 5, products=8)  6.58 us
    pallas_call x1, Pallas kernels, shards(): go(functools.partial(mix_body_for, float(cells * size // 2)), outs=[stack...  4.4 us
    pallas_call x2, Pallas kernels, shards(): go(functools.partial(side_body, names), outs=[stack], out_spaces=[hbm], s...  3.96 us
    pallas_call x1, Pallas kernels, shards(): go(r_body, outs=[panel] * 2, spaces=[vmem] * 6, products=3, limit=24)  3.87 us
  transfers between devices with their start and end apart: 22, of which 9 were waited for; matrix products, arithmetic and copies ran while one was open for 0% of the time, Pallas kernels for 29%

profile of v2, /device:TPU:0, one launch (start us, length us, event | category | flops | bytes accessed | tf_op | source)
XLA Modules:
  0.0 113.3 jit_solution(3455987144913385338)
XLA Ops:
  0.0 3.1 %copy-done = f32[1,1,2,14,256,256]{5,4,3,2,1,0:T(8,128)S(1)} copy-done((f32[1,1,2,14,256,256]{5,4,3,2,1,0:T(8,128)S(1)}, f32[1,1,2,14,256,256]{5,4,3,2,1,0:T(8,128)}, u32[]{:S(2)}) %copy-start) | copy-done | bytes 7340056
  4.4 1.4 %shard_map.37 = (f32[512,512]{1,0:T(8,128)S(1)}, f32[520,256]{1,0:T(8,128)S(1)}, f32[512,512]{1,0:T(8,128)S(1)}, f32[8,256]{1,0:T(8,128)S(1)}) custom-call(s32[2,13]{1,0:T(2,128)S(1)} %bitcast.6, f32[2,14,256,256]{3,2,1,0:T(8,128)S(1)} %bitcast.4, f32[2,256]{1,0:T(2,128)S(1)} %bitcast.11), custom_call_target="tpu_custom_call" | custom-call | flops 80530640 | bytes 7340032 | tf_op jit(solution)/shard_map/pallas_call | solution.py:387
  5.8 5.1 %collective-permute-start.4 = (f32[512,512]{1,0:T(8,128)S(1)}, f32[512,512]{1,0:T(8,128)S(1)}, u32[]{:S(2)}, u32[]{:S(2)}) collective-permute-start(f32[512,512]{1,0:T(8,128)S(1)} %get-tuple-element.36.n_ref.panel_ref.refs_2_), channel_id=1, source_target_pairs={{0,24},{8,0},{16,8},{24,16},{1,25},{9,1},{17,9},{25,17},{2,26},{10... | collective-permute-start | bytes 3145736 | tf_op jit(solution)/shard_map/ppermute | solution.py:373
  10.9 1.8 %shard_map.38 = (f32[512,512]{1,0:T(8,128)S(1)}, f32[512,512]{1,0:T(8,128)S(1)}, f32[512,512]{1,0:T(8,128)S(1)}, f32[8,256]{1,0:T(8,128)S(1)}) custom-call(s32[2,13]{1,0:T(2,128)S(1)} %bitcast.7, f32[2,14,256,256]{3,2,1,0:T(8,128)S(1)} %bitcast.5, f32[8,256]{1,0:T(8,128)S(1)} %get-tuple-element.37.before_ref), custom_call_target="tpu_custom_call" | custom-call | flops 80530640 | bytes 7340032 | tf_op jit(solution)/shard_map/pallas_call | solution.py:392
  12.7 1.7 %collective-permute-start = (f32[512,512]{1,0:T(8,128)S(1)}, f32[512,512]{1,0:T(8,128)S(1)}, u32[]{:S(2)}, u32[]{:S(2)}) collective-permute-start(f32[512,512]{1,0:T(8,128)S(1)} %get-tuple-element.38.st_ref.refs_3_), channel_id=1, source_target_pairs={{0,7},{1,0},{2,1},{3,2},{4,3},{5,4},{6,5},{7,6},{8,15},{9,8},{10,9... | collective-permute-start | bytes 3145736 | tf_op jit(solution)/shard_map/ppermute | solution.py:373
  15.4 1.1 collective-permute-start.12
  16.4 21.6 %collective-permute-done.13 = f32[8,256]{1,0:T(8,128)S(1)} collective-permute-done((f32[8,256]{1,0:T(8,128)S(1)}, f32[8,256]{1,0:T(8,128)S(1)}, u32[]{:S(2)}, u32[]{:S(2)}) %collective-permute-start.13) | collective-permute-done | bytes 8224 | tf_op jit(solution)/shard_map/ppermute | solution.py:373
  38.1 1.3 %collective-permute-start.11 = (f32[8,256]{1,0:T(8,128)S(1)}, f32[8,256]{1,0:T(8,128)S(1)}, u32[]{:S(2)}, u32[]{:S(2)}) collective-permute-start(f32[8,256]{1,0:T(8,128)S(1)} %get-tuple-element.50), channel_id=1, source_target_pairs={{0,5},{1,6},{2,7},{3,0},{4,1},{5,2},{6,3},{7,4},{8,13},{9,14},{10,... | collective-permute-start | bytes 24584 | tf_op jit(solution)/shard_map/ppermute | solution.py:373
  40.0 1.2 %collective-permute-done.11 = f32[8,256]{1,0:T(8,128)S(1)} collective-permute-done((f32[8,256]{1,0:T(8,128)S(1)}, f32[8,256]{1,0:T(8,128)S(1)}, u32[]{:S(2)}, u32[]{:S(2)}) %collective-permute-start.11) | collective-permute-done | bytes 8224 | tf_op jit(solution)/shard_map/ppermute | solution.py:373
  41.3 1.7 %collective-permute-start.9 = (f32[8,256]{1,0:T(8,128)S(1)}, f32[8,256]{1,0:T(8,128)S(1)}, u32[]{:S(2)}, u32[]{:S(2)}) collective-permute-start(f32[8,256]{1,0:T(8,128)S(1)} %get-tuple-element.50), channel_id=1, source_target_pairs={{0,3},{1,4},{2,5},{3,6},{4,7},{5,0},{6,1},{7,2},{8,11},{9,12},{10,... | collective-permute-start | bytes 24584 | tf_op jit(solution)/shard_map/ppermute | solution.py:373
  43.0 2.1 %collective-permute-start.8 = (f32[8,256]{1,0:T(8,128)S(1)}, f32[8,256]{1,0:T(8,128)S(1)}, u32[]{:S(2)}, u32[]{:S(2)}) collective-permute-start(f32[8,256]{1,0:T(8,128)S(1)} %get-tuple-element.50), channel_id=1, source_target_pairs={{0,2},{1,3},{2,4},{3,5},{4,6},{5,7},{6,0},{7,1},{8,10},{9,11},{10,... | collective-permute-start | bytes 24584 | tf_op jit(solution)/shard_map/ppermute | solution.py:373
  46.2 1.4 %collective-permute-done.8 = f32[8,256]{1,0:T(8,128)S(1)} collective-permute-done((f32[8,256]{1,0:T(8,128)S(1)}, f32[8,256]{1,0:T(8,128)S(1)}, u32[]{:S(2)}, u32[]{:S(2)}) %collective-permute-start.8) | collective-permute-done | bytes 8224 | tf_op jit(solution)/shard_map/ppermute | solution.py:373
  48.0 1.1 collective-permute-done.7
  49.1 3.3 %shard_map.43 = (f32[520,256]{1,0:T(8,128)S(1)}, f32[512,512]{1,0:T(8,128)S(1)}, f32[512,512]{1,0:T(8,128)S(1)}, f32[512,512]{1,0:T(8,128)S(1)}) custom-call(f32[512,512]{1,0:T(8,128)S(1)} %get-tuple-element.36.n_ref.panel_ref.refs_2_, f32[512,512]{1,0:T(8,128)S(1)} %get-tuple-element.39.e_ref.refs_4_, f32[512,512]{1,0:T(8,128)S(1)} %get-tuple-element.40.d_ref.refs_5_.panel_ref), custom_call_target="tpu_custom_call" | custom-call | flops 3221225472 | bytes 7340032 | tf_op jit(solution)/shard_map/pallas_call | solution.py:403
  53.2 7.8 %collective-permute-done.3.cx_ref = f32[520,256]{1,0:T(8,128)S(1)} collective-permute-done((f32[520,256]{1,0:T(8,128)S(1)}, f32[520,256]{1,0:T(8,128)S(1)}, u32[]{:S(2)}, u32[]{:S(2)}) %collective-permute-start.3) | collective-permute-done | bytes 532512 | tf_op jit(solution)/shard_map/ppermute | solution.py:373
  61.0 1.0 collective-permute-start.2
  62.0 2.3 %collective-permute-start.16 = (f32[8,256]{1,0:T(8,128)S(1)}, f32[8,256]{1,0:T(8,128)S(1)}, u32[]{:S(2)}, u32[]{:S(2)}) collective-permute-start(f32[8,256]{1,0:T(8,128)S(1)} %add_add_fusion.refs_13_), channel_id=1, source_target_pairs={{0,24},{8,0},{16,8},{24,16},{1,25},{9,1},{17,9},{25,17},{2,26},{10... | collective-permute-start | bytes 24584 | tf_op jit(solution)/shard_map/ppermute | solution.py:373
  64.3 3.9 %shard_map.44 = (f32[512,512]{1,0:T(8,128)}, f32[512,512]{1,0:T(8,128)}) custom-call(f32[512,512]{1,0:T(8,128)S(1)} %get-tuple-element.54.rs0_ref, f32[512,512]{1,0:T(8,128)S(1)} %get-tuple-element.55.re0_ref, f32[512,512]{1,0:T(8,128)S(1)} %collective-permute-done.stu_ref, f32[512,512]{1,0:T(8,128)S(1)} %collective-permute-done.1.eu_ref, ...), custom_call_target="tpu_custom_call" | custom-call | flops 2415919104 | bytes 8388608 | tf_op jit(solution)/shard_map/pallas_call | solution.py:410
  68.9 2.7 %shard_map.47 = (f32[520,256]{1,0:T(8,128)}, f32[512,512]{1,0:T(8,128)}) custom-call(f32[520,256]{1,0:T(8,128)S(1)} %get-tuple-element.60.gc0_ref, f32[512,512]{1,0:T(8,128)S(1)} %get-tuple-element.61.gn0_ref, f32[512,512]{1,0:T(8,128)S(1)} %collective-permute-done.stu_ref, f32[512,512]{1,0:T(8,128)S(1)} %collective-permute-done.1.eu_ref, ...), custom_call_target="tpu_custom_call" | custom-call | flops 1610612736 | bytes 7340032 | tf_op jit(solution)/shard_map/pallas_call | solution.py:405
  72.4 1.2 %collective-permute-done.14.refs_14_ = f32[8,256]{1,0:T(8,128)S(1)} collective-permute-done((f32[8,256]{1,0:T(8,128)S(1)}, f32[8,256]{1,0:T(8,128)S(1)}, u32[]{:S(2)}, u32[]{:S(2)}) %collective-permute-start.14) | collective-permute-done | bytes 8224 | tf_op jit(solution)/shard_map/ppermute | solution.py:373
  73.6 1.7 %collective-permute-start.21 = (f32[512,512]{1,0:T(8,128)}, f32[512,512]{1,0:T(8,128)S(1)}, u32[]{:S(2)}, u32[]{:S(2)}) collective-permute-start(f32[512,512]{1,0:T(8,128)} %get-tuple-element.64), channel_id=1, source_target_pairs={{0,8},{8,16},{16,24},{24,0},{1,9},{9,17},{17,25},{25,1},{2,10},{10... | collective-permute-start | bytes 3145736 | tf_op jit(solution)/shard_map/ppermute | solution.py:373
  75.3 6.6 %shard_map.39 = (f32[520,256]{1,0:T(8,128)S(1)}, f32[512,512]{1,0:T(8,128)S(1)}, f32[512,512]{1,0:T(8,128)S(1)}, f32[512,512]{1,0:T(8,128)S(1)}, f32[512,512]{1,0:T(8,128)S(1)}) custom-call(f32[512,512]{1,0:T(8,128)S(1)} %get-tuple-element.35.c_ref.refs_1_, f32[512,512]{1,0:T(8,128)S(1)} %get-tuple-element.36.n_ref.panel_ref.refs_2_, ...), custom_call_target="tpu_custom_call" | custom-call | flops 6442450944 | bytes 10485760 | tf_op jit(solution)/shard_map/pallas_call | solution.py:404
  81.9 1.7 %collective-permute-start.5 = (f32[520,256]{1,0:T(8,128)S(1)}, f32[520,256]{1,0:T(8,128)S(1)}, u32[]{:S(2)}, u32[]{:S(2)}) collective-permute-start(f32[520,256]{1,0:T(8,128)S(1)} %collective-permute-done.3.cx_ref), channel_id=1, source_target_pairs={{0,7},{1,0},{2,1},{3,2},{4,3},{5,4},{6,5},{7,6},{8,15},{9,8},{10,9... | collective-permute-start | bytes 1597448 | tf_op jit(solution)/shard_map/ppermute | solution.py:373
  84.7 1.0 copy-done.8
  85.8 6.9 %shard_map.40 = (f32[512,512]{1,0:T(8,128)S(1)}, f32[512,512]{1,0:T(8,128)S(1)}, f32[512,512]{1,0:T(8,128)S(1)}) custom-call(f32[512,512]{1,0:T(8,128)S(1)} %get-tuple-element.36.n_ref.panel_ref.refs_2_, f32[512,512]{1,0:T(8,128)S(1)} %get-tuple-element.39.e_ref.refs_4_, f32[512,512]{1,0:T(8,128)S(1)} %get-tuple-element.40.d_ref.refs_5_.panel_ref, ...), custom_call_target="tpu_custom_call" | custom-call | flops 6442450944 | bytes 14680064 | tf_op jit(solution)/shard_map/pallas_call | solution.py:412
  92.7 1.0 copy-done.1
  93.7 2.5 %collective-permute-done.5.refs_11_ = f32[520,256]{1,0:T(8,128)S(1)} collective-permute-done((f32[520,256]{1,0:T(8,128)S(1)}, f32[520,256]{1,0:T(8,128)S(1)}, u32[]{:S(2)}, u32[]{:S(2)}) %collective-permute-start.5) | collective-permute-done | bytes 532512 | tf_op jit(solution)/shard_map/ppermute | solution.py:373
  96.2 4.4 %shard_map.42 = (f32[2,14,256,256]{3,2,1,0:T(8,128)}, f32[520,256]{1,0:T(8,128)S(1)}, f32[512,512]{1,0:T(8,128)S(1)}, f32[512,512]{1,0:T(8,128)S(1)}, f32[512,512]{1,0:T(8,128)S(1)}, /*index=5*/f32[8,256]{1,0:T(8,128)S(1)}) custom-call(s32[2,13]{1,0:T(2,128)S(1)} %bitcast.8, f32[512,512]{1,0:T(8,128)S(1)} %get-tuple-element.35.c_ref.refs_1_, ...), custom_call_target="tpu_custom_call" | custom-call | flops 805306368 | bytes 24117248 | tf_op jit(solution)/shard_map/pallas_call | solution.py:418
  100.6 3.6 %collective-permute-done.18.rest_3_ = f32[512,512]{1,0:T(8,128)S(1)} collective-permute-done((f32[512,512]{1,0:T(8,128)}, f32[512,512]{1,0:T(8,128)S(1)}, u32[]{:S(2)}, u32[]{:S(2)}) %collective-permute-start.18) | collective-permute-done | bytes 1048608 | tf_op jit(solution)/shard_map/ppermute | solution.py:373
  104.2 2.0 %shard_map.45._ = f32[2,14,256,256]{3,2,1,0:T(8,128)} custom-call(s32[2,13]{1,0:T(2,128)S(1)} %bitcast.9, f32[2,14,256,256]{3,2,1,0:T(8,128)} %get-tuple-element.51._, f32[8,256]{1,0:T(8,128)S(1)} %get-tuple-element.52.scale_ref, f32[512,512]{1,0:T(8,128)S(1)} %get-tuple-element.53.rest_0_, ...), custom_call_target="tpu_custom_call", output_to_operand_aliasing={{}: (1, {})} | custom-call | flops 80530640 | bytes 8388608 | tf_op jit(solution)/shard_map/pallas_call | solution.py:426
  106.1 5.0 %collective-permute-done.20.rest_1_ = f32[520,256]{1,0:T(8,128)S(1)} collective-permute-done((f32[520,256]{1,0:T(8,128)}, f32[520,256]{1,0:T(8,128)S(1)}, u32[]{:S(2)}, u32[]{:S(2)}) %collective-permute-start.20) | collective-permute-done | bytes 532512 | tf_op jit(solution)/shard_map/ppermute | solution.py:373
  111.2 2.0 %shard_map.48 = f32[2,14,256,256]{3,2,1,0:T(8,128)} custom-call(s32[2,13]{1,0:T(2,128)S(1)} %bitcast.10, f32[2,14,256,256]{3,2,1,0:T(8,128)} %shard_map.45._, f32[8,256]{1,0:T(8,128)S(1)} %get-tuple-element.52.scale_ref, f32[520,256]{1,0:T(8,128)S(1)} %get-tuple-element.59.rest_0_, ...), custom_call_target="tpu_custom_call", output_to_operand_aliasing={{}: (1, {})} | custom-call | flops 80530640 | bytes 8388608 | tf_op jit(solution)/shard_map/pallas_call | solution.py:426
  (43 shorter events, 8.1 us)
Async XLA Ops:
  0.0 3.1 %copy-start = (f32[1,1,2,14,256,256]{5,4,3,2,1,0:T(8,128)S(1)}, f32[1,1,2,14,256,256]{5,4,3,2,1,0:T(8,128)}, u32[]{:S(2)}) copy-start(f32[1,1,2,14,256,256]{5,4,3,2,1,0:T(8,128)} %param.3) | copy-start | bytes 22020100
  3.1 0.7 copy-start.2
  3.8 0.7 copy-start.4
  5.8 56.2 %collective-permute-start.4 = (f32[512,512]{1,0:T(8,128)S(1)}, f32[512,512]{1,0:T(8,128)S(1)}, u32[]{:S(2)}, u32[]{:S(2)}) collective-permute-start(f32[512,512]{1,0:T(8,128)S(1)} %get-tuple-element.36.n_ref.panel_ref.refs_2_), channel_id=1, source_target_pairs={{0,24},{8,0},{16,8},{24,16},{1,25},{9,1},{17,9},{25,17},{2,26},{10... | collective-permute-start | bytes 3145736 | tf_op jit(solution)/shard_map/ppermute | solution.py:373
  12.7 49.3 %collective-permute-start = (f32[512,512]{1,0:T(8,128)S(1)}, f32[512,512]{1,0:T(8,128)S(1)}, u32[]{:S(2)}, u32[]{:S(2)}) collective-permute-start(f32[512,512]{1,0:T(8,128)S(1)} %get-tuple-element.38.st_ref.refs_3_), channel_id=1, source_target_pairs={{0,7},{1,0},{2,1},{3,2},{4,3},{5,4},{6,5},{7,6},{8,15},{9,8},{10,9... | collective-permute-start | bytes 3145736 | tf_op jit(solution)/shard_map/ppermute | solution.py:373
  14.4 49.9 %collective-permute-start.1 = (f32[512,512]{1,0:T(8,128)S(1)}, f32[512,512]{1,0:T(8,128)S(1)}, u32[]{:S(2)}, u32[]{:S(2)}) collective-permute-start(f32[512,512]{1,0:T(8,128)S(1)} %get-tuple-element.39.e_ref.refs_4_), channel_id=1, source_target_pairs={{0,7},{1,0},{2,1},{3,2},{4,3},{5,4},{6,5},{7,6},{8,15},{9,8},{10,9... | collective-permute-start | bytes 3145736 | tf_op jit(solution)/shard_map/ppermute | solution.py:373
  15.3 22.8 %collective-permute-start.13 = (f32[8,256]{1,0:T(8,128)S(1)}, f32[8,256]{1,0:T(8,128)S(1)}, u32[]{:S(2)}, u32[]{:S(2)}) collective-permute-start(f32[8,256]{1,0:T(8,128)S(1)} %get-tuple-element.50), channel_id=1, source_target_pairs={{0,7},{1,0},{2,1},{3,2},{4,3},{5,4},{6,5},{7,6},{8,15},{9,8},{10,9... | collective-permute-start | bytes 24584 | tf_op jit(solution)/shard_map/ppermute | solution.py:373
  15.4 24.0 %collective-permute-start.12 = (f32[8,256]{1,0:T(8,128)S(1)}, f32[8,256]{1,0:T(8,128)S(1)}, u32[]{:S(2)}, u32[]{:S(2)}) collective-permute-start(f32[8,256]{1,0:T(8,128)S(1)} %get-tuple-element.50), channel_id=1, source_target_pairs={{0,6},{1,7},{2,0},{3,1},{4,2},{5,3},{6,4},{7,5},{8,14},{9,15},{10,... | collective-permute-start | bytes 24584 | tf_op jit(solution)/shard_map/ppermute | solution.py:373
  38.1 3.2 %collective-permute-start.11 = (f32[8,256]{1,0:T(8,128)S(1)}, f32[8,256]{1,0:T(8,128)S(1)}, u32[]{:S(2)}, u32[]{:S(2)}) collective-permute-start(f32[8,256]{1,0:T(8,128)S(1)} %get-tuple-element.50), channel_id=1, source_target_pairs={{0,5},{1,6},{2,7},{3,0},{4,1},{5,2},{6,3},{7,4},{8,13},{9,14},{10,... | collective-permute-start | bytes 24584 | tf_op jit(solution)/shard_map/ppermute | solution.py:373
  39.4 3.7 %collective-permute-start.10 = (f32[8,256]{1,0:T(8,128)S(1)}, f32[8,256]{1,0:T(8,128)S(1)}, u32[]{:S(2)}, u32[]{:S(2)}) collective-permute-start(f32[8,256]{1,0:T(8,128)S(1)} %get-tuple-element.50), channel_id=1, source_target_pairs={{0,4},{1,5},{2,6},{3,7},{4,0},{5,1},{6,2},{7,3},{8,12},{9,13},{10,... | collective-permute-start | bytes 24584 | tf_op jit(solution)/shard_map/ppermute | solution.py:373
  41.3 3.8 %collective-permute-start.9 = (f32[8,256]{1,0:T(8,128)S(1)}, f32[8,256]{1,0:T(8,128)S(1)}, u32[]{:S(2)}, u32[]{:S(2)}) collective-permute-start(f32[8,256]{1,0:T(8,128)S(1)} %get-tuple-element.50), channel_id=1, source_target_pairs={{0,3},{1,4},{2,5},{3,6},{4,7},{5,0},{6,1},{7,2},{8,11},{9,12},{10,... | collective-permute-start | bytes 24584 | tf_op jit(solution)/shard_map/ppermute | solution.py:373
  43.0 4.5 %collective-permute-start.8 = (f32[8,256]{1,0:T(8,128)S(1)}, f32[8,256]{1,0:T(8,128)S(1)}, u32[]{:S(2)}, u32[]{:S(2)}) collective-permute-start(f32[8,256]{1,0:T(8,128)S(1)} %get-tuple-element.50), channel_id=1, source_target_pairs={{0,2},{1,3},{2,4},{3,5},{4,6},{5,7},{6,0},{7,1},{8,10},{9,11},{10,... | collective-permute-start | bytes 24584 | tf_op jit(solution)/shard_map/ppermute | solution.py:373
  45.1 4.0 %collective-permute-start.7 = (f32[8,256]{1,0:T(8,128)S(1)}, f32[8,256]{1,0:T(8,128)S(1)}, u32[]{:S(2)}, u32[]{:S(2)}) collective-permute-start(f32[8,256]{1,0:T(8,128)S(1)} %get-tuple-element.50), channel_id=1, source_target_pairs={{0,1},{1,2},{2,3},{3,4},{4,5},{5,6},{6,7},{7,0},{8,9},{9,10},{10,1... | collective-permute-start | bytes 24584 | tf_op jit(solution)/shard_map/ppermute | solution.py:373
  47.6 13.4 %collective-permute-start.3 = (f32[520,256]{1,0:T(8,128)S(1)}, f32[520,256]{1,0:T(8,128)S(1)}, u32[]{:S(2)}, u32[]{:S(2)}) collective-permute-start(f32[520,256]{1,0:T(8,128)S(1)} %get-tuple-element.42), channel_id=1, source_target_pairs={{0,24},{8,0},{16,8},{24,16},{1,25},{9,1},{17,9},{25,17},{2,26},{10... | collective-permute-start | bytes 1597448 | tf_op jit(solution)/shard_map/ppermute | solution.py:373
  49.1 19.1 %collective-permute-start.19 = (f32[520,256]{1,0:T(8,128)S(1)}, f32[520,256]{1,0:T(8,128)S(1)}, u32[]{:S(2)}, u32[]{:S(2)}) collective-permute-start(f32[520,256]{1,0:T(8,128)S(1)} %shard_map.46), channel_id=1, source_target_pairs={{0,1},{1,2},{2,3},{3,4},{4,5},{5,6},{6,7},{7,0},{8,9},{9,10},{10,1... | collective-permute-start | bytes 1597448 | tf_op jit(solution)/shard_map/ppermute | solution.py:373
  61.0 22.6 %collective-permute-start.2 = (f32[520,256]{1,0:T(8,128)S(1)}, f32[520,256]{1,0:T(8,128)S(1)}, u32[]{:S(2)}, u32[]{:S(2)}) collective-permute-start(f32[520,256]{1,0:T(8,128)S(1)} %get-tuple-element.42), channel_id=1, source_target_pairs={{0,7},{1,0},{2,1},{3,2},{4,3},{5,4},{6,5},{7,6},{8,15},{9,8},{10,9... | collective-permute-start | bytes 1597448 | tf_op jit(solution)/shard_map/ppermute | solution.py:373
  62.0 19.9 %collective-permute-start.6 = (f32[520,256]{1,0:T(8,128)S(1)}, f32[520,256]{1,0:T(8,128)S(1)}, u32[]{:S(2)}, u32[]{:S(2)}) collective-permute-start(f32[520,256]{1,0:T(8,128)S(1)} %shard_map.41), channel_id=1, source_target_pairs={{0,1},{1,2},{2,3},{3,4},{4,5},{5,6},{6,7},{7,0},{8,9},{9,10},{10,1... | collective-permute-start | bytes 1597448 | tf_op jit(solution)/shard_map/ppermute | solution.py:373
  62.0 9.5 %collective-permute-start.16 = (f32[8,256]{1,0:T(8,128)S(1)}, f32[8,256]{1,0:T(8,128)S(1)}, u32[]{:S(2)}, u32[]{:S(2)}) collective-permute-start(f32[8,256]{1,0:T(8,128)S(1)} %add_add_fusion.refs_13_), channel_id=1, source_target_pairs={{0,24},{8,0},{16,8},{24,16},{1,25},{9,1},{17,9},{25,17},{2,26},{10... | collective-permute-start | bytes 24584 | tf_op jit(solution)/shard_map/ppermute | solution.py:373
  64.3 7.2 %copy-start.5 = (f32[512,512]{1,0:T(8,128)}, f32[512,512]{1,0:T(8,128)S(1)}, u32[]{:S(2)}) copy-start(f32[512,512]{1,0:T(8,128)S(1)} %collective-permute-done.1.eu_ref) | copy-start | bytes 3145732
  64.3 7.2 %collective-permute-start.15 = (f32[8,256]{1,0:T(8,128)S(1)}, f32[8,256]{1,0:T(8,128)S(1)}, u32[]{:S(2)}, u32[]{:S(2)}) collective-permute-start(f32[8,256]{1,0:T(8,128)S(1)} %add_add_fusion.refs_13_), channel_id=1, source_target_pairs={{0,16},{8,24},{16,0},{24,8},{1,17},{9,25},{17,1},{25,9},{2,18},{10... | collective-permute-start | bytes 24584 | tf_op jit(solution)/shard_map/ppermute | solution.py:373
  68.2 5.4 %collective-permute-start.14 = (f32[8,256]{1,0:T(8,128)S(1)}, f32[8,256]{1,0:T(8,128)S(1)}, u32[]{:S(2)}, u32[]{:S(2)}) collective-permute-start(f32[8,256]{1,0:T(8,128)S(1)} %add_add_fusion.refs_13_), channel_id=1, source_target_pairs={{0,8},{8,16},{16,24},{24,0},{1,9},{9,17},{17,25},{25,1},{2,10},{10... | collective-permute-start | bytes 24584 | tf_op jit(solution)/shard_map/ppermute | solution.py:373
  71.5 29.1 %collective-permute-start.17 = (f32[512,512]{1,0:T(8,128)}, f32[512,512]{1,0:T(8,128)S(1)}, u32[]{:S(2)}, u32[]{:S(2)}) collective-permute-start(f32[512,512]{1,0:T(8,128)} %get-tuple-element.56), channel_id=1, source_target_pairs={{0,1},{1,2},{2,3},{3,4},{4,5},{5,6},{6,7},{7,0},{8,9},{9,10},{10,1... | collective-permute-start | bytes 3145736 | tf_op jit(solution)/shard_map/ppermute | solution.py:373
  71.5 32.6 %collective-permute-start.18 = (f32[512,512]{1,0:T(8,128)}, f32[512,512]{1,0:T(8,128)S(1)}, u32[]{:S(2)}, u32[]{:S(2)}) collective-permute-start(f32[512,512]{1,0:T(8,128)} %get-tuple-element.58), channel_id=1, source_target_pairs={{0,1},{1,2},{2,3},{3,4},{4,5},{5,6},{6,7},{7,0},{8,9},{9,10},{10,1... | collective-permute-start | bytes 3145736 | tf_op jit(solution)/shard_map/ppermute | solution.py:373
  73.6 37.6 %collective-permute-start.21 = (f32[512,512]{1,0:T(8,128)}, f32[512,512]{1,0:T(8,128)S(1)}, u32[]{:S(2)}, u32[]{:S(2)}) collective-permute-start(f32[512,512]{1,0:T(8,128)} %get-tuple-element.64), channel_id=1, source_target_pairs={{0,8},{8,16},{16,24},{24,0},{1,9},{9,17},{17,25},{25,1},{2,10},{10... | collective-permute-start | bytes 3145736 | tf_op jit(solution)/shard_map/ppermute | solution.py:373
  75.3 9.4 %copy-start.6 = (f32[512,512]{1,0:T(8,128)S(1)}, f32[512,512]{1,0:T(8,128)}, u32[]{:S(2)}) copy-start(f32[512,512]{1,0:T(8,128)} %copy-done.5) | copy-start | bytes 3145732
  81.9 14.3 %collective-permute-start.5 = (f32[520,256]{1,0:T(8,128)S(1)}, f32[520,256]{1,0:T(8,128)S(1)}, u32[]{:S(2)}, u32[]{:S(2)}) collective-permute-start(f32[520,256]{1,0:T(8,128)S(1)} %collective-permute-done.3.cx_ref), channel_id=1, source_target_pairs={{0,7},{1,0},{2,1},{3,2},{4,3},{5,4},{6,5},{7,6},{8,15},{9,8},{10,9... | collective-permute-start | bytes 1597448 | tf_op jit(solution)/shard_map/ppermute | solution.py:373
  83.6 0.8 copy-start.7
  84.4 26.8 %collective-permute-start.20 = (f32[520,256]{1,0:T(8,128)}, f32[520,256]{1,0:T(8,128)S(1)}, u32[]{:S(2)}, u32[]{:S(2)}) collective-permute-start(f32[520,256]{1,0:T(8,128)} %get-tuple-element.62), channel_id=1, source_target_pairs={{0,8},{8,16},{16,24},{24,0},{1,9},{9,17},{17,25},{25,1},{2,10},{10... | collective-permute-start | bytes 1597448 | tf_op jit(solution)/shard_map/ppermute | solution.py:373
  84.7 1.0 copy-start.8
  85.8 10.4 %copy-start.3 = (s32[1,1,2,13]{3,2,1,0:T(2,128)S(1)}, s32[1,1,2,13]{3,2,1,0:T(2,128)}, u32[]{:S(2)}) copy-start(s32[1,1,2,13]{3,2,1,0:T(2,128)} %param.5) | copy-start | bytes 316
  92.7 1.0 copy-start.1

commit v3 on v2

v3 whole, which is shorter than its diff:
```python
import functools

import jax
import jax.numpy as jnp
from jax import lax
from jax.experimental import pallas as pl
from jax.experimental.pallas import tpu as pltpu
from jax.sharding import PartitionSpec as P


F32 = jnp.float32
BF16 = jnp.bfloat16
NN = ((1,), (0,))
NT = ((1,), (1,))
TN = ((0,), (0,))
IN_PLANE = {"C": (0, 0), "N": (0, 1), "S": (1, -1), "E": (1, 0), "D": (1, 1)}


def offset_list():
    steps = (-1, 0, 1)
    return [(i, j, k) for i in steps for j in steps for k in steps if (i, j, k) > (0, 0, 0)]


def slot_number(offset):
    return offset_list().index(offset) + 1


def panel_blocks(name, layers):
    side = IN_PLANE[name]
    found = []
    for low in range(layers):
        for high in range(layers):
            step = high - low
            if abs(step) <= 1 and (*side, step) > (0, 0, 0):
                found.append((low, high, slot_number((*side, step))))
    return found


def sym_rows(layers, size):
    blocks = layers * (layers - 1) // 2 + (layers + 1) // 2
    return -(-blocks // layers) * size + 8


def rows_cols(size):
    return (
        lax.broadcasted_iota(jnp.int32, (size, size), 0),
        lax.broadcasted_iota(jnp.int32, (size, size), 1),
    )


def block_slices(k, layers, size):
    row, col = k // layers * size, k % layers * size
    return slice(row, row + size), slice(col, col + size)


def sym_places(layers):
    above = [(a, b) for a in range(layers) for b in range(a + 1, layers)]
    pairs = list(range(0, layers, 2))
    return list(enumerate(above)), [(len(above) + k, k, a) for k, a in enumerate(pairs)]


def put_sym(ref, get, layers, size, first=0):
    row, col = rows_cols(size)
    above, pairs = sym_places(layers)
    last = first + sym_rows(layers, size) - 8

    def put(k, value):
        rows, cols = block_slices(k, layers, size)
        ref[first + rows.start : first + rows.stop, cols] = value

    ref[last : last + 8, :] = jnp.zeros((8, layers * size), F32)
    if len(above) + len(pairs) < (last - first) // size * layers:
        ref[last - size : last, :] = jnp.zeros((size, layers * size), F32)
    for k, (a, b) in above:
        put(k, get(a, b))
    for k, mark, a in pairs:
        block = get(a, a)
        if a + 1 < layers:
            other = get(a + 1, a + 1)
            line = jnp.sum(jnp.where(row == col, other, 0.0), axis=0, keepdims=True)
            ref[last : last + 8, mark * size : (mark + 1) * size] = jnp.broadcast_to(line, (8, size))
            block = jnp.where(row <= col, block, other)
        put(k, block)


def take_sym(packed, layers, size):
    row, col = rows_cols(size)
    above, pairs = sym_places(layers)
    last = sym_rows(layers, size) - 8
    blocks = {}
    for k, (a, b) in above:
        rows, cols = block_slices(k, layers, size)
        blocks[a, b] = packed[rows, cols]
    for k, mark, a in pairs:
        rows, cols = block_slices(k, layers, size)
        block = packed[rows, cols]
        if a + 1 < layers:
            flipped = block.T
            line = packed[last : last + 1, mark * size : (mark + 1) * size]
            blocks[a, a] = jnp.where(row <= col, block, flipped)
            blocks[a + 1, a + 1] = jnp.where(row == col, line, jnp.where(row < col, flipped, block))
        else:
            blocks[a, a] = block
    return blocks


def whole_sym(blocks, layers):
    rows = []
    for a in range(layers):
        rows.append(
            jnp.concatenate(
                [blocks[a, b] if a <= b else blocks[b, a].T for b in range(layers)], axis=1
            )
        )
    return jnp.concatenate(rows, axis=0)


def split(value):
    high = value.astype(BF16)
    return high, (value - high.astype(F32)).astype(BF16)


def dot3(a, b, dims):
    go = functools.partial(lax.dot_general, dimension_numbers=(dims, ((), ())), preferred_element_type=F32)
    return go(a[0], b[0]) + (go(a[0], b[1]) + go(a[1], b[0]))


def cut(pair, at, size):
    return tuple(part[at : at + size, :] for part in pair)


def sym_product(pair, layers, size, dims):
    blocks = {}
    for a in range(layers):
        if dims == NT:
            left = tuple(part[a * size : (a + 1) * size, :] for part in pair)
            right = tuple(part[a * size :, :] for part in pair)
        else:
            left = tuple(part[:, a * size : (a + 1) * size] for part in pair)
            right = tuple(part[:, a * size :] for part in pair)
        strip = dot3(left, right, dims)
        for b in range(a, layers):
            blocks[a, b] = strip[:, (b - a) * size : (b - a + 1) * size]
    return blocks


def kept(mask_ref, layer, slot):
    return mask_ref[layer, slot - 1] > 0


def load_panel(out_ref, held, first, name, layers, size, mask_ref, flip=False, top=0):
    blocks = panel_blocks(name, layers)
    if layers > 2:
        out_ref[top : top + layers * size, :] = jnp.zeros((layers * size, layers * size), F32)
    for k, (low, high, slot) in enumerate(blocks):
        value = jnp.where(kept(mask_ref, low, slot), held[first + k], 0.0)
        if flip:
            low, high, value = high, low, value.T
        out_ref[top + low * size : top + (low + 1) * size, high * size : (high + 1) * size] = value
    return len(blocks)


def start_loads(stored_ref, held, sems, wanted):
    copies = [
        pltpu.make_async_copy(stored_ref.at[low, slot], held.at[k], sems.at[k])
        for k, (low, slot) in enumerate(wanted)
    ]
    for copy in copies:
        copy.start()
    return copies


def squares_of(value):
    return jnp.sum(value * value)


def wanted_n(layers):
    return [(low, slot) for low, _, slot in panel_blocks("N", layers)]


def pack_n_body(layers, size, mask_ref, stored_ref, n_ref, held, sems):
    for copy in start_loads(stored_ref, held, sems, wanted_n(layers)):
        copy.wait()
    load_panel(n_ref, held, 0, "N", layers, size, mask_ref)


def wanted_rest(layers):
    return (
        [(layer, 0) for layer in range(layers)]
        + [(low, slot) for name in "CSED" for low, _, slot in panel_blocks(name, layers)]
    )


def pack_body(layers, size, mask_ref, stored_ref, onsite_ref, n_ref, packed_ref, down_ref, c_ref, d_ref, sums_ref, held, sems):
    n = layers * size
    copies = start_loads(stored_ref, held, sems, wanted_rest(layers))
    squares = squares_of(n_ref[...])
    row, col = rows_cols(size)
    at = layers + len(panel_blocks("C", layers))
    for copy in copies[:at]:
        copy.wait()
    c_ref[...] = jnp.zeros(c_ref.shape, F32)
    for layer in range(layers):
        block = held[layer]
        block = 0.5 * (block + block.T) + jnp.where(row == col, onsite_ref[layer : layer + 1, :], 0.0)
        c_ref[layer * size : (layer + 1) * size, layer * size : (layer + 1) * size] = block
    for k, (low, high, slot) in enumerate(panel_blocks("C", layers)):
        block = jnp.where(kept(mask_ref, low, slot), held[layers + k], 0.0)
        c_ref[low * size : (low + 1) * size, high * size : (high + 1) * size] = block
        c_ref[high * size : (high + 1) * size, low * size : (low + 1) * size] = block.T
    put_sym(
        packed_ref,
        lambda a, b: c_ref[a * size : (a + 1) * size, b * size : (b + 1) * size],
        layers,
        size,
    )
    down_ref[2 * n : 2 * n + sym_rows(layers, size), :] = packed_ref[...]
    for copy in copies[at:]:
        copy.wait()
    at += load_panel(down_ref, held, at, "S", layers, size, mask_ref, flip=True)
    at += load_panel(down_ref, held, at, "E", layers, size, mask_ref, top=n)
    load_panel(d_ref, held, at, "D", layers, size, mask_ref)
    row, col = rows_cols(n)
    c_now = c_ref[...]
    trace = jnp.sum(jnp.where(row == col, c_now, 0.0))
    squares = squares + squares_of(down_ref[: 2 * n, :]) + squares_of(d_ref[...])
    line = lax.broadcasted_iota(jnp.int32, sums_ref.shape, 0)
    sums_ref[...] = jnp.where(line == 0, trace, squares_of(c_now) + 2.0 * squares)


def up_body(layers, size, n_ref, d_ref, up_ref):
    for k, ref in enumerate((d_ref, n_ref)):
        blocks = sym_product(split(ref[...]), layers, size, TN)
        put_sym(up_ref, lambda a, b: blocks[a, b], layers, size, first=k * sym_rows(layers, size))


def local_g_body(layers, size, n_ref, down_ref, d_ref, g_ref, r_ref):
    n = layers * size
    n_now, e, d = split(n_ref[...]), split(down_ref[n : 2 * n, :]), split(d_ref[...])
    blocks = sym_product(e, layers, size, TN)
    g_ref[:n, :] = dot3(e, d, TN)
    put_sym(g_ref, lambda a, b: blocks[a, b], layers, size, first=n)
    r_ref[:n, :] = dot3(n_now, e, TN)
    r_ref[n:, :] = dot3(n_now, d, TN)


def local_y_body(layers, size, c_ref, n_ref, down_ref, d_ref, yc_ref, yn_ref, ys_ref, ye_ref, yd_ref):
    at = layers * size
    parts = (c_ref[...], n_ref[...], down_ref[:at, :], down_ref[at : 2 * at, :], d_ref[...])
    c, n, st, e, d = (split(part) for part in parts)
    yn_ref[...] = dot3(c, n, NN)
    ys_ref[...] = dot3(c, st, NT)
    ye_ref[...] = dot3(c, e, NN)
    yd_ref[...] = dot3(c, d, NN)
    terms = [
        sym_product(pair, layers, size, dims)
        for pair, dims in ((c, NT), (n, NT), (st, TN), (e, NT), (d, NT))
    ]
    put_sym(yc_ref, lambda a, b: sum(term[a, b] for term in terms), layers, size)


def g_body(layers, size, sums_ref, more_ref, g0_ref, below_ref, up_ref, total_ref, g_ref):
    n, tall = layers * size, sym_rows(layers, size)
    total_ref[...] = sums_ref[...] + more_ref[...]
    stu, eu = split(below_ref[:n, :]), split(below_ref[n : 2 * n, :])
    g_ref[:n, :] = g0_ref[:n, :] + dot3(stu, eu, NN)
    blocks = sym_product(stu, layers, size, NT)
    put_sym(g_ref, lambda a, b: blocks[a, b], layers, size, first=n)
    g_ref[n:, :] += g0_ref[n:, :] + up_ref[:tall, :]


def r_body(layers, size, r0_ref, below_ref, cx_ref, nx_ref, r_ref):
    n = layers * size
    su, eu, nx = split(below_ref[:n, :].T), split(below_ref[n : 2 * n, :]), split(nx_ref[...])
    cx = split(whole_sym(take_sym(cx_ref, layers, size), layers))
    r_ref[:n, :] = r0_ref[:n, :] + dot3(su, cx, NN) + dot3(eu, nx, NT)
    r_ref[n:, :] = r0_ref[n:, :] + dot3(su, nx, NN)


def middle_e_body(layers, size, after_ref, sums_ref, more_ref, n_ref, down_ref, d_ref, below_ref, cx_ref, nx_ref, ye0_ref, total_ref, ye_ref):
    at = layers * size
    total_ref[...] = sums_ref[...] + more_ref[...]
    n, e, d = split(n_ref[...]), split(down_ref[at : 2 * at, :]), split(d_ref[...])
    stu, nx = split(below_ref[:at, :]), split(nx_ref[...])
    cx = split(whole_sym(take_sym(cx_ref, layers, size), layers))
    ye_ref[...] = ye0_ref[...] + dot3(n, stu, NT) + dot3(e, cx, NN) + dot3(d, nx, NT)


def middle_n_body(
    layers, size, sums_ref, more_ref, n_ref, down_ref, d_ref, below_ref, nx_ref, yn0_ref, yd0_ref, total_ref, yn_ref, yd_ref
):
    at = layers * size
    total_ref[...] = sums_ref[...] + more_ref[...]
    n, e, d = split(n_ref[...]), split(down_ref[at : 2 * at, :]), split(d_ref[...])
    stu, eu, nx = split(below_ref[:at, :]), split(below_ref[at : 2 * at, :]), split(nx_ref[...])
    cu = split(whole_sym(take_sym(below_ref[2 * at :, :], layers, size), layers))
    yn_ref[...] = yn0_ref[...] + dot3(n, cu, NN) + dot3(e, stu, NN) + dot3(d, eu, NT)
    yd_ref[...] = yd0_ref[...] + dot3(n, eu, NN) + dot3(e, nx, NN)


def mix_body(
    layers, size, target, mask_ref, c_ref, n_ref, down_ref, d_ref, yc_ref, yn_ref, ys_ref, ye_ref, yd_ref,
    cxu_ref, up_ref, sums_ref, more_ref,
    out_ref, pc_ref, pn_ref, ps_ref, pe_ref, scale_ref, held, zero, sems,
):
    n, tall = layers * size, sym_rows(layers, size)
    sums = sums_ref[...] + more_ref[...]
    t1, t2 = sums[0:1, :], sums[1:2, :]
    twice = 2.0 * jax.nn.sigmoid((jnp.abs(t2 - target) - jnp.abs(2.0 * t1 - t2 - target)) / size)
    scale_ref[...] = jnp.broadcast_to(1.0 - twice, scale_ref.shape)
    slots = out_ref.shape[1]
    zero[...] = jnp.zeros(zero.shape, F32)
    written = {(layer, 0) for layer in range(layers)}
    for name in IN_PLANE:
        written |= {(low, slot) for low, _, slot in panel_blocks(name, layers)}
    copies = []
    for layer in range(layers):
        for slot in range(slots):
            if (layer, slot) not in written:
                copies.append(pltpu.make_async_copy(zero, out_ref.at[layer, slot], sems.at[len(copies)]))
                copies[-1].start()

    def mixed(y, a):
        return y + twice * (a - y)

    cxu = split(whole_sym(take_sym(cxu_ref, layers, size), layers))
    yd = yd_ref[...] + dot3(split(d_ref[...]), cxu, NN)
    for k, (low, high, slot) in enumerate(panel_blocks("D", layers)):
        rows, cols = slice(low * size, (low + 1) * size), slice(high * size, (high + 1) * size)
        held[k] = jnp.where(kept(mask_ref, low, slot), mixed(yd[rows, cols], d_ref[rows, cols]), 0.0)
        copies.append(pltpu.make_async_copy(held.at[k], out_ref.at[low, slot], sems.at[len(copies)]))
        copies[-1].start()
    c_blocks = take_sym(yc_ref[...] + up_ref[tall:, :], layers, size)
    put_sym(
        pc_ref,
        lambda a, b: mixed(c_blocks[a, b], c_ref[a * size : (a + 1) * size, b * size : (b + 1) * size]),
        layers,
        size,
    )
    for layer in range(layers):
        for name, y_ref, a_ref, p_ref in (
            ("N", yn_ref, n_ref, pn_ref),
            ("S", ys_ref, down_ref.at[:n, :], ps_ref),
            ("E", ye_ref, down_ref.at[n : 2 * n, :], pe_ref),
        ):
            rows = slice(layer * size, (layer + 1) * size)
            for other in range(layers):
                cols = slice(other * size, (other + 1) * size)
                a = a_ref[cols, rows].T if name == "S" else a_ref[rows, cols]
                p_ref[rows, cols] = mixed(y_ref[rows, cols], a)
    for copy in copies:
        copy.wait()


def mix_body_for(target, layers, size, *refs):
    mix_body(layers, size, target, *refs)


def side_body(names, layers, size, mask_ref, _, scale_ref, *rest):
    *p_refs, late_ref, out_ref, held, sems = rest
    n = layers * size
    scale = scale_ref[0:1, :]
    wide = jnp.concatenate([scale] * layers, axis=1)
    copies = []

    def send(value, low, slot):
        k = len(copies)
        held[k] = value
        copies.append(pltpu.make_async_copy(held.at[k], out_ref.at[low, slot], sems.at[k]))
        copies[-1].start()

    for at, name in enumerate(names):
        p_ref, top = p_refs[at], at * n
        if name == "C":
            blocks = take_sym(p_ref[...] + wide * late_ref[top:, :], layers, size)
            for layer in range(layers):
                send(blocks[layer, layer], layer, 0)
        for low, high, slot in panel_blocks(name, layers):
            rows, cols = slice(low * size, (low + 1) * size), slice(high * size, (high + 1) * size)
            value = blocks[low, high] if name == "C" else p_ref[rows, cols] + scale * late_ref[top + low * size : top + (low + 1) * size, cols]
            send(jnp.where(kept(mask_ref, low, slot), value, 0.0), low, slot)
    for copy in copies:
        copy.wait()


def call(body, layers, size, outs, spaces, products, scratch=(), limit=40, out_spaces=None, aliases=None):
    n = layers * size
    return pl.pallas_call(
        functools.partial(body, layers, size),
        out_shape=[jax.ShapeDtypeStruct(shape, F32) for shape in outs],
        in_specs=[pl.BlockSpec(memory_space=space) for space in spaces],
        out_specs=[pl.BlockSpec(memory_space=space) for space in out_spaces or [pltpu.VMEM] * len(outs)],
        scratch_shapes=list(scratch),
        input_output_aliases=aliases or {},
        compiler_params=pltpu.CompilerParams(vmem_limit_bytes=limit << 20),
        cost_estimate=pl.CostEstimate(
            flops=int(products * 6 * n**3), bytes_accessed=4 * n * n * (len(outs) + len(spaces)), transcendentals=0
        ),
    )


def passed_along(value, axis, by):
    peers = lax.axis_size(axis)
    return lax.ppermute(value, axis, [(i, (i + by) % peers) for i in range(peers)])


def swapped(value, axis, bit):
    peers = lax.axis_size(axis)
    return lax.ppermute(value, axis, [(i, i ^ bit) for i in range(peers)])


def rounds_of(axis):
    peers = lax.axis_size(axis)
    bits = [1 << k for k in range(peers.bit_length() - 1)]
    return [(axis, bit) for bit in bits[1:2] + bits[:1] + bits[2:]]


def shards(stored_blocks, onsite, bond_mask):
    stored, onsite, mask = stored_blocks[0, 0], onsite[0, 0], bond_mask[0, 0]
    layers, slots, size = stored.shape[:3]
    n, tall = layers * size, sym_rows(layers, size)
    panel, packed, sums = (n, n), (tall, n), (8, size)
    vmem, smem, hbm = pltpu.VMEM, pltpu.SMEM, pltpu.HBM

    def blocks(count):
        return [pltpu.VMEM((count, size, size), F32), pltpu.SemaphoreType.DMA((count,))]

    go = functools.partial(call, layers=layers, size=size)
    (N,) = go(
        pack_n_body, outs=[panel], spaces=[smem, hbm], products=0.1, scratch=blocks(len(wanted_n(layers))), limit=58
    )(mask, stored)
    N_x = passed_along(N, "row", -1)
    Cp, down, C, D, own = go(
        pack_body, outs=[packed, (2 * n + tall, n), panel, panel, sums], spaces=[smem, hbm, vmem, vmem], products=0.1,
        scratch=blocks(len(wanted_rest(layers))), limit=58,
    )(mask, stored, onsite, N)
    Cp_x = passed_along(Cp, "row", -1)
    below = passed_along(down, "col", -1)
    (up,) = go(up_body, outs=[(2 * tall, n)], spaces=[vmem] * 2, products=2, limit=16)(N, D)
    up = passed_along(up, "col", 1)

    if all(lax.axis_size(axis).bit_count() == 1 for axis in ("row", "col")):
        order = rounds_of("row") + rounds_of("col")
    else:
        order, own = [], lax.psum(own, ("row", "col"))
    hosts = 4
    plain = max(len(order) - hosts, 0)
    for axis, bit in order[:plain]:
        own = own + swapped(own, axis, bit)
    order = order[plain:]

    def arriving(value):
        return swapped(value, *order.pop(0)) if order else jnp.zeros_like(value)

    more = arriving(own)
    g0, r0 = go(local_g_body, outs=[(n + tall, n), (2 * n, n)], spaces=[vmem] * 3, products=4, limit=24)(N, down, D)
    yc, yn, ys, ye, yd = go(local_y_body, outs=[packed] + [panel] * 4, spaces=[vmem] * 4, products=8, limit=24)(C, N, down, D)
    own, g = go(g_body, outs=[sums, (n + tall, n)], spaces=[vmem] * 5, products=2, limit=16)(own, more, g0, below, up)
    g = passed_along(g, "row", 1)
    more = arriving(own)
    Cp_xu = passed_along(Cp_x, "col", -1)
    (r,) = go(r_body, outs=[(2 * n, n)], spaces=[vmem] * 4, products=3, limit=24)(r0, below, Cp_x, N_x)
    own, ye = go(middle_e_body, outs=[sums, panel], spaces=[hbm] + [vmem] * 9, products=3, limit=24)(
        r, own, more, N, down, D, below, Cp_x, N_x, ye
    )
    r = passed_along(r, "col", 1)
    more = arriving(own)
    own, yn, yd = go(middle_n_body, outs=[sums, panel, panel], spaces=[vmem] * 9, products=5, limit=24)(
        own, more, N, down, D, below, N_x, yn, yd
    )
    more = arriving(own)
    cells = lax.axis_size("row") * lax.axis_size("col") * layers
    stack = (layers, slots, size, size)
    count = len(panel_blocks("D", layers))
    out, pc, pn, ps, pe, scale = go(
        functools.partial(mix_body_for, float(cells * size // 2)),
        outs=[stack, packed, panel, panel, panel, sums], out_spaces=[hbm] + [vmem] * 5,
        spaces=[smem] + [vmem] * 13, products=1, limit=24,
        scratch=[pltpu.VMEM((count, size, size), F32), pltpu.VMEM((size, size), F32), pltpu.SemaphoreType.DMA((layers * slots,))],
    )(mask, C, N, down, D, yc, yn, ys, ye, yd, Cp_xu, up, own, more)
    for names, terms in ((("S", "E"), (ps, pe, r)), (("N", "C"), (pn, pc, g))):
        count = sum(len(panel_blocks(name, layers)) for name in names) + layers * ("C" in names)
        (out,) = go(
            functools.partial(side_body, names), outs=[stack], out_spaces=[hbm], spaces=[smem, hbm] + [vmem] * 4,
            products=0.1, scratch=blocks(count), limit=16, aliases={1: 0},
        )(mask, out, scale, *terms)
    return out[None, None]


def solution(mesh):
    in_specs = (
        P("row", "col", None, None, None, None),
        P("row", "col", None, None),
        P("row", "col", None, None),
    )
    out_specs = P("row", "col", None, None, None, None)
    return jax.shard_map(shards, mesh=mesh, in_specs=in_specs, out_specs=out_specs, check_vma=False)
```

time: 114 us -> 106 us (0.930)
  waiting for transfers between devices: 45.5 us -> 37.9 us
  local copies, waits for them, and re-layouts: 7.27 us -> 1.75 us
  Pallas kernels: 36.5 us -> 39.6 us
  starting transfers between devices: 23.8 us -> 25.9 us
    ppermute x0 -> x5, starting transfers between devices: none -> 16.3 us  [swapped(): return lax.ppermute(value, axis, [(i, i ^ bit) for i in range(peers)])]
    ppermute x22 -> x7, waiting for transfers between devices: 45.5 us -> 30.9 us  [passed_along(): lax.ppermute(value, axis, [(i, (i + by) % peers) for i in range(peers)])]
    ppermute x22 -> x7, starting transfers between devices: 23.8 us -> 9.65 us  [passed_along(): lax.ppermute(value, axis, [(i, (i + by) % peers) for i in range(peers)])]
    ppermute x0 -> x5, waiting for transfers between devices: none -> 6.99 us  [swapped(): return lax.ppermute(value, axis, [(i, i ^ bit) for i in range(peers)])]
    unnamed x18 -> x14, local copies, waits for them, and re-layouts: 7.27 us -> 1.75 us
    pallas_call x9, Pallas kernels: 28.1 us -> 32.3 us  [the longest x1 6.57 us: shards(): go(local_y_body, outs=[packed] + [panel] * 4, spaces=[vmem] * 4, products...]
  transfers between devices with their start and end apart: 22 -> 12, of which waited for: 9 -> 7; matrix products, arithmetic and copies ran while one was open for 0% -> 0% of each run, Pallas kernels for 29% -> 27%
where the time goes in v3:
time: 106 us; the launch traced here: 105 us
  Pallas kernels  39.6 us (37%)
  waiting for transfers between devices  37.9 us (36%)
  starting transfers between devices  25.9 us (24%)
  local copies, waits for them, and re-layouts  1.75 us (2%)
    ppermute x7, waiting for transfers between devices, passed_along(): lax.ppermute(value, axis, [(i, (i + by) % peers) for i in range(peers)])  30.9 us
    ppermute x5, starting transfers between devices, swapped(): return lax.ppermute(value, axis, [(i, i ^ bit) for i in range(peers)])  16.3 us
    ppermute x7, starting transfers between devices, passed_along(): lax.ppermute(value, axis, [(i, (i + by) % peers) for i in range(peers)])  9.65 us
    ppermute x5, waiting for transfers between devices, swapped(): return lax.ppermute(value, axis, [(i, i ^ bit) for i in range(peers)])  6.99 us
    pallas_call x1, Pallas kernels, shards(): go(local_y_body, outs=[packed] + [panel] * 4, spaces=[vmem] * 4, products...  6.57 us
    pallas_call x1, Pallas kernels, shards(): go(pack_body, outs=[packed, (2 * n + tall, n), panel, panel, sums], space...  6.29 us
    pallas_call x1, Pallas kernels, shards(): go(middle_n_body, outs=[sums, panel, panel], spaces=[vmem] * 9, products=...  4.46 us
    pallas_call x2, Pallas kernels, shards(): go(functools.partial(side_body, names), outs=[stack], out_spaces=[hbm], s...  3.88 us
  transfers between devices with their start and end apart: 12, of which 7 were waited for; matrix products, arithmetic and copies ran while one was open for 0% of the time, Pallas kernels for 27%

profile of v3, /device:TPU:0, one launch (start us, length us, event | category | flops | bytes accessed | tf_op | source)
XLA Modules:
  0.0 105.5 jit_solution(3642036846014006059)
XLA Ops:
  0.0 3.0 %shard_map.37.n_ref.refs_2_ = f32[512,512]{1,0:T(8,128)} custom-call(s32[2,13]{1,0:T(2,128)} %bitcast.4, f32[2,14,256,256]{3,2,1,0:T(8,128)} %bitcast.9), custom_call_target="tpu_custom_call" | custom-call | flops 80530640 | bytes 3145728 | tf_op jit(solution)/shard_map/pallas_call | solution.py:429
  3.0 6.3 %shard_map.38 = (f32[264,512]{1,0:T(8,128)}, f32[1288,512]{1,0:T(8,128)}, f32[512,512]{1,0:T(8,128)}, f32[512,512]{1,0:T(8,128)}, f32[8,256]{1,0:T(8,128)}) custom-call(s32[2,13]{1,0:T(2,128)} %bitcast.5, f32[2,14,256,256]{3,2,1,0:T(8,128)} %bitcast.10, f32[2,256]{1,0:T(2,128)} %bitcast.11, f32[512,512]{1,0:T(8,128)} %shard_map.37.n_ref.refs_2_), custom_call_target="tpu_custom_call" | custom-call | flops 80530640 | bytes 9437184 | tf_op jit(solution)/shard_map/pallas_call | solution.py:433
  9.3 3.4 %collective-permute-start = (f32[1288,512]{1,0:T(8,128)}, f32[1288,512]{1,0:T(8,128)S(1)}, u32[]{:S(2)}, u32[]{:S(2)}) collective-permute-start(f32[1288,512]{1,0:T(8,128)} %get-tuple-element.31.down_ref.refs_3_), channel_id=1, source_target_pairs={{0,7},{1,0},{2,1},{3,2},{4,3},{5,4},{6,5},{7,6},{8,15},{9,8},{10,9... | collective-permute-start | bytes 7913480 | tf_op jit(solution)/shard_map/ppermute | solution.py:404
  12.7 3.6 %collective-permute-start.2 = (f32[512,512]{1,0:T(8,128)S(1)}, f32[512,512]{1,0:T(8,128)S(1)}, u32[]{:S(2)}, u32[]{:S(2)}) collective-permute-start(f32[512,512]{1,0:T(8,128)S(1)} %copy-done), channel_id=1, source_target_pairs={{0,24},{8,0},{16,8},{24,16},{1,25},{9,1},{17,9},{25,17},{2,26},{10... | collective-permute-start | bytes 3145736 | tf_op jit(solution)/shard_map/ppermute | solution.py:404
  16.3 0.4 collective-permute-start.1
  16.7 1.2 %copy-done.2 = f32[512,512]{1,0:T(8,128)S(1)} copy-done((f32[512,512]{1,0:T(8,128)S(1)}, f32[512,512]{1,0:T(8,128)}, u32[]{:S(2)}) %copy-start.2) | copy-done | bytes 1048600
  18.0 1.4 %shard_map.42 = f32[528,512]{1,0:T(8,128)S(1)} custom-call(f32[512,512]{1,0:T(8,128)S(1)} %copy-done, f32[512,512]{1,0:T(8,128)S(1)} %copy-done.2), custom_call_target="tpu_custom_call" | custom-call | flops 1610612736 | bytes 3145728 | tf_op jit(solution)/shard_map/pallas_call | solution.py:439
  19.5 0.2 copy-done.1
  19.7 0.3 copy-done.3
  20.0 3.3 %shard_map.40 = (f32[776,512]{1,0:T(8,128)S(1)}, f32[1024,512]{1,0:T(8,128)S(1)}) custom-call(f32[512,512]{1,0:T(8,128)S(1)} %copy-done, f32[1288,512]{1,0:T(8,128)S(1)} %copy-done.1, f32[512,512]{1,0:T(8,128)S(1)} %copy-done.3), custom_call_target="tpu_custom_call" | custom-call | flops 3221225472 | bytes 5242880 | tf_op jit(solution)/shard_map/pallas_call | solution.py:456
  23.3 25.9 %collective-permute-done.1.cx_ref = f32[264,512]{1,0:T(8,128)S(1)} collective-permute-done((f32[264,512]{1,0:T(8,128)}, f32[264,512]{1,0:T(8,128)S(1)}, u32[]{:S(2)}, u32[]{:S(2)}) %collective-permute-start.1) | collective-permute-done | bytes 540704 | tf_op jit(solution)/shard_map/ppermute | solution.py:404
  49.2 4.7 %collective-permute-done.below_ref = f32[1288,512]{1,0:T(8,128)S(1)} collective-permute-done((f32[1288,512]{1,0:T(8,128)}, f32[1288,512]{1,0:T(8,128)S(1)}, u32[]{:S(2)}, u32[]{:S(2)}) %collective-permute-start) | collective-permute-done | bytes 2637856 | tf_op jit(solution)/shard_map/ppermute | solution.py:404
  53.9 2.9 %shard_map.41.after_ref = f32[1024,512]{1,0:T(8,128)S(1)} custom-call(f32[1024,512]{1,0:T(8,128)S(1)} %get-tuple-element.34.r0_ref, f32[1288,512]{1,0:T(8,128)S(1)} %collective-permute-done.below_ref, f32[264,512]{1,0:T(8,128)S(1)} %collective-permute-done.1.cx_ref, f32[512,512]{1,0:T(8,128)S(1)} %collective-permute-done.2.nx_ref), custom_call_target="tpu_custom_call" | custom-call | flops 2415919104 | bytes 5242880 | tf_op jit(solution)/shard_map/pallas_call | solution.py:462
  56.9 2.6 %collective-permute-start.3 = (f32[8,256]{1,0:T(8,128)S(1)}, f32[8,256]{1,0:T(8,128)S(1)}, u32[]{:S(2)}, u32[]{:S(2)}) collective-permute-start(f32[8,256]{1,0:T(8,128)S(1)} %copy-done.6), channel_id=1, source_target_pairs={{0,16},{8,24},{16,0},{24,8},{1,17},{9,25},{17,1},{25,9},{2,18},{10... | collective-permute-start | bytes 24584 | tf_op jit(solution)/shard_map/ppermute | solution.py:409
  59.5 2.0 %collective-permute-done.3 = f32[8,256]{1,0:T(8,128)S(1)} collective-permute-done((f32[8,256]{1,0:T(8,128)S(1)}, f32[8,256]{1,0:T(8,128)S(1)}, u32[]{:S(2)}, u32[]{:S(2)}) %collective-permute-start.3) | collective-permute-done | bytes 8224 | tf_op jit(solution)/shard_map/ppermute | solution.py:409
  61.5 1.6 %collective-permute-start.4 = (f32[8,256]{1,0:T(8,128)S(1)}, f32[8,256]{1,0:T(8,128)S(1)}, u32[]{:S(2)}, u32[]{:S(2)}) collective-permute-start(f32[8,256]{1,0:T(8,128)S(1)} %add.3.sums_ref), channel_id=1, source_target_pairs={{0,8},{8,0},{16,24},{24,16},{1,9},{9,1},{17,25},{25,17},{2,10},{10... | collective-permute-start | bytes 24584 | tf_op jit(solution)/shard_map/ppermute | solution.py:409
  63.1 2.1 %collective-permute-done.4.more_ref = f32[8,256]{1,0:T(8,128)S(1)} collective-permute-done((f32[8,256]{1,0:T(8,128)S(1)}, f32[8,256]{1,0:T(8,128)S(1)}, u32[]{:S(2)}, u32[]{:S(2)}) %collective-permute-start.4) | collective-permute-done | bytes 8224 | tf_op jit(solution)/shard_map/ppermute | solution.py:409
  65.2 1.7 %shard_map.43 = (f32[8,256]{1,0:T(8,128)S(1)}, f32[776,512]{1,0:T(8,128)S(1)}) custom-call(f32[8,256]{1,0:T(8,128)S(1)} %add.3.sums_ref, f32[8,256]{1,0:T(8,128)S(1)} %collective-permute-done.4.more_ref, f32[776,512]{1,0:T(8,128)S(1)} %get-tuple-element.37.g0_ref, f32[1288,512]{1,0:T(8,128)S(1)} %collective-permute-done.below_ref, ...), custom_call_target="tpu_custom_call" | custom-call | flops 1610612736 | bytes 7340032 | tf_op jit(solution)/shard_map/pallas_call | solution.py:458
  66.9 1.8 %collective-permute-start.11 = (f32[776,512]{1,0:T(8,128)S(1)}, f32[776,512]{1,0:T(8,128)S(1)}, u32[]{:S(2)}, u32[]{:S(2)}) collective-permute-start(f32[776,512]{1,0:T(8,128)S(1)} %get-tuple-element.54), channel_id=1, source_target_pairs={{0,8},{8,16},{16,24},{24,0},{1,9},{9,17},{17,25},{25,1},{2,10},{10... | collective-permute-start | bytes 4767752 | tf_op jit(solution)/shard_map/ppermute | solution.py:404
  68.7 2.0 %collective-permute-start.6 = (f32[8,256]{1,0:T(8,128)S(1)}, f32[8,256]{1,0:T(8,128)S(1)}, u32[]{:S(2)}, u32[]{:S(2)}) collective-permute-start(f32[8,256]{1,0:T(8,128)S(1)} %get-tuple-element.38.sums_ref), channel_id=1, source_target_pairs={{0,2},{1,3},{2,0},{3,1},{4,6},{5,7},{6,4},{7,5},{8,10},{9,11},{10,... | collective-permute-start | bytes 24584 | tf_op jit(solution)/shard_map/ppermute | solution.py:409
  70.7 6.6 %shard_map.39 = (f32[264,512]{1,0:T(8,128)S(1)}, f32[512,512]{1,0:T(8,128)S(1)}, f32[512,512]{1,0:T(8,128)S(1)}, f32[512,512]{1,0:T(8,128)S(1)}, f32[512,512]{1,0:T(8,128)S(1)}) custom-call(f32[512,512]{1,0:T(8,128)S(1)} %copy-done.4, f32[512,512]{1,0:T(8,128)S(1)} %copy-done, f32[1288,512]{1,0:T(8,128)S(1)} %copy-done.1, f32[512,512]{1,0:T(8,128)S(1)} %copy-done.3), custom_call_target="tpu_custom_call" | custom-call | flops 6442450944 | bytes 9437184 | tf_op jit(solution)/shard_map/pallas_call | solution.py:457
  77.3 0.3 collective-permute-start.8
  77.6 2.7 %shard_map.44 = (f32[8,256]{1,0:T(8,128)S(1)}, f32[512,512]{1,0:T(8,128)S(1)}) custom-call(f32[1024,512]{1,0:T(8,128)S(1)} %shard_map.41.after_ref, f32[8,256]{1,0:T(8,128)S(1)} %get-tuple-element.38.sums_ref, f32[8,256]{1,0:T(8,128)S(1)} %collective-permute-done.6.more_ref, f32[512,512]{1,0:T(8,128)S(1)} %copy-done, f32[1288,512]{1,0:T(8,128)S(1)} %copy-done.1, ...), custom_call_target="tpu_custom_call" | custom-call | flops 2415919104 | bytes 12582912 | tf_op jit(solution)/shard_map/pallas_call | solution.py:463
  80.3 8.4 %collective-permute-start.7 = (f32[8,256]{1,0:T(8,128)S(1)}, f32[8,256]{1,0:T(8,128)S(1)}, u32[]{:S(2)}, u32[]{:S(2)}) collective-permute-start(f32[8,256]{1,0:T(8,128)S(1)} %get-tuple-element.40.sums_ref), channel_id=1, source_target_pairs={{0,1},{1,0},{2,3},{3,2},{4,5},{5,4},{6,7},{7,6},{8,9},{9,8},{10,11... | collective-permute-start | bytes 24584 | tf_op jit(solution)/shard_map/ppermute | solution.py:409
  88.8 0.8 collective-permute-done.7.more_ref
  89.6 4.5 %shard_map.45 = (f32[8,256]{1,0:T(8,128)S(1)}, f32[512,512]{1,0:T(8,128)S(1)}, f32[512,512]{1,0:T(8,128)S(1)}) custom-call(f32[8,256]{1,0:T(8,128)S(1)} %get-tuple-element.40.sums_ref, f32[8,256]{1,0:T(8,128)S(1)} %collective-permute-done.7.more_ref, f32[512,512]{1,0:T(8,128)S(1)} %copy-done, f32[1288,512]{1,0:T(8,128)S(1)} %copy-done.1, ...), custom_call_target="tpu_custom_call" | custom-call | flops 4026531840 | bytes 12582912 | tf_op jit(solution)/shard_map/pallas_call | solution.py:468
  94.1 1.6 %collective-permute-start.9 = (f32[8,256]{1,0:T(8,128)S(1)}, f32[8,256]{1,0:T(8,128)S(1)}, u32[]{:S(2)}, u32[]{:S(2)}) collective-permute-start(f32[8,256]{1,0:T(8,128)S(1)} %get-tuple-element.47.refs_12_), channel_id=1, source_target_pairs={{0,4},{1,5},{2,6},{3,7},{4,0},{5,1},{6,2},{7,3},{8,12},{9,13},{10,... | collective-permute-start | bytes 24584 | tf_op jit(solution)/shard_map/ppermute | solution.py:409
  95.7 2.1 %collective-permute-done.9.refs_13_ = f32[8,256]{1,0:T(8,128)S(1)} collective-permute-done((f32[8,256]{1,0:T(8,128)S(1)}, f32[8,256]{1,0:T(8,128)S(1)}, u32[]{:S(2)}, u32[]{:S(2)}) %collective-permute-start.9) | collective-permute-done | bytes 8224 | tf_op jit(solution)/shard_map/ppermute | solution.py:409
  97.8 3.3 %shard_map.46 = (f32[2,14,256,256]{3,2,1,0:T(8,128)}, f32[264,512]{1,0:T(8,128)S(1)}, f32[512,512]{1,0:T(8,128)S(1)}, f32[512,512]{1,0:T(8,128)S(1)}, f32[512,512]{1,0:T(8,128)S(1)}, /*index=5*/f32[8,256]{1,0:T(8,128)S(1)}) custom-call(s32[2,13]{1,0:T(2,128)S(1)} %bitcast.6, f32[512,512]{1,0:T(8,128)S(1)} %copy-done.4, f32[512,512]{1,0:T(8,128)S(1)} %copy-done, ...), custom_call_target="tpu_custom_call" | custom-call | flops 805306368 | bytes 20971520 | tf_op jit(solution)/shard_map/pallas_call | solution.py:475
  101.2 2.0 %shard_map.47._ = f32[2,14,256,256]{3,2,1,0:T(8,128)} custom-call(s32[2,13]{1,0:T(2,128)S(1)} %bitcast.7, f32[2,14,256,256]{3,2,1,0:T(8,128)} %get-tuple-element.48._, f32[8,256]{1,0:T(8,128)S(1)} %get-tuple-element.49.scale_ref, f32[512,512]{1,0:T(8,128)S(1)} %get-tuple-element.50.rest_0_, ...), custom_call_target="tpu_custom_call", output_to_operand_aliasing={{}: (1, {})} | custom-call | flops 80530640 | bytes 7340032 | tf_op jit(solution)/shard_map/pallas_call | solution.py:483
  103.1 0.3 collective-permute-done.11.rest_2_
  103.4 1.9 %shard_map.48 = f32[2,14,256,256]{3,2,1,0:T(8,128)} custom-call(s32[2,13]{1,0:T(2,128)S(1)} %bitcast.8, f32[2,14,256,256]{3,2,1,0:T(8,128)} %shard_map.47._, f32[8,256]{1,0:T(8,128)S(1)} %get-tuple-element.49.scale_ref, f32[512,512]{1,0:T(8,128)S(1)} %get-tuple-element.52.rest_0_, ...), custom_call_target="tpu_custom_call", output_to_operand_aliasing={{}: (1, {})} | custom-call | flops 80530640 | bytes 7340032 | tf_op jit(solution)/shard_map/pallas_call | solution.py:483
  (19 shorter events, 0.2 us)
Async XLA Ops:
  3.0 9.7 %copy-start = (f32[512,512]{1,0:T(8,128)S(1)}, f32[512,512]{1,0:T(8,128)}, u32[]{:S(2)}) copy-start(f32[512,512]{1,0:T(8,128)} %shard_map.37.n_ref.refs_2_) | copy-start | bytes 3145732
  9.3 44.6 %collective-permute-start = (f32[1288,512]{1,0:T(8,128)}, f32[1288,512]{1,0:T(8,128)S(1)}, u32[]{:S(2)}, u32[]{:S(2)}) collective-permute-start(f32[1288,512]{1,0:T(8,128)} %get-tuple-element.31.down_ref.refs_3_), channel_id=1, source_target_pairs={{0,7},{1,0},{2,1},{3,2},{4,3},{5,4},{6,5},{7,6},{8,15},{9,8},{10,9... | collective-permute-start | bytes 7913480 | tf_op jit(solution)/shard_map/ppermute | solution.py:404
  12.7 36.5 %collective-permute-start.2 = (f32[512,512]{1,0:T(8,128)S(1)}, f32[512,512]{1,0:T(8,128)S(1)}, u32[]{:S(2)}, u32[]{:S(2)}) collective-permute-start(f32[512,512]{1,0:T(8,128)S(1)} %copy-done), channel_id=1, source_target_pairs={{0,24},{8,0},{16,8},{24,16},{1,25},{9,1},{17,9},{25,17},{2,26},{10... | collective-permute-start | bytes 3145736 | tf_op jit(solution)/shard_map/ppermute | solution.py:404
  16.3 32.9 %collective-permute-start.1 = (f32[264,512]{1,0:T(8,128)}, f32[264,512]{1,0:T(8,128)S(1)}, u32[]{:S(2)}, u32[]{:S(2)}) collective-permute-start(f32[264,512]{1,0:T(8,128)} %get-tuple-element.35), channel_id=1, source_target_pairs={{0,24},{8,0},{16,8},{24,16},{1,25},{9,1},{17,9},{25,17},{2,26},{10... | collective-permute-start | bytes 1622024 | tf_op jit(solution)/shard_map/ppermute | solution.py:404
  16.7 1.2 %copy-start.2 = (f32[512,512]{1,0:T(8,128)S(1)}, f32[512,512]{1,0:T(8,128)}, u32[]{:S(2)}) copy-start(f32[512,512]{1,0:T(8,128)} %get-tuple-element.32.d_ref.refs_4_) | copy-start | bytes 3145732
  18.0 1.7 %copy-start.1 = (f32[1288,512]{1,0:T(8,128)S(1)}, f32[1288,512]{1,0:T(8,128)}, u32[]{:S(2)}) copy-start(f32[1288,512]{1,0:T(8,128)} %get-tuple-element.31.down_ref.refs_3_) | copy-start | bytes 7913476
  18.0 2.0 %copy-start.3 = (f32[512,512]{1,0:T(8,128)S(1)}, f32[512,512]{1,0:T(8,128)}, u32[]{:S(2)}) copy-start(f32[512,512]{1,0:T(8,128)} %get-tuple-element.32.d_ref.refs_4_) | copy-start | bytes 3145732
  19.4 45.8 %collective-permute-start.5 = (f32[528,512]{1,0:T(8,128)S(1)}, f32[528,512]{1,0:T(8,128)S(1)}, u32[]{:S(2)}, u32[]{:S(2)}) collective-permute-start(f32[528,512]{1,0:T(8,128)S(1)} %shard_map.42), channel_id=1, source_target_pairs={{0,1},{1,2},{2,3},{3,4},{4,5},{5,6},{6,7},{7,0},{8,9},{9,10},{10,1... | collective-permute-start | bytes 3244040 | tf_op jit(solution)/shard_map/ppermute | solution.py:404
  53.9 3.0 %copy-start.6 = (f32[8,256]{1,0:T(8,128)S(1)}, f32[8,256]{1,0:T(8,128)}, u32[]{:S(2)}) copy-start(f32[8,256]{1,0:T(8,128)} %get-tuple-element.36) | copy-start | bytes 24580
  56.8 44.3 %collective-permute-start.10 = (f32[1024,512]{1,0:T(8,128)S(1)}, f32[1024,512]{1,0:T(8,128)S(1)}, u32[]{:S(2)}, u32[]{:S(2)}) collective-permute-start(f32[1024,512]{1,0:T(8,128)S(1)} %shard_map.41.after_ref), channel_id=1, source_target_pairs={{0,1},{1,2},{2,3},{3,4},{4,5},{5,6},{6,7},{7,0},{8,9},{9,10},{10,1... | collective-permute-start | bytes 6291464 | tf_op jit(solution)/shard_map/ppermute | solution.py:404
  56.9 4.6 %collective-permute-start.3 = (f32[8,256]{1,0:T(8,128)S(1)}, f32[8,256]{1,0:T(8,128)S(1)}, u32[]{:S(2)}, u32[]{:S(2)}) collective-permute-start(f32[8,256]{1,0:T(8,128)S(1)} %copy-done.6), channel_id=1, source_target_pairs={{0,16},{8,24},{16,0},{24,8},{1,17},{9,25},{17,1},{25,9},{2,18},{10... | collective-permute-start | bytes 24584 | tf_op jit(solution)/shard_map/ppermute | solution.py:409
  61.5 3.7 %collective-permute-start.4 = (f32[8,256]{1,0:T(8,128)S(1)}, f32[8,256]{1,0:T(8,128)S(1)}, u32[]{:S(2)}, u32[]{:S(2)}) collective-permute-start(f32[8,256]{1,0:T(8,128)S(1)} %add.3.sums_ref), channel_id=1, source_target_pairs={{0,8},{8,0},{16,24},{24,16},{1,9},{9,1},{17,25},{25,17},{2,10},{10... | collective-permute-start | bytes 24584 | tf_op jit(solution)/shard_map/ppermute | solution.py:409
  65.2 5.5 %copy-start.4 = (f32[512,512]{1,0:T(8,128)S(1)}, f32[512,512]{1,0:T(8,128)}, u32[]{:S(2)}) copy-start(f32[512,512]{1,0:T(8,128)} %get-tuple-element.30.c_ref.refs_1_) | copy-start | bytes 3145732
  66.9 36.5 %collective-permute-start.11 = (f32[776,512]{1,0:T(8,128)S(1)}, f32[776,512]{1,0:T(8,128)S(1)}, u32[]{:S(2)}, u32[]{:S(2)}) collective-permute-start(f32[776,512]{1,0:T(8,128)S(1)} %get-tuple-element.54), channel_id=1, source_target_pairs={{0,8},{8,16},{16,24},{24,0},{1,9},{9,17},{17,25},{25,1},{2,10},{10... | collective-permute-start | bytes 4767752 | tf_op jit(solution)/shard_map/ppermute | solution.py:404
  68.7 8.9 %collective-permute-start.6 = (f32[8,256]{1,0:T(8,128)S(1)}, f32[8,256]{1,0:T(8,128)S(1)}, u32[]{:S(2)}, u32[]{:S(2)}) collective-permute-start(f32[8,256]{1,0:T(8,128)S(1)} %get-tuple-element.38.sums_ref), channel_id=1, source_target_pairs={{0,2},{1,3},{2,0},{3,1},{4,6},{5,7},{6,4},{7,5},{8,10},{9,11},{10,... | collective-permute-start | bytes 24584 | tf_op jit(solution)/shard_map/ppermute | solution.py:409
  77.3 18.4 %collective-permute-start.8 = (f32[264,512]{1,0:T(8,128)S(1)}, f32[264,512]{1,0:T(8,128)S(1)}, u32[]{:S(2)}, u32[]{:S(2)}) collective-permute-start(f32[264,512]{1,0:T(8,128)S(1)} %collective-permute-done.1.cx_ref), channel_id=1, source_target_pairs={{0,7},{1,0},{2,1},{3,2},{4,3},{5,4},{6,5},{7,6},{8,15},{9,8},{10,9... | collective-permute-start | bytes 1622024 | tf_op jit(solution)/shard_map/ppermute | solution.py:404
  80.3 9.3 %collective-permute-start.7 = (f32[8,256]{1,0:T(8,128)S(1)}, f32[8,256]{1,0:T(8,128)S(1)}, u32[]{:S(2)}, u32[]{:S(2)}) collective-permute-start(f32[8,256]{1,0:T(8,128)S(1)} %get-tuple-element.40.sums_ref), channel_id=1, source_target_pairs={{0,1},{1,0},{2,3},{3,2},{4,5},{5,4},{6,7},{7,6},{8,9},{9,8},{10,11... | collective-permute-start | bytes 24584 | tf_op jit(solution)/shard_map/ppermute | solution.py:409
  89.6 8.2 %copy-start.5 = (s32[1,1,2,13]{3,2,1,0:T(2,128)S(1)}, s32[1,1,2,13]{3,2,1,0:T(2,128)}, u32[]{:S(2)}) copy-start(s32[1,1,2,13]{3,2,1,0:T(2,128)} %param.5) | copy-start | bytes 316
  94.1 3.7 %collective-permute-start.9 = (f32[8,256]{1,0:T(8,128)S(1)}, f32[8,256]{1,0:T(8,128)S(1)}, u32[]{:S(2)}, u32[]{:S(2)}) collective-permute-start(f32[8,256]{1,0:T(8,128)S(1)} %get-tuple-element.47.refs_12_), channel_id=1, source_target_pairs={{0,4},{1,5},{2,6},{3,7},{4,0},{5,1},{6,2},{7,3},{8,12},{9,13},{10,... | collective-permute-start | bytes 24584 | tf_op jit(solution)/shard_map/ppermute | solution.py:409

commit v4 on v3

v4 whole, which is shorter than its diff:
```python
import functools

import jax
import jax.numpy as jnp
from jax import lax
from jax.experimental import pallas as pl
from jax.experimental.pallas import tpu as pltpu
from jax.sharding import PartitionSpec as P


F32 = jnp.float32
BF16 = jnp.bfloat16
NN = ((1,), (0,))
NT = ((1,), (1,))
TN = ((0,), (0,))
IN_PLANE = {"C": (0, 0), "N": (0, 1), "S": (1, -1), "E": (1, 0), "D": (1, 1)}


def offset_list():
    steps = (-1, 0, 1)
    return [(i, j, k) for i in steps for j in steps for k in steps if (i, j, k) > (0, 0, 0)]


def slot_number(offset):
    return offset_list().index(offset) + 1


def panel_blocks(name, layers):
    side = IN_PLANE[name]
    found = []
    for low in range(layers):
        for high in range(layers):
            step = high - low
            if abs(step) <= 1 and (*side, step) > (0, 0, 0):
                found.append((low, high, slot_number((*side, step))))
    return found


def sym_rows(layers, size):
    blocks = layers * (layers - 1) // 2 + (layers + 1) // 2
    return -(-blocks // layers) * size + 8


def rows_cols(size):
    return (
        lax.broadcasted_iota(jnp.int32, (size, size), 0),
        lax.broadcasted_iota(jnp.int32, (size, size), 1),
    )


def block_slices(k, layers, size):
    row, col = k // layers * size, k % layers * size
    return slice(row, row + size), slice(col, col + size)


def sym_places(layers):
    above = [(a, b) for a in range(layers) for b in range(a + 1, layers)]
    pairs = list(range(0, layers, 2))
    return list(enumerate(above)), [(len(above) + k, k, a) for k, a in enumerate(pairs)]


def put_sym(ref, get, layers, size, first=0):
    row, col = rows_cols(size)
    above, pairs = sym_places(layers)
    last = first + sym_rows(layers, size) - 8

    def put(k, value):
        rows, cols = block_slices(k, layers, size)
        ref[first + rows.start : first + rows.stop, cols] = value

    ref[last : last + 8, :] = jnp.zeros((8, layers * size), F32)
    if len(above) + len(pairs) < (last - first) // size * layers:
        ref[last - size : last, :] = jnp.zeros((size, layers * size), F32)
    for k, (a, b) in above:
        put(k, get(a, b))
    for k, mark, a in pairs:
        block = get(a, a)
        if a + 1 < layers:
            other = get(a + 1, a + 1)
            line = jnp.sum(jnp.where(row == col, other, 0.0), axis=0, keepdims=True)
            ref[last : last + 8, mark * size : (mark + 1) * size] = jnp.broadcast_to(line, (8, size))
            block = jnp.where(row <= col, block, other)
        put(k, block)


def take_sym(packed, layers, size):
    row, col = rows_cols(size)
    above, pairs = sym_places(layers)
    last = sym_rows(layers, size) - 8
    blocks = {}
    for k, (a, b) in above:
        rows, cols = block_slices(k, layers, size)
        blocks[a, b] = packed[rows, cols]
    for k, mark, a in pairs:
        rows, cols = block_slices(k, layers, size)
        block = packed[rows, cols]
        if a + 1 < layers:
            flipped = block.T
            line = packed[last : last + 1, mark * size : (mark + 1) * size]
            blocks[a, a] = jnp.where(row <= col, block, flipped)
            blocks[a + 1, a + 1] = jnp.where(row == col, line, jnp.where(row < col, flipped, block))
        else:
            blocks[a, a] = block
    return blocks


def whole_sym(blocks, layers):
    rows = []
    for a in range(layers):
        rows.append(
            jnp.concatenate(
                [blocks[a, b] if a <= b else blocks[b, a].T for b in range(layers)], axis=1
            )
        )
    return jnp.concatenate(rows, axis=0)


def split(value):
    high = value.astype(BF16)
    return high, (value - high.astype(F32)).astype(BF16)


def dot3(a, b, dims):
    go = functools.partial(lax.dot_general, dimension_numbers=(dims, ((), ())), preferred_element_type=F32)
    return go(a[0], b[0]) + (go(a[0], b[1]) + go(a[1], b[0]))


def cut(pair, at, size):
    return tuple(part[at : at + size, :] for part in pair)


def sym_product(pair, layers, size, dims):
    blocks = {}
    for a in range(layers):
        if dims == NT:
            left = tuple(part[a * size : (a + 1) * size, :] for part in pair)
            right = tuple(part[a * size :, :] for part in pair)
        else:
            left = tuple(part[:, a * size : (a + 1) * size] for part in pair)
            right = tuple(part[:, a * size :] for part in pair)
        strip = dot3(left, right, dims)
        for b in range(a, layers):
            blocks[a, b] = strip[:, (b - a) * size : (b - a + 1) * size]
    return blocks


def kept(mask_ref, layer, slot):
    return mask_ref[layer, slot - 1] > 0


def load_panel(out_ref, held, first, name, layers, size, mask_ref, flip=False, top=0):
    blocks = panel_blocks(name, layers)
    if layers > 2:
        out_ref[top : top + layers * size, :] = jnp.zeros((layers * size, layers * size), F32)
    for k, (low, high, slot) in enumerate(blocks):
        value = jnp.where(kept(mask_ref, low, slot), held[first + k], 0.0)
        if flip:
            low, high, value = high, low, value.T
        out_ref[top + low * size : top + (low + 1) * size, high * size : (high + 1) * size] = value
    return len(blocks)


def start_loads(stored_ref, held, sems, wanted):
    copies = [
        pltpu.make_async_copy(stored_ref.at[low, slot], held.at[k], sems.at[k])
        for k, (low, slot) in enumerate(wanted)
    ]
    for copy in copies:
        copy.start()
    return copies


def squares_of(value):
    return jnp.sum(value * value)


def wanted(layers):
    return [(layer, 0) for layer in range(layers)] + [
        (low, slot) for name in "CSEND" for low, _, slot in panel_blocks(name, layers)
    ]


def pack_body(
    layers, size, mask_ref, stored_ref, onsite_ref, t_ref, packed_ref, c_ref, down_ref, d_ref, sums_ref,
    held, sems, mask, mask_sem, onsite, onsite_sem,
):
    n = layers * size
    small = [
        pltpu.make_async_copy(mask_ref, mask, mask_sem),
        pltpu.make_async_copy(onsite_ref, onsite, onsite_sem),
    ]
    for copy in small:
        copy.start()
    copies = start_loads(stored_ref, held, sems, wanted(layers))
    for copy in small:
        copy.wait()
    row, col = rows_cols(size)
    c_ref[...] = jnp.zeros(c_ref.shape, F32)
    for layer in range(layers):
        copies[layer].wait()
        block = held[layer]
        block = 0.5 * (block + block.T) + jnp.where(row == col, onsite[layer : layer + 1, :], 0.0)
        c_ref[layer * size : (layer + 1) * size, layer * size : (layer + 1) * size] = block
    at = layers
    for low, high, slot in panel_blocks("C", layers):
        copies[at].wait()
        block = jnp.where(kept(mask, low, slot), held[at], 0.0)
        c_ref[low * size : (low + 1) * size, high * size : (high + 1) * size] = block
        c_ref[high * size : (high + 1) * size, low * size : (low + 1) * size] = block.T
        at += 1
    put_sym(
        packed_ref,
        lambda a, b: c_ref[a * size : (a + 1) * size, b * size : (b + 1) * size],
        layers,
        size,
    )
    t_ref[n:, :] = packed_ref[...]
    squares = 0.0
    for name, ref, top in (("S", down_ref, 0), ("E", down_ref, n), ("N", t_ref, 0), ("D", d_ref, 0)):
        count = len(panel_blocks(name, layers))
        for copy in copies[at : at + count]:
            copy.wait()
        load_panel(ref, held, at, name, layers, size, mask, flip=name == "S", top=top)
        squares = squares + squares_of(ref[top : top + n, :])
        at += count
    row, col = rows_cols(n)
    c_now = c_ref[...]
    trace = jnp.sum(jnp.where(row == col, c_now, 0.0))
    line = lax.broadcasted_iota(jnp.int32, sums_ref.shape, 0)
    sums = jnp.where((line == 0) | (line == 4), trace, squares_of(c_now) + 2.0 * squares)
    sums_ref[...] = sums
    last = t_ref.shape[0] - 8
    line = lax.broadcasted_iota(jnp.int32, (8, size), 0)
    for at in range(layers):
        cols = slice(at * size, (at + 1) * size)
        t_ref[last:, cols] = jnp.where(line < 4, t_ref[last:, cols], sums)


def squares_of(value):
    return jnp.sum(value * value)


def up_body(layers, size, n_ref, d_ref, up_ref):
    for k, ref in enumerate((d_ref, n_ref)):
        blocks = sym_product(split(ref[: layers * size, :]), layers, size, TN)
        put_sym(up_ref, lambda a, b: blocks[a, b], layers, size, first=k * sym_rows(layers, size))


def local_g_body(layers, size, _, t_ref, down_ref, d_ref, g_ref, r_ref):
    n = layers * size
    n_now, e, d = split(t_ref[:n, :]), split(down_ref[n:, :]), split(d_ref[...])
    blocks = sym_product(e, layers, size, TN)
    g_ref[:n, :] = dot3(e, d, TN)
    put_sym(g_ref, lambda a, b: blocks[a, b], layers, size, first=n)
    r_ref[:n, :] = dot3(n_now, e, TN)
    r_ref[n:, :] = dot3(n_now, d, TN)


def local_y_body(
    layers, size, _, c_ref, t_ref, down_ref, d_ref, out_ref, yc_ref, yn_ref, ys_ref, ye_ref, yd_ref, zero, sems
):
    at = layers * size
    zero[...] = jnp.zeros(zero.shape, F32)
    written = set(wanted(layers))
    copies = []
    for layer in range(layers):
        for slot in range(out_ref.shape[1]):
            if (layer, slot) not in written:
                copies.append(pltpu.make_async_copy(zero, out_ref.at[layer, slot], sems.at[len(copies)]))
                copies[-1].start()
    parts = (c_ref[...], t_ref[:at, :], down_ref[:at, :], down_ref[at:, :], d_ref[...])
    c, n, st, e, d = (split(part) for part in parts)
    yn_ref[...] = dot3(c, n, NN)
    ys_ref[...] = dot3(c, st, NT)
    ye_ref[...] = dot3(c, e, NN)
    yd_ref[...] = dot3(c, d, NN)
    terms = [
        sym_product(pair, layers, size, dims)
        for pair, dims in ((c, NT), (n, NT), (st, TN), (e, NT), (d, NT))
    ]
    put_sym(yc_ref, lambda a, b: sum(term[a, b] for term in terms), layers, size)
    for copy in copies:
        copy.wait()


def g_body(layers, size, _, sums_ref, g0_ref, below_ref, up_ref, packed_ref, tx_ref, *rest):
    *more_refs, total_ref, g_ref, both_ref = rest
    n, tall = layers * size, sym_rows(layers, size)
    last = n + tall - 8
    beside = tx_ref[last:, :size]
    line = lax.broadcasted_iota(jnp.int32, (8, size), 0)
    total = sums_ref[...] + jnp.where(line == 0, beside[4:5, :], beside[5:6, :])
    for ref in more_refs:
        total = total + ref[...]
    total_ref[...] = total
    both_ref[:tall, :] = packed_ref[...]
    both_ref[tall:, :] = tx_ref[n:, :]
    stu, eu = split(below_ref[:n, :]), split(below_ref[n:, :])
    g_ref[:n, :] = g0_ref[:n, :] + dot3(stu, eu, NN)
    blocks = sym_product(stu, layers, size, NT)
    put_sym(g_ref, lambda a, b: blocks[a, b], layers, size, first=n)
    g_ref[n:, :] += g0_ref[n:, :] + up_ref[:tall, :]


def r_body(layers, size, _, r0_ref, below_ref, tx_ref, rs_ref, re_ref):
    n = layers * size
    su, eu, nx = split(below_ref[:n, :].T), split(below_ref[n:, :]), split(tx_ref[:n, :])
    cx = split(whole_sym(take_sym(tx_ref[n:, :], layers, size), layers))
    rs_ref[...] = r0_ref[:n, :] + dot3(su, cx, NN) + dot3(eu, nx, NT)
    re_ref[...] = r0_ref[n:, :] + dot3(su, nx, NN)


def middle_e_body(
    layers, size, _, sums_ref, more_ref, t_ref, down_ref, d_ref, below_ref, tx_ref, ye0_ref, total_ref, ye_ref
):
    at = layers * size
    total_ref[...] = sums_ref[...] + more_ref[...]
    n, e, d = split(t_ref[:at, :]), split(down_ref[at:, :]), split(d_ref[...])
    stu, nx = split(below_ref[:at, :]), split(tx_ref[:at, :])
    cx = split(whole_sym(take_sym(tx_ref[at:, :], layers, size), layers))
    ye_ref[...] = ye0_ref[...] + dot3(n, stu, NT) + dot3(e, cx, NN) + dot3(d, nx, NT)


def middle_n_body(
    layers, size, _, sums_ref, more_ref, t_ref, down_ref, d_ref, below_ref, both_ref, tx_ref, yn0_ref, yd0_ref,
    total_ref, yn_ref, yd_ref,
):
    total_ref[...] = sums_ref[...] + more_ref[...]
    at, tall = layers * size, sym_rows(layers, size)
    n, e, d = split(t_ref[:at, :]), split(down_ref[at:, :]), split(d_ref[...])
    stu, eu, nx = split(below_ref[:at, :]), split(below_ref[at:, :]), split(tx_ref[:at, :])
    cu = split(whole_sym(take_sym(both_ref[:tall, :], layers, size), layers))
    cxu = split(whole_sym(take_sym(both_ref[tall:, :], layers, size), layers))
    yn_ref[...] = yn0_ref[...] + dot3(n, cu, NN) + dot3(e, stu, NN) + dot3(d, eu, NT)
    yd_ref[...] = yd0_ref[...] + dot3(n, eu, NN) + dot3(e, nx, NN) + dot3(d, cxu, NN)


def twice_h(target, size, sums_ref, more_ref):
    sums = sums_ref[...] + more_ref[...]
    t1, t2 = sums[0:1, :], sums[1:2, :]
    return 2.0 * jax.nn.sigmoid((jnp.abs(t2 - target) - jnp.abs(2.0 * t1 - t2 - target)) / size)


class Sender:
    def __init__(self, mask_ref, out_ref, held, sems):
        self.mask_ref, self.out_ref, self.held, self.sems = mask_ref, out_ref, held, sems
        self.copies = []

    def send(self, value, low, slot):
        k = len(self.copies)
        self.held[k] = jnp.where(kept(self.mask_ref, low, slot), value, 0.0) if slot else value
        self.copies.append(pltpu.make_async_copy(self.held.at[k], self.out_ref.at[low, slot], self.sems.at[k]))
        self.copies[-1].start()

    def wait(self):
        for copy in self.copies:
            copy.wait()


def last_e_body(
    target, layers, size, mask_ref, _, sums_ref, more_ref, ys_ref, ye_ref, yd_ref, down_ref, d_ref, rs_ref, re_ref,
    out_ref, held, sems,
):
    n = layers * size
    twice = twice_h(target, size, sums_ref, more_ref)
    sender = Sender(mask_ref, out_ref, held, sems)
    for name, a_ref, *terms in (
        ("D", d_ref, yd_ref),
        ("S", down_ref.at[:n, :], ys_ref, rs_ref),
        ("E", down_ref.at[n:, :], ye_ref, re_ref),
    ):
        for low, high, slot in panel_blocks(name, layers):
            rows, cols = slice(low * size, (low + 1) * size), slice(high * size, (high + 1) * size)
            y = sum(ref[rows, cols] for ref in terms)
            a = a_ref[cols, rows].T if name == "S" else a_ref[rows, cols]
            sender.send(y + twice * (a - y), low, slot)
    sender.wait()


def last_c_body(
    target, layers, size, mask_ref, _, sums_ref, more_ref, yc_ref, yn_ref, up_ref, c_ref, t_ref, g_ref, out_ref, held, sems
):
    n, tall = layers * size, sym_rows(layers, size)
    twice = twice_h(target, size, sums_ref, more_ref)
    sender = Sender(mask_ref, out_ref, held, sems)
    for low, high, slot in panel_blocks("N", layers):
        rows, cols = slice(low * size, (low + 1) * size), slice(high * size, (high + 1) * size)
        y = yn_ref[rows, cols] + g_ref[rows, cols]
        sender.send(y + twice * (t_ref[rows, cols] - y), low, slot)
    blocks = take_sym(yc_ref[...] + up_ref[tall:, :] + g_ref[n:, :], layers, size)
    for low, high, slot in panel_blocks("C", layers) + [(layer, layer, 0) for layer in range(layers)]:
        rows, cols = slice(low * size, (low + 1) * size), slice(high * size, (high + 1) * size)
        y = blocks[low, high]
        sender.send(y + twice * (c_ref[rows, cols] - y), low, slot)
    sender.wait()


def call(body, layers, size, outs, spaces, scratch=(), limit=24, out_spaces=None, aliases=None):
    return pl.pallas_call(
        functools.partial(body, layers, size),
        out_shape=[jax.ShapeDtypeStruct(shape, F32) for shape in outs],
        in_specs=[pl.BlockSpec(memory_space=space) for space in spaces],
        out_specs=[pl.BlockSpec(memory_space=space) for space in out_spaces or [pltpu.VMEM] * len(outs)],
        scratch_shapes=list(scratch),
        input_output_aliases=aliases or {},
        compiler_params=pltpu.CompilerParams(vmem_limit_bytes=limit << 20),
    )


def passed_along(value, axis, by):
    peers = lax.axis_size(axis)
    return lax.ppermute(value, axis, [(i, (i + by) % peers) for i in range(peers)])


def swapped(value, axis, bit):
    peers = lax.axis_size(axis)
    return lax.ppermute(value, axis, [(i, i ^ bit) for i in range(peers)])


def shards(stored_blocks, onsite, bond_mask):
    stored, onsite, mask = stored_blocks[0, 0], onsite[0, 0], bond_mask[0, 0]
    layers, slots, size = stored.shape[:3]
    n, tall = layers * size, sym_rows(layers, size)
    panel, packed, sums = (n, n), (tall, n), (8, size)
    vmem, smem, hbm = pltpu.VMEM, pltpu.SMEM, pltpu.HBM

    def blocks(count):
        return [pltpu.VMEM((count, size, size), F32), pltpu.SemaphoreType.DMA((count,))]

    go = functools.partial(call, layers=layers, size=size)
    stored, onsite, mask_hbm = (pltpu.with_memory_space_constraint(value, hbm) for value in (stored, onsite, mask))
    T, Cp, C, down, D, own = go(
        pack_body, outs=[(n + tall, n), packed, panel, (2 * n, n), panel, sums], spaces=[hbm] * 3,
        scratch=blocks(len(wanted(layers)))
        + [pltpu.SMEM(mask.shape, mask.dtype), pltpu.SemaphoreType.DMA, pltpu.VMEM(onsite.shape, F32), pltpu.SemaphoreType.DMA],
    )(mask_hbm, stored, onsite)
    T_x = passed_along(T, "row", -1)
    below = passed_along(down, "col", -1)
    (up,) = go(up_body, outs=[(2 * tall, n)], spaces=[vmem] * 2)(T, D)
    up_in = passed_along(up, "col", 1)
    more = [passed_along(own, "row", -by) for by in range(2, lax.axis_size("row"))]
    g0, r0 = go(local_g_body, outs=[(n + tall, n), (2 * n, n)], spaces=[hbm] + [vmem] * 3)(up, T, down, D)
    out, yc, yn, ys, ye, yd = go(
        local_y_body, outs=[(layers, slots, size, size), packed] + [panel] * 4, spaces=[hbm] + [vmem] * 4,
        out_spaces=[hbm] + [vmem] * 5, scratch=[pltpu.VMEM((size, size), F32), pltpu.SemaphoreType.DMA((layers * slots,))],
    )(g0, C, T, down, D)
    own, g, both = go(g_body, outs=[sums, (n + tall, n), (2 * tall, n)], spaces=[hbm] + [vmem] * (6 + len(more)))(
        yc, own, g0, below, up_in, Cp, T_x, *more
    )
    g_in = passed_along(g, "row", 1)
    both_u = passed_along(both, "col", -1)

    peers = lax.axis_size("col")
    bits = [1 << k for k in range(peers.bit_length() - 1)]
    bits = bits[:1] + bits[2:] + bits[1:2]
    if peers.bit_count() > 1:
        own = own + sum(passed_along(own, "col", by) for by in range(1, peers))
        bits = []
    while len(bits) > 3:
        own = own + swapped(own, "col", bits.pop(0))

    def arriving(value):
        return swapped(value, "col", bits.pop(0)) if bits else jnp.zeros_like(value)

    more = arriving(own)
    rs, re = go(r_body, outs=[panel, panel], spaces=[hbm] + [vmem] * 3)(g, r0, below, T_x)
    rs_in, re_in = passed_along(rs, "col", 1), passed_along(re, "col", 1)
    own, ye = go(middle_e_body, outs=[sums, panel], spaces=[hbm] + [vmem] * 8)(rs, own, more, T, down, D, below, T_x, ye)
    more = arriving(own)
    own, yn, yd = go(middle_n_body, outs=[sums, panel, panel], spaces=[hbm] + [vmem] * 10)(
        ye, own, more, T, down, D, below, both_u, T_x, yn, yd
    )
    more = arriving(own)
    cells = lax.axis_size("row") * lax.axis_size("col") * layers
    target = float(cells * size // 2)

    def finish(body, out, names, *terms):
        count = sum(len(panel_blocks(name, layers)) for name in names) + layers * ("C" in names)
        return go(
            functools.partial(body, target), outs=[out.shape], out_spaces=[hbm], spaces=[smem, hbm] + [vmem] * (2 + len(terms)),
            scratch=blocks(count), aliases={1: 0},
        )(mask, out, own, more, *terms)[0]

    out = finish(last_e_body, out, "SED", ys, ye, yd, down, D, rs_in, re_in)
    out = finish(last_c_body, out, "NC", yc, yn, up_in, C, T, g_in)
    return out[None, None]


def solution(mesh):
    in_specs = (
        P("row", "col", None, None, None, None),
        P("row", "col", None, None),
        P("row", "col", None, None),
    )
    out_specs = P("row", "col", None, None, None, None)
    return jax.shard_map(shards, mesh=mesh, in_specs=in_specs, out_specs=out_specs, check_vma=False)
```

time: 106 us -> 92.1 us (0.87)
  starting transfers between devices: 25.9 us -> 13.3 us
  waiting for transfers between devices: 37.9 us -> 43.7 us
  Pallas kernels: 39.6 us -> 34.7 us
  local copies, waits for them, and re-layouts: 1.75 us -> 0.01 us
    ppermute x5 -> x3, starting transfers between devices: 16.3 us -> 1.66 us  [swapped(): return lax.ppermute(value, axis, [(i, i ^ bit) for i in range(peers)])]
    ppermute x7 -> x9, waiting for transfers between devices: 30.9 us -> 38.2 us  [passed_along(): lax.ppermute(value, axis, [(i, (i + by) % peers) for i in range(peers)])]
    pallas_call x12 -> x10, Pallas kernels: 39.6 us -> 34.7 us  [the longest x1 8.11 us: shards(): go(local_y_body, outs=[(layers, slots, size, size), packed] + [panel] * 4...]
    ppermute x7 -> x9, starting transfers between devices: 9.65 us -> 11.6 us  [passed_along(): lax.ppermute(value, axis, [(i, (i + by) % peers) for i in range(peers)])]
    unnamed x14 -> x2, local copies, waits for them, and re-layouts: 1.75 us -> 0.01 us
    ppermute x5 -> x3, waiting for transfers between devices: 6.99 us -> 5.48 us  [swapped(): return lax.ppermute(value, axis, [(i, i ^ bit) for i in range(peers)])]
  transfers between devices with their start and end apart: 12 -> 12, of which waited for: 7 -> 5; matrix products, arithmetic and copies ran while one was open for 0% -> 0% of each run, Pallas kernels for 27% -> 28%
where the time goes in v4:
time: 92.1 us; the launch traced here: 91.9 us
  waiting for transfers between devices  43.7 us (47%)
  Pallas kernels  34.7 us (38%)
  starting transfers between devices  13.3 us (14%)
    ppermute x9, waiting for transfers between devices, passed_along(): lax.ppermute(value, axis, [(i, (i + by) % peers) for i in range(peers)])  38.2 us
    ppermute x9, starting transfers between devices, passed_along(): lax.ppermute(value, axis, [(i, (i + by) % peers) for i in range(peers)])  11.6 us
    pallas_call x1, Pallas kernels, shards(): go(local_y_body, outs=[(layers, slots, size, size), packed] + [panel] * 4...  8.11 us
    ppermute x3, waiting for transfers between devices, swapped(): return lax.ppermute(value, axis, [(i, i ^ bit) for i in range(peers)])  5.48 us
    pallas_call x1, Pallas kernels, shards(): go(middle_n_body, outs=[sums, panel, panel], spaces=[hbm] + [vmem] * 10)  5.26 us
    pallas_call x1, Pallas kernels, shards(): go(pack_body, outs=[(n + tall, n), packed, panel, (2 * n, n), panel, sums...  4.63 us
    pallas_call x2, Pallas kernels, finish(): go(functools.partial(body, target), outs=[out.shape], out_spaces=[hbm], s...  4.58 us
    pallas_call x1, Pallas kernels, shards(): go(local_g_body, outs=[(n + tall, n), (2 * n, n)], spaces=[hbm] + [vmem]...  3.3 us
  transfers between devices with their start and end apart: 12, of which 5 were waited for; matrix products, arithmetic and copies ran while one was open for 0% of the time, Pallas kernels for 28%

profile of v4, /device:TPU:0, one launch (start us, length us, event | category | flops | bytes accessed | tf_op | source)
XLA Modules:
  0.0 91.9 jit_solution(5026627150586955540)
XLA Ops:
  0.0 4.6 %shard_map.37 = (f32[776,512]{1,0:T(8,128)S(1)}, f32[264,512]{1,0:T(8,128)S(1)}, f32[512,512]{1,0:T(8,128)S(1)}, f32[1024,512]{1,0:T(8,128)S(1)}, f32[512,512]{1,0:T(8,128)S(1)}, /*index=5*/f32[8,256]{1,0:T(8,128)S(1)}) custom-call(s32[2,13]{1,0:T(2,128)} %bitcast.4, f32[2,14,256,256]{3,2,1,0:T(8,128)} %bitcast.7, f32[2,256]{1,0:T(2,128)} %bitcast.8), custom_call_target="tpu_custom_call" | custom-call | tf_op jit(solution)/shard_map/pallas_call | solution.py:432
  4.6 3.4 %collective-permute-start = (f32[1024,512]{1,0:T(8,128)S(1)}, f32[1024,512]{1,0:T(8,128)S(1)}, u32[]{:S(2)}, u32[]{:S(2)}) collective-permute-start(f32[1024,512]{1,0:T(8,128)S(1)} %get-tuple-element.31.down_ref), channel_id=1, source_target_pairs={{0,7},{1,0},{2,1},{3,2},{4,3},{5,4},{6,5},{7,6},{8,15},{9,8},{10,9... | collective-permute-start | bytes 6291464 | tf_op jit(solution)/shard_map/ppermute | solution.py:412
  8.0 3.6 %collective-permute-start.2 = (f32[776,512]{1,0:T(8,128)S(1)}, f32[776,512]{1,0:T(8,128)S(1)}, u32[]{:S(2)}, u32[]{:S(2)}) collective-permute-start(f32[776,512]{1,0:T(8,128)S(1)} %get-tuple-element.29.n_ref.t_ref), channel_id=1, source_target_pairs={{0,24},{8,0},{16,8},{24,16},{1,25},{9,1},{17,9},{25,17},{2,26},{10... | collective-permute-start | bytes 4767752 | tf_op jit(solution)/shard_map/ppermute | solution.py:412
  11.6 1.5 %shard_map.38._ = f32[528,512]{1,0:T(8,128)S(1)} custom-call(f32[776,512]{1,0:T(8,128)S(1)} %get-tuple-element.29.n_ref.t_ref, f32[512,512]{1,0:T(8,128)S(1)} %get-tuple-element.30.d_ref), custom_call_target="tpu_custom_call" | custom-call | tf_op jit(solution)/shard_map/pallas_call | solution.py:439
  13.1 0.1 collective-permute-start.1
  13.2 0.2 collective-permute-start.4
  13.4 1.0 %collective-permute-start.3 = (f32[8,256]{1,0:T(8,128)S(1)}, f32[8,256]{1,0:T(8,128)S(1)}, u32[]{:S(2)}, u32[]{:S(2)}) collective-permute-start(f32[8,256]{1,0:T(8,128)S(1)} %get-tuple-element.36.sums_ref), channel_id=1, source_target_pairs={{0,16},{8,24},{16,0},{24,8},{1,17},{9,25},{17,1},{25,9},{2,18},{10... | collective-permute-start | bytes 24584 | tf_op jit(solution)/shard_map/ppermute | solution.py:412
  14.4 3.3 %shard_map.39 = (f32[776,512]{1,0:T(8,128)S(1)}, f32[1024,512]{1,0:T(8,128)S(1)}) custom-call(f32[528,512]{1,0:T(8,128)S(1)} %shard_map.38._, f32[776,512]{1,0:T(8,128)S(1)} %get-tuple-element.29.n_ref.t_ref, f32[1024,512]{1,0:T(8,128)S(1)} %get-tuple-element.31.down_ref, f32[512,512]{1,0:T(8,128)S(1)} %get-tuple-element.30.d_ref), custom_call_target="tpu_custom_call" | custom-call | tf_op jit(solution)/shard_map/pallas_call | solution.py:442
  17.7 8.1 %shard_map.40 = (f32[2,14,256,256]{3,2,1,0:T(8,128)}, f32[264,512]{1,0:T(8,128)S(1)}, f32[512,512]{1,0:T(8,128)S(1)}, f32[512,512]{1,0:T(8,128)S(1)}, f32[512,512]{1,0:T(8,128)S(1)}, /*index=5*/f32[512,512]{1,0:T(8,128)S(1)}) custom-call(f32[776,512]{1,0:T(8,128)S(1)} %get-tuple-element.32._.g0_ref, f32[512,512]{1,0:T(8,128)S(1)} %get-tuple-element.33.c_ref, ...), custom_call_target="tpu_custom_call" | custom-call | tf_op jit(solution)/shard_map/pallas_call | solution.py:443
  25.8 19.8 %collective-permute-done.4.rest_1_ = f32[8,256]{1,0:T(8,128)S(1)} collective-permute-done((f32[8,256]{1,0:T(8,128)S(1)}, f32[8,256]{1,0:T(8,128)S(1)}, u32[]{:S(2)}, u32[]{:S(2)}) %collective-permute-start.4) | collective-permute-done | bytes 8224 | tf_op jit(solution)/shard_map/ppermute | solution.py:412
  45.6 0.0 collective-permute-done.3.rest_0_
  45.6 0.0 collective-permute-done.1.up_ref
  45.6 0.0 collective-permute-done.below_ref
  45.6 1.7 %shard_map.41 = (f32[8,256]{1,0:T(8,128)S(1)}, f32[776,512]{1,0:T(8,128)S(1)}, f32[528,512]{1,0:T(8,128)S(1)}) custom-call(f32[264,512]{1,0:T(8,128)S(1)} %get-tuple-element.35._.yc_ref, f32[8,256]{1,0:T(8,128)S(1)} %get-tuple-element.36.sums_ref, f32[776,512]{1,0:T(8,128)S(1)} %get-tuple-element.32._.g0_ref, ...), custom_call_target="tpu_custom_call" | custom-call | tf_op jit(solution)/shard_map/pallas_call | solution.py:447
  47.4 1.7 %collective-permute-start.11 = (f32[776,512]{1,0:T(8,128)S(1)}, f32[776,512]{1,0:T(8,128)S(1)}, u32[]{:S(2)}, u32[]{:S(2)}) collective-permute-start(f32[776,512]{1,0:T(8,128)S(1)} %get-tuple-element.38._), channel_id=1, source_target_pairs={{0,8},{8,16},{16,24},{24,0},{1,9},{9,17},{17,25},{25,1},{2,10},{10... | collective-permute-start | bytes 4767752 | tf_op jit(solution)/shard_map/ppermute | solution.py:412
  49.0 1.0 %collective-permute-start.7 = (f32[528,512]{1,0:T(8,128)S(1)}, f32[528,512]{1,0:T(8,128)S(1)}, u32[]{:S(2)}, u32[]{:S(2)}) collective-permute-start(f32[528,512]{1,0:T(8,128)S(1)} %get-tuple-element.45), channel_id=1, source_target_pairs={{0,7},{1,0},{2,1},{3,2},{4,3},{5,4},{6,5},{7,6},{8,15},{9,8},{10,9... | collective-permute-start | bytes 3244040 | tf_op jit(solution)/shard_map/ppermute | solution.py:412
  50.1 2.9 %shard_map.42 = (f32[512,512]{1,0:T(8,128)S(1)}, f32[512,512]{1,0:T(8,128)S(1)}) custom-call(f32[776,512]{1,0:T(8,128)S(1)} %get-tuple-element.38._, f32[1024,512]{1,0:T(8,128)S(1)} %get-tuple-element.39.r0_ref, f32[1024,512]{1,0:T(8,128)S(1)} %collective-permute-done.below_ref, f32[776,512]{1,0:T(8,128)S(1)} %collective-permute-done.2.tx_ref), custom_call_target="tpu_custom_call" | custom-call | tf_op jit(solution)/shard_map/pallas_call | solution.py:466
  53.0 0.1 collective-permute-start.10
  53.0 0.5 collective-permute-start.9
  53.6 0.5 collective-permute-start.5
  54.1 2.7 %collective-permute-done.5.more_ref = f32[8,256]{1,0:T(8,128)S(1)} collective-permute-done((f32[8,256]{1,0:T(8,128)S(1)}, f32[8,256]{1,0:T(8,128)S(1)}, u32[]{:S(2)}, u32[]{:S(2)}) %collective-permute-start.5) | collective-permute-done | bytes 8224 | tf_op jit(solution)/shard_map/ppermute | solution.py:417
  56.8 2.7 %shard_map.43 = (f32[8,256]{1,0:T(8,128)S(1)}, f32[512,512]{1,0:T(8,128)S(1)}) custom-call(f32[512,512]{1,0:T(8,128)S(1)} %get-tuple-element.40._, f32[8,256]{1,0:T(8,128)S(1)} %get-tuple-element.41.sums_ref, f32[8,256]{1,0:T(8,128)S(1)} %collective-permute-done.5.more_ref, f32[776,512]{1,0:T(8,128)S(1)} %get-tuple-element.29.n_ref.t_ref, ...), custom_call_target="tpu_custom_call" | custom-call | tf_op jit(solution)/shard_map/pallas_call | solution.py:468
  59.5 1.1 %collective-permute-start.6 = (f32[8,256]{1,0:T(8,128)S(1)}, f32[8,256]{1,0:T(8,128)S(1)}, u32[]{:S(2)}, u32[]{:S(2)}) collective-permute-start(f32[8,256]{1,0:T(8,128)S(1)} %get-tuple-element.44.sums_ref), channel_id=1, source_target_pairs={{0,4},{1,5},{2,6},{3,7},{4,0},{5,1},{6,2},{7,3},{8,12},{9,13},{10,... | collective-permute-start | bytes 24584 | tf_op jit(solution)/shard_map/ppermute | solution.py:417
  60.6 2.7 %collective-permute-done.6.more_ref = f32[8,256]{1,0:T(8,128)S(1)} collective-permute-done((f32[8,256]{1,0:T(8,128)S(1)}, f32[8,256]{1,0:T(8,128)S(1)}, u32[]{:S(2)}, u32[]{:S(2)}) %collective-permute-start.6) | collective-permute-done | bytes 8224 | tf_op jit(solution)/shard_map/ppermute | solution.py:417
  63.3 8.1 %collective-permute-done.7.both_ref = f32[528,512]{1,0:T(8,128)S(1)} collective-permute-done((f32[528,512]{1,0:T(8,128)S(1)}, f32[528,512]{1,0:T(8,128)S(1)}, u32[]{:S(2)}, u32[]{:S(2)}) %collective-permute-start.7) | collective-permute-done | bytes 1081376 | tf_op jit(solution)/shard_map/ppermute | solution.py:412
  71.5 5.3 %shard_map.44 = (f32[8,256]{1,0:T(8,128)S(1)}, f32[512,512]{1,0:T(8,128)S(1)}, f32[512,512]{1,0:T(8,128)S(1)}) custom-call(f32[512,512]{1,0:T(8,128)S(1)} %get-tuple-element.43._.ye_ref, f32[8,256]{1,0:T(8,128)S(1)} %get-tuple-element.44.sums_ref, f32[8,256]{1,0:T(8,128)S(1)} %collective-permute-done.6.more_ref, ...), custom_call_target="tpu_custom_call" | custom-call | tf_op jit(solution)/shard_map/pallas_call | solution.py:470
  76.7 0.1 collective-permute-start.8
  76.8 0.0 collective-permute-done.10.re_ref
  76.8 10.3 %collective-permute-done.9.rs_ref = f32[512,512]{1,0:T(8,128)S(1)} collective-permute-done((f32[512,512]{1,0:T(8,128)S(1)}, f32[512,512]{1,0:T(8,128)S(1)}, u32[]{:S(2)}, u32[]{:S(2)}) %collective-permute-start.9) | collective-permute-done | bytes 1048608 | tf_op jit(solution)/shard_map/ppermute | solution.py:412
  87.2 0.0 collective-permute-done.8.more_ref
  87.2 2.4 %shard_map.45._ = f32[2,14,256,256]{3,2,1,0:T(8,128)} custom-call(s32[2,13]{1,0:T(2,128)S(1)} %bitcast.5, f32[2,14,256,256]{3,2,1,0:T(8,128)} %get-tuple-element.34._, f32[8,256]{1,0:T(8,128)S(1)} %get-tuple-element.48.sums_ref, f32[8,256]{1,0:T(8,128)S(1)} %collective-permute-done.8.more_ref, ...), custom_call_target="tpu_custom_call", output_to_operand_aliasing={{}: (1, {})} | custom-call | tf_op jit(solution)/shard_map/pallas_call | solution.py:479
  89.6 2.1 %shard_map.46 = f32[2,14,256,256]{3,2,1,0:T(8,128)} custom-call(s32[2,13]{1,0:T(2,128)S(1)} %bitcast.6, f32[2,14,256,256]{3,2,1,0:T(8,128)} %shard_map.45._, f32[8,256]{1,0:T(8,128)S(1)} %get-tuple-element.48.sums_ref, f32[8,256]{1,0:T(8,128)S(1)} %collective-permute-done.8.more_ref, ...), custom_call_target="tpu_custom_call", output_to_operand_aliasing={{}: (1, {})} | custom-call | tf_op jit(solution)/shard_map/pallas_call | solution.py:479
  (4 shorter events, 0.0 us)
Async XLA Ops:
  4.6 41.0 %collective-permute-start = (f32[1024,512]{1,0:T(8,128)S(1)}, f32[1024,512]{1,0:T(8,128)S(1)}, u32[]{:S(2)}, u32[]{:S(2)}) collective-permute-start(f32[1024,512]{1,0:T(8,128)S(1)} %get-tuple-element.31.down_ref), channel_id=1, source_target_pairs={{0,7},{1,0},{2,1},{3,2},{4,3},{5,4},{6,5},{7,6},{8,15},{9,8},{10,9... | collective-permute-start | bytes 6291464 | tf_op jit(solution)/shard_map/ppermute | solution.py:412
  8.0 37.6 %collective-permute-start.2 = (f32[776,512]{1,0:T(8,128)S(1)}, f32[776,512]{1,0:T(8,128)S(1)}, u32[]{:S(2)}, u32[]{:S(2)}) collective-permute-start(f32[776,512]{1,0:T(8,128)S(1)} %get-tuple-element.29.n_ref.t_ref), channel_id=1, source_target_pairs={{0,24},{8,0},{16,8},{24,16},{1,25},{9,1},{17,9},{25,17},{2,26},{10... | collective-permute-start | bytes 4767752 | tf_op jit(solution)/shard_map/ppermute | solution.py:412
  13.1 32.5 %collective-permute-start.1 = (f32[528,512]{1,0:T(8,128)S(1)}, f32[528,512]{1,0:T(8,128)S(1)}, u32[]{:S(2)}, u32[]{:S(2)}) collective-permute-start(f32[528,512]{1,0:T(8,128)S(1)} %shard_map.38._), channel_id=1, source_target_pairs={{0,1},{1,2},{2,3},{3,4},{4,5},{5,6},{6,7},{7,0},{8,9},{9,10},{10,1... | collective-permute-start | bytes 3244040 | tf_op jit(solution)/shard_map/ppermute | solution.py:412
  13.2 32.4 %collective-permute-start.4 = (f32[8,256]{1,0:T(8,128)S(1)}, f32[8,256]{1,0:T(8,128)S(1)}, u32[]{:S(2)}, u32[]{:S(2)}) collective-permute-start(f32[8,256]{1,0:T(8,128)S(1)} %get-tuple-element.36.sums_ref), channel_id=1, source_target_pairs={{0,8},{8,16},{16,24},{24,0},{1,9},{9,17},{17,25},{25,1},{2,10},{10... | collective-permute-start | bytes 24584 | tf_op jit(solution)/shard_map/ppermute | solution.py:412
  13.4 32.2 %collective-permute-start.3 = (f32[8,256]{1,0:T(8,128)S(1)}, f32[8,256]{1,0:T(8,128)S(1)}, u32[]{:S(2)}, u32[]{:S(2)}) collective-permute-start(f32[8,256]{1,0:T(8,128)S(1)} %get-tuple-element.36.sums_ref), channel_id=1, source_target_pairs={{0,16},{8,24},{16,0},{24,8},{1,17},{9,25},{17,1},{25,9},{2,18},{10... | collective-permute-start | bytes 24584 | tf_op jit(solution)/shard_map/ppermute | solution.py:412
  47.4 42.3 %collective-permute-start.11 = (f32[776,512]{1,0:T(8,128)S(1)}, f32[776,512]{1,0:T(8,128)S(1)}, u32[]{:S(2)}, u32[]{:S(2)}) collective-permute-start(f32[776,512]{1,0:T(8,128)S(1)} %get-tuple-element.38._), channel_id=1, source_target_pairs={{0,8},{8,16},{16,24},{24,0},{1,9},{9,17},{17,25},{25,1},{2,10},{10... | collective-permute-start | bytes 4767752 | tf_op jit(solution)/shard_map/ppermute | solution.py:412
  49.0 22.4 %collective-permute-start.7 = (f32[528,512]{1,0:T(8,128)S(1)}, f32[528,512]{1,0:T(8,128)S(1)}, u32[]{:S(2)}, u32[]{:S(2)}) collective-permute-start(f32[528,512]{1,0:T(8,128)S(1)} %get-tuple-element.45), channel_id=1, source_target_pairs={{0,7},{1,0},{2,1},{3,2},{4,3},{5,4},{6,5},{7,6},{8,15},{9,8},{10,9... | collective-permute-start | bytes 3244040 | tf_op jit(solution)/shard_map/ppermute | solution.py:412
  53.0 23.8 %collective-permute-start.10 = (f32[512,512]{1,0:T(8,128)S(1)}, f32[512,512]{1,0:T(8,128)S(1)}, u32[]{:S(2)}, u32[]{:S(2)}) collective-permute-start(f32[512,512]{1,0:T(8,128)S(1)} %get-tuple-element.51), channel_id=1, source_target_pairs={{0,1},{1,2},{2,3},{3,4},{4,5},{5,6},{6,7},{7,0},{8,9},{9,10},{10,1... | collective-permute-start | bytes 3145736 | tf_op jit(solution)/shard_map/ppermute | solution.py:412
  53.0 34.1 %collective-permute-start.9 = (f32[512,512]{1,0:T(8,128)S(1)}, f32[512,512]{1,0:T(8,128)S(1)}, u32[]{:S(2)}, u32[]{:S(2)}) collective-permute-start(f32[512,512]{1,0:T(8,128)S(1)} %get-tuple-element.40._), channel_id=1, source_target_pairs={{0,1},{1,2},{2,3},{3,4},{4,5},{5,6},{6,7},{7,0},{8,9},{9,10},{10,1... | collective-permute-start | bytes 3145736 | tf_op jit(solution)/shard_map/ppermute | solution.py:412
  53.6 3.3 %collective-permute-start.5 = (f32[8,256]{1,0:T(8,128)S(1)}, f32[8,256]{1,0:T(8,128)S(1)}, u32[]{:S(2)}, u32[]{:S(2)}) collective-permute-start(f32[8,256]{1,0:T(8,128)S(1)} %get-tuple-element.41.sums_ref), channel_id=1, source_target_pairs={{0,1},{1,0},{2,3},{3,2},{4,5},{5,4},{6,7},{7,6},{8,9},{9,8},{10,11... | collective-permute-start | bytes 24584 | tf_op jit(solution)/shard_map/ppermute | solution.py:417
  59.5 3.8 %collective-permute-start.6 = (f32[8,256]{1,0:T(8,128)S(1)}, f32[8,256]{1,0:T(8,128)S(1)}, u32[]{:S(2)}, u32[]{:S(2)}) collective-permute-start(f32[8,256]{1,0:T(8,128)S(1)} %get-tuple-element.44.sums_ref), channel_id=1, source_target_pairs={{0,4},{1,5},{2,6},{3,7},{4,0},{5,1},{6,2},{7,3},{8,12},{9,13},{10,... | collective-permute-start | bytes 24584 | tf_op jit(solution)/shard_map/ppermute | solution.py:417
  71.5 15.7 %copy-start = (s32[1,1,2,13]{3,2,1,0:T(2,128)S(1)}, s32[1,1,2,13]{3,2,1,0:T(2,128)}, u32[]{:S(2)}) copy-start(s32[1,1,2,13]{3,2,1,0:T(2,128)} %param.5) | copy-start | bytes 316
  76.7 10.4 %collective-permute-start.8 = (f32[8,256]{1,0:T(8,128)S(1)}, f32[8,256]{1,0:T(8,128)S(1)}, u32[]{:S(2)}, u32[]{:S(2)}) collective-permute-start(f32[8,256]{1,0:T(8,128)S(1)} %get-tuple-element.48.sums_ref), channel_id=1, source_target_pairs={{0,2},{1,3},{2,0},{3,1},{4,6},{5,7},{6,4},{7,5},{8,10},{9,11},{10,... | collective-permute-start | bytes 24584 | tf_op jit(solution)/shard_map/ppermute | solution.py:417

commit v5 on v4

--- a/solution.py
+++ b/solution.py
@@ -149,15 +149,13 @@
 
 
 def load_panel(out_ref, held, first, name, layers, size, mask_ref, flip=False, top=0):
-    blocks = panel_blocks(name, layers)
     if layers > 2:
         out_ref[top : top + layers * size, :] = jnp.zeros((layers * size, layers * size), F32)
-    for k, (low, high, slot) in enumerate(blocks):
+    for k, (low, high, slot) in enumerate(panel_blocks(name, layers)):
         value = jnp.where(kept(mask_ref, low, slot), held[first + k], 0.0)
         if flip:
             low, high, value = high, low, value.T
         out_ref[top + low * size : top + (low + 1) * size, high * size : (high + 1) * size] = value
-    return len(blocks)
 
 
 def start_loads(stored_ref, held, sems, wanted):
@@ -174,9 +172,9 @@
     return jnp.sum(value * value)
 
 
-def wanted(layers):
-    return [(layer, 0) for layer in range(layers)] + [
-        (low, slot) for name in "CSEND" for low, _, slot in panel_blocks(name, layers)
+def wanted(names, layers):
+    return [(layer, 0) for layer in range(layers) if "C" in names] + [
+        (low, slot) for name in names for low, _, slot in panel_blocks(name, layers)
     ]
 
 
@@ -191,7 +189,7 @@
     ]
     for copy in small:
         copy.start()
-    copies = start_loads(stored_ref, held, sems, wanted(layers))
+    copies = start_loads(stored_ref, held, sems, wanted("CSEND", layers))
     for copy in small:
         copy.wait()
     row, col = rows_cols(size)
@@ -227,47 +225,118 @@
     c_now = c_ref[...]
     trace = jnp.sum(jnp.where(row == col, c_now, 0.0))
     line = lax.broadcasted_iota(jnp.int32, sums_ref.shape, 0)
-    sums = jnp.where((line == 0) | (line == 4), trace, squares_of(c_now) + 2.0 * squares)
-    sums_ref[...] = sums
-    last = t_ref.shape[0] - 8
-    line = lax.broadcasted_iota(jnp.int32, (8, size), 0)
-    for at in range(layers):
-        cols = slice(at * size, (at + 1) * size)
-        t_ref[last:, cols] = jnp.where(line < 4, t_ref[last:, cols], sums)
+    sums_ref[...] = jnp.where(line % 4 == 0, trace, squares_of(c_now) + 2.0 * squares)
 
 
 def squares_of(value):
     return jnp.sum(value * value)
 
 
-def up_body(layers, size, n_ref, d_ref, up_ref):
-    for k, ref in enumerate((d_ref, n_ref)):
-        blocks = sym_product(split(ref[: layers * size, :]), layers, size, TN)
-        put_sym(up_ref, lambda a, b: blocks[a, b], layers, size, first=k * sym_rows(layers, size))
-
-
-def local_g_body(layers, size, _, t_ref, down_ref, d_ref, g_ref, r_ref):
+def wanted(names, layers):
+    return [(layer, 0) for layer in range(layers) if "C" in names] + [
+        (low, slot) for name in names for low, _, slot in panel_blocks(name, layers)
+    ]
+
+
+def pack_t_body(
+    layers, size, mask_ref, stored_ref, onsite_ref, t_ref, packed_ref, c_ref, sums_ref,
+    held, sems, mask, mask_sem, onsite, onsite_sem,
+):
     n = layers * size
+    small = [
+        pltpu.make_async_copy(mask_ref, mask, mask_sem),
+        pltpu.make_async_copy(onsite_ref, onsite, onsite_sem),
+    ]
+    for copy in small:
+        copy.start()
+    copies = start_loads(stored_ref, held, sems, wanted("CN", layers))
+    for copy in small:
+        copy.wait()
+    row, col = rows_cols(size)
+    c_ref[...] = jnp.zeros(c_ref.shape, F32)
+    for layer in range(layers):
+        copies[layer].wait()
+        block = held[layer]
+        block = 0.5 * (block + block.T) + jnp.where(row == col, onsite[layer : layer + 1, :], 0.0)
+        c_ref[layer * size : (layer + 1) * size, layer * size : (layer + 1) * size] = block
+    at = layers
+    for low, high, slot in panel_blocks("C", layers):
+        copies[at].wait()
+        block = jnp.where(kept(mask, low, slot), held[at], 0.0)
+        c_ref[low * size : (low + 1) * size, high * size : (high + 1) * size] = block
+        c_ref[high * size : (high + 1) * size, low * size : (low + 1) * size] = block.T
+        at += 1
+    put_sym(
+        packed_ref,
+        lambda a, b: c_ref[a * size : (a + 1) * size, b * size : (b + 1) * size],
+        layers,
+        size,
+    )
+    t_ref[n:, :] = packed_ref[...]
+    for copy in copies[at:]:
+        copy.wait()
+    load_panel(t_ref, held, at, "N", layers, size, mask)
+    row, col = rows_cols(n)
+    c_now = c_ref[...]
+    trace = jnp.sum(jnp.where(row == col, c_now, 0.0))
+    line = lax.broadcasted_iota(jnp.int32, sums_ref.shape, 0)
+    sums_ref[...] = jnp.where(line % 4 == 0, trace, squares_of(c_now) + 2.0 * squares_of(t_ref[:n, :]))
+
+
+def pack_e_body(layers, size, mask_ref, stored_ref, before_ref, st_ref, e_ref, d_ref, sums_ref, held, sems, mask, mask_sem):
+    small = pltpu.make_async_copy(mask_ref, mask, mask_sem)
+    small.start()
+    copies = start_loads(stored_ref, held, sems, wanted("SED", layers))
+    small.wait()
+    at = 0
+    squares = 0.0
+    for name, ref in (("S", st_ref), ("E", e_ref), ("D", d_ref)):
+        count = len(panel_blocks(name, layers))
+        for copy in copies[at : at + count]:
+            copy.wait()
+        load_panel(ref, held, at, name, layers, size, mask, flip=name == "S")
+        squares = squares + squares_of(ref[...])
+        at += count
+    line = lax.broadcasted_iota(jnp.int32, sums_ref.shape, 0)
+    sums_ref[...] = before_ref[...] + jnp.where(line % 4 == 0, 0.0, 2.0 * squares)
+
+
+def squares_of(value):
+    return jnp.sum(value * value)
+
+
+def up_body(layers, size, panel_ref, up_ref):
+    blocks = sym_product(split(panel_ref[: layers * size, :]), layers, size, TN)
+    put_sym(up_ref, lambda a, b: blocks[a, b], layers, size)
+
+
+def local_g_body(layers, size, _, sums_ref, more_ref, t_ref, down_ref, d_ref, total_ref, g_ref, r_ref, yc_up_ref):
+    n = layers * size
+    total_ref[...] = sums_ref[...] + more_ref[...]
     n_now, e, d = split(t_ref[:n, :]), split(down_ref[n:, :]), split(d_ref[...])
     blocks = sym_product(e, layers, size, TN)
     g_ref[:n, :] = dot3(e, d, TN)
     put_sym(g_ref, lambda a, b: blocks[a, b], layers, size, first=n)
     r_ref[:n, :] = dot3(n_now, e, TN)
     r_ref[n:, :] = dot3(n_now, d, TN)
+    blocks = sym_product(n_now, layers, size, TN)
+    put_sym(yc_up_ref, lambda a, b: blocks[a, b], layers, size)
 
 
 def local_y_body(
-    layers, size, _, c_ref, t_ref, down_ref, d_ref, out_ref, yc_ref, yn_ref, ys_ref, ye_ref, yd_ref, zero, sems
+    layers, size, _, sums_ref, more_ref, c_ref, t_ref, down_ref, d_ref,
+    total_ref, out_ref, yc_ref, yn_ref, ys_ref, ye_ref, yd_ref, zero, sems,
 ):
-    at = layers * size
+    total_ref[...] = sums_ref[...] + more_ref[...]
     zero[...] = jnp.zeros(zero.shape, F32)
-    written = set(wanted(layers))
+    written = set(wanted(IN_PLANE, layers))
     copies = []
     for layer in range(layers):
         for slot in range(out_ref.shape[1]):
             if (layer, slot) not in written:
                 copies.append(pltpu.make_async_copy(zero, out_ref.at[layer, slot], sems.at[len(copies)]))
                 copies[-1].start()
+    at = layers * size
     parts = (c_ref[...], t_ref[:at, :], down_ref[:at, :], down_ref[at:, :], d_ref[...])
     c, n, st, e, d = (split(part) for part in parts)
     yn_ref[...] = dot3(c, n, NN)
@@ -283,60 +352,68 @@
         copy.wait()
 
 
-def g_body(layers, size, _, sums_ref, g0_ref, below_ref, up_ref, packed_ref, tx_ref, *rest):
-    *more_refs, total_ref, g_ref, both_ref = rest
-    n, tall = layers * size, sym_rows(layers, size)
-    last = n + tall - 8
-    beside = tx_ref[last:, :size]
-    line = lax.broadcasted_iota(jnp.int32, (8, size), 0)
-    total = sums_ref[...] + jnp.where(line == 0, beside[4:5, :], beside[5:6, :])
-    for ref in more_refs:
-        total = total + ref[...]
+def copy_body(layers, size, _, __, from_ref, to_ref):
+    to_ref[...] = from_ref[...]
+
+
+def g_body(layers, size, _, sums_ref, more_ref, g0_ref, below_ref, up_ref, total_ref, g_ref):
+    n, last = layers * size, g_ref.shape[0] - 8
+    total = sums_ref[...] + more_ref[...]
     total_ref[...] = total
-    both_ref[:tall, :] = packed_ref[...]
-    both_ref[tall:, :] = tx_ref[n:, :]
     stu, eu = split(below_ref[:n, :]), split(below_ref[n:, :])
     g_ref[:n, :] = g0_ref[:n, :] + dot3(stu, eu, NN)
     blocks = sym_product(stu, layers, size, NT)
     put_sym(g_ref, lambda a, b: blocks[a, b], layers, size, first=n)
-    g_ref[n:, :] += g0_ref[n:, :] + up_ref[:tall, :]
-
-
-def r_body(layers, size, _, r0_ref, below_ref, tx_ref, rs_ref, re_ref):
+    g_ref[n:, :] += g0_ref[n:, :] + up_ref[...]
+    line = lax.broadcasted_iota(jnp.int32, total.shape, 0)
+    for at in range(layers):
+        cols = slice(at * size, (at + 1) * size)
+        g_ref[last:, cols] = jnp.where(line < 4, g_ref[last:, cols], total)
+
+
+def both_body(layers, size, _, packed_ref, tx_ref, both_ref):
+    n, tall = layers * size, sym_rows(layers, size)
+    both_ref[:tall, :] = packed_ref[...]
+    both_ref[tall:, :] = tx_ref[n:, :]
+
+
+def early_body(layers, size, _, t_ref, e_ref, d_ref, below_ref, yn0_ref, ye0_ref, yd0_ref, yn_ref, ye_ref, yd_ref, su_ref):
+    at = layers * size
+    su_ref[...] = below_ref[:at, :].T
+    n, e, d = split(t_ref[:at, :]), split(e_ref[at:, :]), split(d_ref[...])
+    stu, eu = split(below_ref[:at, :]), split(below_ref[at:, :])
+    yn_ref[...] = yn0_ref[...] + dot3(e, stu, NN) + dot3(d, eu, NT)
+    ye_ref[...] = ye0_ref[...] + dot3(n, stu, NT)
+    yd_ref[...] = yd0_ref[...] + dot3(n, eu, NN)
+
+
+def r_body(layers, size, _, __, r0_ref, su_ref, below_ref, tx_ref, rs_ref, re_ref):
     n = layers * size
-    su, eu, nx = split(below_ref[:n, :].T), split(below_ref[n:, :]), split(tx_ref[:n, :])
+    su, eu, nx = split(su_ref[...]), split(below_ref[n:, :]), split(tx_ref[:n, :])
     cx = split(whole_sym(take_sym(tx_ref[n:, :], layers, size), layers))
     rs_ref[...] = r0_ref[:n, :] + dot3(su, cx, NN) + dot3(eu, nx, NT)
     re_ref[...] = r0_ref[n:, :] + dot3(su, nx, NN)
 
 
-def middle_e_body(
-    layers, size, _, sums_ref, more_ref, t_ref, down_ref, d_ref, below_ref, tx_ref, ye0_ref, total_ref, ye_ref
-):
+def middle_body(layers, size, _, e_ref, d_ref, tx_ref, ye0_ref, yd0_ref, ye_ref, yd_ref):
     at = layers * size
-    total_ref[...] = sums_ref[...] + more_ref[...]
-    n, e, d = split(t_ref[:at, :]), split(down_ref[at:, :]), split(d_ref[...])
-    stu, nx = split(below_ref[:at, :]), split(tx_ref[:at, :])
+    e, d, nx = split(e_ref[at:, :]), split(d_ref[...]), split(tx_ref[:at, :])
     cx = split(whole_sym(take_sym(tx_ref[at:, :], layers, size), layers))
-    ye_ref[...] = ye0_ref[...] + dot3(n, stu, NT) + dot3(e, cx, NN) + dot3(d, nx, NT)
-
-
-def middle_n_body(
-    layers, size, _, sums_ref, more_ref, t_ref, down_ref, d_ref, below_ref, both_ref, tx_ref, yn0_ref, yd0_ref,
-    total_ref, yn_ref, yd_ref,
-):
-    total_ref[...] = sums_ref[...] + more_ref[...]
+    ye_ref[...] = ye0_ref[...] + dot3(e, cx, NN) + dot3(d, nx, NT)
+    yd_ref[...] = yd0_ref[...] + dot3(e, nx, NN)
+
+
+def middle_c_body(layers, size, sums_ref, t_ref, d_ref, both_ref, yn0_ref, yd0_ref, total_ref, yn_ref, yd_ref):
     at, tall = layers * size, sym_rows(layers, size)
-    n, e, d = split(t_ref[:at, :]), split(down_ref[at:, :]), split(d_ref[...])
-    stu, eu, nx = split(below_ref[:at, :]), split(below_ref[at:, :]), split(tx_ref[:at, :])
+    total_ref[...] = sums_ref[...]
+    n, d = split(t_ref[:at, :]), split(d_ref[...])
     cu = split(whole_sym(take_sym(both_ref[:tall, :], layers, size), layers))
     cxu = split(whole_sym(take_sym(both_ref[tall:, :], layers, size), layers))
-    yn_ref[...] = yn0_ref[...] + dot3(n, cu, NN) + dot3(e, stu, NN) + dot3(d, eu, NT)
-    yd_ref[...] = yd0_ref[...] + dot3(n, eu, NN) + dot3(e, nx, NN) + dot3(d, cxu, NN)
-
-
-def twice_h(target, size, sums_ref, more_ref):
-    sums = sums_ref[...] + more_ref[...]
+    yn_ref[...] = yn0_ref[...] + dot3(n, cu, NN)
+    yd_ref[...] = yd0_ref[...] + dot3(d, cxu, NN)
+
+
+def twice_h(target, size, sums):
     t1, t2 = sums[0:1, :], sums[1:2, :]
     return 2.0 * jax.nn.sigmoid((jnp.abs(t2 - target) - jnp.abs(2.0 * t1 - t2 - target)) / size)
 
@@ -357,37 +434,29 @@
             copy.wait()
 
 
-def last_e_body(
-    target, layers, size, mask_ref, _, sums_ref, more_ref, ys_ref, ye_ref, yd_ref, down_ref, d_ref, rs_ref, re_ref,
-    out_ref, held, sems,
+def last_body(
+    target, layers, size, mask_ref, _, c_ref, t_ref, down_ref, d_ref,
+    yc_ref, yn_ref, ys_ref, ye_ref, yd_ref, yc_in_ref, rs_ref, re_ref, g_ref, *rest,
 ):
-    n = layers * size
-    twice = twice_h(target, size, sums_ref, more_ref)
+    *sums_refs, out_ref, held, sems = rest
+    n, last = layers * size, g_ref.shape[0] - 8
+    line = lax.broadcasted_iota(jnp.int32, (8, size), 0)
+    beside = g_ref[last:, :size]
+    sums = jnp.where(line == 0, beside[4:5, :], beside[5:6, :])
+    twice = twice_h(target, size, sum((ref[...] for ref in sums_refs), start=sums))
     sender = Sender(mask_ref, out_ref, held, sems)
     for name, a_ref, *terms in (
         ("D", d_ref, yd_ref),
+        ("E", down_ref.at[n:, :], ye_ref, re_ref),
         ("S", down_ref.at[:n, :], ys_ref, rs_ref),
-        ("E", down_ref.at[n:, :], ye_ref, re_ref),
+        ("N", t_ref.at[:n, :], yn_ref, g_ref),
     ):
         for low, high, slot in panel_blocks(name, layers):
             rows, cols = slice(low * size, (low + 1) * size), slice(high * size, (high + 1) * size)
             y = sum(ref[rows, cols] for ref in terms)
             a = a_ref[cols, rows].T if name == "S" else a_ref[rows, cols]
             sender.send(y + twice * (a - y), low, slot)
-    sender.wait()
-
-
-def last_c_body(
-    target, layers, size, mask_ref, _, sums_ref, more_ref, yc_ref, yn_ref, up_ref, c_ref, t_ref, g_ref, out_ref, held, sems
-):
-    n, tall = layers * size, sym_rows(layers, size)
-    twice = twice_h(target, size, sums_ref, more_ref)
-    sender = Sender(mask_ref, out_ref, held, sems)
-    for low, high, slot in panel_blocks("N", layers):
-        rows, cols = slice(low * size, (low + 1) * size), slice(high * size, (high + 1) * size)
-        y = yn_ref[rows, cols] + g_ref[rows, cols]
-        sender.send(y + twice * (t_ref[rows, cols] - y), low, slot)
-    blocks = take_sym(yc_ref[...] + up_ref[tall:, :] + g_ref[n:, :], layers, size)
+    blocks = take_sym(yc_ref[...] + yc_in_ref[...] + g_ref[n:, :], layers, size)
     for low, high, slot in panel_blocks("C", layers) + [(layer, layer, 0) for layer in range(layers)]:
         rows, cols = slice(low * size, (low + 1) * size), slice(high * size, (high + 1) * size)
         y = blocks[low, high]
@@ -429,60 +498,56 @@
 
     go = functools.partial(call, layers=layers, size=size)
     stored, onsite, mask_hbm = (pltpu.with_memory_space_constraint(value, hbm) for value in (stored, onsite, mask))
+
+    peers = lax.axis_size("col")
+    bits = [1 << k for k in range(peers.bit_length() - 1)]
+    bits = bits[:1] + bits[2:] + bits[1:2]
+
+    def arriving(value):
+        return swapped(value, "col", bits.pop(0)) if bits else jnp.zeros_like(value)
+
     T, Cp, C, down, D, own = go(
         pack_body, outs=[(n + tall, n), packed, panel, (2 * n, n), panel, sums], spaces=[hbm] * 3,
-        scratch=blocks(len(wanted(layers)))
+        scratch=blocks(len(wanted(IN_PLANE, layers)))
         + [pltpu.SMEM(mask.shape, mask.dtype), pltpu.SemaphoreType.DMA, pltpu.VMEM(onsite.shape, F32), pltpu.SemaphoreType.DMA],
     )(mask_hbm, stored, onsite)
     T_x = passed_along(T, "row", -1)
     below = passed_along(down, "col", -1)
-    (up,) = go(up_body, outs=[(2 * tall, n)], spaces=[vmem] * 2)(T, D)
-    up_in = passed_along(up, "col", 1)
-    more = [passed_along(own, "row", -by) for by in range(2, lax.axis_size("row"))]
-    g0, r0 = go(local_g_body, outs=[(n + tall, n), (2 * n, n)], spaces=[hbm] + [vmem] * 3)(up, T, down, D)
-    out, yc, yn, ys, ye, yd = go(
-        local_y_body, outs=[(layers, slots, size, size), packed] + [panel] * 4, spaces=[hbm] + [vmem] * 4,
-        out_spaces=[hbm] + [vmem] * 5, scratch=[pltpu.VMEM((size, size), F32), pltpu.SemaphoreType.DMA((layers * slots,))],
-    )(g0, C, T, down, D)
-    own, g, both = go(g_body, outs=[sums, (n + tall, n), (2 * tall, n)], spaces=[hbm] + [vmem] * (6 + len(more)))(
-        yc, own, g0, below, up_in, Cp, T_x, *more
-    )
-    g_in = passed_along(g, "row", 1)
-    both_u = passed_along(both, "col", -1)
-
-    peers = lax.axis_size("col")
-    bits = [1 << k for k in range(peers.bit_length() - 1)]
-    bits = bits[:1] + bits[2:] + bits[1:2]
+    (gc,) = go(up_body, outs=[packed], spaces=[vmem])(D)
+    gc_in = passed_along(gc, "col", 1)
     if peers.bit_count() > 1:
         own = own + sum(passed_along(own, "col", by) for by in range(1, peers))
         bits = []
     while len(bits) > 3:
-        own = own + swapped(own, "col", bits.pop(0))
-
-    def arriving(value):
-        return swapped(value, "col", bits.pop(0)) if bits else jnp.zeros_like(value)
-
+        own = own + arriving(own)
     more = arriving(own)
-    rs, re = go(r_body, outs=[panel, panel], spaces=[hbm] + [vmem] * 3)(g, r0, below, T_x)
-    rs_in, re_in = passed_along(rs, "col", 1), passed_along(re, "col", 1)
-    own, ye = go(middle_e_body, outs=[sums, panel], spaces=[hbm] + [vmem] * 8)(rs, own, more, T, down, D, below, T_x, ye)
-    more = arriving(own)
-    own, yn, yd = go(middle_n_body, outs=[sums, panel, panel], spaces=[hbm] + [vmem] * 10)(
-        ye, own, more, T, down, D, below, both_u, T_x, yn, yd
+    own, g0, r0, yc_up = go(local_g_body, outs=[sums, (n + tall, n), (2 * n, n), packed], spaces=[hbm] + [vmem] * 5)(
+        gc, own, more, T, down, D
     )
     more = arriving(own)
+    own, out, yc, yn, ys, ye, yd = go(
+        local_y_body, outs=[sums, (layers, slots, size, size), packed] + [panel] * 4, spaces=[hbm] + [vmem] * 6,
+        out_spaces=[vmem, hbm] + [vmem] * 5, scratch=[pltpu.VMEM((size, size), F32), pltpu.SemaphoreType.DMA((layers * slots,))],
+    )(g0, own, more, C, T, down, D)
+    more = arriving(own)
+    (yc_up,) = go(copy_body, outs=[packed], spaces=[hbm] * 2 + [vmem])(yc, below, yc_up)
+    yc_in = passed_along(yc_up, "col", 1)
+    own, g = go(g_body, outs=[sums, (n + tall, n)], spaces=[hbm] + [vmem] * 5)(yc_up, own, more, g0, below, gc_in)
+    g_in = passed_along(g, "row", 1)
+    yn, ye, yd, S_u = go(early_body, outs=[panel] * 4, spaces=[hbm] + [vmem] * 7)(g, T, down, D, below, yn, ye, yd)
+    (both,) = go(both_body, outs=[(2 * tall, n)], spaces=[hbm] + [vmem] * 2)(yn, Cp, T_x)
+    both_u = passed_along(both, "col", -1)
+    rs, re = go(r_body, outs=[panel, panel], spaces=[hbm] * 2 + [vmem] * 4)(both, yc_in, r0, S_u, below, T_x)
+    rs_in, re_in = passed_along(rs, "col", 1), passed_along(re, "col", 1)
+    ye, yd = go(middle_body, outs=[panel] * 2, spaces=[hbm] + [vmem] * 5)(rs, down, D, T_x, ye, yd)
+    own, yn, yd = go(middle_c_body, outs=[sums, panel, panel], spaces=[vmem] * 6)(own, T, D, both_u, yn, yd)
+    every = [own] + [passed_along(own, "row", -by) for by in range(1, lax.axis_size("row") - 1)]
     cells = lax.axis_size("row") * lax.axis_size("col") * layers
     target = float(cells * size // 2)
-
-    def finish(body, out, names, *terms):
-        count = sum(len(panel_blocks(name, layers)) for name in names) + layers * ("C" in names)
-        return go(
-            functools.partial(body, target), outs=[out.shape], out_spaces=[hbm], spaces=[smem, hbm] + [vmem] * (2 + len(terms)),
-            scratch=blocks(count), aliases={1: 0},
-        )(mask, out, own, more, *terms)[0]
-
-    out = finish(last_e_body, out, "SED", ys, ye, yd, down, D, rs_in, re_in)
-    out = finish(last_c_body, out, "NC", yc, yn, up_in, C, T, g_in)
+    (out,) = go(
+        functools.partial(last_body, target), outs=[out.shape], out_spaces=[hbm],
+        spaces=[smem, hbm] + [vmem] * (13 + len(every)), scratch=blocks(len(wanted(IN_PLANE, layers))), aliases={1: 0},
+    )(mask, out, C, T, down, D, yc, yn, ys, ye, yd, yc_in, rs_in, re_in, g_in, *every)
     return out[None, None]
 
 

time: 92.1 us -> 86.9 us (0.944)
  waiting for transfers between devices: 43.7 us -> 37.9 us
  starting transfers between devices: 13.3 us -> 15.5 us
  Pallas kernels: 34.7 us -> 33.1 us
    ppermute x9 -> x10, waiting for transfers between devices: 38.2 us -> 33.2 us  [passed_along(): lax.ppermute(value, axis, [(i, (i + by) % peers) for i in range(peers)])]
    ppermute x9 -> x10, starting transfers between devices: 11.6 us -> 13.4 us  [passed_along(): lax.ppermute(value, axis, [(i, (i + by) % peers) for i in range(peers)])]
    pallas_call x9 -> x11, Pallas kernels: 30 us -> 28.5 us  [the longest x1 8 us: shards(): go(local_y_body, outs=[sums, (layers, slots, size, size), packed] + [pane...]
  transfers between devices with their start and end apart: 12 -> 13, of which waited for: 5 -> 9; matrix products, arithmetic and copies ran while one was open for 0% -> 0% of each run, Pallas kernels for 28% -> 29%
where the time goes in v5:
time: 86.9 us; the launch traced here: 86.8 us
  waiting for transfers between devices  37.9 us (44%)
  Pallas kernels  33.1 us (38%)
  starting transfers between devices  15.5 us (18%)
    ppermute x10, waiting for transfers between devices, passed_along(): lax.ppermute(value, axis, [(i, (i + by) % peers) for i in range(peers)])  33.2 us
    ppermute x10, starting transfers between devices, passed_along(): lax.ppermute(value, axis, [(i, (i + by) % peers) for i in range(peers)])  13.4 us
    pallas_call x1, Pallas kernels, shards(): go(local_y_body, outs=[sums, (layers, slots, size, size), packed] + [pane...  8 us
    ppermute x3, waiting for transfers between devices, swapped(): return lax.ppermute(value, axis, [(i, i ^ bit) for i in range(peers)])  4.68 us
    pallas_call x1, Pallas kernels, shards(): go(pack_body, outs=[(n + tall, n), packed, panel, (2 * n, n), panel, sums...  4.61 us
    pallas_call x1, Pallas kernels, shards(): go(local_g_body, outs=[sums, (n + tall, n), (2 * n, n), packed], spaces=[...  3.89 us
    pallas_call x1, Pallas kernels, shards(): go(early_body, outs=[panel] * 4, spaces=[hbm] + [vmem] * 7)  3.43 us
    pallas_call x1, Pallas kernels, shards(): go(functools.partial(last_body, target), outs=[out.shape], out_spaces=[hb...  3.23 us
  transfers between devices with their start and end apart: 13, of which 9 were waited for; matrix products, arithmetic and copies ran while one was open for 0% of the time, Pallas kernels for 29%

profile of v5, /device:TPU:0, one launch (start us, length us, event | category | flops | bytes accessed | tf_op | source)
XLA Modules:
  0.0 86.8 jit_solution(4614225373185800640)
XLA Ops:
  0.0 4.6 %shard_map.37 = (f32[776,512]{1,0:T(8,128)S(1)}, f32[264,512]{1,0:T(8,128)S(1)}, f32[512,512]{1,0:T(8,128)S(1)}, f32[1024,512]{1,0:T(8,128)S(1)}, f32[512,512]{1,0:T(8,128)S(1)}, /*index=5*/f32[8,256]{1,0:T(8,128)S(1)}) custom-call(s32[2,13]{1,0:T(2,128)} %bitcast.4, f32[2,14,256,256]{3,2,1,0:T(8,128)} %bitcast.6, f32[2,256]{1,0:T(2,128)} %bitcast.7), custom_call_target="tpu_custom_call" | custom-call | tf_op jit(solution)/shard_map/pallas_call | solution.py:509
  4.6 3.4 %collective-permute-start.2 = (f32[1024,512]{1,0:T(8,128)S(1)}, f32[1024,512]{1,0:T(8,128)S(1)}, u32[]{:S(2)}, u32[]{:S(2)}) collective-permute-start(f32[1024,512]{1,0:T(8,128)S(1)} %get-tuple-element.38.down_ref.e_ref), channel_id=1, source_target_pairs={{0,7},{1,0},{2,1},{3,2},{4,3},{5,4},{6,5},{7,6},{8,15},{9,8},{10,9... | collective-permute-start | bytes 6291464 | tf_op jit(solution)/shard_map/ppermute | solution.py:481
  8.0 3.6 %collective-permute-start.5 = (f32[776,512]{1,0:T(8,128)S(1)}, f32[776,512]{1,0:T(8,128)S(1)}, u32[]{:S(2)}, u32[]{:S(2)}) collective-permute-start(f32[776,512]{1,0:T(8,128)S(1)} %get-tuple-element.37.t_ref), channel_id=1, source_target_pairs={{0,24},{8,0},{16,8},{24,16},{1,25},{9,1},{17,9},{25,17},{2,26},{10... | collective-permute-start | bytes 4767752 | tf_op jit(solution)/shard_map/ppermute | solution.py:481
  11.6 0.8 shard_map.38._
  12.4 0.1 collective-permute-start.4
  12.5 0.1 collective-permute-start
  12.6 1.5 %collective-permute-done.more_ref = f32[8,256]{1,0:T(8,128)S(1)} collective-permute-done((f32[8,256]{1,0:T(8,128)S(1)}, f32[8,256]{1,0:T(8,128)S(1)}, u32[]{:S(2)}, u32[]{:S(2)}) %collective-permute-start) | collective-permute-done | bytes 8224 | tf_op jit(solution)/shard_map/ppermute | solution.py:486
  14.0 3.9 %shard_map.39 = (f32[8,256]{1,0:T(8,128)S(1)}, f32[776,512]{1,0:T(8,128)S(1)}, f32[1024,512]{1,0:T(8,128)S(1)}, f32[264,512]{1,0:T(8,128)S(1)}) custom-call(f32[264,512]{1,0:T(8,128)S(1)} %shard_map.38._, f32[8,256]{1,0:T(8,128)S(1)} %get-tuple-element.36.sums_ref, f32[8,256]{1,0:T(8,128)S(1)} %collective-permute-done.more_ref, ...), custom_call_target="tpu_custom_call" | custom-call | tf_op jit(solution)/shard_map/pallas_call | solution.py:524
  17.9 0.6 collective-permute-start.1
  18.6 3.2 %collective-permute-done.1.more_ref = f32[8,256]{1,0:T(8,128)S(1)} collective-permute-done((f32[8,256]{1,0:T(8,128)S(1)}, f32[8,256]{1,0:T(8,128)S(1)}, u32[]{:S(2)}, u32[]{:S(2)}) %collective-permute-start.1) | collective-permute-done | bytes 8224 | tf_op jit(solution)/shard_map/ppermute | solution.py:486
  21.8 8.0 %shard_map.40 = (f32[8,256]{1,0:T(8,128)S(1)}, f32[2,14,256,256]{3,2,1,0:T(8,128)}, f32[264,512]{1,0:T(8,128)S(1)}, f32[512,512]{1,0:T(8,128)S(1)}, f32[512,512]...) custom-call(f32[776,512]{1,0:T(8,128)S(1)} %get-tuple-element.39._.g0_ref, ...), custom_call_target="tpu_custom_call" | custom-call | tf_op jit(solution)/shard_map/pallas_call | solution.py:528
  29.8 1.4 %collective-permute-start.3 = (f32[8,256]{1,0:T(8,128)S(1)}, f32[8,256]{1,0:T(8,128)S(1)}, u32[]{:S(2)}, u32[]{:S(2)}) collective-permute-start(f32[8,256]{1,0:T(8,128)S(1)} %get-tuple-element.45.sums_ref), channel_id=1, source_target_pairs={{0,2},{1,3},{2,0},{3,1},{4,6},{5,7},{6,4},{7,5},{8,10},{9,11},{10,... | collective-permute-start | bytes 24584 | tf_op jit(solution)/shard_map/ppermute | solution.py:486
  31.1 6.3 %collective-permute-done.2.__.below_ref = f32[1024,512]{1,0:T(8,128)S(1)} collective-permute-done((f32[1024,512]{1,0:T(8,128)S(1)}, f32[1024,512]{1,0:T(8,128)S(1)}, u32[]{:S(2)}, u32[]{:S(2)}) %collective-permute-start.2) | collective-permute-done | bytes 2097184 | tf_op jit(solution)/shard_map/ppermute | solution.py:481
  37.5 0.4 collective-permute-start.7
  37.9 1.6 %shard_map.42 = (f32[8,256]{1,0:T(8,128)S(1)}, f32[776,512]{1,0:T(8,128)S(1)}) custom-call(f32[264,512]{1,0:T(8,128)S(1)} %shard_map.41._, f32[8,256]{1,0:T(8,128)S(1)} %get-tuple-element.45.sums_ref, f32[8,256]{1,0:T(8,128)S(1)} %collective-permute-done.3.more_ref, f32[776,512]{1,0:T(8,128)S(1)} %get-tuple-element.39._.g0_ref, ...), custom_call_target="tpu_custom_call" | custom-call | tf_op jit(solution)/shard_map/pallas_call | solution.py:535
  39.5 1.6 %collective-permute-start.10 = (f32[776,512]{1,0:T(8,128)S(1)}, f32[776,512]{1,0:T(8,128)S(1)}, u32[]{:S(2)}, u32[]{:S(2)}) collective-permute-start(f32[776,512]{1,0:T(8,128)S(1)} %get-tuple-element.47._), channel_id=1, source_target_pairs={{0,8},{8,16},{16,24},{24,0},{1,9},{9,17},{17,25},{25,1},{2,10},{10... | collective-permute-start | bytes 4767752 | tf_op jit(solution)/shard_map/ppermute | solution.py:481
  41.2 3.4 %shard_map.43 = (f32[512,512]{1,0:T(8,128)S(1)}, f32[512,512]{1,0:T(8,128)S(1)}, f32[512,512]{1,0:T(8,128)S(1)}, f32[512,512]{1,0:T(8,128)S(1)}) custom-call(f32[776,512]{1,0:T(8,128)S(1)} %get-tuple-element.47._, f32[776,512]{1,0:T(8,128)S(1)} %get-tuple-element.37.t_ref, f32[1024,512]{1,0:T(8,128)S(1)} %get-tuple-element.38.down_ref.e_ref, ...), custom_call_target="tpu_custom_call" | custom-call | tf_op jit(solution)/shard_map/pallas_call | solution.py:537
  44.6 2.2 %collective-permute-done.5.tx_ref = f32[776,512]{1,0:T(8,128)S(1)} collective-permute-done((f32[776,512]{1,0:T(8,128)S(1)}, f32[776,512]{1,0:T(8,128)S(1)}, u32[]{:S(2)}, u32[]{:S(2)}) %collective-permute-start.5) | collective-permute-done | bytes 1589280 | tf_op jit(solution)/shard_map/ppermute | solution.py:481
  46.8 0.1 shard_map.44._
  46.9 0.2 collective-permute-start.6
  47.1 0.4 collective-permute-done.7.__.yc_in_ref
  47.6 2.7 %shard_map.45 = (f32[512,512]{1,0:T(8,128)S(1)}, f32[512,512]{1,0:T(8,128)S(1)}) custom-call(f32[528,512]{1,0:T(8,128)S(1)} %shard_map.44._, f32[264,512]{1,0:T(8,128)S(1)} %collective-permute-done.7.__.yc_in_ref, f32[1024,512]{1,0:T(8,128)S(1)} %get-tuple-element.53.r0_ref, f32[512,512]{1,0:T(8,128)S(1)} %get-tuple-element.54.su_ref, ...), custom_call_target="tpu_custom_call" | custom-call | tf_op jit(solution)/shard_map/pallas_call | solution.py:540
  50.3 0.1 collective-permute-start.8
  50.3 0.1 collective-permute-start.9
  50.4 2.7 %shard_map.46 = (f32[512,512]{1,0:T(8,128)S(1)}, f32[512,512]{1,0:T(8,128)S(1)}) custom-call(f32[512,512]{1,0:T(8,128)S(1)} %get-tuple-element.55._, f32[1024,512]{1,0:T(8,128)S(1)} %get-tuple-element.38.down_ref.e_ref, f32[512,512]{1,0:T(8,128)S(1)} %get-tuple-element.35.panel_ref.d_ref, f32[776,512]{1,0:T(8,128)S(1)} %collective-permute-done.5.tx_ref, ...), custom_call_target="tpu_custom_call" | custom-call | tf_op jit(solution)/shard_map/pallas_call | solution.py:542
  53.2 15.7 %collective-permute-done.6.both_ref = f32[528,512]{1,0:T(8,128)S(1)} collective-permute-done((f32[528,512]{1,0:T(8,128)S(1)}, f32[528,512]{1,0:T(8,128)S(1)}, u32[]{:S(2)}, u32[]{:S(2)}) %collective-permute-start.6) | collective-permute-done | bytes 1081376 | tf_op jit(solution)/shard_map/ppermute | solution.py:481
  68.9 1.9 %shard_map.47 = (f32[8,256]{1,0:T(8,128)S(1)}, f32[512,512]{1,0:T(8,128)S(1)}, f32[512,512]{1,0:T(8,128)S(1)}) custom-call(f32[8,256]{1,0:T(8,128)S(1)} %get-tuple-element.46.sums_ref, f32[776,512]{1,0:T(8,128)S(1)} %get-tuple-element.37.t_ref, f32[512,512]{1,0:T(8,128)S(1)} %get-tuple-element.35.panel_ref.d_ref, ...), custom_call_target="tpu_custom_call" | custom-call | tf_op jit(solution)/shard_map/pallas_call | solution.py:543
  70.8 4.0 %collective-permute-start.11 = (f32[8,256]{1,0:T(8,128)S(1)}, f32[8,256]{1,0:T(8,128)S(1)}, u32[]{:S(2)}, u32[]{:S(2)}) collective-permute-start(f32[8,256]{1,0:T(8,128)S(1)} %get-tuple-element.64.rest_0_), channel_id=1, source_target_pairs={{0,24},{8,0},{16,8},{24,16},{1,25},{9,1},{17,9},{25,17},{2,26},{10... | collective-permute-start | bytes 24584 | tf_op jit(solution)/shard_map/ppermute | solution.py:481
  74.8 3.9 %collective-permute-done.11.rest_1_ = f32[8,256]{1,0:T(8,128)S(1)} collective-permute-done((f32[8,256]{1,0:T(8,128)S(1)}, f32[8,256]{1,0:T(8,128)S(1)}, u32[]{:S(2)}, u32[]{:S(2)}) %collective-permute-start.11) | collective-permute-done | bytes 8224 | tf_op jit(solution)/shard_map/ppermute | solution.py:481
  78.7 1.2 %collective-permute-done.12.rest_2_ = f32[8,256]{1,0:T(8,128)S(1)} collective-permute-done((f32[8,256]{1,0:T(8,128)S(1)}, f32[8,256]{1,0:T(8,128)S(1)}, u32[]{:S(2)}, u32[]{:S(2)}) %collective-permute-start.12) | collective-permute-done | bytes 8224 | tf_op jit(solution)/shard_map/ppermute | solution.py:481
  79.9 3.5 %collective-permute-done.9.re_ref = f32[512,512]{1,0:T(8,128)S(1)} collective-permute-done((f32[512,512]{1,0:T(8,128)S(1)}, f32[512,512]{1,0:T(8,128)S(1)}, u32[]{:S(2)}, u32[]{:S(2)}) %collective-permute-start.9) | collective-permute-done | bytes 1048608 | tf_op jit(solution)/shard_map/ppermute | solution.py:481
  83.4 3.2 %shard_map.48 = f32[2,14,256,256]{3,2,1,0:T(8,128)} custom-call(s32[2,13]{1,0:T(2,128)S(1)} %bitcast.5, f32[2,14,256,256]{3,2,1,0:T(8,128)} %get-tuple-element.42._, f32[512,512]{1,0:T(8,128)S(1)} %get-tuple-element.41.c_ref, f32[776,512]{1,0:T(8,128)S(1)} %get-tuple-element.37.t_ref, ...), custom_call_target="tpu_custom_call", output_to_operand_aliasing={{}: (1, {})} | custom-call | tf_op jit(solution)/shard_map/pallas_call | solution.py:547
  (8 shorter events, 0.1 us)
Async XLA Ops:
  4.6 32.8 %collective-permute-start.2 = (f32[1024,512]{1,0:T(8,128)S(1)}, f32[1024,512]{1,0:T(8,128)S(1)}, u32[]{:S(2)}, u32[]{:S(2)}) collective-permute-start(f32[1024,512]{1,0:T(8,128)S(1)} %get-tuple-element.38.down_ref.e_ref), channel_id=1, source_target_pairs={{0,7},{1,0},{2,1},{3,2},{4,3},{5,4},{6,5},{7,6},{8,15},{9,8},{10,9... | collective-permute-start | bytes 6291464 | tf_op jit(solution)/shard_map/ppermute | solution.py:481
  8.0 38.8 %collective-permute-start.5 = (f32[776,512]{1,0:T(8,128)S(1)}, f32[776,512]{1,0:T(8,128)S(1)}, u32[]{:S(2)}, u32[]{:S(2)}) collective-permute-start(f32[776,512]{1,0:T(8,128)S(1)} %get-tuple-element.37.t_ref), channel_id=1, source_target_pairs={{0,24},{8,0},{16,8},{24,16},{1,25},{9,1},{17,9},{25,17},{2,26},{10... | collective-permute-start | bytes 4767752 | tf_op jit(solution)/shard_map/ppermute | solution.py:481
  12.4 25.5 %collective-permute-start.4 = (f32[264,512]{1,0:T(8,128)S(1)}, f32[264,512]{1,0:T(8,128)S(1)}, u32[]{:S(2)}, u32[]{:S(2)}) collective-permute-start(f32[264,512]{1,0:T(8,128)S(1)} %shard_map.38._), channel_id=1, source_target_pairs={{0,1},{1,2},{2,3},{3,4},{4,5},{5,6},{6,7},{7,0},{8,9},{9,10},{10,1... | collective-permute-start | bytes 1622024 | tf_op jit(solution)/shard_map/ppermute | solution.py:481
  12.5 1.6 %collective-permute-start = (f32[8,256]{1,0:T(8,128)S(1)}, f32[8,256]{1,0:T(8,128)S(1)}, u32[]{:S(2)}, u32[]{:S(2)}) collective-permute-start(f32[8,256]{1,0:T(8,128)S(1)} %get-tuple-element.36.sums_ref), channel_id=1, source_target_pairs={{0,1},{1,0},{2,3},{3,2},{4,5},{5,4},{6,7},{7,6},{8,9},{9,8},{10,11... | collective-permute-start | bytes 24584 | tf_op jit(solution)/shard_map/ppermute | solution.py:486
  17.9 3.8 %collective-permute-start.1 = (f32[8,256]{1,0:T(8,128)S(1)}, f32[8,256]{1,0:T(8,128)S(1)}, u32[]{:S(2)}, u32[]{:S(2)}) collective-permute-start(f32[8,256]{1,0:T(8,128)S(1)} %get-tuple-element.40.sums_ref), channel_id=1, source_target_pairs={{0,4},{1,5},{2,6},{3,7},{4,0},{5,1},{6,2},{7,3},{8,12},{9,13},{10,... | collective-permute-start | bytes 24584 | tf_op jit(solution)/shard_map/ppermute | solution.py:486
  29.8 8.1 %collective-permute-start.3 = (f32[8,256]{1,0:T(8,128)S(1)}, f32[8,256]{1,0:T(8,128)S(1)}, u32[]{:S(2)}, u32[]{:S(2)}) collective-permute-start(f32[8,256]{1,0:T(8,128)S(1)} %get-tuple-element.45.sums_ref), channel_id=1, source_target_pairs={{0,2},{1,3},{2,0},{3,1},{4,6},{5,7},{6,4},{7,5},{8,10},{9,11},{10,... | collective-permute-start | bytes 24584 | tf_op jit(solution)/shard_map/ppermute | solution.py:486
  37.5 10.1 %collective-permute-start.7 = (f32[264,512]{1,0:T(8,128)S(1)}, f32[264,512]{1,0:T(8,128)S(1)}, u32[]{:S(2)}, u32[]{:S(2)}) collective-permute-start(f32[264,512]{1,0:T(8,128)S(1)} %shard_map.41._), channel_id=1, source_target_pairs={{0,1},{1,2},{2,3},{3,4},{4,5},{5,6},{6,7},{7,0},{8,9},{9,10},{10,1... | collective-permute-start | bytes 1622024 | tf_op jit(solution)/shard_map/ppermute | solution.py:481
  39.5 43.8 %collective-permute-start.10 = (f32[776,512]{1,0:T(8,128)S(1)}, f32[776,512]{1,0:T(8,128)S(1)}, u32[]{:S(2)}, u32[]{:S(2)}) collective-permute-start(f32[776,512]{1,0:T(8,128)S(1)} %get-tuple-element.47._), channel_id=1, source_target_pairs={{0,8},{8,16},{16,24},{24,0},{1,9},{9,17},{17,25},{25,1},{2,10},{10... | collective-permute-start | bytes 4767752 | tf_op jit(solution)/shard_map/ppermute | solution.py:481
  46.9 22.0 %collective-permute-start.6 = (f32[528,512]{1,0:T(8,128)S(1)}, f32[528,512]{1,0:T(8,128)S(1)}, u32[]{:S(2)}, u32[]{:S(2)}) collective-permute-start(f32[528,512]{1,0:T(8,128)S(1)} %shard_map.44._), channel_id=1, source_target_pairs={{0,7},{1,0},{2,1},{3,2},{4,3},{5,4},{6,5},{7,6},{8,15},{9,8},{10,9... | collective-permute-start | bytes 3244040 | tf_op jit(solution)/shard_map/ppermute | solution.py:481
  50.3 29.6 %collective-permute-start.8 = (f32[512,512]{1,0:T(8,128)S(1)}, f32[512,512]{1,0:T(8,128)S(1)}, u32[]{:S(2)}, u32[]{:S(2)}) collective-permute-start(f32[512,512]{1,0:T(8,128)S(1)} %get-tuple-element.55._), channel_id=1, source_target_pairs={{0,1},{1,2},{2,3},{3,4},{4,5},{5,6},{6,7},{7,0},{8,9},{9,10},{10,1... | collective-permute-start | bytes 3145736 | tf_op jit(solution)/shard_map/ppermute | solution.py:481
  50.3 33.0 %collective-permute-start.9 = (f32[512,512]{1,0:T(8,128)S(1)}, f32[512,512]{1,0:T(8,128)S(1)}, u32[]{:S(2)}, u32[]{:S(2)}) collective-permute-start(f32[512,512]{1,0:T(8,128)S(1)} %get-tuple-element.63), channel_id=1, source_target_pairs={{0,1},{1,2},{2,3},{3,4},{4,5},{5,6},{6,7},{7,0},{8,9},{9,10},{10,1... | collective-permute-start | bytes 3145736 | tf_op jit(solution)/shard_map/ppermute | solution.py:481
  68.9 14.5 %copy-start = (s32[1,1,2,13]{3,2,1,0:T(2,128)S(1)}, s32[1,1,2,13]{3,2,1,0:T(2,128)}, u32[]{:S(2)}) copy-start(s32[1,1,2,13]{3,2,1,0:T(2,128)} %param.5) | copy-start | bytes 316
  70.8 7.9 %collective-permute-start.11 = (f32[8,256]{1,0:T(8,128)S(1)}, f32[8,256]{1,0:T(8,128)S(1)}, u32[]{:S(2)}, u32[]{:S(2)}) collective-permute-start(f32[8,256]{1,0:T(8,128)S(1)} %get-tuple-element.64.rest_0_), channel_id=1, source_target_pairs={{0,24},{8,0},{16,8},{24,16},{1,25},{9,1},{17,9},{25,17},{2,26},{10... | collective-permute-start | bytes 24584 | tf_op jit(solution)/shard_map/ppermute | solution.py:481
  74.8 5.1 %collective-permute-start.12 = (f32[8,256]{1,0:T(8,128)S(1)}, f32[8,256]{1,0:T(8,128)S(1)}, u32[]{:S(2)}, u32[]{:S(2)}) collective-permute-start(f32[8,256]{1,0:T(8,128)S(1)} %get-tuple-element.64.rest_0_), channel_id=1, source_target_pairs={{0,16},{8,24},{16,0},{24,8},{1,17},{9,25},{17,1},{25,9},{2,18},{10... | collective-permute-start | bytes 24584 | tf_op jit(solution)/shard_map/ppermute | solution.py:481

commit v6 on v5

--- a/solution.py
+++ b/solution.py
@@ -148,14 +148,15 @@
     return mask_ref[layer, slot - 1] > 0
 
 
-def load_panel(out_ref, held, first, name, layers, size, mask_ref, flip=False, top=0):
+def load_panel(out_ref, held, first, name, layers, size, mask_ref, top=0):
     if layers > 2:
         out_ref[top : top + layers * size, :] = jnp.zeros((layers * size, layers * size), F32)
+    squares = 0.0
     for k, (low, high, slot) in enumerate(panel_blocks(name, layers)):
         value = jnp.where(kept(mask_ref, low, slot), held[first + k], 0.0)
-        if flip:
-            low, high, value = high, low, value.T
         out_ref[top + low * size : top + (low + 1) * size, high * size : (high + 1) * size] = value
+        squares = squares + squares_of(value)
+    return squares
 
 
 def start_loads(stored_ref, held, sems, wanted):
@@ -168,8 +169,12 @@
     return copies
 
 
+def lanes(value):
+    return jnp.sum(value.reshape(-1, 8, value.shape[-1]), axis=0)
+
+
 def squares_of(value):
-    return jnp.sum(value * value)
+    return lanes(value * value)
 
 
 def wanted(names, layers):
@@ -178,68 +183,25 @@
     ]
 
 
-def pack_body(
-    layers, size, mask_ref, stored_ref, onsite_ref, t_ref, packed_ref, c_ref, down_ref, d_ref, sums_ref,
-    held, sems, mask, mask_sem, onsite, onsite_sem,
-):
+def pack_e_body(layers, size, mask_ref, stored_ref, down_ref, sums_ref, held, sems, mask, mask_sem):
     n = layers * size
-    small = [
-        pltpu.make_async_copy(mask_ref, mask, mask_sem),
-        pltpu.make_async_copy(onsite_ref, onsite, onsite_sem),
-    ]
-    for copy in small:
-        copy.start()
-    copies = start_loads(stored_ref, held, sems, wanted("CSEND", layers))
-    for copy in small:
-        copy.wait()
-    row, col = rows_cols(size)
-    c_ref[...] = jnp.zeros(c_ref.shape, F32)
-    for layer in range(layers):
-        copies[layer].wait()
-        block = held[layer]
-        block = 0.5 * (block + block.T) + jnp.where(row == col, onsite[layer : layer + 1, :], 0.0)
-        c_ref[layer * size : (layer + 1) * size, layer * size : (layer + 1) * size] = block
-    at = layers
-    for low, high, slot in panel_blocks("C", layers):
-        copies[at].wait()
-        block = jnp.where(kept(mask, low, slot), held[at], 0.0)
-        c_ref[low * size : (low + 1) * size, high * size : (high + 1) * size] = block
-        c_ref[high * size : (high + 1) * size, low * size : (low + 1) * size] = block.T
-        at += 1
-    put_sym(
-        packed_ref,
-        lambda a, b: c_ref[a * size : (a + 1) * size, b * size : (b + 1) * size],
-        layers,
-        size,
-    )
-    t_ref[n:, :] = packed_ref[...]
+    small = pltpu.make_async_copy(mask_ref, mask, mask_sem)
+    small.start()
+    copies = start_loads(stored_ref, held, sems, wanted("SE", layers))
+    small.wait()
+    at = 0
     squares = 0.0
-    for name, ref, top in (("S", down_ref, 0), ("E", down_ref, n), ("N", t_ref, 0), ("D", d_ref, 0)):
+    for name, top in (("S", 0), ("E", n)):
         count = len(panel_blocks(name, layers))
         for copy in copies[at : at + count]:
             copy.wait()
-        load_panel(ref, held, at, name, layers, size, mask, flip=name == "S", top=top)
-        squares = squares + squares_of(ref[top : top + n, :])
+        squares = squares + load_panel(down_ref, held, at, name, layers, size, mask, top=top)
         at += count
-    row, col = rows_cols(n)
-    c_now = c_ref[...]
-    trace = jnp.sum(jnp.where(row == col, c_now, 0.0))
-    line = lax.broadcasted_iota(jnp.int32, sums_ref.shape, 0)
-    sums_ref[...] = jnp.where(line % 4 == 0, trace, squares_of(c_now) + 2.0 * squares)
-
-
-def squares_of(value):
-    return jnp.sum(value * value)
-
-
-def wanted(names, layers):
-    return [(layer, 0) for layer in range(layers) if "C" in names] + [
-        (low, slot) for name in names for low, _, slot in panel_blocks(name, layers)
-    ]
+    sums_ref[...] = 2.0 * squares
 
 
 def pack_t_body(
-    layers, size, mask_ref, stored_ref, onsite_ref, t_ref, packed_ref, c_ref, sums_ref,
+    layers, size, mask_ref, stored_ref, onsite_ref, before_ref, t_ref, packed_ref, c_ref, sums_ref,
     held, sems, mask, mask_sem, onsite, onsite_sem,
 ):
     n = layers * size
@@ -253,16 +215,22 @@
     for copy in small:
         copy.wait()
     row, col = rows_cols(size)
-    c_ref[...] = jnp.zeros(c_ref.shape, F32)
+    if layers > 2:
+        c_ref[...] = jnp.zeros(c_ref.shape, F32)
+    trace = squares = 0.0
     for layer in range(layers):
         copies[layer].wait()
         block = held[layer]
-        block = 0.5 * (block + block.T) + jnp.where(row == col, onsite[layer : layer + 1, :], 0.0)
+        diagonal = jnp.where(row == col, onsite[layer : layer + 1, :], 0.0)
+        trace = trace + lanes(jnp.where(row == col, block, 0.0) + diagonal)
+        block = 0.5 * (block + block.T) + diagonal
+        squares = squares + squares_of(block)
         c_ref[layer * size : (layer + 1) * size, layer * size : (layer + 1) * size] = block
     at = layers
     for low, high, slot in panel_blocks("C", layers):
         copies[at].wait()
         block = jnp.where(kept(mask, low, slot), held[at], 0.0)
+        squares = squares + 2.0 * squares_of(block)
         c_ref[low * size : (low + 1) * size, high * size : (high + 1) * size] = block
         c_ref[high * size : (high + 1) * size, low * size : (low + 1) * size] = block.T
         at += 1
@@ -275,38 +243,21 @@
     t_ref[n:, :] = packed_ref[...]
     for copy in copies[at:]:
         copy.wait()
-    load_panel(t_ref, held, at, "N", layers, size, mask)
-    row, col = rows_cols(n)
-    c_now = c_ref[...]
-    trace = jnp.sum(jnp.where(row == col, c_now, 0.0))
-    line = lax.broadcasted_iota(jnp.int32, sums_ref.shape, 0)
-    sums_ref[...] = jnp.where(line % 4 == 0, trace, squares_of(c_now) + 2.0 * squares_of(t_ref[:n, :]))
-
-
-def pack_e_body(layers, size, mask_ref, stored_ref, before_ref, st_ref, e_ref, d_ref, sums_ref, held, sems, mask, mask_sem):
+    sums_ref[:8, :] = trace
+    squares = squares + 2.0 * load_panel(t_ref, held, at, "N", layers, size, mask)
+    sums_ref[8:, :] = before_ref[...] + squares
+
+
+def pack_d_body(layers, size, mask_ref, stored_ref, before_ref, d_ref, up_ref, sums_ref, held, sems, mask, mask_sem):
     small = pltpu.make_async_copy(mask_ref, mask, mask_sem)
     small.start()
-    copies = start_loads(stored_ref, held, sems, wanted("SED", layers))
+    copies = start_loads(stored_ref, held, sems, wanted("D", layers))
     small.wait()
-    at = 0
-    squares = 0.0
-    for name, ref in (("S", st_ref), ("E", e_ref), ("D", d_ref)):
-        count = len(panel_blocks(name, layers))
-        for copy in copies[at : at + count]:
-            copy.wait()
-        load_panel(ref, held, at, name, layers, size, mask, flip=name == "S")
-        squares = squares + squares_of(ref[...])
-        at += count
-    line = lax.broadcasted_iota(jnp.int32, sums_ref.shape, 0)
-    sums_ref[...] = before_ref[...] + jnp.where(line % 4 == 0, 0.0, 2.0 * squares)
-
-
-def squares_of(value):
-    return jnp.sum(value * value)
-
-
-def up_body(layers, size, panel_ref, up_ref):
-    blocks = sym_product(split(panel_ref[: layers * size, :]), layers, size, TN)
+    for copy in copies:
+        copy.wait()
+    sums_ref[:8, :] = before_ref[:8, :]
+    sums_ref[8:, :] = before_ref[8:, :] + 2.0 * load_panel(d_ref, held, 0, "D", layers, size, mask)
+    blocks = sym_product(split(d_ref[...]), layers, size, TN)
     put_sym(up_ref, lambda a, b: blocks[a, b], layers, size)
 
 
@@ -338,14 +289,14 @@
                 copies[-1].start()
     at = layers * size
     parts = (c_ref[...], t_ref[:at, :], down_ref[:at, :], down_ref[at:, :], d_ref[...])
-    c, n, st, e, d = (split(part) for part in parts)
+    c, n, s, e, d = (split(part) for part in parts)
     yn_ref[...] = dot3(c, n, NN)
-    ys_ref[...] = dot3(c, st, NT)
+    ys_ref[...] = dot3(c, s, NN)
     ye_ref[...] = dot3(c, e, NN)
     yd_ref[...] = dot3(c, d, NN)
     terms = [
         sym_product(pair, layers, size, dims)
-        for pair, dims in ((c, NT), (n, NT), (st, TN), (e, NT), (d, NT))
+        for pair, dims in ((c, NT), (n, NT), (s, NT), (e, NT), (d, NT))
     ]
     put_sym(yc_ref, lambda a, b: sum(term[a, b] for term in terms), layers, size)
     for copy in copies:
@@ -358,14 +309,15 @@
 
 def g_body(layers, size, _, sums_ref, more_ref, g0_ref, below_ref, up_ref, total_ref, g_ref):
     n, last = layers * size, g_ref.shape[0] - 8
-    total = sums_ref[...] + more_ref[...]
+    parts = sums_ref[...] + more_ref[...]
+    line = lax.broadcasted_iota(jnp.int32, total_ref.shape, 0)
+    total = jnp.where(line % 4 == 0, jnp.sum(parts[:8, :]), jnp.sum(parts[8:, :]))
     total_ref[...] = total
-    stu, eu = split(below_ref[:n, :]), split(below_ref[n:, :])
+    stu, eu = split(below_ref[:n, :].T), split(below_ref[n:, :])
     g_ref[:n, :] = g0_ref[:n, :] + dot3(stu, eu, NN)
     blocks = sym_product(stu, layers, size, NT)
     put_sym(g_ref, lambda a, b: blocks[a, b], layers, size, first=n)
     g_ref[n:, :] += g0_ref[n:, :] + up_ref[...]
-    line = lax.broadcasted_iota(jnp.int32, total.shape, 0)
     for at in range(layers):
         cols = slice(at * size, (at + 1) * size)
         g_ref[last:, cols] = jnp.where(line < 4, g_ref[last:, cols], total)
@@ -377,19 +329,18 @@
     both_ref[tall:, :] = tx_ref[n:, :]
 
 
-def early_body(layers, size, _, t_ref, e_ref, d_ref, below_ref, yn0_ref, ye0_ref, yd0_ref, yn_ref, ye_ref, yd_ref, su_ref):
+def early_body(layers, size, _, t_ref, e_ref, d_ref, below_ref, yn0_ref, ye0_ref, yd0_ref, yn_ref, ye_ref, yd_ref):
     at = layers * size
-    su_ref[...] = below_ref[:at, :].T
     n, e, d = split(t_ref[:at, :]), split(e_ref[at:, :]), split(d_ref[...])
-    stu, eu = split(below_ref[:at, :]), split(below_ref[at:, :])
-    yn_ref[...] = yn0_ref[...] + dot3(e, stu, NN) + dot3(d, eu, NT)
-    ye_ref[...] = ye0_ref[...] + dot3(n, stu, NT)
+    su, eu = split(below_ref[:at, :]), split(below_ref[at:, :])
+    yn_ref[...] = yn0_ref[...] + dot3(e, su, NT) + dot3(d, eu, NT)
+    ye_ref[...] = ye0_ref[...] + dot3(n, su, NN)
     yd_ref[...] = yd0_ref[...] + dot3(n, eu, NN)
 
 
-def r_body(layers, size, _, __, r0_ref, su_ref, below_ref, tx_ref, rs_ref, re_ref):
+def r_body(layers, size, _, __, r0_ref, below_ref, tx_ref, rs_ref, re_ref):
     n = layers * size
-    su, eu, nx = split(su_ref[...]), split(below_ref[n:, :]), split(tx_ref[:n, :])
+    su, eu, nx = split(below_ref[:n, :]), split(below_ref[n:, :]), split(tx_ref[:n, :])
     cx = split(whole_sym(take_sym(tx_ref[n:, :], layers, size), layers))
     rs_ref[...] = r0_ref[:n, :] + dot3(su, cx, NN) + dot3(eu, nx, NT)
     re_ref[...] = r0_ref[n:, :] + dot3(su, nx, NN)
@@ -429,38 +380,46 @@
         self.copies.append(pltpu.make_async_copy(self.held.at[k], self.out_ref.at[low, slot], self.sems.at[k]))
         self.copies[-1].start()
 
+    def send_panel(self, name, twice, a_ref, terms, layers, size):
+        for low, high, slot in panel_blocks(name, layers):
+            rows, cols = slice(low * size, (low + 1) * size), slice(high * size, (high + 1) * size)
+            y = sum(ref[rows, cols] for ref in terms)
+            self.send(y + twice * (a_ref[rows, cols] - y), low, slot)
+
     def wait(self):
         for copy in self.copies:
             copy.wait()
 
 
-def last_body(
-    target, layers, size, mask_ref, _, c_ref, t_ref, down_ref, d_ref,
-    yc_ref, yn_ref, ys_ref, ye_ref, yd_ref, yc_in_ref, rs_ref, re_ref, g_ref, *rest,
+def last_c_body(
+    target, layers, size, mask_ref, _, c_ref, t_ref, down_ref, d_ref, yc_ref, yn_ref, ys_ref, yd_ref, yc_in_ref, rs_ref, g_ref,
+    *rest,
 ):
-    *sums_refs, out_ref, held, sems = rest
+    *sums_refs, out_ref, twice_ref, held, sems = rest
     n, last = layers * size, g_ref.shape[0] - 8
     line = lax.broadcasted_iota(jnp.int32, (8, size), 0)
     beside = g_ref[last:, :size]
     sums = jnp.where(line == 0, beside[4:5, :], beside[5:6, :])
     twice = twice_h(target, size, sum((ref[...] for ref in sums_refs), start=sums))
+    twice_ref[...] = jnp.broadcast_to(twice, twice_ref.shape)
     sender = Sender(mask_ref, out_ref, held, sems)
     for name, a_ref, *terms in (
         ("D", d_ref, yd_ref),
-        ("E", down_ref.at[n:, :], ye_ref, re_ref),
+        ("N", t_ref.at[:n, :], yn_ref, g_ref),
         ("S", down_ref.at[:n, :], ys_ref, rs_ref),
-        ("N", t_ref.at[:n, :], yn_ref, g_ref),
     ):
-        for low, high, slot in panel_blocks(name, layers):
-            rows, cols = slice(low * size, (low + 1) * size), slice(high * size, (high + 1) * size)
-            y = sum(ref[rows, cols] for ref in terms)
-            a = a_ref[cols, rows].T if name == "S" else a_ref[rows, cols]
-            sender.send(y + twice * (a - y), low, slot)
+        sender.send_panel(name, twice, a_ref, terms, layers, size)
     blocks = take_sym(yc_ref[...] + yc_in_ref[...] + g_ref[n:, :], layers, size)
     for low, high, slot in panel_blocks("C", layers) + [(layer, layer, 0) for layer in range(layers)]:
         rows, cols = slice(low * size, (low + 1) * size), slice(high * size, (high + 1) * size)
         y = blocks[low, high]
         sender.send(y + twice * (c_ref[rows, cols] - y), low, slot)
+    sender.wait()
+
+
+def last_e_body(layers, size, mask_ref, _, twice_ref, down_ref, ye_ref, re_ref, out_ref, held, sems):
+    sender = Sender(mask_ref, out_ref, held, sems)
+    sender.send_panel("E", twice_ref[0:1, :], down_ref.at[layers * size :, :], [ye_ref, re_ref], layers, size)
     sender.wait()
 
 
@@ -490,7 +449,7 @@
     stored, onsite, mask = stored_blocks[0, 0], onsite[0, 0], bond_mask[0, 0]
     layers, slots, size = stored.shape[:3]
     n, tall = layers * size, sym_rows(layers, size)
-    panel, packed, sums = (n, n), (tall, n), (8, size)
+    panel, packed, sums, total = (n, n), (tall, n), (16, size), (8, size)
     vmem, smem, hbm = pltpu.VMEM, pltpu.SMEM, pltpu.HBM
 
     def blocks(count):
@@ -506,14 +465,19 @@
     def arriving(value):
         return swapped(value, "col", bits.pop(0)) if bits else jnp.zeros_like(value)
 
-    T, Cp, C, down, D, own = go(
-        pack_body, outs=[(n + tall, n), packed, panel, (2 * n, n), panel, sums], spaces=[hbm] * 3,
-        scratch=blocks(len(wanted(IN_PLANE, layers)))
-        + [pltpu.SMEM(mask.shape, mask.dtype), pltpu.SemaphoreType.DMA, pltpu.VMEM(onsite.shape, F32), pltpu.SemaphoreType.DMA],
-    )(mask_hbm, stored, onsite)
+    small = [pltpu.SMEM(mask.shape, mask.dtype), pltpu.SemaphoreType.DMA]
+    down, own = go(
+        pack_e_body, outs=[(2 * n, n), total], spaces=[hbm] * 2, scratch=blocks(len(wanted("SE", layers))) + small
+    )(mask_hbm, stored)
+    below = passed_along(down, "col", -1)
+    T, Cp, C, own = go(
+        pack_t_body, outs=[(n + tall, n), packed, panel, sums], spaces=[hbm] * 3 + [vmem],
+        scratch=blocks(len(wanted("CN", layers))) + small + [pltpu.VMEM(onsite.shape, F32), pltpu.SemaphoreType.DMA],
+    )(mask_hbm, stored, onsite, own)
     T_x = passed_along(T, "row", -1)
-    below = passed_along(down, "col", -1)
-    (gc,) = go(up_body, outs=[packed], spaces=[vmem])(D)
+    D, gc, own = go(
+        pack_d_body, outs=[panel, packed, sums], spaces=[hbm] * 2 + [vmem], scratch=blocks(len(wanted("D", layers))) + small
+    )(mask_hbm, stored, own)
     gc_in = passed_along(gc, "col", 1)
     if peers.bit_count() > 1:
         own = own + sum(passed_along(own, "col", by) for by in range(1, peers))
@@ -532,22 +496,26 @@
     more = arriving(own)
     (yc_up,) = go(copy_body, outs=[packed], spaces=[hbm] * 2 + [vmem])(yc, below, yc_up)
     yc_in = passed_along(yc_up, "col", 1)
-    own, g = go(g_body, outs=[sums, (n + tall, n)], spaces=[hbm] + [vmem] * 5)(yc_up, own, more, g0, below, gc_in)
+    own, g = go(g_body, outs=[total, (n + tall, n)], spaces=[hbm] + [vmem] * 5)(yc_up, own, more, g0, below, gc_in)
     g_in = passed_along(g, "row", 1)
-    yn, ye, yd, S_u = go(early_body, outs=[panel] * 4, spaces=[hbm] + [vmem] * 7)(g, T, down, D, below, yn, ye, yd)
-    (both,) = go(both_body, outs=[(2 * tall, n)], spaces=[hbm] + [vmem] * 2)(yn, Cp, T_x)
+    (both,) = go(both_body, outs=[(2 * tall, n)], spaces=[hbm] + [vmem] * 2)(g, Cp, T_x)
     both_u = passed_along(both, "col", -1)
-    rs, re = go(r_body, outs=[panel, panel], spaces=[hbm] * 2 + [vmem] * 4)(both, yc_in, r0, S_u, below, T_x)
+    rs, re = go(r_body, outs=[panel, panel], spaces=[hbm] * 2 + [vmem] * 3)(both, yc_in, r0, below, T_x)
     rs_in, re_in = passed_along(rs, "col", 1), passed_along(re, "col", 1)
-    ye, yd = go(middle_body, outs=[panel] * 2, spaces=[hbm] + [vmem] * 5)(rs, down, D, T_x, ye, yd)
-    own, yn, yd = go(middle_c_body, outs=[sums, panel, panel], spaces=[vmem] * 6)(own, T, D, both_u, yn, yd)
+    yn, ye, yd = go(early_body, outs=[panel] * 3, spaces=[hbm] + [vmem] * 7)(rs, T, down, D, below, yn, ye, yd)
+    ye, yd = go(middle_body, outs=[panel] * 2, spaces=[hbm] + [vmem] * 5)(yn, down, D, T_x, ye, yd)
+    own, yn, yd = go(middle_c_body, outs=[total, panel, panel], spaces=[vmem] * 6)(own, T, D, both_u, yn, yd)
     every = [own] + [passed_along(own, "row", -by) for by in range(1, lax.axis_size("row") - 1)]
     cells = lax.axis_size("row") * lax.axis_size("col") * layers
     target = float(cells * size // 2)
+    out, twice = go(
+        functools.partial(last_c_body, target), outs=[out.shape, total], out_spaces=[hbm, vmem],
+        spaces=[smem, hbm] + [vmem] * (11 + len(every)), scratch=blocks(len(wanted("CNSD", layers))), aliases={1: 0},
+    )(mask, out, C, T, down, D, yc, yn, ys, yd, yc_in, rs_in, g_in, *every)
     (out,) = go(
-        functools.partial(last_body, target), outs=[out.shape], out_spaces=[hbm],
-        spaces=[smem, hbm] + [vmem] * (13 + len(every)), scratch=blocks(len(wanted(IN_PLANE, layers))), aliases={1: 0},
-    )(mask, out, C, T, down, D, yc, yn, ys, ye, yd, yc_in, rs_in, re_in, g_in, *every)
+        last_e_body, outs=[out.shape], out_spaces=[hbm], spaces=[smem, hbm] + [vmem] * 4,
+        scratch=blocks(len(wanted("E", layers))), aliases={1: 0},
+    )(mask, out, twice, down, ye, re_in)
     return out[None, None]
 
 

time: 86.9 us -> 84 us (0.967)
  waiting for transfers between devices: 37.9 us -> 32.5 us
  Pallas kernels: 33.1 us -> 34.7 us
    ppermute x10, waiting for transfers between devices: 33.2 us -> 27.6 us  [passed_along(): lax.ppermute(value, axis, [(i, (i + by) % peers) for i in range(peers)])]
    pallas_call x8 -> x10, Pallas kernels: 18.4 us -> 20.2 us  [the longest x1 3.45 us: shards(): go(early_body, outs=[panel] * 3, spaces=[hbm] + [vmem] * 7)]
  transfers between devices with their start and end apart: 13 -> 13, of which waited for: 9 -> 7; matrix products, arithmetic and copies ran while one was open for 0% -> 0% of each run, Pallas kernels for 29% -> 38%
where the time goes in v6:
time: 84 us; the launch traced here: 83.8 us
  Pallas kernels  34.7 us (41%)
  waiting for transfers between devices  32.5 us (39%)
  starting transfers between devices  16.3 us (19%)
    ppermute x10, waiting for transfers between devices, passed_along(): lax.ppermute(value, axis, [(i, (i + by) % peers) for i in range(peers)])  27.6 us
    ppermute x10, starting transfers between devices, passed_along(): lax.ppermute(value, axis, [(i, (i + by) % peers) for i in range(peers)])  14.2 us
    pallas_call x1, Pallas kernels, shards(): go(local_y_body, outs=[sums, (layers, slots, size, size), packed] + [pane...  7.91 us
    ppermute x3, waiting for transfers between devices, swapped(): return lax.ppermute(value, axis, [(i, i ^ bit) for i in range(peers)])  4.9 us
    pallas_call x1, Pallas kernels, shards(): go(local_g_body, outs=[sums, (n + tall, n), (2 * n, n), packed], spaces=[...  3.89 us
    pallas_call x1, Pallas kernels, shards(): go(early_body, outs=[panel] * 3, spaces=[hbm] + [vmem] * 7)  3.45 us
    pallas_call x1, Pallas kernels, shards(): go(functools.partial(last_c_body, target), outs=[out.shape, total], out_s...  3.01 us
    pallas_call x1, Pallas kernels, shards(): go(r_body, outs=[panel, panel], spaces=[hbm] * 2 + [vmem] * 3)  2.72 us
  transfers between devices with their start and end apart: 13, of which 7 were waited for; matrix products, arithmetic and copies ran while one was open for 0% of the time, Pallas kernels for 38%

profile of v6, /device:TPU:0, one launch (start us, length us, event | category | flops | bytes accessed | tf_op | source)
XLA Modules:
  0.0 83.8 jit_solution(5961173221019430569)
XLA Ops:
  0.0 1.7 %shard_map.37 = (f32[1024,512]{1,0:T(8,128)S(1)}, f32[8,256]{1,0:T(8,128)S(1)}) custom-call(s32[2,13]{1,0:T(2,128)} %bitcast.4, f32[2,14,256,256]{3,2,1,0:T(8,128)} %bitcast.9), custom_call_target="tpu_custom_call" | custom-call | tf_op jit(solution)/shard_map/pallas_call | solution.py:469
  1.7 3.4 %collective-permute-start.2 = (f32[1024,512]{1,0:T(8,128)S(1)}, f32[1024,512]{1,0:T(8,128)S(1)}, u32[]{:S(2)}, u32[]{:S(2)}) collective-permute-start(f32[1024,512]{1,0:T(8,128)S(1)} %get-tuple-element.44.down_ref.e_ref), channel_id=1, source_target_pairs={{0,7},{1,0},{2,1},{3,2},{4,3},{5,4},{6,5},{7,6},{8,15},{9,8},{10,9... | collective-permute-start | bytes 6291464 | tf_op jit(solution)/shard_map/ppermute | solution.py:440
  5.1 1.9 %shard_map.38 = (f32[776,512]{1,0:T(8,128)S(1)}, f32[264,512]{1,0:T(8,128)S(1)}, f32[512,512]{1,0:T(8,128)S(1)}, f32[16,256]{1,0:T(8,128)S(1)}) custom-call(s32[2,13]{1,0:T(2,128)} %bitcast.5, f32[2,14,256,256]{3,2,1,0:T(8,128)} %bitcast.10, f32[2,256]{1,0:T(2,128)} %bitcast.12, f32[8,256]{1,0:T(8,128)S(1)} %get-tuple-element.39.before_ref), custom_call_target="tpu_custom_call" | custom-call | tf_op jit(solution)/shard_map/pallas_call | solution.py:473
  7.0 3.7 %collective-permute-start.5 = (f32[776,512]{1,0:T(8,128)S(1)}, f32[776,512]{1,0:T(8,128)S(1)}, u32[]{:S(2)}, u32[]{:S(2)}) collective-permute-start(f32[776,512]{1,0:T(8,128)S(1)} %get-tuple-element.43.t_ref), channel_id=1, source_target_pairs={{0,24},{8,0},{16,8},{24,16},{1,25},{9,1},{17,9},{25,17},{2,26},{10... | collective-permute-start | bytes 4767752 | tf_op jit(solution)/shard_map/ppermute | solution.py:440
  10.6 2.1 %shard_map.39 = (f32[512,512]{1,0:T(8,128)S(1)}, f32[264,512]{1,0:T(8,128)S(1)}, f32[16,256]{1,0:T(8,128)S(1)}) custom-call(s32[2,13]{1,0:T(2,128)} %bitcast.6, f32[2,14,256,256]{3,2,1,0:T(8,128)} %bitcast.11, f32[16,256]{1,0:T(8,128)S(1)} %get-tuple-element.40.before_ref), custom_call_target="tpu_custom_call" | custom-call | tf_op jit(solution)/shard_map/pallas_call | solution.py:478
  12.8 0.1 collective-permute-start
  12.9 1.5 %collective-permute-done.more_ref = f32[16,256]{1,0:T(8,128)S(1)} collective-permute-done((f32[16,256]{1,0:T(8,128)S(1)}, f32[16,256]{1,0:T(8,128)S(1)}, u32[]{:S(2)}, u32[]{:S(2)}) %collective-permute-start) | collective-permute-done | bytes 16416 | tf_op jit(solution)/shard_map/ppermute | solution.py:445
  14.4 3.9 %shard_map.40 = (f32[16,256]{1,0:T(8,128)S(1)}, f32[776,512]{1,0:T(8,128)S(1)}, f32[1024,512]{1,0:T(8,128)S(1)}, f32[264,512]{1,0:T(8,128)S(1)}) custom-call(f32[264,512]{1,0:T(8,128)S(1)} %get-tuple-element.41._, f32[16,256]{1,0:T(8,128)S(1)} %get-tuple-element.42.sums_ref, f32[16,256]{1,0:T(8,128)S(1)} %collective-permute-done.more_ref, ...), custom_call_target="tpu_custom_call" | custom-call | tf_op jit(solution)/shard_map/pallas_call | solution.py:488
  18.3 0.6 collective-permute-start.1
  18.9 3.4 %collective-permute-done.1.more_ref = f32[16,256]{1,0:T(8,128)S(1)} collective-permute-done((f32[16,256]{1,0:T(8,128)S(1)}, f32[16,256]{1,0:T(8,128)S(1)}, u32[]{:S(2)}, u32[]{:S(2)}) %collective-permute-start.1) | collective-permute-done | bytes 16416 | tf_op jit(solution)/shard_map/ppermute | solution.py:445
  22.3 7.9 %shard_map.41 = (f32[16,256]{1,0:T(8,128)S(1)}, f32[2,14,256,256]{3,2,1,0:T(8,128)}, f32[264,512]{1,0:T(8,128)S(1)}, f32[512,512]{1,0:T(8,128)S(1)}, f32[512,512...) custom-call(f32[776,512]{1,0:T(8,128)S(1)} %get-tuple-element.46._.g0_ref, ...), custom_call_target="tpu_custom_call" | custom-call | tf_op jit(solution)/shard_map/pallas_call | solution.py:492
  30.2 1.4 %collective-permute-start.3 = (f32[16,256]{1,0:T(8,128)S(1)}, f32[16,256]{1,0:T(8,128)S(1)}, u32[]{:S(2)}, u32[]{:S(2)}) collective-permute-start(f32[16,256]{1,0:T(8,128)S(1)} %get-tuple-element.52.sums_ref), channel_id=1, source_target_pairs={{0,2},{1,3},{2,0},{3,1},{4,6},{5,7},{6,4},{7,5},{8,10},{9,11},{10,... | collective-permute-start | bytes 49160 | tf_op jit(solution)/shard_map/ppermute | solution.py:445
  31.6 3.1 %collective-permute-done.2.__.below_ref = f32[1024,512]{1,0:T(8,128)S(1)} collective-permute-done((f32[1024,512]{1,0:T(8,128)S(1)}, f32[1024,512]{1,0:T(8,128)S(1)}, u32[]{:S(2)}, u32[]{:S(2)}) %collective-permute-start.2) | collective-permute-done | bytes 2097184 | tf_op jit(solution)/shard_map/ppermute | solution.py:440
  34.7 0.2 collective-permute-start.7
  34.9 1.7 %shard_map.43 = (f32[8,256]{1,0:T(8,128)S(1)}, f32[776,512]{1,0:T(8,128)S(1)}) custom-call(f32[264,512]{1,0:T(8,128)S(1)} %shard_map.42._, f32[16,256]{1,0:T(8,128)S(1)} %get-tuple-element.52.sums_ref, f32[16,256]{1,0:T(8,128)S(1)} %collective-permute-done.3.more_ref, f32[776,512]{1,0:T(8,128)S(1)} %get-tuple-element.46._.g0_ref, ...), custom_call_target="tpu_custom_call" | custom-call | tf_op jit(solution)/shard_map/pallas_call | solution.py:499
  36.6 1.8 %collective-permute-start.9 = (f32[776,512]{1,0:T(8,128)S(1)}, f32[776,512]{1,0:T(8,128)S(1)}, u32[]{:S(2)}, u32[]{:S(2)}) collective-permute-start(f32[776,512]{1,0:T(8,128)S(1)} %get-tuple-element.54._), channel_id=1, source_target_pairs={{0,8},{8,16},{16,24},{24,0},{1,9},{9,17},{17,25},{25,1},{2,10},{10... | collective-permute-start | bytes 4767752 | tf_op jit(solution)/shard_map/ppermute | solution.py:440
  38.4 7.4 %collective-permute-done.5.tx_ref = f32[776,512]{1,0:T(8,128)S(1)} collective-permute-done((f32[776,512]{1,0:T(8,128)S(1)}, f32[776,512]{1,0:T(8,128)S(1)}, u32[]{:S(2)}, u32[]{:S(2)}) %collective-permute-start.5) | collective-permute-done | bytes 1589280 | tf_op jit(solution)/shard_map/ppermute | solution.py:440
  45.9 0.1 shard_map.44._
  45.9 0.1 collective-permute-start.6
  46.0 2.7 %shard_map.45 = (f32[512,512]{1,0:T(8,128)S(1)}, f32[512,512]{1,0:T(8,128)S(1)}) custom-call(f32[528,512]{1,0:T(8,128)S(1)} %shard_map.44._, f32[264,512]{1,0:T(8,128)S(1)} %collective-permute-done.7.__.yc_in_ref, f32[1024,512]{1,0:T(8,128)S(1)} %get-tuple-element.56.r0_ref, f32[1024,512]{1,0:T(8,128)S(1)} %collective-permute-done.2.__.below_ref, ...), custom_call_target="tpu_custom_call" | custom-call | tf_op jit(solution)/shard_map/pallas_call | solution.py:503
  48.7 0.5 collective-permute-start.8
  49.3 0.1 collective-permute-start.12
  49.4 3.4 %shard_map.46 = (f32[512,512]{1,0:T(8,128)S(1)}, f32[512,512]{1,0:T(8,128)S(1)}, f32[512,512]{1,0:T(8,128)S(1)}) custom-call(f32[512,512]{1,0:T(8,128)S(1)} %get-tuple-element.57._, f32[776,512]{1,0:T(8,128)S(1)} %get-tuple-element.43.t_ref, f32[1024,512]{1,0:T(8,128)S(1)} %get-tuple-element.44.down_ref.e_ref, f32[512,512]{1,0:T(8,128)S(1)} %get-tuple-element.45.d_ref, ...), custom_call_target="tpu_custom_call" | custom-call | tf_op jit(solution)/shard_map/pallas_call | solution.py:505
  52.8 2.7 %shard_map.47 = (f32[512,512]{1,0:T(8,128)S(1)}, f32[512,512]{1,0:T(8,128)S(1)}) custom-call(f32[512,512]{1,0:T(8,128)S(1)} %get-tuple-element.61._.yn0_ref, f32[1024,512]{1,0:T(8,128)S(1)} %get-tuple-element.44.down_ref.e_ref, f32[512,512]{1,0:T(8,128)S(1)} %get-tuple-element.45.d_ref, f32[776,512]{1,0:T(8,128)S(1)} %collective-permute-done.5.tx_ref, ...), custom_call_target="tpu_custom_call" | custom-call | tf_op jit(solution)/shard_map/pallas_call | solution.py:506
  55.5 12.0 %collective-permute-done.6.both_ref = f32[528,512]{1,0:T(8,128)S(1)} collective-permute-done((f32[528,512]{1,0:T(8,128)S(1)}, f32[528,512]{1,0:T(8,128)S(1)}, u32[]{:S(2)}, u32[]{:S(2)}) %collective-permute-start.6) | collective-permute-done | bytes 1081376 | tf_op jit(solution)/shard_map/ppermute | solution.py:440
  67.6 1.9 %shard_map.48 = (f32[8,256]{1,0:T(8,128)S(1)}, f32[512,512]{1,0:T(8,128)S(1)}, f32[512,512]{1,0:T(8,128)S(1)}) custom-call(f32[8,256]{1,0:T(8,128)S(1)} %get-tuple-element.53.sums_ref, f32[776,512]{1,0:T(8,128)S(1)} %get-tuple-element.43.t_ref, f32[512,512]{1,0:T(8,128)S(1)} %get-tuple-element.45.d_ref, f32[528,512]{1,0:T(8,128)S(1)} %collective-permute-done.6.both_ref, ...), custom_call_target="tpu_custom_call" | custom-call | tf_op jit(solution)/shard_map/pallas_call | solution.py:507
  69.5 1.5 %collective-permute-start.11 = (f32[8,256]{1,0:T(8,128)S(1)}, f32[8,256]{1,0:T(8,128)S(1)}, u32[]{:S(2)}, u32[]{:S(2)}) collective-permute-start(f32[8,256]{1,0:T(8,128)S(1)} %get-tuple-element.68.rest_0_), channel_id=1, source_target_pairs={{0,16},{8,24},{16,0},{24,8},{1,17},{9,25},{17,1},{25,9},{2,18},{10... | collective-permute-start | bytes 24584 | tf_op jit(solution)/shard_map/ppermute | solution.py:440
  71.0 2.9 %collective-permute-start.10 = (f32[8,256]{1,0:T(8,128)S(1)}, f32[8,256]{1,0:T(8,128)S(1)}, u32[]{:S(2)}, u32[]{:S(2)}) collective-permute-start(f32[8,256]{1,0:T(8,128)S(1)} %get-tuple-element.68.rest_0_), channel_id=1, source_target_pairs={{0,24},{8,0},{16,8},{24,16},{1,25},{9,1},{17,9},{25,17},{2,26},{10... | collective-permute-start | bytes 24584 | tf_op jit(solution)/shard_map/ppermute | solution.py:440
  74.0 4.9 %collective-permute-done.11.rest_2_ = f32[8,256]{1,0:T(8,128)S(1)} collective-permute-done((f32[8,256]{1,0:T(8,128)S(1)}, f32[8,256]{1,0:T(8,128)S(1)}, u32[]{:S(2)}, u32[]{:S(2)}) %collective-permute-start.11) | collective-permute-done | bytes 8224 | tf_op jit(solution)/shard_map/ppermute | solution.py:440
  78.9 3.0 %shard_map.49 = (f32[2,14,256,256]{3,2,1,0:T(8,128)}, f32[8,256]{1,0:T(8,128)S(1)}) custom-call(s32[2,13]{1,0:T(2,128)S(1)} %bitcast.7, f32[2,14,256,256]{3,2,1,0:T(8,128)} %get-tuple-element.49._, f32[512,512]{1,0:T(8,128)S(1)} %get-tuple-element.48.c_ref, f32[776,512]{1,0:T(8,128)S(1)} %get-tuple-element.43.t_ref, ...), custom_call_target="tpu_custom_call", output_to_operand_aliasing={{0}: (1, {})} | custom-call | tf_op jit(solution)/shard_map/pallas_call | solution.py:511
  81.9 0.2 collective-permute-done.12.re_ref
  82.0 1.6 %shard_map.50 = f32[2,14,256,256]{3,2,1,0:T(8,128)} custom-call(s32[2,13]{1,0:T(2,128)S(1)} %bitcast.8, f32[2,14,256,256]{3,2,1,0:T(8,128)} %get-tuple-element.69._, f32[8,256]{1,0:T(8,128)S(1)} %get-tuple-element.70.twice_ref, f32[1024,512]{1,0:T(8,128)S(1)} %get-tuple-element.44.down_ref.e_ref, ...), custom_call_target="tpu_custom_call", output_to_operand_aliasing={{}: (1, {})} | custom-call | tf_op jit(solution)/shard_map/pallas_call | solution.py:515
  (10 shorter events, 0.1 us)
Async XLA Ops:
  1.7 32.9 %collective-permute-start.2 = (f32[1024,512]{1,0:T(8,128)S(1)}, f32[1024,512]{1,0:T(8,128)S(1)}, u32[]{:S(2)}, u32[]{:S(2)}) collective-permute-start(f32[1024,512]{1,0:T(8,128)S(1)} %get-tuple-element.44.down_ref.e_ref), channel_id=1, source_target_pairs={{0,7},{1,0},{2,1},{3,2},{4,3},{5,4},{6,5},{7,6},{8,15},{9,8},{10,9... | collective-permute-start | bytes 6291464 | tf_op jit(solution)/shard_map/ppermute | solution.py:440
  7.0 38.9 %collective-permute-start.5 = (f32[776,512]{1,0:T(8,128)S(1)}, f32[776,512]{1,0:T(8,128)S(1)}, u32[]{:S(2)}, u32[]{:S(2)}) collective-permute-start(f32[776,512]{1,0:T(8,128)S(1)} %get-tuple-element.43.t_ref), channel_id=1, source_target_pairs={{0,24},{8,0},{16,8},{24,16},{1,25},{9,1},{17,9},{25,17},{2,26},{10... | collective-permute-start | bytes 4767752 | tf_op jit(solution)/shard_map/ppermute | solution.py:440
  12.7 22.2 %collective-permute-start.4 = (f32[264,512]{1,0:T(8,128)S(1)}, f32[264,512]{1,0:T(8,128)S(1)}, u32[]{:S(2)}, u32[]{:S(2)}) collective-permute-start(f32[264,512]{1,0:T(8,128)S(1)} %get-tuple-element.41._), channel_id=1, source_target_pairs={{0,1},{1,2},{2,3},{3,4},{4,5},{5,6},{6,7},{7,0},{8,9},{9,10},{10,1... | collective-permute-start | bytes 1622024 | tf_op jit(solution)/shard_map/ppermute | solution.py:440
  12.8 1.6 %collective-permute-start = (f32[16,256]{1,0:T(8,128)S(1)}, f32[16,256]{1,0:T(8,128)S(1)}, u32[]{:S(2)}, u32[]{:S(2)}) collective-permute-start(f32[16,256]{1,0:T(8,128)S(1)} %get-tuple-element.42.sums_ref), channel_id=1, source_target_pairs={{0,1},{1,0},{2,3},{3,2},{4,5},{5,4},{6,7},{7,6},{8,9},{9,8},{10,11... | collective-permute-start | bytes 49160 | tf_op jit(solution)/shard_map/ppermute | solution.py:445
  18.3 4.0 %collective-permute-start.1 = (f32[16,256]{1,0:T(8,128)S(1)}, f32[16,256]{1,0:T(8,128)S(1)}, u32[]{:S(2)}, u32[]{:S(2)}) collective-permute-start(f32[16,256]{1,0:T(8,128)S(1)} %get-tuple-element.47.sums_ref), channel_id=1, source_target_pairs={{0,4},{1,5},{2,6},{3,7},{4,0},{5,1},{6,2},{7,3},{8,12},{9,13},{10,... | collective-permute-start | bytes 49160 | tf_op jit(solution)/shard_map/ppermute | solution.py:445
  30.2 4.7 %collective-permute-start.3 = (f32[16,256]{1,0:T(8,128)S(1)}, f32[16,256]{1,0:T(8,128)S(1)}, u32[]{:S(2)}, u32[]{:S(2)}) collective-permute-start(f32[16,256]{1,0:T(8,128)S(1)} %get-tuple-element.52.sums_ref), channel_id=1, source_target_pairs={{0,2},{1,3},{2,0},{3,1},{4,6},{5,7},{6,4},{7,5},{8,10},{9,11},{10,... | collective-permute-start | bytes 49160 | tf_op jit(solution)/shard_map/ppermute | solution.py:445
  34.7 11.3 %collective-permute-start.7 = (f32[264,512]{1,0:T(8,128)S(1)}, f32[264,512]{1,0:T(8,128)S(1)}, u32[]{:S(2)}, u32[]{:S(2)}) collective-permute-start(f32[264,512]{1,0:T(8,128)S(1)} %shard_map.42._), channel_id=1, source_target_pairs={{0,1},{1,2},{2,3},{3,4},{4,5},{5,6},{6,7},{7,0},{8,9},{9,10},{10,1... | collective-permute-start | bytes 1622024 | tf_op jit(solution)/shard_map/ppermute | solution.py:440
  36.6 42.2 %collective-permute-start.9 = (f32[776,512]{1,0:T(8,128)S(1)}, f32[776,512]{1,0:T(8,128)S(1)}, u32[]{:S(2)}, u32[]{:S(2)}) collective-permute-start(f32[776,512]{1,0:T(8,128)S(1)} %get-tuple-element.54._), channel_id=1, source_target_pairs={{0,8},{8,16},{16,24},{24,0},{1,9},{9,17},{17,25},{25,1},{2,10},{10... | collective-permute-start | bytes 4767752 | tf_op jit(solution)/shard_map/ppermute | solution.py:440
  45.9 21.6 %collective-permute-start.6 = (f32[528,512]{1,0:T(8,128)S(1)}, f32[528,512]{1,0:T(8,128)S(1)}, u32[]{:S(2)}, u32[]{:S(2)}) collective-permute-start(f32[528,512]{1,0:T(8,128)S(1)} %shard_map.44._), channel_id=1, source_target_pairs={{0,7},{1,0},{2,1},{3,2},{4,3},{5,4},{6,5},{7,6},{8,15},{9,8},{10,9... | collective-permute-start | bytes 3244040 | tf_op jit(solution)/shard_map/ppermute | solution.py:440
  48.7 30.1 %collective-permute-start.8 = (f32[512,512]{1,0:T(8,128)S(1)}, f32[512,512]{1,0:T(8,128)S(1)}, u32[]{:S(2)}, u32[]{:S(2)}) collective-permute-start(f32[512,512]{1,0:T(8,128)S(1)} %get-tuple-element.57._), channel_id=1, source_target_pairs={{0,1},{1,2},{2,3},{3,4},{4,5},{5,6},{6,7},{7,0},{8,9},{9,10},{10,1... | collective-permute-start | bytes 3145736 | tf_op jit(solution)/shard_map/ppermute | solution.py:440
  49.3 32.7 %collective-permute-start.12 = (f32[512,512]{1,0:T(8,128)S(1)}, f32[512,512]{1,0:T(8,128)S(1)}, u32[]{:S(2)}, u32[]{:S(2)}) collective-permute-start(f32[512,512]{1,0:T(8,128)S(1)} %get-tuple-element.72), channel_id=1, source_target_pairs={{0,1},{1,2},{2,3},{3,4},{4,5},{5,6},{6,7},{7,0},{8,9},{9,10},{10,1... | collective-permute-start | bytes 3145736 | tf_op jit(solution)/shard_map/ppermute | solution.py:440
  67.6 11.3 %copy-start = (s32[1,1,2,13]{3,2,1,0:T(2,128)S(1)}, s32[1,1,2,13]{3,2,1,0:T(2,128)}, u32[]{:S(2)}) copy-start(s32[1,1,2,13]{3,2,1,0:T(2,128)} %param.5) | copy-start | bytes 316
  69.5 9.3 %collective-permute-start.11 = (f32[8,256]{1,0:T(8,128)S(1)}, f32[8,256]{1,0:T(8,128)S(1)}, u32[]{:S(2)}, u32[]{:S(2)}) collective-permute-start(f32[8,256]{1,0:T(8,128)S(1)} %get-tuple-element.68.rest_0_), channel_id=1, source_target_pairs={{0,16},{8,24},{16,0},{24,8},{1,17},{9,25},{17,1},{25,9},{2,18},{10... | collective-permute-start | bytes 24584 | tf_op jit(solution)/shard_map/ppermute | solution.py:440
  71.0 7.8 %collective-permute-start.10 = (f32[8,256]{1,0:T(8,128)S(1)}, f32[8,256]{1,0:T(8,128)S(1)}, u32[]{:S(2)}, u32[]{:S(2)}) collective-permute-start(f32[8,256]{1,0:T(8,128)S(1)} %get-tuple-element.68.rest_0_), channel_id=1, source_target_pairs={{0,24},{8,0},{16,8},{24,16},{1,25},{9,1},{17,9},{25,17},{2,26},{10... | collective-permute-start | bytes 24584 | tf_op jit(solution)/shard_map/ppermute | solution.py:440

commit v7 on v6

--- a/solution.py
+++ b/solution.py
@@ -148,15 +148,27 @@
     return mask_ref[layer, slot - 1] > 0
 
 
-def load_panel(out_ref, held, first, name, layers, size, mask_ref, top=0):
-    if layers > 2:
-        out_ref[top : top + layers * size, :] = jnp.zeros((layers * size, layers * size), F32)
-    squares = 0.0
+def start_panel(stored_ref, out_ref, sems, first, name, layers, size, top=0):
+    copies = []
     for k, (low, high, slot) in enumerate(panel_blocks(name, layers)):
-        value = jnp.where(kept(mask_ref, low, slot), held[first + k], 0.0)
-        out_ref[top + low * size : top + (low + 1) * size, high * size : (high + 1) * size] = value
-        squares = squares + squares_of(value)
-    return squares
+        place = out_ref.at[pl.ds(top + low * size, size), pl.ds(high * size, size)]
+        copies.append(pltpu.make_async_copy(stored_ref.at[low, slot], place, sems.at[first + k]))
+        copies[-1].start()
+    return copies
+
+
+def end_panel(copies, out_ref, name, layers, size, mask_ref, top=0):
+    blocks = panel_blocks(name, layers)
+    for low in range(layers):
+        for high in range(layers):
+            if (low, high) not in [block[:2] for block in blocks]:
+                out_ref[top + low * size : top + (low + 1) * size, high * size : (high + 1) * size] = jnp.zeros((size, size), F32)
+    for copy, (low, high, slot) in zip(copies, blocks, strict=True):
+        copy.wait()
+
+        @pl.when(jnp.logical_not(kept(mask_ref, low, slot)))
+        def _(low=low, high=high):
+            out_ref[top + low * size : top + (low + 1) * size, high * size : (high + 1) * size] = jnp.zeros((size, size), F32)
 
 
 def start_loads(stored_ref, held, sems, wanted):
@@ -183,27 +195,18 @@
     ]
 
 
-def pack_e_body(layers, size, mask_ref, stored_ref, down_ref, sums_ref, held, sems, mask, mask_sem):
+def pack_e_body(layers, size, mask_ref, stored_ref, down_ref, sems, mask, mask_sem):
     n = layers * size
     small = pltpu.make_async_copy(mask_ref, mask, mask_sem)
     small.start()
-    copies = start_loads(stored_ref, held, sems, wanted("SE", layers))
+    first = start_panel(stored_ref, down_ref, sems, 0, "S", layers, size)
+    second = start_panel(stored_ref, down_ref, sems, len(first), "E", layers, size, top=n)
     small.wait()
-    at = 0
-    squares = 0.0
-    for name, top in (("S", 0), ("E", n)):
-        count = len(panel_blocks(name, layers))
-        for copy in copies[at : at + count]:
-            copy.wait()
-        squares = squares + load_panel(down_ref, held, at, name, layers, size, mask, top=top)
-        at += count
-    sums_ref[...] = 2.0 * squares
-
-
-def pack_t_body(
-    layers, size, mask_ref, stored_ref, onsite_ref, before_ref, t_ref, packed_ref, c_ref, sums_ref,
-    held, sems, mask, mask_sem, onsite, onsite_sem,
-):
+    end_panel(first, down_ref, "S", layers, size, mask)
+    end_panel(second, down_ref, "E", layers, size, mask, top=n)
+
+
+def pack_t_body(layers, size, mask_ref, stored_ref, onsite_ref, _, t_ref, held, sems, mask, mask_sem, onsite, onsite_sem):
     n = layers * size
     small = [
         pltpu.make_async_copy(mask_ref, mask, mask_sem),
@@ -211,54 +214,52 @@
     ]
     for copy in small:
         copy.start()
-    copies = start_loads(stored_ref, held, sems, wanted("CN", layers))
+    copies = start_loads(stored_ref, held, sems, wanted("C", layers))
+    panel = start_panel(stored_ref, t_ref, sems, len(copies), "N", layers, size)
     for copy in small:
         copy.wait()
     row, col = rows_cols(size)
-    if layers > 2:
-        c_ref[...] = jnp.zeros(c_ref.shape, F32)
-    trace = squares = 0.0
+    blocks = {}
     for layer in range(layers):
         copies[layer].wait()
         block = held[layer]
-        diagonal = jnp.where(row == col, onsite[layer : layer + 1, :], 0.0)
-        trace = trace + lanes(jnp.where(row == col, block, 0.0) + diagonal)
-        block = 0.5 * (block + block.T) + diagonal
-        squares = squares + squares_of(block)
-        c_ref[layer * size : (layer + 1) * size, layer * size : (layer + 1) * size] = block
-    at = layers
-    for low, high, slot in panel_blocks("C", layers):
-        copies[at].wait()
-        block = jnp.where(kept(mask, low, slot), held[at], 0.0)
-        squares = squares + 2.0 * squares_of(block)
-        c_ref[low * size : (low + 1) * size, high * size : (high + 1) * size] = block
-        c_ref[high * size : (high + 1) * size, low * size : (low + 1) * size] = block.T
-        at += 1
-    put_sym(
-        packed_ref,
-        lambda a, b: c_ref[a * size : (a + 1) * size, b * size : (b + 1) * size],
-        layers,
-        size,
-    )
-    t_ref[n:, :] = packed_ref[...]
-    for copy in copies[at:]:
-        copy.wait()
-    sums_ref[:8, :] = trace
-    squares = squares + 2.0 * load_panel(t_ref, held, at, "N", layers, size, mask)
-    sums_ref[8:, :] = before_ref[...] + squares
-
-
-def pack_d_body(layers, size, mask_ref, stored_ref, before_ref, d_ref, up_ref, sums_ref, held, sems, mask, mask_sem):
+        blocks[layer, layer] = 0.5 * (block + block.T) + jnp.where(row == col, onsite[layer : layer + 1, :], 0.0)
+    for k, (low, high, slot) in enumerate(panel_blocks("C", layers), start=layers):
+        copies[k].wait()
+        blocks[low, high] = jnp.where(kept(mask, low, slot), held[k], 0.0)
+    put_sym(t_ref, lambda a, b: blocks.get((a, b), jnp.zeros((size, size), F32)), layers, size, first=n)
+    end_panel(panel, t_ref, "N", layers, size, mask)
+
+
+def pack_d_body(layers, size, mask_ref, stored_ref, _, d_ref, up_ref, sems, mask, mask_sem):
     small = pltpu.make_async_copy(mask_ref, mask, mask_sem)
     small.start()
-    copies = start_loads(stored_ref, held, sems, wanted("D", layers))
+    copies = start_panel(stored_ref, d_ref, sems, 0, "D", layers, size)
     small.wait()
-    for copy in copies:
-        copy.wait()
-    sums_ref[:8, :] = before_ref[:8, :]
-    sums_ref[8:, :] = before_ref[8:, :] + 2.0 * load_panel(d_ref, held, 0, "D", layers, size, mask)
+    end_panel(copies, d_ref, "D", layers, size, mask)
     blocks = sym_product(split(d_ref[...]), layers, size, TN)
     put_sym(up_ref, lambda a, b: blocks[a, b], layers, size)
+
+
+def sums_body(layers, size, mask_ref, _, down_ref, t_ref, d_ref, packed_ref, c_ref, keep_ref, sums_ref):
+    n = layers * size
+    packed_ref[...] = t_ref[n:, :]
+    c_ref[...] = whole_sym(take_sym(t_ref[n:, :], layers, size), layers)
+    keep_ref[...] = jnp.zeros(keep_ref.shape, F32)
+    slots = keep_ref.shape[0] // layers
+    for low, slot in wanted(IN_PLANE, layers):
+        here = 1.0 if slot == 0 else jnp.where(kept(mask_ref, low, slot), 1.0, 0.0)
+        keep_ref[low * slots + slot : low * slots + slot + 1, :] = jnp.full((1, size), here, F32)
+    row, col = rows_cols(size)
+    trace = 0.0
+    for layer in range(layers):
+        here = slice(layer * size, (layer + 1) * size)
+        trace = trace + lanes(jnp.where(row == col, c_ref[here, here], 0.0))
+    sums_ref[:8, :] = trace
+    squares = squares_of(c_ref[...])
+    for ref in (down_ref.at[:n, :], down_ref.at[n:, :], t_ref.at[:n, :], d_ref):
+        squares = squares + 2.0 * squares_of(ref[...])
+    sums_ref[8:, :] = sum(squares[:, at * size : (at + 1) * size] for at in range(layers))
 
 
 def local_g_body(layers, size, _, sums_ref, more_ref, t_ref, down_ref, d_ref, total_ref, g_ref, r_ref, yc_up_ref):
@@ -323,17 +324,12 @@
         g_ref[last:, cols] = jnp.where(line < 4, g_ref[last:, cols], total)
 
 
-def both_body(layers, size, _, packed_ref, tx_ref, both_ref):
-    n, tall = layers * size, sym_rows(layers, size)
-    both_ref[:tall, :] = packed_ref[...]
-    both_ref[tall:, :] = tx_ref[n:, :]
-
-
-def early_body(layers, size, _, t_ref, e_ref, d_ref, below_ref, yn0_ref, ye0_ref, yd0_ref, yn_ref, ye_ref, yd_ref):
+def early_body(layers, size, _, t_ref, e_ref, d_ref, below_ref, cu_ref, yn0_ref, ye0_ref, yd0_ref, yn_ref, ye_ref, yd_ref):
     at = layers * size
     n, e, d = split(t_ref[:at, :]), split(e_ref[at:, :]), split(d_ref[...])
     su, eu = split(below_ref[:at, :]), split(below_ref[at:, :])
-    yn_ref[...] = yn0_ref[...] + dot3(e, su, NT) + dot3(d, eu, NT)
+    cu = split(whole_sym(take_sym(cu_ref, layers, size), layers))
+    yn_ref[...] = yn0_ref[...] + dot3(e, su, NT) + dot3(d, eu, NT) + dot3(n, cu, NN)
     ye_ref[...] = ye0_ref[...] + dot3(n, su, NN)
     yd_ref[...] = yd0_ref[...] + dot3(n, eu, NN)
 
@@ -346,6 +342,10 @@
     re_ref[...] = r0_ref[n:, :] + dot3(su, nx, NN)
 
 
+def hand_body(layers, size, _, __, tx_ref, cx_ref):
+    cx_ref[...] = tx_ref[layers * size :, :]
+
+
 def middle_body(layers, size, _, e_ref, d_ref, tx_ref, ye0_ref, yd0_ref, ye_ref, yd_ref):
     at = layers * size
     e, d, nx = split(e_ref[at:, :]), split(d_ref[...]), split(tx_ref[:at, :])
@@ -354,14 +354,10 @@
     yd_ref[...] = yd0_ref[...] + dot3(e, nx, NN)
 
 
-def middle_c_body(layers, size, sums_ref, t_ref, d_ref, both_ref, yn0_ref, yd0_ref, total_ref, yn_ref, yd_ref):
-    at, tall = layers * size, sym_rows(layers, size)
+def middle_c_body(layers, size, _, sums_ref, d_ref, cxu_ref, yd0_ref, total_ref, yd_ref):
     total_ref[...] = sums_ref[...]
-    n, d = split(t_ref[:at, :]), split(d_ref[...])
-    cu = split(whole_sym(take_sym(both_ref[:tall, :], layers, size), layers))
-    cxu = split(whole_sym(take_sym(both_ref[tall:, :], layers, size), layers))
-    yn_ref[...] = yn0_ref[...] + dot3(n, cu, NN)
-    yd_ref[...] = yd0_ref[...] + dot3(d, cxu, NN)
+    cxu = split(whole_sym(take_sym(cxu_ref, layers, size), layers))
+    yd_ref[...] = yd0_ref[...] + dot3(split(d_ref[...]), cxu, NN)
 
 
 def twice_h(target, size, sums):
@@ -370,21 +366,20 @@
 
 
 class Sender:
-    def __init__(self, mask_ref, out_ref, held, sems):
-        self.mask_ref, self.out_ref, self.held, self.sems = mask_ref, out_ref, held, sems
+    def __init__(self, twice, keep_ref, out_ref, held, sems):
+        self.twice, self.keep_ref, self.out_ref, self.held, self.sems = twice, keep_ref, out_ref, held, sems
         self.copies = []
 
-    def send(self, value, low, slot):
-        k = len(self.copies)
-        self.held[k] = jnp.where(kept(self.mask_ref, low, slot), value, 0.0) if slot else value
+    def send(self, y, a, low, slot):
+        k, at = len(self.copies), low * self.out_ref.shape[1] + slot
+        self.held[k] = self.keep_ref[at : at + 1, :] * (y + self.twice * (a - y))
         self.copies.append(pltpu.make_async_copy(self.held.at[k], self.out_ref.at[low, slot], self.sems.at[k]))
         self.copies[-1].start()
 
-    def send_panel(self, name, twice, a_ref, terms, layers, size):
+    def send_panel(self, name, a_ref, terms, layers, size):
         for low, high, slot in panel_blocks(name, layers):
             rows, cols = slice(low * size, (low + 1) * size), slice(high * size, (high + 1) * size)
-            y = sum(ref[rows, cols] for ref in terms)
-            self.send(y + twice * (a_ref[rows, cols] - y), low, slot)
+            self.send(sum(ref[rows, cols] for ref in terms), a_ref[rows, cols], low, slot)
 
     def wait(self):
         for copy in self.copies:
@@ -392,8 +387,7 @@
 
 
 def last_c_body(
-    target, layers, size, mask_ref, _, c_ref, t_ref, down_ref, d_ref, yc_ref, yn_ref, ys_ref, yd_ref, yc_in_ref, rs_ref, g_ref,
-    *rest,
+    target, layers, size, keep_ref, _, c_ref, t_ref, s_ref, d_ref, yc_ref, yn_ref, ys_ref, yd_ref, yc_in_ref, rs_ref, g_ref, *rest
 ):
     *sums_refs, out_ref, twice_ref, held, sems = rest
     n, last = layers * size, g_ref.shape[0] - 8
@@ -402,24 +396,20 @@
     sums = jnp.where(line == 0, beside[4:5, :], beside[5:6, :])
     twice = twice_h(target, size, sum((ref[...] for ref in sums_refs), start=sums))
     twice_ref[...] = jnp.broadcast_to(twice, twice_ref.shape)
-    sender = Sender(mask_ref, out_ref, held, sems)
-    for name, a_ref, *terms in (
-        ("D", d_ref, yd_ref),
-        ("N", t_ref.at[:n, :], yn_ref, g_ref),
-        ("S", down_ref.at[:n, :], ys_ref, rs_ref),
-    ):
-        sender.send_panel(name, twice, a_ref, terms, layers, size)
+    sender = Sender(twice, keep_ref, out_ref, held, sems)
+    sender.send_panel("D", d_ref, [yd_ref], layers, size)
+    sender.send_panel("S", s_ref, [ys_ref, rs_ref], layers, size)
+    sender.send_panel("N", t_ref, [yn_ref, g_ref], layers, size)
     blocks = take_sym(yc_ref[...] + yc_in_ref[...] + g_ref[n:, :], layers, size)
     for low, high, slot in panel_blocks("C", layers) + [(layer, layer, 0) for layer in range(layers)]:
         rows, cols = slice(low * size, (low + 1) * size), slice(high * size, (high + 1) * size)
-        y = blocks[low, high]
-        sender.send(y + twice * (c_ref[rows, cols] - y), low, slot)
+        sender.send(blocks[low, high], c_ref[rows, cols], low, slot)
     sender.wait()
 
 
-def last_e_body(layers, size, mask_ref, _, twice_ref, down_ref, ye_ref, re_ref, out_ref, held, sems):
-    sender = Sender(mask_ref, out_ref, held, sems)
-    sender.send_panel("E", twice_ref[0:1, :], down_ref.at[layers * size :, :], [ye_ref, re_ref], layers, size)
+def last_e_body(layers, size, keep_ref, _, twice_ref, down_ref, ye_ref, re_ref, out_ref, held, sems):
+    sender = Sender(twice_ref[0:1, :], keep_ref, out_ref, held, sems)
+    sender.send_panel("E", down_ref.at[layers * size :, :], [ye_ref, re_ref], layers, size)
     sender.wait()
 
 
@@ -466,19 +456,24 @@
         return swapped(value, "col", bits.pop(0)) if bits else jnp.zeros_like(value)
 
     small = [pltpu.SMEM(mask.shape, mask.dtype), pltpu.SemaphoreType.DMA]
-    down, own = go(
-        pack_e_body, outs=[(2 * n, n), total], spaces=[hbm] * 2, scratch=blocks(len(wanted("SE", layers))) + small
+    count = {name: len(wanted(name, layers)) for name in IN_PLANE}
+    (down,) = go(
+        pack_e_body, outs=[(2 * n, n)], spaces=[hbm] * 2, scratch=[pltpu.SemaphoreType.DMA((count["S"] + count["E"],))] + small
     )(mask_hbm, stored)
     below = passed_along(down, "col", -1)
-    T, Cp, C, own = go(
-        pack_t_body, outs=[(n + tall, n), packed, panel, sums], spaces=[hbm] * 3 + [vmem],
-        scratch=blocks(len(wanted("CN", layers))) + small + [pltpu.VMEM(onsite.shape, F32), pltpu.SemaphoreType.DMA],
-    )(mask_hbm, stored, onsite, own)
+    (T,) = go(
+        pack_t_body, outs=[(n + tall, n)], spaces=[hbm] * 4,
+        scratch=[pltpu.VMEM((count["C"], size, size), F32), pltpu.SemaphoreType.DMA((count["C"] + count["N"],))]
+        + small + [pltpu.VMEM(onsite.shape, F32), pltpu.SemaphoreType.DMA],
+    )(mask_hbm, stored, onsite, down)
     T_x = passed_along(T, "row", -1)
-    D, gc, own = go(
-        pack_d_body, outs=[panel, packed, sums], spaces=[hbm] * 2 + [vmem], scratch=blocks(len(wanted("D", layers))) + small
-    )(mask_hbm, stored, own)
+    D, gc = go(
+        pack_d_body, outs=[panel, packed], spaces=[hbm] * 3, scratch=[pltpu.SemaphoreType.DMA((count["D"],))] + small
+    )(mask_hbm, stored, T)
     gc_in = passed_along(gc, "col", 1)
+    Cp, C, keep, own = go(sums_body, outs=[packed, panel, (layers * slots, size), sums], spaces=[smem, hbm] + [vmem] * 3)(
+        mask, gc, down, T, D
+    )
     if peers.bit_count() > 1:
         own = own + sum(passed_along(own, "col", by) for by in range(1, peers))
         bits = []
@@ -498,24 +493,25 @@
     yc_in = passed_along(yc_up, "col", 1)
     own, g = go(g_body, outs=[total, (n + tall, n)], spaces=[hbm] + [vmem] * 5)(yc_up, own, more, g0, below, gc_in)
     g_in = passed_along(g, "row", 1)
-    (both,) = go(both_body, outs=[(2 * tall, n)], spaces=[hbm] + [vmem] * 2)(g, Cp, T_x)
-    both_u = passed_along(both, "col", -1)
-    rs, re = go(r_body, outs=[panel, panel], spaces=[hbm] * 2 + [vmem] * 3)(both, yc_in, r0, below, T_x)
+    Cp_u = passed_along(Cp, "col", -1)
+    rs, re = go(r_body, outs=[panel, panel], spaces=[hbm] * 2 + [vmem] * 3)(g, yc_in, r0, below, T_x)
     rs_in, re_in = passed_along(rs, "col", 1), passed_along(re, "col", 1)
-    yn, ye, yd = go(early_body, outs=[panel] * 3, spaces=[hbm] + [vmem] * 7)(rs, T, down, D, below, yn, ye, yd)
-    ye, yd = go(middle_body, outs=[panel] * 2, spaces=[hbm] + [vmem] * 5)(yn, down, D, T_x, ye, yd)
-    own, yn, yd = go(middle_c_body, outs=[total, panel, panel], spaces=[vmem] * 6)(own, T, D, both_u, yn, yd)
+    (Cp_x,) = go(hand_body, outs=[packed], spaces=[hbm] * 2 + [vmem])(rs, Cp_u, T_x)
+    Cp_xu = passed_along(Cp_x, "col", -1)
+    yn, ye, yd = go(early_body, outs=[panel] * 3, spaces=[hbm] + [vmem] * 8)(Cp_x, T, down, D, below, Cp_u, yn, ye, yd)
+    ye, yd = go(middle_body, outs=[panel, panel], spaces=[hbm] + [vmem] * 5)(yn, down, D, T_x, ye, yd)
+    own, yd = go(middle_c_body, outs=[total, panel], spaces=[hbm] + [vmem] * 4)(ye, own, D, Cp_xu, yd)
     every = [own] + [passed_along(own, "row", -by) for by in range(1, lax.axis_size("row") - 1)]
     cells = lax.axis_size("row") * lax.axis_size("col") * layers
     target = float(cells * size // 2)
     out, twice = go(
         functools.partial(last_c_body, target), outs=[out.shape, total], out_spaces=[hbm, vmem],
-        spaces=[smem, hbm] + [vmem] * (11 + len(every)), scratch=blocks(len(wanted("CNSD", layers))), aliases={1: 0},
-    )(mask, out, C, T, down, D, yc, yn, ys, yd, yc_in, rs_in, g_in, *every)
+        spaces=[vmem, hbm] + [vmem] * (11 + len(every)), scratch=blocks(len(wanted("CNSD", layers))), aliases={1: 0},
+    )(keep, out, C, T, down, D, yc, yn, ys, yd, yc_in, rs_in, g_in, *every)
     (out,) = go(
-        last_e_body, outs=[out.shape], out_spaces=[hbm], spaces=[smem, hbm] + [vmem] * 4,
-        scratch=blocks(len(wanted("E", layers))), aliases={1: 0},
-    )(mask, out, twice, down, ye, re_in)
+        last_e_body, outs=[out.shape], out_spaces=[hbm], spaces=[vmem, hbm] + [vmem] * 4,
+        scratch=blocks(count["E"]), aliases={1: 0},
+    )(keep, out, twice, down, ye, re_in)
     return out[None, None]
 
 

time: 84 us -> 82.6 us (0.983)
  waiting for transfers between devices: 32.5 us -> 25.1 us
  starting transfers between devices: 16.3 us -> 22.6 us
    ppermute x10 -> x11, waiting for transfers between devices: 27.6 us -> 20.9 us  [passed_along(): lax.ppermute(value, axis, [(i, (i + by) % peers) for i in range(peers)])]
    ppermute x10 -> x11, starting transfers between devices: 14.2 us -> 19.8 us  [passed_along(): lax.ppermute(value, axis, [(i, (i + by) % peers) for i in range(peers)])]
    pallas_call x8 -> x9, Pallas kernels: 15.5 us -> 15.5 us  [the longest x1 4.27 us: shards(): go(early_body, outs=[panel] * 3, spaces=[hbm] + [vmem] * 8)]
  transfers between devices with their start and end apart: 13 -> 14, of which waited for: 7 -> 7; matrix products, arithmetic and copies ran while one was open for 0% -> 0% of each run, Pallas kernels for 38% -> 38%
where the time goes in v7:
time: 82.6 us; the launch traced here: 82.2 us
  Pallas kernels  34.2 us (41%)
  waiting for transfers between devices  25.1 us (30%)
  starting transfers between devices  22.6 us (27%)
    ppermute x11, waiting for transfers between devices, passed_along(): lax.ppermute(value, axis, [(i, (i + by) % peers) for i in range(peers)])  20.9 us
    ppermute x11, starting transfers between devices, passed_along(): lax.ppermute(value, axis, [(i, (i + by) % peers) for i in range(peers)])  19.8 us
    pallas_call x1, Pallas kernels, shards(): go(local_y_body, outs=[sums, (layers, slots, size, size), packed] + [pane...  7.91 us
    pallas_call x1, Pallas kernels, shards(): go(early_body, outs=[panel] * 3, spaces=[hbm] + [vmem] * 8)  4.27 us
    ppermute x3, waiting for transfers between devices, swapped(): return lax.ppermute(value, axis, [(i, i ^ bit) for i in range(peers)])  4.19 us
    pallas_call x1, Pallas kernels, shards(): go(local_g_body, outs=[sums, (n + tall, n), (2 * n, n), packed], spaces=[...  3.88 us
    ppermute x3, starting transfers between devices, swapped(): return lax.ppermute(value, axis, [(i, i ^ bit) for i in range(peers)])  2.82 us
    pallas_call x1, Pallas kernels, shards(): go(middle_body, outs=[panel, panel], spaces=[hbm] + [vmem] * 5)  2.73 us
  transfers between devices with their start and end apart: 14, of which 7 were waited for; matrix products, arithmetic and copies ran while one was open for 0% of the time, Pallas kernels for 38%

profile of v7, /device:TPU:0, one launch (start us, length us, event | category | flops | bytes accessed | tf_op | source)
XLA Modules:
  0.0 82.2 jit_solution(10779796110860543030)
XLA Ops:
  0.0 1.6 %shard_map.37._.down_ref.e_ref.s_ref = f32[1024,512]{1,0:T(8,128)S(1)} custom-call(s32[2,13]{1,0:T(2,128)} %bitcast.4, f32[2,14,256,256]{3,2,1,0:T(8,128)} %bitcast.8), custom_call_target="tpu_custom_call" | custom-call | tf_op jit(solution)/shard_map/pallas_call | solution.py:460
  1.6 3.4 %collective-permute-start.2 = (f32[1024,512]{1,0:T(8,128)S(1)}, f32[1024,512]{1,0:T(8,128)S(1)}, u32[]{:S(2)}, u32[]{:S(2)}) collective-permute-start(f32[1024,512]{1,0:T(8,128)S(1)} %shard_map.37._.down_ref.e_ref.s_ref), channel_id=1, source_target_pairs={{0,7},{1,0},{2,1},{3,2},{4,3},{5,4},{6,5},{7,6},{8,15},{9,8},{10,9... | collective-permute-start | bytes 6291464 | tf_op jit(solution)/shard_map/ppermute | solution.py:430
  5.0 1.6 %shard_map.38._.t_ref = f32[776,512]{1,0:T(8,128)S(1)} custom-call(s32[2,13]{1,0:T(2,128)} %bitcast.5, f32[2,14,256,256]{3,2,1,0:T(8,128)} %bitcast.9, f32[2,256]{1,0:T(2,128)} %bitcast.11, f32[1024,512]{1,0:T(8,128)S(1)} %shard_map.37._.down_ref.e_ref.s_ref), custom_call_target="tpu_custom_call" | custom-call | tf_op jit(solution)/shard_map/pallas_call | solution.py:464
  6.6 3.6 %collective-permute-start.6 = (f32[776,512]{1,0:T(8,128)S(1)}, f32[776,512]{1,0:T(8,128)S(1)}, u32[]{:S(2)}, u32[]{:S(2)}) collective-permute-start(f32[776,512]{1,0:T(8,128)S(1)} %shard_map.38._.t_ref), channel_id=1, source_target_pairs={{0,24},{8,0},{16,8},{24,16},{1,25},{9,1},{17,9},{25,17},{2,26},{10... | collective-permute-start | bytes 4767752 | tf_op jit(solution)/shard_map/ppermute | solution.py:430
  10.3 2.1 %shard_map.39 = (f32[512,512]{1,0:T(8,128)S(1)}, f32[264,512]{1,0:T(8,128)S(1)}) custom-call(s32[2,13]{1,0:T(2,128)} %bitcast.6, f32[2,14,256,256]{3,2,1,0:T(8,128)} %bitcast.10, f32[776,512]{1,0:T(8,128)S(1)} %shard_map.38._.t_ref), custom_call_target="tpu_custom_call" | custom-call | tf_op jit(solution)/shard_map/pallas_call | solution.py:470
  12.4 1.1 %shard_map.40 = (f32[264,512]{1,0:T(8,128)S(1)}, f32[512,512]{1,0:T(8,128)S(1)}, f32[28,256]{1,0:T(8,128)S(1)}, f32[16,256]{1,0:T(8,128)S(1)}) custom-call(s32[2,13]{1,0:T(2,128)S(1)} %bitcast.7, f32[264,512]{1,0:T(8,128)S(1)} %get-tuple-element.35._, f32[1024,512]{1,0:T(8,128)S(1)} %shard_map.37._.down_ref.e_ref.s_ref, f32[776,512]{1,0:T(8,128)S(1)} %shard_map.38._.t_ref, ...), custom_call_target="tpu_custom_call" | custom-call | tf_op jit(solution)/shard_map/pallas_call | solution.py:474
  13.5 0.1 collective-permute-start
  13.6 1.2 %collective-permute-done.more_ref = f32[16,256]{1,0:T(8,128)S(1)} collective-permute-done((f32[16,256]{1,0:T(8,128)S(1)}, f32[16,256]{1,0:T(8,128)S(1)}, u32[]{:S(2)}, u32[]{:S(2)}) %collective-permute-start) | collective-permute-done | bytes 16416 | tf_op jit(solution)/shard_map/ppermute | solution.py:435
  14.7 3.9 %shard_map.41 = (f32[16,256]{1,0:T(8,128)S(1)}, f32[776,512]{1,0:T(8,128)S(1)}, f32[1024,512]{1,0:T(8,128)S(1)}, f32[264,512]{1,0:T(8,128)S(1)}) custom-call(f32[264,512]{1,0:T(8,128)S(1)} %get-tuple-element.35._, f32[16,256]{1,0:T(8,128)S(1)} %get-tuple-element.38.sums_ref, f32[16,256]{1,0:T(8,128)S(1)} %collective-permute-done.more_ref, ...), custom_call_target="tpu_custom_call" | custom-call | tf_op jit(solution)/shard_map/pallas_call | solution.py:483
  18.6 1.0 %collective-permute-start.1 = (f32[16,256]{1,0:T(8,128)S(1)}, f32[16,256]{1,0:T(8,128)S(1)}, u32[]{:S(2)}, u32[]{:S(2)}) collective-permute-start(f32[16,256]{1,0:T(8,128)S(1)} %get-tuple-element.40.sums_ref), channel_id=1, source_target_pairs={{0,4},{1,5},{2,6},{3,7},{4,0},{5,1},{6,2},{7,3},{8,12},{9,13},{10,... | collective-permute-start | bytes 49160 | tf_op jit(solution)/shard_map/ppermute | solution.py:435
  19.6 3.0 %collective-permute-done.1.more_ref = f32[16,256]{1,0:T(8,128)S(1)} collective-permute-done((f32[16,256]{1,0:T(8,128)S(1)}, f32[16,256]{1,0:T(8,128)S(1)}, u32[]{:S(2)}, u32[]{:S(2)}) %collective-permute-start.1) | collective-permute-done | bytes 16416 | tf_op jit(solution)/shard_map/ppermute | solution.py:435
  22.6 7.9 %shard_map.42 = (f32[16,256]{1,0:T(8,128)S(1)}, f32[2,14,256,256]{3,2,1,0:T(8,128)}, f32[264,512]{1,0:T(8,128)S(1)}, f32[512,512]{1,0:T(8,128)S(1)}, f32[512,512...) custom-call(f32[776,512]{1,0:T(8,128)S(1)} %get-tuple-element.39._.g0_ref, ...), custom_call_target="tpu_custom_call" | custom-call | tf_op jit(solution)/shard_map/pallas_call | solution.py:487
  30.5 1.8 %collective-permute-start.3 = (f32[16,256]{1,0:T(8,128)S(1)}, f32[16,256]{1,0:T(8,128)S(1)}, u32[]{:S(2)}, u32[]{:S(2)}) collective-permute-start(f32[16,256]{1,0:T(8,128)S(1)} %get-tuple-element.45.sums_ref), channel_id=1, source_target_pairs={{0,2},{1,3},{2,0},{3,1},{4,6},{5,7},{6,4},{7,5},{8,10},{9,11},{10,... | collective-permute-start | bytes 49160 | tf_op jit(solution)/shard_map/ppermute | solution.py:435
  32.3 2.2 %collective-permute-done.2.__.below_ref = f32[1024,512]{1,0:T(8,128)S(1)} collective-permute-done((f32[1024,512]{1,0:T(8,128)S(1)}, f32[1024,512]{1,0:T(8,128)S(1)}, u32[]{:S(2)}, u32[]{:S(2)}) %collective-permute-start.2) | collective-permute-done | bytes 2097184 | tf_op jit(solution)/shard_map/ppermute | solution.py:430
  34.6 0.2 collective-permute-start.5
  34.8 1.7 %shard_map.44 = (f32[8,256]{1,0:T(8,128)S(1)}, f32[776,512]{1,0:T(8,128)S(1)}) custom-call(f32[264,512]{1,0:T(8,128)S(1)} %shard_map.43._, f32[16,256]{1,0:T(8,128)S(1)} %get-tuple-element.45.sums_ref, f32[16,256]{1,0:T(8,128)S(1)} %collective-permute-done.3.more_ref, f32[776,512]{1,0:T(8,128)S(1)} %get-tuple-element.39._.g0_ref, ...), custom_call_target="tpu_custom_call" | custom-call | tf_op jit(solution)/shard_map/pallas_call | solution.py:494
  36.5 1.8 %collective-permute-start.10 = (f32[776,512]{1,0:T(8,128)S(1)}, f32[776,512]{1,0:T(8,128)S(1)}, u32[]{:S(2)}, u32[]{:S(2)}) collective-permute-start(f32[776,512]{1,0:T(8,128)S(1)} %get-tuple-element.46._), channel_id=1, source_target_pairs={{0,8},{8,16},{16,24},{24,0},{1,9},{9,17},{17,25},{25,1},{2,10},{10... | collective-permute-start | bytes 4767752 | tf_op jit(solution)/shard_map/ppermute | solution.py:430
  38.3 2.4 %collective-permute-start.7 = (f32[264,512]{1,0:T(8,128)S(1)}, f32[264,512]{1,0:T(8,128)S(1)}, u32[]{:S(2)}, u32[]{:S(2)}) collective-permute-start(f32[264,512]{1,0:T(8,128)S(1)} %get-tuple-element.49), channel_id=1, source_target_pairs={{0,7},{1,0},{2,1},{3,2},{4,3},{5,4},{6,5},{7,6},{8,15},{9,8},{10,9... | collective-permute-start | bytes 1622024 | tf_op jit(solution)/shard_map/ppermute | solution.py:430
  40.7 4.8 %collective-permute-done.6.tx_ref = f32[776,512]{1,0:T(8,128)S(1)} collective-permute-done((f32[776,512]{1,0:T(8,128)S(1)}, f32[776,512]{1,0:T(8,128)S(1)}, u32[]{:S(2)}, u32[]{:S(2)}) %collective-permute-start.6) | collective-permute-done | bytes 1589280 | tf_op jit(solution)/shard_map/ppermute | solution.py:430
  45.5 0.5 collective-permute-done.5.__.yc_in_ref
  46.0 2.7 %shard_map.45 = (f32[512,512]{1,0:T(8,128)S(1)}, f32[512,512]{1,0:T(8,128)S(1)}) custom-call(f32[776,512]{1,0:T(8,128)S(1)} %get-tuple-element.46._, f32[264,512]{1,0:T(8,128)S(1)} %collective-permute-done.5.__.yc_in_ref, f32[1024,512]{1,0:T(8,128)S(1)} %get-tuple-element.47.r0_ref, f32[1024,512]{1,0:T(8,128)S(1)} %collective-permute-done.2.__.below_ref, ...), custom_call_target="tpu_custom_call" | custom-call | tf_op jit(solution)/shard_map/pallas_call | solution.py:497
  48.8 0.1 collective-permute-start.13
  48.9 2.7 %collective-permute-start.8 = (f32[264,512]{1,0:T(8,128)S(1)}, f32[264,512]{1,0:T(8,128)S(1)}, u32[]{:S(2)}, u32[]{:S(2)}) collective-permute-start(f32[264,512]{1,0:T(8,128)S(1)} %shard_map.46._), channel_id=1, source_target_pairs={{0,7},{1,0},{2,1},{3,2},{4,3},{5,4},{6,5},{7,6},{8,15},{9,8},{10,9... | collective-permute-start | bytes 1622024 | tf_op jit(solution)/shard_map/ppermute | solution.py:430
  51.6 4.3 %shard_map.47 = (f32[512,512]{1,0:T(8,128)S(1)}, f32[512,512]{1,0:T(8,128)S(1)}, f32[512,512]{1,0:T(8,128)S(1)}) custom-call(f32[264,512]{1,0:T(8,128)S(1)} %shard_map.46._, f32[776,512]{1,0:T(8,128)S(1)} %shard_map.38._.t_ref, f32[1024,512]{1,0:T(8,128)S(1)} %shard_map.37._.down_ref.e_ref.s_ref, f32[512,512]{1,0:T(8,128)S(1)} %get-tuple-element.36.d_ref, ...), custom_call_target="tpu_custom_call" | custom-call | tf_op jit(solution)/shard_map/pallas_call | solution.py:501
  55.9 2.7 %shard_map.48 = (f32[512,512]{1,0:T(8,128)S(1)}, f32[512,512]{1,0:T(8,128)S(1)}) custom-call(f32[512,512]{1,0:T(8,128)S(1)} %get-tuple-element.53._.yn_ref, f32[1024,512]{1,0:T(8,128)S(1)} %shard_map.37._.down_ref.e_ref.s_ref, f32[512,512]{1,0:T(8,128)S(1)} %get-tuple-element.36.d_ref, f32[776,512]{1,0:T(8,128)S(1)} %collective-permute-done.6.tx_ref, ...), custom_call_target="tpu_custom_call" | custom-call | tf_op jit(solution)/shard_map/pallas_call | solution.py:502
  58.6 5.7 %collective-permute-done.8.cxu_ref = f32[264,512]{1,0:T(8,128)S(1)} collective-permute-done((f32[264,512]{1,0:T(8,128)S(1)}, f32[264,512]{1,0:T(8,128)S(1)}, u32[]{:S(2)}, u32[]{:S(2)}) %collective-permute-start.8) | collective-permute-done | bytes 540704 | tf_op jit(solution)/shard_map/ppermute | solution.py:430
  64.3 1.1 %shard_map.49 = (f32[8,256]{1,0:T(8,128)S(1)}, f32[512,512]{1,0:T(8,128)S(1)}) custom-call(f32[512,512]{1,0:T(8,128)S(1)} %get-tuple-element.57._.ye_ref, f32[8,256]{1,0:T(8,128)S(1)} %get-tuple-element.58.sums_ref, f32[512,512]{1,0:T(8,128)S(1)} %get-tuple-element.36.d_ref, f32[264,512]{1,0:T(8,128)S(1)} %collective-permute-done.8.cxu_ref, ...), custom_call_target="tpu_custom_call" | custom-call | tf_op jit(solution)/shard_map/pallas_call | solution.py:503
  65.4 2.5 %collective-permute-start.12 = (f32[8,256]{1,0:T(8,128)S(1)}, f32[8,256]{1,0:T(8,128)S(1)}, u32[]{:S(2)}, u32[]{:S(2)}) collective-permute-start(f32[8,256]{1,0:T(8,128)S(1)} %get-tuple-element.61.rest_0_), channel_id=1, source_target_pairs={{0,16},{8,24},{16,0},{24,8},{1,17},{9,25},{17,1},{25,9},{2,18},{10... | collective-permute-start | bytes 24584 | tf_op jit(solution)/shard_map/ppermute | solution.py:430
  67.9 3.0 %collective-permute-start.11 = (f32[8,256]{1,0:T(8,128)S(1)}, f32[8,256]{1,0:T(8,128)S(1)}, u32[]{:S(2)}, u32[]{:S(2)}) collective-permute-start(f32[8,256]{1,0:T(8,128)S(1)} %get-tuple-element.61.rest_0_), channel_id=1, source_target_pairs={{0,24},{8,0},{16,8},{24,16},{1,25},{9,1},{17,9},{25,17},{2,26},{10... | collective-permute-start | bytes 24584 | tf_op jit(solution)/shard_map/ppermute | solution.py:430
  70.9 7.6 %collective-permute-done.12.rest_2_ = f32[8,256]{1,0:T(8,128)S(1)} collective-permute-done((f32[8,256]{1,0:T(8,128)S(1)}, f32[8,256]{1,0:T(8,128)S(1)}, u32[]{:S(2)}, u32[]{:S(2)}) %collective-permute-start.12) | collective-permute-done | bytes 8224 | tf_op jit(solution)/shard_map/ppermute | solution.py:430
  78.5 2.5 %shard_map.50 = (f32[2,14,256,256]{3,2,1,0:T(8,128)}, f32[8,256]{1,0:T(8,128)S(1)}) custom-call(f32[28,256]{1,0:T(8,128)S(1)} %get-tuple-element.37.keep_ref, f32[2,14,256,256]{3,2,1,0:T(8,128)} %get-tuple-element.42._, f32[512,512]{1,0:T(8,128)S(1)} %get-tuple-element.41.c_ref, f32[776,512]{1,0:T(8,128)S(1)} %shard_map.38._.t_ref, ...), custom_call_target="tpu_custom_call", output_to_operand_aliasing={{0}: (1, {})} | custom-call | tf_op jit(solution)/shard_map/pallas_call | solution.py:507
  81.0 1.1 %shard_map.51 = f32[2,14,256,256]{3,2,1,0:T(8,128)} custom-call(f32[28,256]{1,0:T(8,128)S(1)} %get-tuple-element.37.keep_ref, f32[2,14,256,256]{3,2,1,0:T(8,128)} %get-tuple-element.62._, f32[8,256]{1,0:T(8,128)S(1)} %get-tuple-element.63.twice_ref, f32[1024,512]{1,0:T(8,128)S(1)} %shard_map.37._.down_ref.e_ref.s_ref, ...), custom_call_target="tpu_custom_call", output_to_operand_aliasing={{}: (1, {})} | custom-call | tf_op jit(solution)/shard_map/pallas_call | solution.py:511
  (13 shorter events, 0.2 us)
Async XLA Ops:
  1.6 32.9 %collective-permute-start.2 = (f32[1024,512]{1,0:T(8,128)S(1)}, f32[1024,512]{1,0:T(8,128)S(1)}, u32[]{:S(2)}, u32[]{:S(2)}) collective-permute-start(f32[1024,512]{1,0:T(8,128)S(1)} %shard_map.37._.down_ref.e_ref.s_ref), channel_id=1, source_target_pairs={{0,7},{1,0},{2,1},{3,2},{4,3},{5,4},{6,5},{7,6},{8,15},{9,8},{10,9... | collective-permute-start | bytes 6291464 | tf_op jit(solution)/shard_map/ppermute | solution.py:430
  6.6 5.8 %copy-start = (s32[1,1,2,13]{3,2,1,0:T(2,128)S(1)}, s32[1,1,2,13]{3,2,1,0:T(2,128)}, u32[]{:S(2)}) copy-start(s32[1,1,2,13]{3,2,1,0:T(2,128)} %param.5) | copy-start | bytes 316
  6.6 38.9 %collective-permute-start.6 = (f32[776,512]{1,0:T(8,128)S(1)}, f32[776,512]{1,0:T(8,128)S(1)}, u32[]{:S(2)}, u32[]{:S(2)}) collective-permute-start(f32[776,512]{1,0:T(8,128)S(1)} %shard_map.38._.t_ref), channel_id=1, source_target_pairs={{0,24},{8,0},{16,8},{24,16},{1,25},{9,1},{17,9},{25,17},{2,26},{10... | collective-permute-start | bytes 4767752 | tf_op jit(solution)/shard_map/ppermute | solution.py:430
  12.3 22.4 %collective-permute-start.4 = (f32[264,512]{1,0:T(8,128)S(1)}, f32[264,512]{1,0:T(8,128)S(1)}, u32[]{:S(2)}, u32[]{:S(2)}) collective-permute-start(f32[264,512]{1,0:T(8,128)S(1)} %get-tuple-element.35._), channel_id=1, source_target_pairs={{0,1},{1,2},{2,3},{3,4},{4,5},{5,6},{6,7},{7,0},{8,9},{9,10},{10,1... | collective-permute-start | bytes 1622024 | tf_op jit(solution)/shard_map/ppermute | solution.py:430
  13.5 1.2 %collective-permute-start = (f32[16,256]{1,0:T(8,128)S(1)}, f32[16,256]{1,0:T(8,128)S(1)}, u32[]{:S(2)}, u32[]{:S(2)}) collective-permute-start(f32[16,256]{1,0:T(8,128)S(1)} %get-tuple-element.38.sums_ref), channel_id=1, source_target_pairs={{0,1},{1,0},{2,3},{3,2},{4,5},{5,4},{6,7},{7,6},{8,9},{9,8},{10,11... | collective-permute-start | bytes 49160 | tf_op jit(solution)/shard_map/ppermute | solution.py:435
  18.6 4.0 %collective-permute-start.1 = (f32[16,256]{1,0:T(8,128)S(1)}, f32[16,256]{1,0:T(8,128)S(1)}, u32[]{:S(2)}, u32[]{:S(2)}) collective-permute-start(f32[16,256]{1,0:T(8,128)S(1)} %get-tuple-element.40.sums_ref), channel_id=1, source_target_pairs={{0,4},{1,5},{2,6},{3,7},{4,0},{5,1},{6,2},{7,3},{8,12},{9,13},{10,... | collective-permute-start | bytes 49160 | tf_op jit(solution)/shard_map/ppermute | solution.py:435
  30.5 4.3 %collective-permute-start.3 = (f32[16,256]{1,0:T(8,128)S(1)}, f32[16,256]{1,0:T(8,128)S(1)}, u32[]{:S(2)}, u32[]{:S(2)}) collective-permute-start(f32[16,256]{1,0:T(8,128)S(1)} %get-tuple-element.45.sums_ref), channel_id=1, source_target_pairs={{0,2},{1,3},{2,0},{3,1},{4,6},{5,7},{6,4},{7,5},{8,10},{9,11},{10,... | collective-permute-start | bytes 49160 | tf_op jit(solution)/shard_map/ppermute | solution.py:435
  34.6 11.4 %collective-permute-start.5 = (f32[264,512]{1,0:T(8,128)S(1)}, f32[264,512]{1,0:T(8,128)S(1)}, u32[]{:S(2)}, u32[]{:S(2)}) collective-permute-start(f32[264,512]{1,0:T(8,128)S(1)} %shard_map.43._), channel_id=1, source_target_pairs={{0,1},{1,2},{2,3},{3,4},{4,5},{5,6},{6,7},{7,0},{8,9},{9,10},{10,1... | collective-permute-start | bytes 1622024 | tf_op jit(solution)/shard_map/ppermute | solution.py:430
  36.5 42.0 %collective-permute-start.10 = (f32[776,512]{1,0:T(8,128)S(1)}, f32[776,512]{1,0:T(8,128)S(1)}, u32[]{:S(2)}, u32[]{:S(2)}) collective-permute-start(f32[776,512]{1,0:T(8,128)S(1)} %get-tuple-element.46._), channel_id=1, source_target_pairs={{0,8},{8,16},{16,24},{24,0},{1,9},{9,17},{17,25},{25,1},{2,10},{10... | collective-permute-start | bytes 4767752 | tf_op jit(solution)/shard_map/ppermute | solution.py:430
  38.3 10.5 %collective-permute-start.7 = (f32[264,512]{1,0:T(8,128)S(1)}, f32[264,512]{1,0:T(8,128)S(1)}, u32[]{:S(2)}, u32[]{:S(2)}) collective-permute-start(f32[264,512]{1,0:T(8,128)S(1)} %get-tuple-element.49), channel_id=1, source_target_pairs={{0,7},{1,0},{2,1},{3,2},{4,3},{5,4},{6,5},{7,6},{8,15},{9,8},{10,9... | collective-permute-start | bytes 1622024 | tf_op jit(solution)/shard_map/ppermute | solution.py:430
  48.7 29.8 %collective-permute-start.9 = (f32[512,512]{1,0:T(8,128)S(1)}, f32[512,512]{1,0:T(8,128)S(1)}, u32[]{:S(2)}, u32[]{:S(2)}) collective-permute-start(f32[512,512]{1,0:T(8,128)S(1)} %get-tuple-element.48._), channel_id=1, source_target_pairs={{0,1},{1,2},{2,3},{3,4},{4,5},{5,6},{6,7},{7,0},{8,9},{9,10},{10,1... | collective-permute-start | bytes 3145736 | tf_op jit(solution)/shard_map/ppermute | solution.py:430
  48.8 32.2 %collective-permute-start.13 = (f32[512,512]{1,0:T(8,128)S(1)}, f32[512,512]{1,0:T(8,128)S(1)}, u32[]{:S(2)}, u32[]{:S(2)}) collective-permute-start(f32[512,512]{1,0:T(8,128)S(1)} %get-tuple-element.64), channel_id=1, source_target_pairs={{0,1},{1,2},{2,3},{3,4},{4,5},{5,6},{6,7},{7,0},{8,9},{9,10},{10,1... | collective-permute-start | bytes 3145736 | tf_op jit(solution)/shard_map/ppermute | solution.py:430
  48.9 15.4 %collective-permute-start.8 = (f32[264,512]{1,0:T(8,128)S(1)}, f32[264,512]{1,0:T(8,128)S(1)}, u32[]{:S(2)}, u32[]{:S(2)}) collective-permute-start(f32[264,512]{1,0:T(8,128)S(1)} %shard_map.46._), channel_id=1, source_target_pairs={{0,7},{1,0},{2,1},{3,2},{4,3},{5,4},{6,5},{7,6},{8,15},{9,8},{10,9... | collective-permute-start | bytes 1622024 | tf_op jit(solution)/shard_map/ppermute | solution.py:430
  65.4 13.1 %collective-permute-start.12 = (f32[8,256]{1,0:T(8,128)S(1)}, f32[8,256]{1,0:T(8,128)S(1)}, u32[]{:S(2)}, u32[]{:S(2)}) collective-permute-start(f32[8,256]{1,0:T(8,128)S(1)} %get-tuple-element.61.rest_0_), channel_id=1, source_target_pairs={{0,16},{8,24},{16,0},{24,8},{1,17},{9,25},{17,1},{25,9},{2,18},{10... | collective-permute-start | bytes 24584 | tf_op jit(solution)/shard_map/ppermute | solution.py:430
  67.9 10.6 %collective-permute-start.11 = (f32[8,256]{1,0:T(8,128)S(1)}, f32[8,256]{1,0:T(8,128)S(1)}, u32[]{:S(2)}, u32[]{:S(2)}) collective-permute-start(f32[8,256]{1,0:T(8,128)S(1)} %get-tuple-element.61.rest_0_), channel_id=1, source_target_pairs={{0,24},{8,0},{16,8},{24,16},{1,25},{9,1},{17,9},{25,17},{2,26},{10... | collective-permute-start | bytes 24584 | tf_op jit(solution)/shard_map/ppermute | solution.py:430

commit v8 on v7

--- a/solution.py
+++ b/solution.py
@@ -195,18 +195,9 @@
     ]
 
 
-def pack_e_body(layers, size, mask_ref, stored_ref, down_ref, sems, mask, mask_sem):
-    n = layers * size
-    small = pltpu.make_async_copy(mask_ref, mask, mask_sem)
-    small.start()
-    first = start_panel(stored_ref, down_ref, sems, 0, "S", layers, size)
-    second = start_panel(stored_ref, down_ref, sems, len(first), "E", layers, size, top=n)
-    small.wait()
-    end_panel(first, down_ref, "S", layers, size, mask)
-    end_panel(second, down_ref, "E", layers, size, mask, top=n)
-
-
-def pack_t_body(layers, size, mask_ref, stored_ref, onsite_ref, _, t_ref, held, sems, mask, mask_sem, onsite, onsite_sem):
+def pack_body(
+    layers, size, mask_ref, stored_ref, onsite_ref, t_ref, down_ref, held, sems, mask, mask_sem, onsite, onsite_sem
+):
     n = layers * size
     small = [
         pltpu.make_async_copy(mask_ref, mask, mask_sem),
@@ -215,7 +206,11 @@
     for copy in small:
         copy.start()
     copies = start_loads(stored_ref, held, sems, wanted("C", layers))
-    panel = start_panel(stored_ref, t_ref, sems, len(copies), "N", layers, size)
+    panels = []
+    at = len(copies)
+    for name, ref, top in (("N", t_ref, 0), ("S", down_ref, 0), ("E", down_ref, n)):
+        panels.append((start_panel(stored_ref, ref, sems, at, name, layers, size, top=top), ref, name, top))
+        at += len(panels[-1][0])
     for copy in small:
         copy.wait()
     row, col = rows_cols(size)
@@ -228,7 +223,8 @@
         copies[k].wait()
         blocks[low, high] = jnp.where(kept(mask, low, slot), held[k], 0.0)
     put_sym(t_ref, lambda a, b: blocks.get((a, b), jnp.zeros((size, size), F32)), layers, size, first=n)
-    end_panel(panel, t_ref, "N", layers, size, mask)
+    for started, ref, name, top in panels:
+        end_panel(started, ref, name, layers, size, mask, top=top)
 
 
 def pack_d_body(layers, size, mask_ref, stored_ref, _, d_ref, up_ref, sems, mask, mask_sem):
@@ -308,6 +304,12 @@
     to_ref[...] = from_ref[...]
 
 
+def yc_body(layers, size, _, __, from_ref, to_ref):
+    tall = from_ref.shape[0]
+    to_ref[:tall, :] = from_ref[...]
+    to_ref[tall:, :] = jnp.zeros((8, layers * size), F32)
+
+
 def g_body(layers, size, _, sums_ref, more_ref, g0_ref, below_ref, up_ref, total_ref, g_ref):
     n, last = layers * size, g_ref.shape[0] - 8
     parts = sums_ref[...] + more_ref[...]
@@ -334,7 +336,7 @@
     yd_ref[...] = yd0_ref[...] + dot3(n, eu, NN)
 
 
-def r_body(layers, size, _, __, r0_ref, below_ref, tx_ref, rs_ref, re_ref):
+def r_body(layers, size, _, r0_ref, below_ref, tx_ref, rs_ref, re_ref):
     n = layers * size
     su, eu, nx = split(below_ref[:n, :]), split(below_ref[n:, :]), split(tx_ref[:n, :])
     cx = split(whole_sym(take_sym(tx_ref[n:, :], layers, size), layers))
@@ -387,7 +389,7 @@
 
 
 def last_c_body(
-    target, layers, size, keep_ref, _, c_ref, t_ref, s_ref, d_ref, yc_ref, yn_ref, ys_ref, yd_ref, yc_in_ref, rs_ref, g_ref, *rest
+    target, layers, size, keep_ref, _, c_ref, t_ref, e_ref, d_ref, yc_ref, yn_ref, ye_ref, yd_ref, yc_in_ref, re_ref, g_ref, *rest
 ):
     *sums_refs, out_ref, twice_ref, held, sems = rest
     n, last = layers * size, g_ref.shape[0] - 8
@@ -398,18 +400,18 @@
     twice_ref[...] = jnp.broadcast_to(twice, twice_ref.shape)
     sender = Sender(twice, keep_ref, out_ref, held, sems)
     sender.send_panel("D", d_ref, [yd_ref], layers, size)
-    sender.send_panel("S", s_ref, [ys_ref, rs_ref], layers, size)
+    sender.send_panel("E", e_ref.at[n:, :], [ye_ref, re_ref], layers, size)
     sender.send_panel("N", t_ref, [yn_ref, g_ref], layers, size)
-    blocks = take_sym(yc_ref[...] + yc_in_ref[...] + g_ref[n:, :], layers, size)
+    blocks = take_sym(yc_ref[...] + yc_in_ref[: yc_ref.shape[0], :] + g_ref[n:, :], layers, size)
     for low, high, slot in panel_blocks("C", layers) + [(layer, layer, 0) for layer in range(layers)]:
         rows, cols = slice(low * size, (low + 1) * size), slice(high * size, (high + 1) * size)
         sender.send(blocks[low, high], c_ref[rows, cols], low, slot)
     sender.wait()
 
 
-def last_e_body(layers, size, keep_ref, _, twice_ref, down_ref, ye_ref, re_ref, out_ref, held, sems):
+def last_s_body(layers, size, keep_ref, _, twice_ref, down_ref, ys_ref, rs_ref, out_ref, held, sems):
     sender = Sender(twice_ref[0:1, :], keep_ref, out_ref, held, sems)
-    sender.send_panel("E", down_ref.at[layers * size :, :], [ye_ref, re_ref], layers, size)
+    sender.send_panel("S", down_ref, [ys_ref, rs_ref], layers, size)
     sender.wait()
 
 
@@ -457,16 +459,13 @@
 
     small = [pltpu.SMEM(mask.shape, mask.dtype), pltpu.SemaphoreType.DMA]
     count = {name: len(wanted(name, layers)) for name in IN_PLANE}
-    (down,) = go(
-        pack_e_body, outs=[(2 * n, n)], spaces=[hbm] * 2, scratch=[pltpu.SemaphoreType.DMA((count["S"] + count["E"],))] + small
-    )(mask_hbm, stored)
+    T, down = go(
+        pack_body, outs=[(n + tall, n), (2 * n, n)], spaces=[hbm] * 3,
+        scratch=[pltpu.VMEM((count["C"], size, size), F32), pltpu.SemaphoreType.DMA((len(wanted("CNSE", layers)),))]
+        + small + [pltpu.VMEM(onsite.shape, F32), pltpu.SemaphoreType.DMA],
+    )(mask_hbm, stored, onsite)
+    T_x = passed_along(T, "row", -1)
     below = passed_along(down, "col", -1)
-    (T,) = go(
-        pack_t_body, outs=[(n + tall, n)], spaces=[hbm] * 4,
-        scratch=[pltpu.VMEM((count["C"], size, size), F32), pltpu.SemaphoreType.DMA((count["C"] + count["N"],))]
-        + small + [pltpu.VMEM(onsite.shape, F32), pltpu.SemaphoreType.DMA],
-    )(mask_hbm, stored, onsite, down)
-    T_x = passed_along(T, "row", -1)
     D, gc = go(
         pack_d_body, outs=[panel, packed], spaces=[hbm] * 3, scratch=[pltpu.SemaphoreType.DMA((count["D"],))] + small
     )(mask_hbm, stored, T)
@@ -489,12 +488,13 @@
         out_spaces=[vmem, hbm] + [vmem] * 5, scratch=[pltpu.VMEM((size, size), F32), pltpu.SemaphoreType.DMA((layers * slots,))],
     )(g0, own, more, C, T, down, D)
     more = arriving(own)
-    (yc_up,) = go(copy_body, outs=[packed], spaces=[hbm] * 2 + [vmem])(yc, below, yc_up)
+    (yc_up,) = go(yc_body, outs=[(tall + 8, n)], spaces=[hbm] * 2 + [vmem])(yc, below, yc_up)
     yc_in = passed_along(yc_up, "col", 1)
     own, g = go(g_body, outs=[total, (n + tall, n)], spaces=[hbm] + [vmem] * 5)(yc_up, own, more, g0, below, gc_in)
     g_in = passed_along(g, "row", 1)
     Cp_u = passed_along(Cp, "col", -1)
-    rs, re = go(r_body, outs=[panel, panel], spaces=[hbm] * 2 + [vmem] * 3)(g, yc_in, r0, below, T_x)
+    rs, re = go(r_body, outs=[panel, panel], spaces=[hbm] + [vmem] * 3)(g, r0, below, T_x)
+    (rs,) = go(copy_body, outs=[panel], spaces=[hbm] * 2 + [vmem])(yc_in, re, rs)
     rs_in, re_in = passed_along(rs, "col", 1), passed_along(re, "col", 1)
     (Cp_x,) = go(hand_body, outs=[packed], spaces=[hbm] * 2 + [vmem])(rs, Cp_u, T_x)
     Cp_xu = passed_along(Cp_x, "col", -1)
@@ -506,12 +506,12 @@
     target = float(cells * size // 2)
     out, twice = go(
         functools.partial(last_c_body, target), outs=[out.shape, total], out_spaces=[hbm, vmem],
-        spaces=[vmem, hbm] + [vmem] * (11 + len(every)), scratch=blocks(len(wanted("CNSD", layers))), aliases={1: 0},
-    )(keep, out, C, T, down, D, yc, yn, ys, yd, yc_in, rs_in, g_in, *every)
+        spaces=[vmem, hbm] + [vmem] * (11 + len(every)), scratch=blocks(len(wanted("CNED", layers))), aliases={1: 0},
+    )(keep, out, C, T, down, D, yc, yn, ye, yd, yc_in, re_in, g_in, *every)
     (out,) = go(
-        last_e_body, outs=[out.shape], out_spaces=[hbm], spaces=[vmem, hbm] + [vmem] * 4,
-        scratch=blocks(count["E"]), aliases={1: 0},
-    )(keep, out, twice, down, ye, re_in)
+        last_s_body, outs=[out.shape], out_spaces=[hbm], spaces=[vmem, hbm] + [vmem] * 4,
+        scratch=blocks(count["S"]), aliases={1: 0},
+    )(keep, out, twice, down, ys, rs_in)
     return out[None, None]
 
 

time: 82.6 us -> 81.6 us (0.988)
  transfers between devices with their start and end apart: 14 -> 14, of which waited for: 7 -> 7; matrix products, arithmetic and copies ran while one was open for 0% -> 0% of each run, Pallas kernels for 38% -> 37%
where the time goes in v8:
time: 81.6 us; the launch traced here: 81.4 us
  Pallas kernels  33.6 us (41%)
  waiting for transfers between devices  24.6 us (30%)
  starting transfers between devices  22.9 us (28%)
    ppermute x11, waiting for transfers between devices, passed_along(): lax.ppermute(value, axis, [(i, (i + by) % peers) for i in range(peers)])  20.4 us
    ppermute x11, starting transfers between devices, passed_along(): lax.ppermute(value, axis, [(i, (i + by) % peers) for i in range(peers)])  20.1 us
    pallas_call x1, Pallas kernels, shards(): go(local_y_body, outs=[sums, (layers, slots, size, size), packed] + [pane...  7.91 us
    pallas_call x1, Pallas kernels, shards(): go(early_body, outs=[panel] * 3, spaces=[hbm] + [vmem] * 8)  4.27 us
    ppermute x3, waiting for transfers between devices, swapped(): return lax.ppermute(value, axis, [(i, i ^ bit) for i in range(peers)])  4.19 us
    pallas_call x1, Pallas kernels, shards(): go(local_g_body, outs=[sums, (n + tall, n), (2 * n, n), packed], spaces=[...  3.88 us
    ppermute x3, starting transfers between devices, swapped(): return lax.ppermute(value, axis, [(i, i ^ bit) for i in range(peers)])  2.79 us
    pallas_call x1, Pallas kernels, shards(): go(middle_body, outs=[panel, panel], spaces=[hbm] + [vmem] * 5)  2.72 us
  transfers between devices with their start and end apart: 14, of which 7 were waited for; matrix products, arithmetic and copies ran while one was open for 0% of the time, Pallas kernels for 37%

profile of v8, /device:TPU:0, one launch (start us, length us, event | category | flops | bytes accessed | tf_op | source)
XLA Modules:
  0.0 81.4 jit_solution(6069012209743225784)
XLA Ops:
  0.0 2.6 %shard_map.37 = (f32[776,512]{1,0:T(8,128)S(1)}, f32[1024,512]{1,0:T(8,128)S(1)}) custom-call(s32[2,13]{1,0:T(2,128)} %bitcast.4, f32[2,14,256,256]{3,2,1,0:T(8,128)} %bitcast.7, f32[2,256]{1,0:T(2,128)} %bitcast.9), custom_call_target="tpu_custom_call" | custom-call | tf_op jit(solution)/shard_map/pallas_call | solution.py:462
  2.6 3.4 %collective-permute-start.2 = (f32[1024,512]{1,0:T(8,128)S(1)}, f32[1024,512]{1,0:T(8,128)S(1)}, u32[]{:S(2)}, u32[]{:S(2)}) collective-permute-start(f32[1024,512]{1,0:T(8,128)S(1)} %get-tuple-element.39.down_ref.e_ref), channel_id=1, source_target_pairs={{0,7},{1,0},{2,1},{3,2},{4,3},{5,4},{6,5},{7,6},{8,15},{9,8},{10,9... | collective-permute-start | bytes 6291464 | tf_op jit(solution)/shard_map/ppermute | solution.py:432
  5.9 3.6 %collective-permute-start.6 = (f32[776,512]{1,0:T(8,128)S(1)}, f32[776,512]{1,0:T(8,128)S(1)}, u32[]{:S(2)}, u32[]{:S(2)}) collective-permute-start(f32[776,512]{1,0:T(8,128)S(1)} %get-tuple-element.37._.t_ref), channel_id=1, source_target_pairs={{0,24},{8,0},{16,8},{24,16},{1,25},{9,1},{17,9},{25,17},{2,26},{10... | collective-permute-start | bytes 4767752 | tf_op jit(solution)/shard_map/ppermute | solution.py:432
  9.6 2.0 %shard_map.38 = (f32[512,512]{1,0:T(8,128)S(1)}, f32[264,512]{1,0:T(8,128)S(1)}) custom-call(s32[2,13]{1,0:T(2,128)} %bitcast.5, f32[2,14,256,256]{3,2,1,0:T(8,128)} %bitcast.8, f32[776,512]{1,0:T(8,128)S(1)} %get-tuple-element.37._.t_ref), custom_call_target="tpu_custom_call" | custom-call | tf_op jit(solution)/shard_map/pallas_call | solution.py:469
  11.7 1.1 %shard_map.39 = (f32[264,512]{1,0:T(8,128)S(1)}, f32[512,512]{1,0:T(8,128)S(1)}, f32[28,256]{1,0:T(8,128)S(1)}, f32[16,256]{1,0:T(8,128)S(1)}) custom-call(s32[2,13]{1,0:T(2,128)S(1)} %bitcast.6, f32[264,512]{1,0:T(8,128)S(1)} %get-tuple-element.38._, f32[1024,512]{1,0:T(8,128)S(1)} %get-tuple-element.39.down_ref.e_ref, ...), custom_call_target="tpu_custom_call" | custom-call | tf_op jit(solution)/shard_map/pallas_call | solution.py:473
  12.8 0.1 collective-permute-start
  12.8 1.2 %collective-permute-done.more_ref = f32[16,256]{1,0:T(8,128)S(1)} collective-permute-done((f32[16,256]{1,0:T(8,128)S(1)}, f32[16,256]{1,0:T(8,128)S(1)}, u32[]{:S(2)}, u32[]{:S(2)}) %collective-permute-start) | collective-permute-done | bytes 16416 | tf_op jit(solution)/shard_map/ppermute | solution.py:437
  14.0 3.9 %shard_map.40 = (f32[16,256]{1,0:T(8,128)S(1)}, f32[776,512]{1,0:T(8,128)S(1)}, f32[1024,512]{1,0:T(8,128)S(1)}, f32[264,512]{1,0:T(8,128)S(1)}) custom-call(f32[264,512]{1,0:T(8,128)S(1)} %get-tuple-element.38._, f32[16,256]{1,0:T(8,128)S(1)} %get-tuple-element.42.sums_ref, f32[16,256]{1,0:T(8,128)S(1)} %collective-permute-done.more_ref, ...), custom_call_target="tpu_custom_call" | custom-call | tf_op jit(solution)/shard_map/pallas_call | solution.py:482
  17.9 1.0 %collective-permute-start.1 = (f32[16,256]{1,0:T(8,128)S(1)}, f32[16,256]{1,0:T(8,128)S(1)}, u32[]{:S(2)}, u32[]{:S(2)}) collective-permute-start(f32[16,256]{1,0:T(8,128)S(1)} %get-tuple-element.44.sums_ref), channel_id=1, source_target_pairs={{0,4},{1,5},{2,6},{3,7},{4,0},{5,1},{6,2},{7,3},{8,12},{9,13},{10,... | collective-permute-start | bytes 49160 | tf_op jit(solution)/shard_map/ppermute | solution.py:437
  18.9 3.0 %collective-permute-done.1.more_ref = f32[16,256]{1,0:T(8,128)S(1)} collective-permute-done((f32[16,256]{1,0:T(8,128)S(1)}, f32[16,256]{1,0:T(8,128)S(1)}, u32[]{:S(2)}, u32[]{:S(2)}) %collective-permute-start.1) | collective-permute-done | bytes 16416 | tf_op jit(solution)/shard_map/ppermute | solution.py:437
  21.9 7.9 %shard_map.41 = (f32[16,256]{1,0:T(8,128)S(1)}, f32[2,14,256,256]{3,2,1,0:T(8,128)}, f32[264,512]{1,0:T(8,128)S(1)}, f32[512,512]{1,0:T(8,128)S(1)}, f32[512,512...) custom-call(f32[776,512]{1,0:T(8,128)S(1)} %get-tuple-element.43._.g0_ref, ...), custom_call_target="tpu_custom_call" | custom-call | tf_op jit(solution)/shard_map/pallas_call | solution.py:486
  29.8 1.8 %collective-permute-start.4 = (f32[16,256]{1,0:T(8,128)S(1)}, f32[16,256]{1,0:T(8,128)S(1)}, u32[]{:S(2)}, u32[]{:S(2)}) collective-permute-start(f32[16,256]{1,0:T(8,128)S(1)} %get-tuple-element.49.sums_ref), channel_id=1, source_target_pairs={{0,2},{1,3},{2,0},{3,1},{4,6},{5,7},{6,4},{7,5},{8,10},{9,11},{10,... | collective-permute-start | bytes 49160 | tf_op jit(solution)/shard_map/ppermute | solution.py:437
  31.6 3.9 %collective-permute-done.2.__.below_ref = f32[1024,512]{1,0:T(8,128)S(1)} collective-permute-done((f32[1024,512]{1,0:T(8,128)S(1)}, f32[1024,512]{1,0:T(8,128)S(1)}, u32[]{:S(2)}, u32[]{:S(2)}) %collective-permute-start.2) | collective-permute-done | bytes 2097184 | tf_op jit(solution)/shard_map/ppermute | solution.py:432
  35.5 0.2 collective-permute-start.3
  35.8 1.7 %shard_map.43 = (f32[8,256]{1,0:T(8,128)S(1)}, f32[776,512]{1,0:T(8,128)S(1)}) custom-call(f32[272,512]{1,0:T(8,128)S(1)} %shard_map.42._, f32[16,256]{1,0:T(8,128)S(1)} %get-tuple-element.49.sums_ref, f32[16,256]{1,0:T(8,128)S(1)} %collective-permute-done.4.more_ref, f32[776,512]{1,0:T(8,128)S(1)} %get-tuple-element.43._.g0_ref, ...), custom_call_target="tpu_custom_call" | custom-call | tf_op jit(solution)/shard_map/pallas_call | solution.py:493
  37.5 1.8 %collective-permute-start.10 = (f32[776,512]{1,0:T(8,128)S(1)}, f32[776,512]{1,0:T(8,128)S(1)}, u32[]{:S(2)}, u32[]{:S(2)}) collective-permute-start(f32[776,512]{1,0:T(8,128)S(1)} %get-tuple-element.50._), channel_id=1, source_target_pairs={{0,8},{8,16},{16,24},{24,0},{1,9},{9,17},{17,25},{25,1},{2,10},{10... | collective-permute-start | bytes 4767752 | tf_op jit(solution)/shard_map/ppermute | solution.py:432
  39.3 2.4 %collective-permute-start.7 = (f32[264,512]{1,0:T(8,128)S(1)}, f32[264,512]{1,0:T(8,128)S(1)}, u32[]{:S(2)}, u32[]{:S(2)}) collective-permute-start(f32[264,512]{1,0:T(8,128)S(1)} %get-tuple-element.54), channel_id=1, source_target_pairs={{0,7},{1,0},{2,1},{3,2},{4,3},{5,4},{6,5},{7,6},{8,15},{9,8},{10,9... | collective-permute-start | bytes 1622024 | tf_op jit(solution)/shard_map/ppermute | solution.py:432
  41.7 3.1 %collective-permute-done.6.tx_ref = f32[776,512]{1,0:T(8,128)S(1)} collective-permute-done((f32[776,512]{1,0:T(8,128)S(1)}, f32[776,512]{1,0:T(8,128)S(1)}, u32[]{:S(2)}, u32[]{:S(2)}) %collective-permute-start.6) | collective-permute-done | bytes 1589280 | tf_op jit(solution)/shard_map/ppermute | solution.py:432
  44.8 2.7 %shard_map.44 = (f32[512,512]{1,0:T(8,128)S(1)}, f32[512,512]{1,0:T(8,128)S(1)}) custom-call(f32[776,512]{1,0:T(8,128)S(1)} %get-tuple-element.50._, f32[1024,512]{1,0:T(8,128)S(1)} %get-tuple-element.51.r0_ref, f32[1024,512]{1,0:T(8,128)S(1)} %collective-permute-done.2.__.below_ref, f32[776,512]{1,0:T(8,128)S(1)} %collective-permute-done.6.tx_ref), custom_call_target="tpu_custom_call" | custom-call | tf_op jit(solution)/shard_map/pallas_call | solution.py:496
  47.5 0.1 collective-permute-start.9
  47.6 0.1 shard_map.45._
  47.7 1.6 %collective-permute-done.7.__.cu_ref = f32[264,512]{1,0:T(8,128)S(1)} collective-permute-done((f32[264,512]{1,0:T(8,128)S(1)}, f32[264,512]{1,0:T(8,128)S(1)}, u32[]{:S(2)}, u32[]{:S(2)}) %collective-permute-start.7) | collective-permute-done | bytes 540704 | tf_op jit(solution)/shard_map/ppermute | solution.py:432
  49.4 3.2 %collective-permute-start.8 = (f32[264,512]{1,0:T(8,128)S(1)}, f32[264,512]{1,0:T(8,128)S(1)}, u32[]{:S(2)}, u32[]{:S(2)}) collective-permute-start(f32[264,512]{1,0:T(8,128)S(1)} %shard_map.46._), channel_id=1, source_target_pairs={{0,7},{1,0},{2,1},{3,2},{4,3},{5,4},{6,5},{7,6},{8,15},{9,8},{10,9... | collective-permute-start | bytes 1622024 | tf_op jit(solution)/shard_map/ppermute | solution.py:432
  52.5 4.3 %shard_map.47 = (f32[512,512]{1,0:T(8,128)S(1)}, f32[512,512]{1,0:T(8,128)S(1)}, f32[512,512]{1,0:T(8,128)S(1)}) custom-call(f32[264,512]{1,0:T(8,128)S(1)} %shard_map.46._, f32[776,512]{1,0:T(8,128)S(1)} %get-tuple-element.37._.t_ref, f32[1024,512]{1,0:T(8,128)S(1)} %get-tuple-element.39.down_ref.e_ref, f32[512,512]{1,0:T(8,128)S(1)} %get-tuple-element.40.d_ref, ...), custom_call_target="tpu_custom_call" | custom-call | tf_op jit(solution)/shard_map/pallas_call | solution.py:501
  56.8 2.7 %shard_map.48 = (f32[512,512]{1,0:T(8,128)S(1)}, f32[512,512]{1,0:T(8,128)S(1)}) custom-call(f32[512,512]{1,0:T(8,128)S(1)} %get-tuple-element.58._.yn_ref, f32[1024,512]{1,0:T(8,128)S(1)} %get-tuple-element.39.down_ref.e_ref, f32[512,512]{1,0:T(8,128)S(1)} %get-tuple-element.40.d_ref, f32[776,512]{1,0:T(8,128)S(1)} %collective-permute-done.6.tx_ref, ...), custom_call_target="tpu_custom_call" | custom-call | tf_op jit(solution)/shard_map/pallas_call | solution.py:502
  59.5 5.7 %collective-permute-done.8.cxu_ref = f32[264,512]{1,0:T(8,128)S(1)} collective-permute-done((f32[264,512]{1,0:T(8,128)S(1)}, f32[264,512]{1,0:T(8,128)S(1)}, u32[]{:S(2)}, u32[]{:S(2)}) %collective-permute-start.8) | collective-permute-done | bytes 540704 | tf_op jit(solution)/shard_map/ppermute | solution.py:432
  65.3 1.1 %shard_map.49 = (f32[8,256]{1,0:T(8,128)S(1)}, f32[512,512]{1,0:T(8,128)S(1)}) custom-call(f32[512,512]{1,0:T(8,128)S(1)} %get-tuple-element.61._.ye_ref, f32[8,256]{1,0:T(8,128)S(1)} %get-tuple-element.62.sums_ref, f32[512,512]{1,0:T(8,128)S(1)} %get-tuple-element.40.d_ref, f32[264,512]{1,0:T(8,128)S(1)} %collective-permute-done.8.cxu_ref, ...), custom_call_target="tpu_custom_call" | custom-call | tf_op jit(solution)/shard_map/pallas_call | solution.py:503
  66.4 4.4 %collective-permute-start.12 = (f32[8,256]{1,0:T(8,128)S(1)}, f32[8,256]{1,0:T(8,128)S(1)}, u32[]{:S(2)}, u32[]{:S(2)}) collective-permute-start(f32[8,256]{1,0:T(8,128)S(1)} %get-tuple-element.65.rest_0_), channel_id=1, source_target_pairs={{0,16},{8,24},{16,0},{24,8},{1,17},{9,25},{17,1},{25,9},{2,18},{10... | collective-permute-start | bytes 24584 | tf_op jit(solution)/shard_map/ppermute | solution.py:432
  70.8 0.9 %collective-permute-start.11 = (f32[8,256]{1,0:T(8,128)S(1)}, f32[8,256]{1,0:T(8,128)S(1)}, u32[]{:S(2)}, u32[]{:S(2)}) collective-permute-start(f32[8,256]{1,0:T(8,128)S(1)} %get-tuple-element.65.rest_0_), channel_id=1, source_target_pairs={{0,24},{8,0},{16,8},{24,16},{1,25},{9,1},{17,9},{25,17},{2,26},{10... | collective-permute-start | bytes 24584 | tf_op jit(solution)/shard_map/ppermute | solution.py:432
  71.7 6.1 %collective-permute-done.12.rest_2_ = f32[8,256]{1,0:T(8,128)S(1)} collective-permute-done((f32[8,256]{1,0:T(8,128)S(1)}, f32[8,256]{1,0:T(8,128)S(1)}, u32[]{:S(2)}, u32[]{:S(2)}) %collective-permute-start.12) | collective-permute-done | bytes 8224 | tf_op jit(solution)/shard_map/ppermute | solution.py:432
  77.7 2.5 %shard_map.50 = (f32[2,14,256,256]{3,2,1,0:T(8,128)}, f32[8,256]{1,0:T(8,128)S(1)}) custom-call(f32[28,256]{1,0:T(8,128)S(1)} %get-tuple-element.41.keep_ref, f32[2,14,256,256]{3,2,1,0:T(8,128)} %get-tuple-element.46._, f32[512,512]{1,0:T(8,128)S(1)} %get-tuple-element.45.c_ref, ...), custom_call_target="tpu_custom_call", output_to_operand_aliasing={{0}: (1, {})} | custom-call | tf_op jit(solution)/shard_map/pallas_call | solution.py:507
  80.2 1.1 %shard_map.51 = f32[2,14,256,256]{3,2,1,0:T(8,128)} custom-call(f32[28,256]{1,0:T(8,128)S(1)} %get-tuple-element.41.keep_ref, f32[2,14,256,256]{3,2,1,0:T(8,128)} %get-tuple-element.66._, f32[8,256]{1,0:T(8,128)S(1)} %get-tuple-element.67.twice_ref, f32[1024,512]{1,0:T(8,128)S(1)} %get-tuple-element.39.down_ref.e_ref, ...), custom_call_target="tpu_custom_call", output_to_operand_aliasing={{}: (1, {})} | custom-call | tf_op jit(solution)/shard_map/pallas_call | solution.py:511
  (13 shorter events, 0.2 us)
Async XLA Ops:
  2.6 32.9 %collective-permute-start.2 = (f32[1024,512]{1,0:T(8,128)S(1)}, f32[1024,512]{1,0:T(8,128)S(1)}, u32[]{:S(2)}, u32[]{:S(2)}) collective-permute-start(f32[1024,512]{1,0:T(8,128)S(1)} %get-tuple-element.39.down_ref.e_ref), channel_id=1, source_target_pairs={{0,7},{1,0},{2,1},{3,2},{4,3},{5,4},{6,5},{7,6},{8,15},{9,8},{10,9... | collective-permute-start | bytes 6291464 | tf_op jit(solution)/shard_map/ppermute | solution.py:432
  5.9 5.7 %copy-start = (s32[1,1,2,13]{3,2,1,0:T(2,128)S(1)}, s32[1,1,2,13]{3,2,1,0:T(2,128)}, u32[]{:S(2)}) copy-start(s32[1,1,2,13]{3,2,1,0:T(2,128)} %param.5) | copy-start | bytes 316
  5.9 38.8 %collective-permute-start.6 = (f32[776,512]{1,0:T(8,128)S(1)}, f32[776,512]{1,0:T(8,128)S(1)}, u32[]{:S(2)}, u32[]{:S(2)}) collective-permute-start(f32[776,512]{1,0:T(8,128)S(1)} %get-tuple-element.37._.t_ref), channel_id=1, source_target_pairs={{0,24},{8,0},{16,8},{24,16},{1,25},{9,1},{17,9},{25,17},{2,26},{10... | collective-permute-start | bytes 4767752 | tf_op jit(solution)/shard_map/ppermute | solution.py:432
  11.6 24.1 %collective-permute-start.5 = (f32[264,512]{1,0:T(8,128)S(1)}, f32[264,512]{1,0:T(8,128)S(1)}, u32[]{:S(2)}, u32[]{:S(2)}) collective-permute-start(f32[264,512]{1,0:T(8,128)S(1)} %get-tuple-element.38._), channel_id=1, source_target_pairs={{0,1},{1,2},{2,3},{3,4},{4,5},{5,6},{6,7},{7,0},{8,9},{9,10},{10,1... | collective-permute-start | bytes 1622024 | tf_op jit(solution)/shard_map/ppermute | solution.py:432
  12.8 1.2 %collective-permute-start = (f32[16,256]{1,0:T(8,128)S(1)}, f32[16,256]{1,0:T(8,128)S(1)}, u32[]{:S(2)}, u32[]{:S(2)}) collective-permute-start(f32[16,256]{1,0:T(8,128)S(1)} %get-tuple-element.42.sums_ref), channel_id=1, source_target_pairs={{0,1},{1,0},{2,3},{3,2},{4,5},{5,4},{6,7},{7,6},{8,9},{9,8},{10,11... | collective-permute-start | bytes 49160 | tf_op jit(solution)/shard_map/ppermute | solution.py:437
  17.9 4.0 %collective-permute-start.1 = (f32[16,256]{1,0:T(8,128)S(1)}, f32[16,256]{1,0:T(8,128)S(1)}, u32[]{:S(2)}, u32[]{:S(2)}) collective-permute-start(f32[16,256]{1,0:T(8,128)S(1)} %get-tuple-element.44.sums_ref), channel_id=1, source_target_pairs={{0,4},{1,5},{2,6},{3,7},{4,0},{5,1},{6,2},{7,3},{8,12},{9,13},{10,... | collective-permute-start | bytes 49160 | tf_op jit(solution)/shard_map/ppermute | solution.py:437
  29.8 5.9 %collective-permute-start.4 = (f32[16,256]{1,0:T(8,128)S(1)}, f32[16,256]{1,0:T(8,128)S(1)}, u32[]{:S(2)}, u32[]{:S(2)}) collective-permute-start(f32[16,256]{1,0:T(8,128)S(1)} %get-tuple-element.49.sums_ref), channel_id=1, source_target_pairs={{0,2},{1,3},{2,0},{3,1},{4,6},{5,7},{6,4},{7,5},{8,10},{9,11},{10,... | collective-permute-start | bytes 49160 | tf_op jit(solution)/shard_map/ppermute | solution.py:437
  35.5 12.1 %collective-permute-start.3 = (f32[272,512]{1,0:T(8,128)S(1)}, f32[272,512]{1,0:T(8,128)S(1)}, u32[]{:S(2)}, u32[]{:S(2)}) collective-permute-start(f32[272,512]{1,0:T(8,128)S(1)} %shard_map.42._), channel_id=1, source_target_pairs={{0,1},{1,2},{2,3},{3,4},{4,5},{5,6},{6,7},{7,0},{8,9},{9,10},{10,1... | collective-permute-start | bytes 1671176 | tf_op jit(solution)/shard_map/ppermute | solution.py:432
  37.5 40.3 %collective-permute-start.10 = (f32[776,512]{1,0:T(8,128)S(1)}, f32[776,512]{1,0:T(8,128)S(1)}, u32[]{:S(2)}, u32[]{:S(2)}) collective-permute-start(f32[776,512]{1,0:T(8,128)S(1)} %get-tuple-element.50._), channel_id=1, source_target_pairs={{0,8},{8,16},{16,24},{24,0},{1,9},{9,17},{17,25},{25,1},{2,10},{10... | collective-permute-start | bytes 4767752 | tf_op jit(solution)/shard_map/ppermute | solution.py:432
  39.3 10.1 %collective-permute-start.7 = (f32[264,512]{1,0:T(8,128)S(1)}, f32[264,512]{1,0:T(8,128)S(1)}, u32[]{:S(2)}, u32[]{:S(2)}) collective-permute-start(f32[264,512]{1,0:T(8,128)S(1)} %get-tuple-element.54), channel_id=1, source_target_pairs={{0,7},{1,0},{2,1},{3,2},{4,3},{5,4},{6,5},{7,6},{8,15},{9,8},{10,9... | collective-permute-start | bytes 1622024 | tf_op jit(solution)/shard_map/ppermute | solution.py:432
  47.5 24.2 %collective-permute-start.9 = (f32[512,512]{1,0:T(8,128)S(1)}, f32[512,512]{1,0:T(8,128)S(1)}, u32[]{:S(2)}, u32[]{:S(2)}) collective-permute-start(f32[512,512]{1,0:T(8,128)S(1)} %get-tuple-element.52.__), channel_id=1, source_target_pairs={{0,1},{1,2},{2,3},{3,4},{4,5},{5,6},{6,7},{7,0},{8,9},{9,10},{10,1... | collective-permute-start | bytes 3145736 | tf_op jit(solution)/shard_map/ppermute | solution.py:432
  47.6 32.6 %collective-permute-start.13 = (f32[512,512]{1,0:T(8,128)S(1)}, f32[512,512]{1,0:T(8,128)S(1)}, u32[]{:S(2)}, u32[]{:S(2)}) collective-permute-start(f32[512,512]{1,0:T(8,128)S(1)} %shard_map.45._), channel_id=1, source_target_pairs={{0,1},{1,2},{2,3},{3,4},{4,5},{5,6},{6,7},{7,0},{8,9},{9,10},{10,1... | collective-permute-start | bytes 3145736 | tf_op jit(solution)/shard_map/ppermute | solution.py:432
  49.4 15.9 %collective-permute-start.8 = (f32[264,512]{1,0:T(8,128)S(1)}, f32[264,512]{1,0:T(8,128)S(1)}, u32[]{:S(2)}, u32[]{:S(2)}) collective-permute-start(f32[264,512]{1,0:T(8,128)S(1)} %shard_map.46._), channel_id=1, source_target_pairs={{0,7},{1,0},{2,1},{3,2},{4,3},{5,4},{6,5},{7,6},{8,15},{9,8},{10,9... | collective-permute-start | bytes 1622024 | tf_op jit(solution)/shard_map/ppermute | solution.py:432
  66.4 11.4 %collective-permute-start.12 = (f32[8,256]{1,0:T(8,128)S(1)}, f32[8,256]{1,0:T(8,128)S(1)}, u32[]{:S(2)}, u32[]{:S(2)}) collective-permute-start(f32[8,256]{1,0:T(8,128)S(1)} %get-tuple-element.65.rest_0_), channel_id=1, source_target_pairs={{0,16},{8,24},{16,0},{24,8},{1,17},{9,25},{17,1},{25,9},{2,18},{10... | collective-permute-start | bytes 24584 | tf_op jit(solution)/shard_map/ppermute | solution.py:432
  70.8 7.0 %collective-permute-start.11 = (f32[8,256]{1,0:T(8,128)S(1)}, f32[8,256]{1,0:T(8,128)S(1)}, u32[]{:S(2)}, u32[]{:S(2)}) collective-permute-start(f32[8,256]{1,0:T(8,128)S(1)} %get-tuple-element.65.rest_0_), channel_id=1, source_target_pairs={{0,24},{8,0},{16,8},{24,16},{1,25},{9,1},{17,9},{25,17},{2,26},{10... | collective-permute-start | bytes 24584 | tf_op jit(solution)/shard_map/ppermute | solution.py:432

commit v9 on v8

--- a/solution.py
+++ b/solution.py
@@ -372,24 +372,48 @@
         self.twice, self.keep_ref, self.out_ref, self.held, self.sems = twice, keep_ref, out_ref, held, sems
         self.copies = []
 
-    def send(self, y, a, low, slot):
-        k, at = len(self.copies), low * self.out_ref.shape[1] + slot
-        self.held[k] = self.keep_ref[at : at + 1, :] * (y + self.twice * (a - y))
+    def put(self, value, low, slot):
+        k = len(self.copies)
+        self.held[k] = value
         self.copies.append(pltpu.make_async_copy(self.held.at[k], self.out_ref.at[low, slot], self.sems.at[k]))
         self.copies[-1].start()
+
+    def send(self, y, a, low, slot):
+        at = low * self.out_ref.shape[1] + slot
+        self.put(self.keep_ref[at : at + 1, :] * (y + self.twice * (a - y)), low, slot)
 
     def send_panel(self, name, a_ref, terms, layers, size):
         for low, high, slot in panel_blocks(name, layers):
             rows, cols = slice(low * size, (low + 1) * size), slice(high * size, (high + 1) * size)
             self.send(sum(ref[rows, cols] for ref in terms), a_ref[rows, cols], low, slot)
 
+    def send_ready(self, name, y_ref, gap_ref, layers, size):
+        for low, high, slot in panel_blocks(name, layers):
+            rows, cols = slice(low * size, (low + 1) * size), slice(high * size, (high + 1) * size)
+            self.put(y_ref[rows, cols] + self.twice * gap_ref[rows, cols], low, slot)
+
     def wait(self):
         for copy in self.copies:
             copy.wait()
 
 
+def ready_body(layers, size, keep_ref, _, sums_ref, d_ref, e_ref, yd_ref, ye_ref, re_ref, total_ref, *outs):
+    n, slots = layers * size, keep_ref.shape[0] // layers
+    total_ref[...] = sums_ref[...]
+    for name, a_ref, terms, y_out, gap_out in (
+        ("D", d_ref, [yd_ref], *outs[:2]),
+        ("E", e_ref.at[n:, :], [ye_ref, re_ref], *outs[2:]),
+    ):
+        for low, high, slot in panel_blocks(name, layers):
+            rows, cols = slice(low * size, (low + 1) * size), slice(high * size, (high + 1) * size)
+            at = low * slots + slot
+            y = keep_ref[at : at + 1, :] * sum(ref[rows, cols] for ref in terms)
+            y_out[rows, cols] = y
+            gap_out[rows, cols] = a_ref[rows, cols] - y
+
+
 def last_c_body(
-    target, layers, size, keep_ref, _, c_ref, t_ref, e_ref, d_ref, yc_ref, yn_ref, ye_ref, yd_ref, yc_in_ref, re_ref, g_ref, *rest
+    target, layers, size, keep_ref, _, c_ref, t_ref, yc_ref, yn_ref, yc_in_ref, g_ref, pd_ref, qd_ref, pe_ref, qe_ref, *rest
 ):
     *sums_refs, out_ref, twice_ref, held, sems = rest
     n, last = layers * size, g_ref.shape[0] - 8
@@ -399,8 +423,8 @@
     twice = twice_h(target, size, sum((ref[...] for ref in sums_refs), start=sums))
     twice_ref[...] = jnp.broadcast_to(twice, twice_ref.shape)
     sender = Sender(twice, keep_ref, out_ref, held, sems)
-    sender.send_panel("D", d_ref, [yd_ref], layers, size)
-    sender.send_panel("E", e_ref.at[n:, :], [ye_ref, re_ref], layers, size)
+    sender.send_ready("D", pd_ref, qd_ref, layers, size)
+    sender.send_ready("E", pe_ref, qe_ref, layers, size)
     sender.send_panel("N", t_ref, [yn_ref, g_ref], layers, size)
     blocks = take_sym(yc_ref[...] + yc_in_ref[: yc_ref.shape[0], :] + g_ref[n:, :], layers, size)
     for low, high, slot in panel_blocks("C", layers) + [(layer, layer, 0) for layer in range(layers)]:
@@ -502,12 +526,15 @@
     ye, yd = go(middle_body, outs=[panel, panel], spaces=[hbm] + [vmem] * 5)(yn, down, D, T_x, ye, yd)
     own, yd = go(middle_c_body, outs=[total, panel], spaces=[hbm] + [vmem] * 4)(ye, own, D, Cp_xu, yd)
     every = [own] + [passed_along(own, "row", -by) for by in range(1, lax.axis_size("row") - 1)]
+    _, *ready = go(ready_body, outs=[total] + [panel] * 4, spaces=[vmem, hbm] + [vmem] * 6)(
+        keep, yd, own, D, down, yd, ye, re_in
+    )
     cells = lax.axis_size("row") * lax.axis_size("col") * layers
     target = float(cells * size // 2)
     out, twice = go(
         functools.partial(last_c_body, target), outs=[out.shape, total], out_spaces=[hbm, vmem],
-        spaces=[vmem, hbm] + [vmem] * (11 + len(every)), scratch=blocks(len(wanted("CNED", layers))), aliases={1: 0},
-    )(keep, out, C, T, down, D, yc, yn, ye, yd, yc_in, re_in, g_in, *every)
+        spaces=[vmem, hbm] + [vmem] * (10 + len(every)), scratch=blocks(len(wanted("CNED", layers))), aliases={1: 0},
+    )(keep, out, C, T, yc, yn, yc_in, g_in, *ready, *every)
     (out,) = go(
         last_s_body, outs=[out.shape], out_spaces=[hbm], spaces=[vmem, hbm] + [vmem] * 4,
         scratch=blocks(count["S"]), aliases={1: 0},

time: 81.6 us -> 81.3 us (level)
  waiting for transfers between devices: 24.6 us -> 23.7 us
    pallas_call x0 -> x1, Pallas kernels: none -> 0.97 us  [shards(): go(ready_body, outs=[total] + [panel] * 4, spaces=[vmem, hbm] + [vmem] * 6)]
    ppermute x11, waiting for transfers between devices: 20.4 us -> 19.6 us  [passed_along(): lax.ppermute(value, axis, [(i, (i + by) % peers) for i in range(peers)])]
  transfers between devices with their start and end apart: 14 -> 14, of which waited for: 7 -> 7; matrix products, arithmetic and copies ran while one was open for 0% -> 0% of each run, Pallas kernels for 37% -> 38%
where the time goes in v9:
time: 81.3 us; the launch traced here: 81.1 us
  Pallas kernels  34.2 us (42%)
  waiting for transfers between devices  23.7 us (29%)
  starting transfers between devices  22.9 us (28%)
    ppermute x11, starting transfers between devices, passed_along(): lax.ppermute(value, axis, [(i, (i + by) % peers) for i in range(peers)])  20 us
    ppermute x11, waiting for transfers between devices, passed_along(): lax.ppermute(value, axis, [(i, (i + by) % peers) for i in range(peers)])  19.6 us
    pallas_call x1, Pallas kernels, shards(): go(local_y_body, outs=[sums, (layers, slots, size, size), packed] + [pane...  7.91 us
    pallas_call x1, Pallas kernels, shards(): go(early_body, outs=[panel] * 3, spaces=[hbm] + [vmem] * 8)  4.26 us
    ppermute x3, waiting for transfers between devices, swapped(): return lax.ppermute(value, axis, [(i, i ^ bit) for i in range(peers)])  4.11 us
    pallas_call x1, Pallas kernels, shards(): go(local_g_body, outs=[sums, (n + tall, n), (2 * n, n), packed], spaces=[...  3.88 us
    ppermute x3, starting transfers between devices, swapped(): return lax.ppermute(value, axis, [(i, i ^ bit) for i in range(peers)])  2.88 us
    pallas_call x1, Pallas kernels, shards(): go(middle_body, outs=[panel, panel], spaces=[hbm] + [vmem] * 5)  2.73 us
  transfers between devices with their start and end apart: 14, of which 7 were waited for; matrix products, arithmetic and copies ran while one was open for 0% of the time, Pallas kernels for 38%

profile of v9, /device:TPU:0, one launch (start us, length us, event | category | flops | bytes accessed | tf_op | source)
XLA Modules:
  0.0 81.1 jit_solution(9481232798125844573)
XLA Ops:
  0.0 2.5 %shard_map.37 = (f32[776,512]{1,0:T(8,128)S(1)}, f32[1024,512]{1,0:T(8,128)S(1)}) custom-call(s32[2,13]{1,0:T(2,128)} %bitcast.4, f32[2,14,256,256]{3,2,1,0:T(8,128)} %bitcast.7, f32[2,256]{1,0:T(2,128)} %bitcast.9), custom_call_target="tpu_custom_call" | custom-call | tf_op jit(solution)/shard_map/pallas_call | solution.py:486
  2.5 3.4 %collective-permute-start.2 = (f32[1024,512]{1,0:T(8,128)S(1)}, f32[1024,512]{1,0:T(8,128)S(1)}, u32[]{:S(2)}, u32[]{:S(2)}) collective-permute-start(f32[1024,512]{1,0:T(8,128)S(1)} %get-tuple-element.43.down_ref.e_ref), channel_id=1, source_target_pairs={{0,7},{1,0},{2,1},{3,2},{4,3},{5,4},{6,5},{7,6},{8,15},{9,8},{10,9... | collective-permute-start | bytes 6291464 | tf_op jit(solution)/shard_map/ppermute | solution.py:456
  5.9 3.6 %collective-permute-start.6 = (f32[776,512]{1,0:T(8,128)S(1)}, f32[776,512]{1,0:T(8,128)S(1)}, u32[]{:S(2)}, u32[]{:S(2)}) collective-permute-start(f32[776,512]{1,0:T(8,128)S(1)} %get-tuple-element.41._.t_ref), channel_id=1, source_target_pairs={{0,24},{8,0},{16,8},{24,16},{1,25},{9,1},{17,9},{25,17},{2,26},{10... | collective-permute-start | bytes 4767752 | tf_op jit(solution)/shard_map/ppermute | solution.py:456
  9.5 2.1 %shard_map.38 = (f32[512,512]{1,0:T(8,128)S(1)}, f32[264,512]{1,0:T(8,128)S(1)}) custom-call(s32[2,13]{1,0:T(2,128)} %bitcast.5, f32[2,14,256,256]{3,2,1,0:T(8,128)} %bitcast.8, f32[776,512]{1,0:T(8,128)S(1)} %get-tuple-element.41._.t_ref), custom_call_target="tpu_custom_call" | custom-call | tf_op jit(solution)/shard_map/pallas_call | solution.py:493
  11.7 1.1 %shard_map.39 = (f32[264,512]{1,0:T(8,128)S(1)}, f32[512,512]{1,0:T(8,128)S(1)}, f32[28,256]{1,0:T(8,128)S(1)}, f32[16,256]{1,0:T(8,128)S(1)}) custom-call(s32[2,13]{1,0:T(2,128)S(1)} %bitcast.6, f32[264,512]{1,0:T(8,128)S(1)} %get-tuple-element.42._, f32[1024,512]{1,0:T(8,128)S(1)} %get-tuple-element.43.down_ref.e_ref, ...), custom_call_target="tpu_custom_call" | custom-call | tf_op jit(solution)/shard_map/pallas_call | solution.py:497
  12.8 0.1 collective-permute-start
  12.8 1.2 %collective-permute-done.more_ref = f32[16,256]{1,0:T(8,128)S(1)} collective-permute-done((f32[16,256]{1,0:T(8,128)S(1)}, f32[16,256]{1,0:T(8,128)S(1)}, u32[]{:S(2)}, u32[]{:S(2)}) %collective-permute-start) | collective-permute-done | bytes 16416 | tf_op jit(solution)/shard_map/ppermute | solution.py:461
  14.0 3.9 %shard_map.40 = (f32[16,256]{1,0:T(8,128)S(1)}, f32[776,512]{1,0:T(8,128)S(1)}, f32[1024,512]{1,0:T(8,128)S(1)}, f32[264,512]{1,0:T(8,128)S(1)}) custom-call(f32[264,512]{1,0:T(8,128)S(1)} %get-tuple-element.42._, f32[16,256]{1,0:T(8,128)S(1)} %get-tuple-element.46.sums_ref, f32[16,256]{1,0:T(8,128)S(1)} %collective-permute-done.more_ref, ...), custom_call_target="tpu_custom_call" | custom-call | tf_op jit(solution)/shard_map/pallas_call | solution.py:506
  17.9 1.0 %collective-permute-start.1 = (f32[16,256]{1,0:T(8,128)S(1)}, f32[16,256]{1,0:T(8,128)S(1)}, u32[]{:S(2)}, u32[]{:S(2)}) collective-permute-start(f32[16,256]{1,0:T(8,128)S(1)} %get-tuple-element.48.sums_ref), channel_id=1, source_target_pairs={{0,4},{1,5},{2,6},{3,7},{4,0},{5,1},{6,2},{7,3},{8,12},{9,13},{10,... | collective-permute-start | bytes 49160 | tf_op jit(solution)/shard_map/ppermute | solution.py:461
  18.9 2.9 %collective-permute-done.1.more_ref = f32[16,256]{1,0:T(8,128)S(1)} collective-permute-done((f32[16,256]{1,0:T(8,128)S(1)}, f32[16,256]{1,0:T(8,128)S(1)}, u32[]{:S(2)}, u32[]{:S(2)}) %collective-permute-start.1) | collective-permute-done | bytes 16416 | tf_op jit(solution)/shard_map/ppermute | solution.py:461
  21.9 7.9 %shard_map.41 = (f32[16,256]{1,0:T(8,128)S(1)}, f32[2,14,256,256]{3,2,1,0:T(8,128)}, f32[264,512]{1,0:T(8,128)S(1)}, f32[512,512]{1,0:T(8,128)S(1)}, f32[512,512...) custom-call(f32[776,512]{1,0:T(8,128)S(1)} %get-tuple-element.47._.g0_ref, ...), custom_call_target="tpu_custom_call" | custom-call | tf_op jit(solution)/shard_map/pallas_call | solution.py:510
  29.8 1.8 %collective-permute-start.4 = (f32[16,256]{1,0:T(8,128)S(1)}, f32[16,256]{1,0:T(8,128)S(1)}, u32[]{:S(2)}, u32[]{:S(2)}) collective-permute-start(f32[16,256]{1,0:T(8,128)S(1)} %get-tuple-element.53.sums_ref), channel_id=1, source_target_pairs={{0,2},{1,3},{2,0},{3,1},{4,6},{5,7},{6,4},{7,5},{8,10},{9,11},{10,... | collective-permute-start | bytes 49160 | tf_op jit(solution)/shard_map/ppermute | solution.py:461
  31.6 3.9 %collective-permute-done.2.__.below_ref = f32[1024,512]{1,0:T(8,128)S(1)} collective-permute-done((f32[1024,512]{1,0:T(8,128)S(1)}, f32[1024,512]{1,0:T(8,128)S(1)}, u32[]{:S(2)}, u32[]{:S(2)}) %collective-permute-start.2) | collective-permute-done | bytes 2097184 | tf_op jit(solution)/shard_map/ppermute | solution.py:456
  35.5 0.2 collective-permute-start.3
  35.7 1.7 %shard_map.43 = (f32[8,256]{1,0:T(8,128)S(1)}, f32[776,512]{1,0:T(8,128)S(1)}) custom-call(f32[272,512]{1,0:T(8,128)S(1)} %shard_map.42._, f32[16,256]{1,0:T(8,128)S(1)} %get-tuple-element.53.sums_ref, f32[16,256]{1,0:T(8,128)S(1)} %collective-permute-done.4.more_ref, f32[776,512]{1,0:T(8,128)S(1)} %get-tuple-element.47._.g0_ref, ...), custom_call_target="tpu_custom_call" | custom-call | tf_op jit(solution)/shard_map/pallas_call | solution.py:517
  37.4 1.8 %collective-permute-start.8 = (f32[776,512]{1,0:T(8,128)S(1)}, f32[776,512]{1,0:T(8,128)S(1)}, u32[]{:S(2)}, u32[]{:S(2)}) collective-permute-start(f32[776,512]{1,0:T(8,128)S(1)} %get-tuple-element.54._), channel_id=1, source_target_pairs={{0,8},{8,16},{16,24},{24,0},{1,9},{9,17},{17,25},{25,1},{2,10},{10... | collective-permute-start | bytes 4767752 | tf_op jit(solution)/shard_map/ppermute | solution.py:456
  39.3 2.4 %collective-permute-start.7 = (f32[264,512]{1,0:T(8,128)S(1)}, f32[264,512]{1,0:T(8,128)S(1)}, u32[]{:S(2)}, u32[]{:S(2)}) collective-permute-start(f32[264,512]{1,0:T(8,128)S(1)} %get-tuple-element.58), channel_id=1, source_target_pairs={{0,7},{1,0},{2,1},{3,2},{4,3},{5,4},{6,5},{7,6},{8,15},{9,8},{10,9... | collective-permute-start | bytes 1622024 | tf_op jit(solution)/shard_map/ppermute | solution.py:456
  41.6 3.1 %collective-permute-done.6.tx_ref = f32[776,512]{1,0:T(8,128)S(1)} collective-permute-done((f32[776,512]{1,0:T(8,128)S(1)}, f32[776,512]{1,0:T(8,128)S(1)}, u32[]{:S(2)}, u32[]{:S(2)}) %collective-permute-start.6) | collective-permute-done | bytes 1589280 | tf_op jit(solution)/shard_map/ppermute | solution.py:456
  44.7 2.7 %shard_map.44 = (f32[512,512]{1,0:T(8,128)S(1)}, f32[512,512]{1,0:T(8,128)S(1)}) custom-call(f32[776,512]{1,0:T(8,128)S(1)} %get-tuple-element.54._, f32[1024,512]{1,0:T(8,128)S(1)} %get-tuple-element.55.r0_ref, f32[1024,512]{1,0:T(8,128)S(1)} %collective-permute-done.2.__.below_ref, f32[776,512]{1,0:T(8,128)S(1)} %collective-permute-done.6.tx_ref), custom_call_target="tpu_custom_call" | custom-call | tf_op jit(solution)/shard_map/pallas_call | solution.py:520
  47.5 0.1 shard_map.45._
  47.7 1.7 %collective-permute-done.7.__.cu_ref = f32[264,512]{1,0:T(8,128)S(1)} collective-permute-done((f32[264,512]{1,0:T(8,128)S(1)}, f32[264,512]{1,0:T(8,128)S(1)}, u32[]{:S(2)}, u32[]{:S(2)}) %collective-permute-start.7) | collective-permute-done | bytes 540704 | tf_op jit(solution)/shard_map/ppermute | solution.py:456
  49.4 3.2 %collective-permute-start.9 = (f32[264,512]{1,0:T(8,128)S(1)}, f32[264,512]{1,0:T(8,128)S(1)}, u32[]{:S(2)}, u32[]{:S(2)}) collective-permute-start(f32[264,512]{1,0:T(8,128)S(1)} %shard_map.46._), channel_id=1, source_target_pairs={{0,7},{1,0},{2,1},{3,2},{4,3},{5,4},{6,5},{7,6},{8,15},{9,8},{10,9... | collective-permute-start | bytes 1622024 | tf_op jit(solution)/shard_map/ppermute | solution.py:456
  52.6 4.3 %shard_map.47 = (f32[512,512]{1,0:T(8,128)S(1)}, f32[512,512]{1,0:T(8,128)S(1)}, f32[512,512]{1,0:T(8,128)S(1)}) custom-call(f32[264,512]{1,0:T(8,128)S(1)} %shard_map.46._, f32[776,512]{1,0:T(8,128)S(1)} %get-tuple-element.41._.t_ref, f32[1024,512]{1,0:T(8,128)S(1)} %get-tuple-element.43.down_ref.e_ref, f32[512,512]{1,0:T(8,128)S(1)} %get-tuple-element.44.d_ref, ...), custom_call_target="tpu_custom_call" | custom-call | tf_op jit(solution)/shard_map/pallas_call | solution.py:525
  56.8 2.7 %shard_map.48 = (f32[512,512]{1,0:T(8,128)S(1)}, f32[512,512]{1,0:T(8,128)S(1)}) custom-call(f32[512,512]{1,0:T(8,128)S(1)} %get-tuple-element.62._.yn_ref, f32[1024,512]{1,0:T(8,128)S(1)} %get-tuple-element.43.down_ref.e_ref, f32[512,512]{1,0:T(8,128)S(1)} %get-tuple-element.44.d_ref, f32[776,512]{1,0:T(8,128)S(1)} %collective-permute-done.6.tx_ref, ...), custom_call_target="tpu_custom_call" | custom-call | tf_op jit(solution)/shard_map/pallas_call | solution.py:526
  59.6 5.7 %collective-permute-done.9.cxu_ref = f32[264,512]{1,0:T(8,128)S(1)} collective-permute-done((f32[264,512]{1,0:T(8,128)S(1)}, f32[264,512]{1,0:T(8,128)S(1)}, u32[]{:S(2)}, u32[]{:S(2)}) %collective-permute-start.9) | collective-permute-done | bytes 540704 | tf_op jit(solution)/shard_map/ppermute | solution.py:456
  65.3 1.1 %shard_map.49 = (f32[8,256]{1,0:T(8,128)S(1)}, f32[512,512]{1,0:T(8,128)S(1)}) custom-call(f32[512,512]{1,0:T(8,128)S(1)} %get-tuple-element.65._.ye_ref, f32[8,256]{1,0:T(8,128)S(1)} %get-tuple-element.66.sums_ref, f32[512,512]{1,0:T(8,128)S(1)} %get-tuple-element.44.d_ref, f32[264,512]{1,0:T(8,128)S(1)} %collective-permute-done.9.cxu_ref, ...), custom_call_target="tpu_custom_call" | custom-call | tf_op jit(solution)/shard_map/pallas_call | solution.py:527
  66.4 4.3 %collective-permute-start.12 = (f32[8,256]{1,0:T(8,128)S(1)}, f32[8,256]{1,0:T(8,128)S(1)}, u32[]{:S(2)}, u32[]{:S(2)}) collective-permute-start(f32[8,256]{1,0:T(8,128)S(1)} %get-tuple-element.69.sums_ref.rest_0_), channel_id=1, source_target_pairs={{0,16},{8,24},{16,0},{24,8},{1,17},{9,25},{17,1},{25,9},{2,18},{10... | collective-permute-start | bytes 24584 | tf_op jit(solution)/shard_map/ppermute | solution.py:456
  70.7 1.0 %collective-permute-start.11 = (f32[8,256]{1,0:T(8,128)S(1)}, f32[8,256]{1,0:T(8,128)S(1)}, u32[]{:S(2)}, u32[]{:S(2)}) collective-permute-start(f32[8,256]{1,0:T(8,128)S(1)} %get-tuple-element.69.sums_ref.rest_0_), channel_id=1, source_target_pairs={{0,24},{8,0},{16,8},{24,16},{1,25},{9,1},{17,9},{25,17},{2,26},{10... | collective-permute-start | bytes 24584 | tf_op jit(solution)/shard_map/ppermute | solution.py:456
  71.6 1.0 %shard_map.50 = (f32[8,256]{1,0:T(8,128)}, f32[512,512]{1,0:T(8,128)S(1)}, f32[512,512]{1,0:T(8,128)S(1)}, f32[512,512]{1,0:T(8,128)S(1)}, f32[512,512]{1,0:T(8,128)S(1)}) custom-call(f32[28,256]{1,0:T(8,128)S(1)} %get-tuple-element.45.keep_ref, f32[512,512]{1,0:T(8,128)S(1)} %get-tuple-element.68._.yd_ref, f32[8,256]{1,0:T(8,128)S(1)} %get-tuple-element.69.sums_ref.rest_0_, ...), custom_call_target="tpu_custom_call" | custom-call | tf_op jit(solution)/shard_map/pallas_call | solution.py:529
  72.6 5.1 %collective-permute-done.12.rest_2_ = f32[8,256]{1,0:T(8,128)S(1)} collective-permute-done((f32[8,256]{1,0:T(8,128)S(1)}, f32[8,256]{1,0:T(8,128)S(1)}, u32[]{:S(2)}, u32[]{:S(2)}) %collective-permute-start.12) | collective-permute-done | bytes 8224 | tf_op jit(solution)/shard_map/ppermute | solution.py:456
  77.7 2.1 %shard_map.51 = (f32[2,14,256,256]{3,2,1,0:T(8,128)}, f32[8,256]{1,0:T(8,128)S(1)}) custom-call(f32[28,256]{1,0:T(8,128)S(1)} %get-tuple-element.45.keep_ref, f32[2,14,256,256]{3,2,1,0:T(8,128)} %get-tuple-element.50._, f32[512,512]{1,0:T(8,128)S(1)} %get-tuple-element.49.c_ref, ...), custom_call_target="tpu_custom_call", output_to_operand_aliasing={{0}: (1, {})} | custom-call | tf_op jit(solution)/shard_map/pallas_call | solution.py:534
  79.9 1.1 %shard_map.52 = f32[2,14,256,256]{3,2,1,0:T(8,128)} custom-call(f32[28,256]{1,0:T(8,128)S(1)} %get-tuple-element.45.keep_ref, f32[2,14,256,256]{3,2,1,0:T(8,128)} %get-tuple-element.74._, f32[8,256]{1,0:T(8,128)S(1)} %get-tuple-element.75.twice_ref, f32[1024,512]{1,0:T(8,128)S(1)} %get-tuple-element.43.down_ref.e_ref, ...), custom_call_target="tpu_custom_call", output_to_operand_aliasing={{}: (1, {})} | custom-call | tf_op jit(solution)/shard_map/pallas_call | solution.py:538
  (14 shorter events, 0.3 us)
Async XLA Ops:
  2.5 32.9 %collective-permute-start.2 = (f32[1024,512]{1,0:T(8,128)S(1)}, f32[1024,512]{1,0:T(8,128)S(1)}, u32[]{:S(2)}, u32[]{:S(2)}) collective-permute-start(f32[1024,512]{1,0:T(8,128)S(1)} %get-tuple-element.43.down_ref.e_ref), channel_id=1, source_target_pairs={{0,7},{1,0},{2,1},{3,2},{4,3},{5,4},{6,5},{7,6},{8,15},{9,8},{10,9... | collective-permute-start | bytes 6291464 | tf_op jit(solution)/shard_map/ppermute | solution.py:456
  5.9 5.7 %copy-start = (s32[1,1,2,13]{3,2,1,0:T(2,128)S(1)}, s32[1,1,2,13]{3,2,1,0:T(2,128)}, u32[]{:S(2)}) copy-start(s32[1,1,2,13]{3,2,1,0:T(2,128)} %param.5) | copy-start | bytes 316
  5.9 38.8 %collective-permute-start.6 = (f32[776,512]{1,0:T(8,128)S(1)}, f32[776,512]{1,0:T(8,128)S(1)}, u32[]{:S(2)}, u32[]{:S(2)}) collective-permute-start(f32[776,512]{1,0:T(8,128)S(1)} %get-tuple-element.41._.t_ref), channel_id=1, source_target_pairs={{0,24},{8,0},{16,8},{24,16},{1,25},{9,1},{17,9},{25,17},{2,26},{10... | collective-permute-start | bytes 4767752 | tf_op jit(solution)/shard_map/ppermute | solution.py:456
  11.6 24.1 %collective-permute-start.5 = (f32[264,512]{1,0:T(8,128)S(1)}, f32[264,512]{1,0:T(8,128)S(1)}, u32[]{:S(2)}, u32[]{:S(2)}) collective-permute-start(f32[264,512]{1,0:T(8,128)S(1)} %get-tuple-element.42._), channel_id=1, source_target_pairs={{0,1},{1,2},{2,3},{3,4},{4,5},{5,6},{6,7},{7,0},{8,9},{9,10},{10,1... | collective-permute-start | bytes 1622024 | tf_op jit(solution)/shard_map/ppermute | solution.py:456
  12.8 1.2 %collective-permute-start = (f32[16,256]{1,0:T(8,128)S(1)}, f32[16,256]{1,0:T(8,128)S(1)}, u32[]{:S(2)}, u32[]{:S(2)}) collective-permute-start(f32[16,256]{1,0:T(8,128)S(1)} %get-tuple-element.46.sums_ref), channel_id=1, source_target_pairs={{0,1},{1,0},{2,3},{3,2},{4,5},{5,4},{6,7},{7,6},{8,9},{9,8},{10,11... | collective-permute-start | bytes 49160 | tf_op jit(solution)/shard_map/ppermute | solution.py:461
  17.9 4.0 %collective-permute-start.1 = (f32[16,256]{1,0:T(8,128)S(1)}, f32[16,256]{1,0:T(8,128)S(1)}, u32[]{:S(2)}, u32[]{:S(2)}) collective-permute-start(f32[16,256]{1,0:T(8,128)S(1)} %get-tuple-element.48.sums_ref), channel_id=1, source_target_pairs={{0,4},{1,5},{2,6},{3,7},{4,0},{5,1},{6,2},{7,3},{8,12},{9,13},{10,... | collective-permute-start | bytes 49160 | tf_op jit(solution)/shard_map/ppermute | solution.py:461
  29.8 5.9 %collective-permute-start.4 = (f32[16,256]{1,0:T(8,128)S(1)}, f32[16,256]{1,0:T(8,128)S(1)}, u32[]{:S(2)}, u32[]{:S(2)}) collective-permute-start(f32[16,256]{1,0:T(8,128)S(1)} %get-tuple-element.53.sums_ref), channel_id=1, source_target_pairs={{0,2},{1,3},{2,0},{3,1},{4,6},{5,7},{6,4},{7,5},{8,10},{9,11},{10,... | collective-permute-start | bytes 49160 | tf_op jit(solution)/shard_map/ppermute | solution.py:461
  35.5 12.0 %collective-permute-start.3 = (f32[272,512]{1,0:T(8,128)S(1)}, f32[272,512]{1,0:T(8,128)S(1)}, u32[]{:S(2)}, u32[]{:S(2)}) collective-permute-start(f32[272,512]{1,0:T(8,128)S(1)} %shard_map.42._), channel_id=1, source_target_pairs={{0,1},{1,2},{2,3},{3,4},{4,5},{5,6},{6,7},{7,0},{8,9},{9,10},{10,1... | collective-permute-start | bytes 1671176 | tf_op jit(solution)/shard_map/ppermute | solution.py:456
  37.4 40.3 %collective-permute-start.8 = (f32[776,512]{1,0:T(8,128)S(1)}, f32[776,512]{1,0:T(8,128)S(1)}, u32[]{:S(2)}, u32[]{:S(2)}) collective-permute-start(f32[776,512]{1,0:T(8,128)S(1)} %get-tuple-element.54._), channel_id=1, source_target_pairs={{0,8},{8,16},{16,24},{24,0},{1,9},{9,17},{17,25},{25,1},{2,10},{10... | collective-permute-start | bytes 4767752 | tf_op jit(solution)/shard_map/ppermute | solution.py:456
  39.3 10.1 %collective-permute-start.7 = (f32[264,512]{1,0:T(8,128)S(1)}, f32[264,512]{1,0:T(8,128)S(1)}, u32[]{:S(2)}, u32[]{:S(2)}) collective-permute-start(f32[264,512]{1,0:T(8,128)S(1)} %get-tuple-element.58), channel_id=1, source_target_pairs={{0,7},{1,0},{2,1},{3,2},{4,3},{5,4},{6,5},{7,6},{8,15},{9,8},{10,9... | collective-permute-start | bytes 1622024 | tf_op jit(solution)/shard_map/ppermute | solution.py:456
  47.5 24.2 %collective-permute-start.10 = (f32[512,512]{1,0:T(8,128)S(1)}, f32[512,512]{1,0:T(8,128)S(1)}, u32[]{:S(2)}, u32[]{:S(2)}) collective-permute-start(f32[512,512]{1,0:T(8,128)S(1)} %get-tuple-element.56.__), channel_id=1, source_target_pairs={{0,1},{1,2},{2,3},{3,4},{4,5},{5,6},{6,7},{7,0},{8,9},{9,10},{10,1... | collective-permute-start | bytes 3145736 | tf_op jit(solution)/shard_map/ppermute | solution.py:456
  47.6 32.3 %collective-permute-start.13 = (f32[512,512]{1,0:T(8,128)S(1)}, f32[512,512]{1,0:T(8,128)S(1)}, u32[]{:S(2)}, u32[]{:S(2)}) collective-permute-start(f32[512,512]{1,0:T(8,128)S(1)} %shard_map.45._), channel_id=1, source_target_pairs={{0,1},{1,2},{2,3},{3,4},{4,5},{5,6},{6,7},{7,0},{8,9},{9,10},{10,1... | collective-permute-start | bytes 3145736 | tf_op jit(solution)/shard_map/ppermute | solution.py:456
  49.4 15.9 %collective-permute-start.9 = (f32[264,512]{1,0:T(8,128)S(1)}, f32[264,512]{1,0:T(8,128)S(1)}, u32[]{:S(2)}, u32[]{:S(2)}) collective-permute-start(f32[264,512]{1,0:T(8,128)S(1)} %shard_map.46._), channel_id=1, source_target_pairs={{0,7},{1,0},{2,1},{3,2},{4,3},{5,4},{6,5},{7,6},{8,15},{9,8},{10,9... | collective-permute-start | bytes 1622024 | tf_op jit(solution)/shard_map/ppermute | solution.py:456
  66.4 11.4 %collective-permute-start.12 = (f32[8,256]{1,0:T(8,128)S(1)}, f32[8,256]{1,0:T(8,128)S(1)}, u32[]{:S(2)}, u32[]{:S(2)}) collective-permute-start(f32[8,256]{1,0:T(8,128)S(1)} %get-tuple-element.69.sums_ref.rest_0_), channel_id=1, source_target_pairs={{0,16},{8,24},{16,0},{24,8},{1,17},{9,25},{17,1},{25,9},{2,18},{10... | collective-permute-start | bytes 24584 | tf_op jit(solution)/shard_map/ppermute | solution.py:456
  70.7 7.1 %collective-permute-start.11 = (f32[8,256]{1,0:T(8,128)S(1)}, f32[8,256]{1,0:T(8,128)S(1)}, u32[]{:S(2)}, u32[]{:S(2)}) collective-permute-start(f32[8,256]{1,0:T(8,128)S(1)} %get-tuple-element.69.sums_ref.rest_0_), channel_id=1, source_target_pairs={{0,24},{8,0},{16,8},{24,16},{1,25},{9,1},{17,9},{25,17},{2,26},{10... | collective-permute-start | bytes 24584 | tf_op jit(solution)/shard_map/ppermute | solution.py:456

commit v10 on v9

--- a/solution.py
+++ b/solution.py
@@ -336,12 +336,17 @@
     yd_ref[...] = yd0_ref[...] + dot3(n, eu, NN)
 
 
-def r_body(layers, size, _, r0_ref, below_ref, tx_ref, rs_ref, re_ref):
+def r_e_body(layers, size, _, r0_ref, below_ref, tx_ref, re_ref):
+    n = layers * size
+    su, nx = split(below_ref[:n, :]), split(tx_ref[:n, :])
+    re_ref[...] = r0_ref[n:, :] + dot3(su, nx, NN)
+
+
+def r_s_body(layers, size, _, r0_ref, below_ref, tx_ref, rs_ref):
     n = layers * size
     su, eu, nx = split(below_ref[:n, :]), split(below_ref[n:, :]), split(tx_ref[:n, :])
     cx = split(whole_sym(take_sym(tx_ref[n:, :], layers, size), layers))
     rs_ref[...] = r0_ref[:n, :] + dot3(su, cx, NN) + dot3(eu, nx, NT)
-    re_ref[...] = r0_ref[n:, :] + dot3(su, nx, NN)
 
 
 def hand_body(layers, size, _, __, tx_ref, cx_ref):
@@ -370,27 +375,40 @@
 class Sender:
     def __init__(self, twice, keep_ref, out_ref, held, sems):
         self.twice, self.keep_ref, self.out_ref, self.held, self.sems = twice, keep_ref, out_ref, held, sems
-        self.copies = []
-
-    def put(self, value, low, slot):
-        k = len(self.copies)
-        self.held[k] = value
-        self.copies.append(pltpu.make_async_copy(self.held.at[k], self.out_ref.at[low, slot], self.sems.at[k]))
+        self.copies, self.used = [], 0
+
+    def put(self, values, low, slot):
+        first = self.used
+        for value in values:
+            self.held[self.used] = value
+            self.used += 1
+        here = self.held.at[pl.ds(first, len(values))]
+        there = self.out_ref.at[low, pl.ds(slot, len(values))]
+        self.copies.append(pltpu.make_async_copy(here, there, self.sems.at[first]))
         self.copies[-1].start()
 
-    def send(self, y, a, low, slot):
+    def mixed(self, y, a, low, slot):
         at = low * self.out_ref.shape[1] + slot
-        self.put(self.keep_ref[at : at + 1, :] * (y + self.twice * (a - y)), low, slot)
+        return self.keep_ref[at : at + 1, :] * (y + self.twice * (a - y))
+
+    def send_rows(self, name, layers, make):
+        for layer in range(layers):
+            run = [block for block in panel_blocks(name, layers) if block[0] == layer]
+            self.put([make(*block) for block in run], layer, run[0][2])
 
     def send_panel(self, name, a_ref, terms, layers, size):
-        for low, high, slot in panel_blocks(name, layers):
+        def make(low, high, slot):
             rows, cols = slice(low * size, (low + 1) * size), slice(high * size, (high + 1) * size)
-            self.send(sum(ref[rows, cols] for ref in terms), a_ref[rows, cols], low, slot)
+            return self.mixed(sum(ref[rows, cols] for ref in terms), a_ref[rows, cols], low, slot)
+
+        self.send_rows(name, layers, make)
 
     def send_ready(self, name, y_ref, gap_ref, layers, size):
-        for low, high, slot in panel_blocks(name, layers):
+        def make(low, high, slot):
             rows, cols = slice(low * size, (low + 1) * size), slice(high * size, (high + 1) * size)
-            self.put(y_ref[rows, cols] + self.twice * gap_ref[rows, cols], low, slot)
+            return y_ref[rows, cols] + self.twice * gap_ref[rows, cols]
+
+        self.send_rows(name, layers, make)
 
     def wait(self):
         for copy in self.copies:
@@ -427,9 +445,12 @@
     sender.send_ready("E", pe_ref, qe_ref, layers, size)
     sender.send_panel("N", t_ref, [yn_ref, g_ref], layers, size)
     blocks = take_sym(yc_ref[...] + yc_in_ref[: yc_ref.shape[0], :] + g_ref[n:, :], layers, size)
-    for low, high, slot in panel_blocks("C", layers) + [(layer, layer, 0) for layer in range(layers)]:
-        rows, cols = slice(low * size, (low + 1) * size), slice(high * size, (high + 1) * size)
-        sender.send(blocks[low, high], c_ref[rows, cols], low, slot)
+    for layer in range(layers):
+        values = []
+        for low, high, slot in [(layer, layer, 0)] + [block for block in panel_blocks("C", layers) if block[0] == layer]:
+            rows, cols = slice(low * size, (low + 1) * size), slice(high * size, (high + 1) * size)
+            values.append(sender.mixed(blocks[low, high], c_ref[rows, cols], low, slot))
+        sender.put(values, layer, 0)
     sender.wait()
 
 
@@ -517,7 +538,8 @@
     own, g = go(g_body, outs=[total, (n + tall, n)], spaces=[hbm] + [vmem] * 5)(yc_up, own, more, g0, below, gc_in)
     g_in = passed_along(g, "row", 1)
     Cp_u = passed_along(Cp, "col", -1)
-    rs, re = go(r_body, outs=[panel, panel], spaces=[hbm] + [vmem] * 3)(g, r0, below, T_x)
+    (re,) = go(r_e_body, outs=[panel], spaces=[hbm] + [vmem] * 3)(g, r0, below, T_x)
+    (rs,) = go(r_s_body, outs=[panel], spaces=[hbm] + [vmem] * 3)(re, r0, below, T_x)
     (rs,) = go(copy_body, outs=[panel], spaces=[hbm] * 2 + [vmem])(yc_in, re, rs)
     rs_in, re_in = passed_along(rs, "col", 1), passed_along(re, "col", 1)
     (Cp_x,) = go(hand_body, outs=[packed], spaces=[hbm] * 2 + [vmem])(rs, Cp_u, T_x)

time: 81.3 us -> 81.3 us (level)
    pallas_call x1 -> x2, Pallas kernels: 2.72 us -> 2.89 us  [the longest x1 1.91 us: shards(): go(r_s_body, outs=[panel], spaces=[hbm] + [vmem] * 3)(re, r0, below, T_x)]
where the time goes in v10:
time: 81.3 us; the launch traced here: 81.2 us
  Pallas kernels  34.5 us (42%)
  waiting for transfers between devices  23.4 us (29%)
  starting transfers between devices  22.9 us (28%)
    ppermute x11, starting transfers between devices, passed_along(): lax.ppermute(value, axis, [(i, (i + by) % peers) for i in range(peers)])  20.1 us
    ppermute x11, waiting for transfers between devices, passed_along(): lax.ppermute(value, axis, [(i, (i + by) % peers) for i in range(peers)])  19.3 us
    pallas_call x1, Pallas kernels, shards(): go(local_y_body, outs=[sums, (layers, slots, size, size), packed] + [pane...  7.91 us
    pallas_call x1, Pallas kernels, shards(): go(early_body, outs=[panel] * 3, spaces=[hbm] + [vmem] * 8)  4.27 us
    ppermute x3, waiting for transfers between devices, swapped(): return lax.ppermute(value, axis, [(i, i ^ bit) for i in range(peers)])  4.12 us
    pallas_call x1, Pallas kernels, shards(): go(local_g_body, outs=[sums, (n + tall, n), (2 * n, n), packed], spaces=[...  3.88 us
    ppermute x3, starting transfers between devices, swapped(): return lax.ppermute(value, axis, [(i, i ^ bit) for i in range(peers)])  2.85 us
    pallas_call x1, Pallas kernels, shards(): go(middle_body, outs=[panel, panel], spaces=[hbm] + [vmem] * 5)  2.72 us
  transfers between devices with their start and end apart: 14, of which 7 were waited for; matrix products, arithmetic and copies ran while one was open for 0% of the time, Pallas kernels for 38%

profile of v10, /device:TPU:0, one launch (start us, length us, event | category | flops | bytes accessed | tf_op | source)
XLA Modules:
  0.0 81.2 jit_solution(16468002824338731526)
XLA Ops:
  0.0 2.5 %shard_map.37 = (f32[776,512]{1,0:T(8,128)S(1)}, f32[1024,512]{1,0:T(8,128)S(1)}) custom-call(s32[2,13]{1,0:T(2,128)} %bitcast.4, f32[2,14,256,256]{3,2,1,0:T(8,128)} %bitcast.7, f32[2,256]{1,0:T(2,128)} %bitcast.9), custom_call_target="tpu_custom_call" | custom-call | tf_op jit(solution)/shard_map/pallas_call | solution.py:507
  2.5 3.4 %collective-permute-start.2 = (f32[1024,512]{1,0:T(8,128)S(1)}, f32[1024,512]{1,0:T(8,128)S(1)}, u32[]{:S(2)}, u32[]{:S(2)}) collective-permute-start(f32[1024,512]{1,0:T(8,128)S(1)} %get-tuple-element.41.down_ref.e_ref), channel_id=1, source_target_pairs={{0,7},{1,0},{2,1},{3,2},{4,3},{5,4},{6,5},{7,6},{8,15},{9,8},{10,9... | collective-permute-start | bytes 6291464 | tf_op jit(solution)/shard_map/ppermute | solution.py:477
  5.9 3.6 %collective-permute-start.6 = (f32[776,512]{1,0:T(8,128)S(1)}, f32[776,512]{1,0:T(8,128)S(1)}, u32[]{:S(2)}, u32[]{:S(2)}) collective-permute-start(f32[776,512]{1,0:T(8,128)S(1)} %get-tuple-element.39._.t_ref), channel_id=1, source_target_pairs={{0,24},{8,0},{16,8},{24,16},{1,25},{9,1},{17,9},{25,17},{2,26},{10... | collective-permute-start | bytes 4767752 | tf_op jit(solution)/shard_map/ppermute | solution.py:477
  9.6 2.1 %shard_map.38 = (f32[512,512]{1,0:T(8,128)S(1)}, f32[264,512]{1,0:T(8,128)S(1)}) custom-call(s32[2,13]{1,0:T(2,128)} %bitcast.5, f32[2,14,256,256]{3,2,1,0:T(8,128)} %bitcast.8, f32[776,512]{1,0:T(8,128)S(1)} %get-tuple-element.39._.t_ref), custom_call_target="tpu_custom_call" | custom-call | tf_op jit(solution)/shard_map/pallas_call | solution.py:514
  11.7 1.1 %shard_map.39 = (f32[264,512]{1,0:T(8,128)S(1)}, f32[512,512]{1,0:T(8,128)S(1)}, f32[28,256]{1,0:T(8,128)S(1)}, f32[16,256]{1,0:T(8,128)S(1)}) custom-call(s32[2,13]{1,0:T(2,128)S(1)} %bitcast.6, f32[264,512]{1,0:T(8,128)S(1)} %get-tuple-element.40._, f32[1024,512]{1,0:T(8,128)S(1)} %get-tuple-element.41.down_ref.e_ref, ...), custom_call_target="tpu_custom_call" | custom-call | tf_op jit(solution)/shard_map/pallas_call | solution.py:518
  12.8 0.1 collective-permute-start
  12.9 1.2 %collective-permute-done.more_ref = f32[16,256]{1,0:T(8,128)S(1)} collective-permute-done((f32[16,256]{1,0:T(8,128)S(1)}, f32[16,256]{1,0:T(8,128)S(1)}, u32[]{:S(2)}, u32[]{:S(2)}) %collective-permute-start) | collective-permute-done | bytes 16416 | tf_op jit(solution)/shard_map/ppermute | solution.py:482
  14.0 3.9 %shard_map.40 = (f32[16,256]{1,0:T(8,128)S(1)}, f32[776,512]{1,0:T(8,128)S(1)}, f32[1024,512]{1,0:T(8,128)S(1)}, f32[264,512]{1,0:T(8,128)S(1)}) custom-call(f32[264,512]{1,0:T(8,128)S(1)} %get-tuple-element.40._, f32[16,256]{1,0:T(8,128)S(1)} %get-tuple-element.44.sums_ref, f32[16,256]{1,0:T(8,128)S(1)} %collective-permute-done.more_ref, ...), custom_call_target="tpu_custom_call" | custom-call | tf_op jit(solution)/shard_map/pallas_call | solution.py:527
  17.9 1.0 %collective-permute-start.1 = (f32[16,256]{1,0:T(8,128)S(1)}, f32[16,256]{1,0:T(8,128)S(1)}, u32[]{:S(2)}, u32[]{:S(2)}) collective-permute-start(f32[16,256]{1,0:T(8,128)S(1)} %get-tuple-element.46.sums_ref), channel_id=1, source_target_pairs={{0,4},{1,5},{2,6},{3,7},{4,0},{5,1},{6,2},{7,3},{8,12},{9,13},{10,... | collective-permute-start | bytes 49160 | tf_op jit(solution)/shard_map/ppermute | solution.py:482
  18.9 2.9 %collective-permute-done.1.more_ref = f32[16,256]{1,0:T(8,128)S(1)} collective-permute-done((f32[16,256]{1,0:T(8,128)S(1)}, f32[16,256]{1,0:T(8,128)S(1)}, u32[]{:S(2)}, u32[]{:S(2)}) %collective-permute-start.1) | collective-permute-done | bytes 16416 | tf_op jit(solution)/shard_map/ppermute | solution.py:482
  21.9 7.9 %shard_map.41 = (f32[16,256]{1,0:T(8,128)S(1)}, f32[2,14,256,256]{3,2,1,0:T(8,128)}, f32[264,512]{1,0:T(8,128)S(1)}, f32[512,512]{1,0:T(8,128)S(1)}, f32[512,512...) custom-call(f32[776,512]{1,0:T(8,128)S(1)} %get-tuple-element.45._.g0_ref, ...), custom_call_target="tpu_custom_call" | custom-call | tf_op jit(solution)/shard_map/pallas_call | solution.py:531
  29.8 1.8 %collective-permute-start.4 = (f32[16,256]{1,0:T(8,128)S(1)}, f32[16,256]{1,0:T(8,128)S(1)}, u32[]{:S(2)}, u32[]{:S(2)}) collective-permute-start(f32[16,256]{1,0:T(8,128)S(1)} %get-tuple-element.51.sums_ref), channel_id=1, source_target_pairs={{0,2},{1,3},{2,0},{3,1},{4,6},{5,7},{6,4},{7,5},{8,10},{9,11},{10,... | collective-permute-start | bytes 49160 | tf_op jit(solution)/shard_map/ppermute | solution.py:482
  31.6 3.9 %collective-permute-done.2.__.below_ref = f32[1024,512]{1,0:T(8,128)S(1)} collective-permute-done((f32[1024,512]{1,0:T(8,128)S(1)}, f32[1024,512]{1,0:T(8,128)S(1)}, u32[]{:S(2)}, u32[]{:S(2)}) %collective-permute-start.2) | collective-permute-done | bytes 2097184 | tf_op jit(solution)/shard_map/ppermute | solution.py:477
  35.5 0.3 collective-permute-start.3
  35.8 1.7 %shard_map.43 = (f32[8,256]{1,0:T(8,128)S(1)}, f32[776,512]{1,0:T(8,128)S(1)}) custom-call(f32[272,512]{1,0:T(8,128)S(1)} %shard_map.42._, f32[16,256]{1,0:T(8,128)S(1)} %get-tuple-element.51.sums_ref, f32[16,256]{1,0:T(8,128)S(1)} %collective-permute-done.4.more_ref, f32[776,512]{1,0:T(8,128)S(1)} %get-tuple-element.45._.g0_ref, ...), custom_call_target="tpu_custom_call" | custom-call | tf_op jit(solution)/shard_map/pallas_call | solution.py:538
  37.5 1.8 %collective-permute-start.8 = (f32[776,512]{1,0:T(8,128)S(1)}, f32[776,512]{1,0:T(8,128)S(1)}, u32[]{:S(2)}, u32[]{:S(2)}) collective-permute-start(f32[776,512]{1,0:T(8,128)S(1)} %get-tuple-element.52._), channel_id=1, source_target_pairs={{0,8},{8,16},{16,24},{24,0},{1,9},{9,17},{17,25},{25,1},{2,10},{10... | collective-permute-start | bytes 4767752 | tf_op jit(solution)/shard_map/ppermute | solution.py:477
  39.3 2.3 %collective-permute-start.7 = (f32[264,512]{1,0:T(8,128)S(1)}, f32[264,512]{1,0:T(8,128)S(1)}, u32[]{:S(2)}, u32[]{:S(2)}) collective-permute-start(f32[264,512]{1,0:T(8,128)S(1)} %get-tuple-element.54), channel_id=1, source_target_pairs={{0,7},{1,0},{2,1},{3,2},{4,3},{5,4},{6,5},{7,6},{8,15},{9,8},{10,9... | collective-permute-start | bytes 1622024 | tf_op jit(solution)/shard_map/ppermute | solution.py:477
  41.6 3.1 %collective-permute-done.6.tx_ref = f32[776,512]{1,0:T(8,128)S(1)} collective-permute-done((f32[776,512]{1,0:T(8,128)S(1)}, f32[776,512]{1,0:T(8,128)S(1)}, u32[]{:S(2)}, u32[]{:S(2)}) %collective-permute-start.6) | collective-permute-done | bytes 1589280 | tf_op jit(solution)/shard_map/ppermute | solution.py:477
  44.8 1.0 %shard_map.44._.__ = f32[512,512]{1,0:T(8,128)S(1)} custom-call(f32[776,512]{1,0:T(8,128)S(1)} %get-tuple-element.52._, f32[1024,512]{1,0:T(8,128)S(1)} %get-tuple-element.53.r0_ref, f32[1024,512]{1,0:T(8,128)S(1)} %collective-permute-done.2.__.below_ref, f32[776,512]{1,0:T(8,128)S(1)} %collective-permute-done.6.tx_ref), custom_call_target="tpu_custom_call" | custom-call | tf_op jit(solution)/shard_map/pallas_call | solution.py:541
  45.8 1.9 %shard_map.45.from_ref = f32[512,512]{1,0:T(8,128)S(1)} custom-call(f32[512,512]{1,0:T(8,128)S(1)} %shard_map.44._.__, f32[1024,512]{1,0:T(8,128)S(1)} %get-tuple-element.53.r0_ref, f32[1024,512]{1,0:T(8,128)S(1)} %collective-permute-done.2.__.below_ref, f32[776,512]{1,0:T(8,128)S(1)} %collective-permute-done.6.tx_ref), custom_call_target="tpu_custom_call" | custom-call | tf_op jit(solution)/shard_map/pallas_call | solution.py:542
  47.9 3.2 %collective-permute-done.7.__.cu_ref = f32[264,512]{1,0:T(8,128)S(1)} collective-permute-done((f32[264,512]{1,0:T(8,128)S(1)}, f32[264,512]{1,0:T(8,128)S(1)}, u32[]{:S(2)}, u32[]{:S(2)}) %collective-permute-start.7) | collective-permute-done | bytes 540704 | tf_op jit(solution)/shard_map/ppermute | solution.py:477
  51.1 3.2 %collective-permute-start.9 = (f32[264,512]{1,0:T(8,128)S(1)}, f32[264,512]{1,0:T(8,128)S(1)}, u32[]{:S(2)}, u32[]{:S(2)}) collective-permute-start(f32[264,512]{1,0:T(8,128)S(1)} %shard_map.47._), channel_id=1, source_target_pairs={{0,7},{1,0},{2,1},{3,2},{4,3},{5,4},{6,5},{7,6},{8,15},{9,8},{10,9... | collective-permute-start | bytes 1622024 | tf_op jit(solution)/shard_map/ppermute | solution.py:477
  54.2 4.3 %shard_map.48 = (f32[512,512]{1,0:T(8,128)S(1)}, f32[512,512]{1,0:T(8,128)S(1)}, f32[512,512]{1,0:T(8,128)S(1)}) custom-call(f32[264,512]{1,0:T(8,128)S(1)} %shard_map.47._, f32[776,512]{1,0:T(8,128)S(1)} %get-tuple-element.39._.t_ref, f32[1024,512]{1,0:T(8,128)S(1)} %get-tuple-element.41.down_ref.e_ref, f32[512,512]{1,0:T(8,128)S(1)} %get-tuple-element.42.d_ref, ...), custom_call_target="tpu_custom_call" | custom-call | tf_op jit(solution)/shard_map/pallas_call | solution.py:547
  58.5 2.7 %shard_map.49 = (f32[512,512]{1,0:T(8,128)S(1)}, f32[512,512]{1,0:T(8,128)S(1)}) custom-call(f32[512,512]{1,0:T(8,128)S(1)} %get-tuple-element.58._.yn_ref, f32[1024,512]{1,0:T(8,128)S(1)} %get-tuple-element.41.down_ref.e_ref, f32[512,512]{1,0:T(8,128)S(1)} %get-tuple-element.42.d_ref, f32[776,512]{1,0:T(8,128)S(1)} %collective-permute-done.6.tx_ref, ...), custom_call_target="tpu_custom_call" | custom-call | tf_op jit(solution)/shard_map/pallas_call | solution.py:548
  61.3 5.7 %collective-permute-done.9.cxu_ref = f32[264,512]{1,0:T(8,128)S(1)} collective-permute-done((f32[264,512]{1,0:T(8,128)S(1)}, f32[264,512]{1,0:T(8,128)S(1)}, u32[]{:S(2)}, u32[]{:S(2)}) %collective-permute-start.9) | collective-permute-done | bytes 540704 | tf_op jit(solution)/shard_map/ppermute | solution.py:477
  67.0 1.1 %shard_map.50 = (f32[8,256]{1,0:T(8,128)S(1)}, f32[512,512]{1,0:T(8,128)S(1)}) custom-call(f32[512,512]{1,0:T(8,128)S(1)} %get-tuple-element.61._.ye_ref, f32[8,256]{1,0:T(8,128)S(1)} %get-tuple-element.62.sums_ref, f32[512,512]{1,0:T(8,128)S(1)} %get-tuple-element.42.d_ref, f32[264,512]{1,0:T(8,128)S(1)} %collective-permute-done.9.cxu_ref, ...), custom_call_target="tpu_custom_call" | custom-call | tf_op jit(solution)/shard_map/pallas_call | solution.py:549
  68.1 4.4 %collective-permute-start.12 = (f32[8,256]{1,0:T(8,128)S(1)}, f32[8,256]{1,0:T(8,128)S(1)}, u32[]{:S(2)}, u32[]{:S(2)}) collective-permute-start(f32[8,256]{1,0:T(8,128)S(1)} %get-tuple-element.65.sums_ref.rest_0_), channel_id=1, source_target_pairs={{0,16},{8,24},{16,0},{24,8},{1,17},{9,25},{17,1},{25,9},{2,18},{10... | collective-permute-start | bytes 24584 | tf_op jit(solution)/shard_map/ppermute | solution.py:477
  72.5 0.9 %collective-permute-start.11 = (f32[8,256]{1,0:T(8,128)S(1)}, f32[8,256]{1,0:T(8,128)S(1)}, u32[]{:S(2)}, u32[]{:S(2)}) collective-permute-start(f32[8,256]{1,0:T(8,128)S(1)} %get-tuple-element.65.sums_ref.rest_0_), channel_id=1, source_target_pairs={{0,24},{8,0},{16,8},{24,16},{1,25},{9,1},{17,9},{25,17},{2,26},{10... | collective-permute-start | bytes 24584 | tf_op jit(solution)/shard_map/ppermute | solution.py:477
  73.4 1.0 %shard_map.51 = (f32[8,256]{1,0:T(8,128)}, f32[512,512]{1,0:T(8,128)S(1)}, f32[512,512]{1,0:T(8,128)S(1)}, f32[512,512]{1,0:T(8,128)S(1)}, f32[512,512]{1,0:T(8,128)S(1)}) custom-call(f32[28,256]{1,0:T(8,128)S(1)} %get-tuple-element.43.keep_ref, f32[512,512]{1,0:T(8,128)S(1)} %get-tuple-element.64._.yd_ref, f32[8,256]{1,0:T(8,128)S(1)} %get-tuple-element.65.sums_ref.rest_0_, ...), custom_call_target="tpu_custom_call" | custom-call | tf_op jit(solution)/shard_map/pallas_call | solution.py:551
  74.4 3.4 %collective-permute-done.12.rest_2_ = f32[8,256]{1,0:T(8,128)S(1)} collective-permute-done((f32[8,256]{1,0:T(8,128)S(1)}, f32[8,256]{1,0:T(8,128)S(1)}, u32[]{:S(2)}, u32[]{:S(2)}) %collective-permute-start.12) | collective-permute-done | bytes 8224 | tf_op jit(solution)/shard_map/ppermute | solution.py:477
  77.7 2.2 %shard_map.52 = (f32[2,14,256,256]{3,2,1,0:T(8,128)}, f32[8,256]{1,0:T(8,128)S(1)}) custom-call(f32[28,256]{1,0:T(8,128)S(1)} %get-tuple-element.43.keep_ref, f32[2,14,256,256]{3,2,1,0:T(8,128)} %get-tuple-element.48._, f32[512,512]{1,0:T(8,128)S(1)} %get-tuple-element.47.c_ref, ...), custom_call_target="tpu_custom_call", output_to_operand_aliasing={{0}: (1, {})} | custom-call | tf_op jit(solution)/shard_map/pallas_call | solution.py:556
  79.9 1.1 %shard_map.53 = f32[2,14,256,256]{3,2,1,0:T(8,128)} custom-call(f32[28,256]{1,0:T(8,128)S(1)} %get-tuple-element.43.keep_ref, f32[2,14,256,256]{3,2,1,0:T(8,128)} %get-tuple-element.70._, f32[8,256]{1,0:T(8,128)S(1)} %get-tuple-element.71.twice_ref, f32[1024,512]{1,0:T(8,128)S(1)} %get-tuple-element.41.down_ref.e_ref, ...), custom_call_target="tpu_custom_call", output_to_operand_aliasing={{}: (1, {})} | custom-call | tf_op jit(solution)/shard_map/pallas_call | solution.py:560
  (15 shorter events, 0.3 us)
Async XLA Ops:
  2.5 32.9 %collective-permute-start.2 = (f32[1024,512]{1,0:T(8,128)S(1)}, f32[1024,512]{1,0:T(8,128)S(1)}, u32[]{:S(2)}, u32[]{:S(2)}) collective-permute-start(f32[1024,512]{1,0:T(8,128)S(1)} %get-tuple-element.41.down_ref.e_ref), channel_id=1, source_target_pairs={{0,7},{1,0},{2,1},{3,2},{4,3},{5,4},{6,5},{7,6},{8,15},{9,8},{10,9... | collective-permute-start | bytes 6291464 | tf_op jit(solution)/shard_map/ppermute | solution.py:477
  5.9 5.8 %copy-start = (s32[1,1,2,13]{3,2,1,0:T(2,128)S(1)}, s32[1,1,2,13]{3,2,1,0:T(2,128)}, u32[]{:S(2)}) copy-start(s32[1,1,2,13]{3,2,1,0:T(2,128)} %param.5) | copy-start | bytes 316
  5.9 38.8 %collective-permute-start.6 = (f32[776,512]{1,0:T(8,128)S(1)}, f32[776,512]{1,0:T(8,128)S(1)}, u32[]{:S(2)}, u32[]{:S(2)}) collective-permute-start(f32[776,512]{1,0:T(8,128)S(1)} %get-tuple-element.39._.t_ref), channel_id=1, source_target_pairs={{0,24},{8,0},{16,8},{24,16},{1,25},{9,1},{17,9},{25,17},{2,26},{10... | collective-permute-start | bytes 4767752 | tf_op jit(solution)/shard_map/ppermute | solution.py:477
  11.6 24.1 %collective-permute-start.5 = (f32[264,512]{1,0:T(8,128)S(1)}, f32[264,512]{1,0:T(8,128)S(1)}, u32[]{:S(2)}, u32[]{:S(2)}) collective-permute-start(f32[264,512]{1,0:T(8,128)S(1)} %get-tuple-element.40._), channel_id=1, source_target_pairs={{0,1},{1,2},{2,3},{3,4},{4,5},{5,6},{6,7},{7,0},{8,9},{9,10},{10,1... | collective-permute-start | bytes 1622024 | tf_op jit(solution)/shard_map/ppermute | solution.py:477
  12.8 1.2 %collective-permute-start = (f32[16,256]{1,0:T(8,128)S(1)}, f32[16,256]{1,0:T(8,128)S(1)}, u32[]{:S(2)}, u32[]{:S(2)}) collective-permute-start(f32[16,256]{1,0:T(8,128)S(1)} %get-tuple-element.44.sums_ref), channel_id=1, source_target_pairs={{0,1},{1,0},{2,3},{3,2},{4,5},{5,4},{6,7},{7,6},{8,9},{9,8},{10,11... | collective-permute-start | bytes 49160 | tf_op jit(solution)/shard_map/ppermute | solution.py:482
  17.9 4.0 %collective-permute-start.1 = (f32[16,256]{1,0:T(8,128)S(1)}, f32[16,256]{1,0:T(8,128)S(1)}, u32[]{:S(2)}, u32[]{:S(2)}) collective-permute-start(f32[16,256]{1,0:T(8,128)S(1)} %get-tuple-element.46.sums_ref), channel_id=1, source_target_pairs={{0,4},{1,5},{2,6},{3,7},{4,0},{5,1},{6,2},{7,3},{8,12},{9,13},{10,... | collective-permute-start | bytes 49160 | tf_op jit(solution)/shard_map/ppermute | solution.py:482
  29.8 6.0 %collective-permute-start.4 = (f32[16,256]{1,0:T(8,128)S(1)}, f32[16,256]{1,0:T(8,128)S(1)}, u32[]{:S(2)}, u32[]{:S(2)}) collective-permute-start(f32[16,256]{1,0:T(8,128)S(1)} %get-tuple-element.51.sums_ref), channel_id=1, source_target_pairs={{0,2},{1,3},{2,0},{3,1},{4,6},{5,7},{6,4},{7,5},{8,10},{9,11},{10,... | collective-permute-start | bytes 49160 | tf_op jit(solution)/shard_map/ppermute | solution.py:482
  35.5 12.2 %collective-permute-start.3 = (f32[272,512]{1,0:T(8,128)S(1)}, f32[272,512]{1,0:T(8,128)S(1)}, u32[]{:S(2)}, u32[]{:S(2)}) collective-permute-start(f32[272,512]{1,0:T(8,128)S(1)} %shard_map.42._), channel_id=1, source_target_pairs={{0,1},{1,2},{2,3},{3,4},{4,5},{5,6},{6,7},{7,0},{8,9},{9,10},{10,1... | collective-permute-start | bytes 1671176 | tf_op jit(solution)/shard_map/ppermute | solution.py:477
  37.5 40.3 %collective-permute-start.8 = (f32[776,512]{1,0:T(8,128)S(1)}, f32[776,512]{1,0:T(8,128)S(1)}, u32[]{:S(2)}, u32[]{:S(2)}) collective-permute-start(f32[776,512]{1,0:T(8,128)S(1)} %get-tuple-element.52._), channel_id=1, source_target_pairs={{0,8},{8,16},{16,24},{24,0},{1,9},{9,17},{17,25},{25,1},{2,10},{10... | collective-permute-start | bytes 4767752 | tf_op jit(solution)/shard_map/ppermute | solution.py:477
  39.3 11.7 %collective-permute-start.7 = (f32[264,512]{1,0:T(8,128)S(1)}, f32[264,512]{1,0:T(8,128)S(1)}, u32[]{:S(2)}, u32[]{:S(2)}) collective-permute-start(f32[264,512]{1,0:T(8,128)S(1)} %get-tuple-element.54), channel_id=1, source_target_pairs={{0,7},{1,0},{2,1},{3,2},{4,3},{5,4},{6,5},{7,6},{8,15},{9,8},{10,9... | collective-permute-start | bytes 1622024 | tf_op jit(solution)/shard_map/ppermute | solution.py:477
  45.7 27.6 %collective-permute-start.10 = (f32[512,512]{1,0:T(8,128)S(1)}, f32[512,512]{1,0:T(8,128)S(1)}, u32[]{:S(2)}, u32[]{:S(2)}) collective-permute-start(f32[512,512]{1,0:T(8,128)S(1)} %shard_map.44._.__), channel_id=1, source_target_pairs={{0,1},{1,2},{2,3},{3,4},{4,5},{5,6},{6,7},{7,0},{8,9},{9,10},{10,1... | collective-permute-start | bytes 3145736 | tf_op jit(solution)/shard_map/ppermute | solution.py:477
  47.8 32.1 %collective-permute-start.13 = (f32[512,512]{1,0:T(8,128)S(1)}, f32[512,512]{1,0:T(8,128)S(1)}, u32[]{:S(2)}, u32[]{:S(2)}) collective-permute-start(f32[512,512]{1,0:T(8,128)S(1)} %shard_map.46._), channel_id=1, source_target_pairs={{0,1},{1,2},{2,3},{3,4},{4,5},{5,6},{6,7},{7,0},{8,9},{9,10},{10,1... | collective-permute-start | bytes 3145736 | tf_op jit(solution)/shard_map/ppermute | solution.py:477
  51.1 15.9 %collective-permute-start.9 = (f32[264,512]{1,0:T(8,128)S(1)}, f32[264,512]{1,0:T(8,128)S(1)}, u32[]{:S(2)}, u32[]{:S(2)}) collective-permute-start(f32[264,512]{1,0:T(8,128)S(1)} %shard_map.47._), channel_id=1, source_target_pairs={{0,7},{1,0},{2,1},{3,2},{4,3},{5,4},{6,5},{7,6},{8,15},{9,8},{10,9... | collective-permute-start | bytes 1622024 | tf_op jit(solution)/shard_map/ppermute | solution.py:477
  68.1 9.6 %collective-permute-start.12 = (f32[8,256]{1,0:T(8,128)S(1)}, f32[8,256]{1,0:T(8,128)S(1)}, u32[]{:S(2)}, u32[]{:S(2)}) collective-permute-start(f32[8,256]{1,0:T(8,128)S(1)} %get-tuple-element.65.sums_ref.rest_0_), channel_id=1, source_target_pairs={{0,16},{8,24},{16,0},{24,8},{1,17},{9,25},{17,1},{25,9},{2,18},{10... | collective-permute-start | bytes 24584 | tf_op jit(solution)/shard_map/ppermute | solution.py:477
  72.5 5.2 %collective-permute-start.11 = (f32[8,256]{1,0:T(8,128)S(1)}, f32[8,256]{1,0:T(8,128)S(1)}, u32[]{:S(2)}, u32[]{:S(2)}) collective-permute-start(f32[8,256]{1,0:T(8,128)S(1)} %get-tuple-element.65.sums_ref.rest_0_), channel_id=1, source_target_pairs={{0,24},{8,0},{16,8},{24,16},{1,25},{9,1},{17,9},{25,17},{2,26},{10... | collective-permute-start | bytes 24584 | tf_op jit(solution)/shard_map/ppermute | solution.py:477

commit v11 on v9

--- a/solution.py
+++ b/solution.py
@@ -524,8 +524,9 @@
     Cp_xu = passed_along(Cp_x, "col", -1)
     yn, ye, yd = go(early_body, outs=[panel] * 3, spaces=[hbm] + [vmem] * 8)(Cp_x, T, down, D, below, Cp_u, yn, ye, yd)
     ye, yd = go(middle_body, outs=[panel, panel], spaces=[hbm] + [vmem] * 5)(yn, down, D, T_x, ye, yd)
+    early_sums = own
     own, yd = go(middle_c_body, outs=[total, panel], spaces=[hbm] + [vmem] * 4)(ye, own, D, Cp_xu, yd)
-    every = [own] + [passed_along(own, "row", -by) for by in range(1, lax.axis_size("row") - 1)]
+    every = [own] + [passed_along(own if by == 1 else early_sums, "row", -by) for by in range(1, lax.axis_size("row") - 1)]
     _, *ready = go(ready_body, outs=[total] + [panel] * 4, spaces=[vmem, hbm] + [vmem] * 6)(
         keep, yd, own, D, down, yd, ye, re_in
     )

time: 81.3 us -> 81.3 us (level)
  starting transfers between devices: 22.9 us -> 25 us
  waiting for transfers between devices: 23.7 us -> 21.6 us
    ppermute x11, starting transfers between devices: 20 us -> 22.1 us  [passed_along(): lax.ppermute(value, axis, [(i, (i + by) % peers) for i in range(peers)])]
    ppermute x11, waiting for transfers between devices: 19.6 us -> 17.5 us  [passed_along(): lax.ppermute(value, axis, [(i, (i + by) % peers) for i in range(peers)])]
where the time goes in v11:
time: 81.3 us; the launch traced here: 81.2 us
  Pallas kernels  34.2 us (42%)
  starting transfers between devices  25 us (31%)
  waiting for transfers between devices  21.6 us (27%)
    ppermute x11, starting transfers between devices, passed_along(): lax.ppermute(value, axis, [(i, (i + by) % peers) for i in range(peers)])  22.1 us
    ppermute x11, waiting for transfers between devices, passed_along(): lax.ppermute(value, axis, [(i, (i + by) % peers) for i in range(peers)])  17.5 us
    pallas_call x1, Pallas kernels, shards(): go(local_y_body, outs=[sums, (layers, slots, size, size), packed] + [pane...  7.91 us
    pallas_call x1, Pallas kernels, shards(): go(early_body, outs=[panel] * 3, spaces=[hbm] + [vmem] * 8)  4.26 us
    ppermute x3, waiting for transfers between devices, swapped(): return lax.ppermute(value, axis, [(i, i ^ bit) for i in range(peers)])  4.13 us
    pallas_call x1, Pallas kernels, shards(): go(local_g_body, outs=[sums, (n + tall, n), (2 * n, n), packed], spaces=[...  3.88 us
    ppermute x3, starting transfers between devices, swapped(): return lax.ppermute(value, axis, [(i, i ^ bit) for i in range(peers)])  2.91 us
    pallas_call x1, Pallas kernels, shards(): go(middle_body, outs=[panel, panel], spaces=[hbm] + [vmem] * 5)  2.73 us
  transfers between devices with their start and end apart: 14, of which 7 were waited for; matrix products, arithmetic and copies ran while one was open for 0% of the time, Pallas kernels for 38%

profile of v11, /device:TPU:0, one launch (start us, length us, event | category | flops | bytes accessed | tf_op | source)
XLA Modules:
  0.0 81.2 jit_solution(18078235727689652833)
XLA Ops:
  0.0 2.5 %shard_map.37 = (f32[776,512]{1,0:T(8,128)S(1)}, f32[1024,512]{1,0:T(8,128)S(1)}) custom-call(s32[2,13]{1,0:T(2,128)} %bitcast.4, f32[2,14,256,256]{3,2,1,0:T(8,128)} %bitcast.7, f32[2,256]{1,0:T(2,128)} %bitcast.9), custom_call_target="tpu_custom_call" | custom-call | tf_op jit(solution)/shard_map/pallas_call | solution.py:486
  2.5 3.4 %collective-permute-start.2 = (f32[1024,512]{1,0:T(8,128)S(1)}, f32[1024,512]{1,0:T(8,128)S(1)}, u32[]{:S(2)}, u32[]{:S(2)}) collective-permute-start(f32[1024,512]{1,0:T(8,128)S(1)} %get-tuple-element.43.down_ref.e_ref), channel_id=1, source_target_pairs={{0,7},{1,0},{2,1},{3,2},{4,3},{5,4},{6,5},{7,6},{8,15},{9,8},{10,9... | collective-permute-start | bytes 6291464 | tf_op jit(solution)/shard_map/ppermute | solution.py:456
  6.0 3.6 %collective-permute-start.6 = (f32[776,512]{1,0:T(8,128)S(1)}, f32[776,512]{1,0:T(8,128)S(1)}, u32[]{:S(2)}, u32[]{:S(2)}) collective-permute-start(f32[776,512]{1,0:T(8,128)S(1)} %get-tuple-element.41._.t_ref), channel_id=1, source_target_pairs={{0,24},{8,0},{16,8},{24,16},{1,25},{9,1},{17,9},{25,17},{2,26},{10... | collective-permute-start | bytes 4767752 | tf_op jit(solution)/shard_map/ppermute | solution.py:456
  9.5 2.0 %shard_map.38 = (f32[512,512]{1,0:T(8,128)S(1)}, f32[264,512]{1,0:T(8,128)S(1)}) custom-call(s32[2,13]{1,0:T(2,128)} %bitcast.5, f32[2,14,256,256]{3,2,1,0:T(8,128)} %bitcast.8, f32[776,512]{1,0:T(8,128)S(1)} %get-tuple-element.41._.t_ref), custom_call_target="tpu_custom_call" | custom-call | tf_op jit(solution)/shard_map/pallas_call | solution.py:493
  11.7 1.1 %shard_map.39 = (f32[264,512]{1,0:T(8,128)S(1)}, f32[512,512]{1,0:T(8,128)S(1)}, f32[28,256]{1,0:T(8,128)S(1)}, f32[16,256]{1,0:T(8,128)S(1)}) custom-call(s32[2,13]{1,0:T(2,128)S(1)} %bitcast.6, f32[264,512]{1,0:T(8,128)S(1)} %get-tuple-element.42._, f32[1024,512]{1,0:T(8,128)S(1)} %get-tuple-element.43.down_ref.e_ref, ...), custom_call_target="tpu_custom_call" | custom-call | tf_op jit(solution)/shard_map/pallas_call | solution.py:497
  12.7 0.1 collective-permute-start
  12.8 1.2 %collective-permute-done.more_ref = f32[16,256]{1,0:T(8,128)S(1)} collective-permute-done((f32[16,256]{1,0:T(8,128)S(1)}, f32[16,256]{1,0:T(8,128)S(1)}, u32[]{:S(2)}, u32[]{:S(2)}) %collective-permute-start) | collective-permute-done | bytes 16416 | tf_op jit(solution)/shard_map/ppermute | solution.py:461
  14.0 3.9 %shard_map.40 = (f32[16,256]{1,0:T(8,128)S(1)}, f32[776,512]{1,0:T(8,128)S(1)}, f32[1024,512]{1,0:T(8,128)S(1)}, f32[264,512]{1,0:T(8,128)S(1)}) custom-call(f32[264,512]{1,0:T(8,128)S(1)} %get-tuple-element.42._, f32[16,256]{1,0:T(8,128)S(1)} %get-tuple-element.46.sums_ref, f32[16,256]{1,0:T(8,128)S(1)} %collective-permute-done.more_ref, ...), custom_call_target="tpu_custom_call" | custom-call | tf_op jit(solution)/shard_map/pallas_call | solution.py:506
  17.9 1.0 %collective-permute-start.1 = (f32[16,256]{1,0:T(8,128)S(1)}, f32[16,256]{1,0:T(8,128)S(1)}, u32[]{:S(2)}, u32[]{:S(2)}) collective-permute-start(f32[16,256]{1,0:T(8,128)S(1)} %get-tuple-element.48.sums_ref), channel_id=1, source_target_pairs={{0,4},{1,5},{2,6},{3,7},{4,0},{5,1},{6,2},{7,3},{8,12},{9,13},{10,... | collective-permute-start | bytes 49160 | tf_op jit(solution)/shard_map/ppermute | solution.py:461
  18.9 3.0 %collective-permute-done.1.more_ref = f32[16,256]{1,0:T(8,128)S(1)} collective-permute-done((f32[16,256]{1,0:T(8,128)S(1)}, f32[16,256]{1,0:T(8,128)S(1)}, u32[]{:S(2)}, u32[]{:S(2)}) %collective-permute-start.1) | collective-permute-done | bytes 16416 | tf_op jit(solution)/shard_map/ppermute | solution.py:461
  21.8 7.9 %shard_map.41 = (f32[16,256]{1,0:T(8,128)S(1)}, f32[2,14,256,256]{3,2,1,0:T(8,128)}, f32[264,512]{1,0:T(8,128)S(1)}, f32[512,512]{1,0:T(8,128)S(1)}, f32[512,512...) custom-call(f32[776,512]{1,0:T(8,128)S(1)} %get-tuple-element.47._.g0_ref, ...), custom_call_target="tpu_custom_call" | custom-call | tf_op jit(solution)/shard_map/pallas_call | solution.py:510
  29.8 1.8 %collective-permute-start.4 = (f32[16,256]{1,0:T(8,128)S(1)}, f32[16,256]{1,0:T(8,128)S(1)}, u32[]{:S(2)}, u32[]{:S(2)}) collective-permute-start(f32[16,256]{1,0:T(8,128)S(1)} %get-tuple-element.53.sums_ref), channel_id=1, source_target_pairs={{0,2},{1,3},{2,0},{3,1},{4,6},{5,7},{6,4},{7,5},{8,10},{9,11},{10,... | collective-permute-start | bytes 49160 | tf_op jit(solution)/shard_map/ppermute | solution.py:461
  31.6 3.9 %collective-permute-done.2.__.below_ref = f32[1024,512]{1,0:T(8,128)S(1)} collective-permute-done((f32[1024,512]{1,0:T(8,128)S(1)}, f32[1024,512]{1,0:T(8,128)S(1)}, u32[]{:S(2)}, u32[]{:S(2)}) %collective-permute-start.2) | collective-permute-done | bytes 2097184 | tf_op jit(solution)/shard_map/ppermute | solution.py:456
  35.5 0.2 collective-permute-start.3
  35.8 1.7 %shard_map.43 = (f32[8,256]{1,0:T(8,128)S(1)}, f32[776,512]{1,0:T(8,128)S(1)}) custom-call(f32[272,512]{1,0:T(8,128)S(1)} %shard_map.42._, f32[16,256]{1,0:T(8,128)S(1)} %get-tuple-element.53.sums_ref, f32[16,256]{1,0:T(8,128)S(1)} %collective-permute-done.4.more_ref, f32[776,512]{1,0:T(8,128)S(1)} %get-tuple-element.47._.g0_ref, ...), custom_call_target="tpu_custom_call" | custom-call | tf_op jit(solution)/shard_map/pallas_call | solution.py:517
  37.5 1.8 %collective-permute-start.8 = (f32[776,512]{1,0:T(8,128)S(1)}, f32[776,512]{1,0:T(8,128)S(1)}, u32[]{:S(2)}, u32[]{:S(2)}) collective-permute-start(f32[776,512]{1,0:T(8,128)S(1)} %get-tuple-element.54._), channel_id=1, source_target_pairs={{0,8},{8,16},{16,24},{24,0},{1,9},{9,17},{17,25},{25,1},{2,10},{10... | collective-permute-start | bytes 4767752 | tf_op jit(solution)/shard_map/ppermute | solution.py:456
  39.3 2.4 %collective-permute-start.7 = (f32[264,512]{1,0:T(8,128)S(1)}, f32[264,512]{1,0:T(8,128)S(1)}, u32[]{:S(2)}, u32[]{:S(2)}) collective-permute-start(f32[264,512]{1,0:T(8,128)S(1)} %get-tuple-element.58), channel_id=1, source_target_pairs={{0,7},{1,0},{2,1},{3,2},{4,3},{5,4},{6,5},{7,6},{8,15},{9,8},{10,9... | collective-permute-start | bytes 1622024 | tf_op jit(solution)/shard_map/ppermute | solution.py:456
  41.7 3.1 %collective-permute-done.6.tx_ref = f32[776,512]{1,0:T(8,128)S(1)} collective-permute-done((f32[776,512]{1,0:T(8,128)S(1)}, f32[776,512]{1,0:T(8,128)S(1)}, u32[]{:S(2)}, u32[]{:S(2)}) %collective-permute-start.6) | collective-permute-done | bytes 1589280 | tf_op jit(solution)/shard_map/ppermute | solution.py:456
  44.7 2.7 %shard_map.44 = (f32[512,512]{1,0:T(8,128)S(1)}, f32[512,512]{1,0:T(8,128)S(1)}) custom-call(f32[776,512]{1,0:T(8,128)S(1)} %get-tuple-element.54._, f32[1024,512]{1,0:T(8,128)S(1)} %get-tuple-element.55.r0_ref, f32[1024,512]{1,0:T(8,128)S(1)} %collective-permute-done.2.__.below_ref, f32[776,512]{1,0:T(8,128)S(1)} %collective-permute-done.6.tx_ref), custom_call_target="tpu_custom_call" | custom-call | tf_op jit(solution)/shard_map/pallas_call | solution.py:520
  47.5 0.1 shard_map.45._
  47.7 1.7 %collective-permute-done.7.__.cu_ref = f32[264,512]{1,0:T(8,128)S(1)} collective-permute-done((f32[264,512]{1,0:T(8,128)S(1)}, f32[264,512]{1,0:T(8,128)S(1)}, u32[]{:S(2)}, u32[]{:S(2)}) %collective-permute-start.7) | collective-permute-done | bytes 540704 | tf_op jit(solution)/shard_map/ppermute | solution.py:456
  49.4 3.2 %collective-permute-start.9 = (f32[264,512]{1,0:T(8,128)S(1)}, f32[264,512]{1,0:T(8,128)S(1)}, u32[]{:S(2)}, u32[]{:S(2)}) collective-permute-start(f32[264,512]{1,0:T(8,128)S(1)} %shard_map.46._), channel_id=1, source_target_pairs={{0,7},{1,0},{2,1},{3,2},{4,3},{5,4},{6,5},{7,6},{8,15},{9,8},{10,9... | collective-permute-start | bytes 1622024 | tf_op jit(solution)/shard_map/ppermute | solution.py:456
  52.6 4.3 %collective-permute-start.12 = (f32[8,256]{1,0:T(8,128)S(1)}, f32[8,256]{1,0:T(8,128)S(1)}, u32[]{:S(2)}, u32[]{:S(2)}) collective-permute-start(f32[8,256]{1,0:T(8,128)S(1)} %get-tuple-element.66.sums_ref), channel_id=1, source_target_pairs={{0,16},{8,24},{16,0},{24,8},{1,17},{9,25},{17,1},{25,9},{2,18},{10... | collective-permute-start | bytes 24584 | tf_op jit(solution)/shard_map/ppermute | solution.py:456
  56.9 4.3 %shard_map.47 = (f32[512,512]{1,0:T(8,128)S(1)}, f32[512,512]{1,0:T(8,128)S(1)}, f32[512,512]{1,0:T(8,128)S(1)}) custom-call(f32[264,512]{1,0:T(8,128)S(1)} %shard_map.46._, f32[776,512]{1,0:T(8,128)S(1)} %get-tuple-element.41._.t_ref, f32[1024,512]{1,0:T(8,128)S(1)} %get-tuple-element.43.down_ref.e_ref, f32[512,512]{1,0:T(8,128)S(1)} %get-tuple-element.44.d_ref, ...), custom_call_target="tpu_custom_call" | custom-call | tf_op jit(solution)/shard_map/pallas_call | solution.py:525
  61.1 2.7 %shard_map.48 = (f32[512,512]{1,0:T(8,128)S(1)}, f32[512,512]{1,0:T(8,128)S(1)}) custom-call(f32[512,512]{1,0:T(8,128)S(1)} %get-tuple-element.62._.yn_ref, f32[1024,512]{1,0:T(8,128)S(1)} %get-tuple-element.43.down_ref.e_ref, f32[512,512]{1,0:T(8,128)S(1)} %get-tuple-element.44.d_ref, f32[776,512]{1,0:T(8,128)S(1)} %collective-permute-done.6.tx_ref, ...), custom_call_target="tpu_custom_call" | custom-call | tf_op jit(solution)/shard_map/pallas_call | solution.py:526
  63.9 1.4 %collective-permute-done.9.cxu_ref = f32[264,512]{1,0:T(8,128)S(1)} collective-permute-done((f32[264,512]{1,0:T(8,128)S(1)}, f32[264,512]{1,0:T(8,128)S(1)}, u32[]{:S(2)}, u32[]{:S(2)}) %collective-permute-start.9) | collective-permute-done | bytes 540704 | tf_op jit(solution)/shard_map/ppermute | solution.py:456
  65.3 1.1 %shard_map.49 = (f32[8,256]{1,0:T(8,128)S(1)}, f32[512,512]{1,0:T(8,128)S(1)}) custom-call(f32[512,512]{1,0:T(8,128)S(1)} %get-tuple-element.65._.ye_ref, f32[8,256]{1,0:T(8,128)S(1)} %get-tuple-element.66.sums_ref, f32[512,512]{1,0:T(8,128)S(1)} %get-tuple-element.44.d_ref, f32[264,512]{1,0:T(8,128)S(1)} %collective-permute-done.9.cxu_ref, ...), custom_call_target="tpu_custom_call" | custom-call | tf_op jit(solution)/shard_map/pallas_call | solution.py:528
  66.4 3.0 %collective-permute-start.11 = (f32[8,256]{1,0:T(8,128)S(1)}, f32[8,256]{1,0:T(8,128)S(1)}, u32[]{:S(2)}, u32[]{:S(2)}) collective-permute-start(f32[8,256]{1,0:T(8,128)S(1)} %get-tuple-element.69.sums_ref.rest_0_), channel_id=1, source_target_pairs={{0,24},{8,0},{16,8},{24,16},{1,25},{9,1},{17,9},{25,17},{2,26},{10... | collective-permute-start | bytes 24584 | tf_op jit(solution)/shard_map/ppermute | solution.py:456
  69.4 1.0 %shard_map.50 = (f32[8,256]{1,0:T(8,128)}, f32[512,512]{1,0:T(8,128)S(1)}, f32[512,512]{1,0:T(8,128)S(1)}, f32[512,512]{1,0:T(8,128)S(1)}, f32[512,512]{1,0:T(8,128)S(1)}) custom-call(f32[28,256]{1,0:T(8,128)S(1)} %get-tuple-element.45.keep_ref, f32[512,512]{1,0:T(8,128)S(1)} %get-tuple-element.68._.yd_ref, f32[8,256]{1,0:T(8,128)S(1)} %get-tuple-element.69.sums_ref.rest_0_, ...), custom_call_target="tpu_custom_call" | custom-call | tf_op jit(solution)/shard_map/pallas_call | solution.py:530
  70.4 7.4 %collective-permute-done.12.rest_2_ = f32[8,256]{1,0:T(8,128)S(1)} collective-permute-done((f32[8,256]{1,0:T(8,128)S(1)}, f32[8,256]{1,0:T(8,128)S(1)}, u32[]{:S(2)}, u32[]{:S(2)}) %collective-permute-start.12) | collective-permute-done | bytes 8224 | tf_op jit(solution)/shard_map/ppermute | solution.py:456
  77.8 2.1 %shard_map.51 = (f32[2,14,256,256]{3,2,1,0:T(8,128)}, f32[8,256]{1,0:T(8,128)S(1)}) custom-call(f32[28,256]{1,0:T(8,128)S(1)} %get-tuple-element.45.keep_ref, f32[2,14,256,256]{3,2,1,0:T(8,128)} %get-tuple-element.50._, f32[512,512]{1,0:T(8,128)S(1)} %get-tuple-element.49.c_ref, ...), custom_call_target="tpu_custom_call", output_to_operand_aliasing={{0}: (1, {})} | custom-call | tf_op jit(solution)/shard_map/pallas_call | solution.py:535
  79.9 1.1 %shard_map.52 = f32[2,14,256,256]{3,2,1,0:T(8,128)} custom-call(f32[28,256]{1,0:T(8,128)S(1)} %get-tuple-element.45.keep_ref, f32[2,14,256,256]{3,2,1,0:T(8,128)} %get-tuple-element.74._, f32[8,256]{1,0:T(8,128)S(1)} %get-tuple-element.75.twice_ref, f32[1024,512]{1,0:T(8,128)S(1)} %get-tuple-element.43.down_ref.e_ref, ...), custom_call_target="tpu_custom_call", output_to_operand_aliasing={{}: (1, {})} | custom-call | tf_op jit(solution)/shard_map/pallas_call | solution.py:539
  (14 shorter events, 0.3 us)
Async XLA Ops:
  2.5 32.9 %collective-permute-start.2 = (f32[1024,512]{1,0:T(8,128)S(1)}, f32[1024,512]{1,0:T(8,128)S(1)}, u32[]{:S(2)}, u32[]{:S(2)}) collective-permute-start(f32[1024,512]{1,0:T(8,128)S(1)} %get-tuple-element.43.down_ref.e_ref), channel_id=1, source_target_pairs={{0,7},{1,0},{2,1},{3,2},{4,3},{5,4},{6,5},{7,6},{8,15},{9,8},{10,9... | collective-permute-start | bytes 6291464 | tf_op jit(solution)/shard_map/ppermute | solution.py:456
  5.9 5.7 %copy-start = (s32[1,1,2,13]{3,2,1,0:T(2,128)S(1)}, s32[1,1,2,13]{3,2,1,0:T(2,128)}, u32[]{:S(2)}) copy-start(s32[1,1,2,13]{3,2,1,0:T(2,128)} %param.5) | copy-start | bytes 316
  6.0 38.8 %collective-permute-start.6 = (f32[776,512]{1,0:T(8,128)S(1)}, f32[776,512]{1,0:T(8,128)S(1)}, u32[]{:S(2)}, u32[]{:S(2)}) collective-permute-start(f32[776,512]{1,0:T(8,128)S(1)} %get-tuple-element.41._.t_ref), channel_id=1, source_target_pairs={{0,24},{8,0},{16,8},{24,16},{1,25},{9,1},{17,9},{25,17},{2,26},{10... | collective-permute-start | bytes 4767752 | tf_op jit(solution)/shard_map/ppermute | solution.py:456
  11.6 24.2 %collective-permute-start.5 = (f32[264,512]{1,0:T(8,128)S(1)}, f32[264,512]{1,0:T(8,128)S(1)}, u32[]{:S(2)}, u32[]{:S(2)}) collective-permute-start(f32[264,512]{1,0:T(8,128)S(1)} %get-tuple-element.42._), channel_id=1, source_target_pairs={{0,1},{1,2},{2,3},{3,4},{4,5},{5,6},{6,7},{7,0},{8,9},{9,10},{10,1... | collective-permute-start | bytes 1622024 | tf_op jit(solution)/shard_map/ppermute | solution.py:456
  12.7 1.2 %collective-permute-start = (f32[16,256]{1,0:T(8,128)S(1)}, f32[16,256]{1,0:T(8,128)S(1)}, u32[]{:S(2)}, u32[]{:S(2)}) collective-permute-start(f32[16,256]{1,0:T(8,128)S(1)} %get-tuple-element.46.sums_ref), channel_id=1, source_target_pairs={{0,1},{1,0},{2,3},{3,2},{4,5},{5,4},{6,7},{7,6},{8,9},{9,8},{10,11... | collective-permute-start | bytes 49160 | tf_op jit(solution)/shard_map/ppermute | solution.py:461
  17.9 4.0 %collective-permute-start.1 = (f32[16,256]{1,0:T(8,128)S(1)}, f32[16,256]{1,0:T(8,128)S(1)}, u32[]{:S(2)}, u32[]{:S(2)}) collective-permute-start(f32[16,256]{1,0:T(8,128)S(1)} %get-tuple-element.48.sums_ref), channel_id=1, source_target_pairs={{0,4},{1,5},{2,6},{3,7},{4,0},{5,1},{6,2},{7,3},{8,12},{9,13},{10,... | collective-permute-start | bytes 49160 | tf_op jit(solution)/shard_map/ppermute | solution.py:461
  29.8 6.0 %collective-permute-start.4 = (f32[16,256]{1,0:T(8,128)S(1)}, f32[16,256]{1,0:T(8,128)S(1)}, u32[]{:S(2)}, u32[]{:S(2)}) collective-permute-start(f32[16,256]{1,0:T(8,128)S(1)} %get-tuple-element.53.sums_ref), channel_id=1, source_target_pairs={{0,2},{1,3},{2,0},{3,1},{4,6},{5,7},{6,4},{7,5},{8,10},{9,11},{10,... | collective-permute-start | bytes 49160 | tf_op jit(solution)/shard_map/ppermute | solution.py:461
  35.5 12.0 %collective-permute-start.3 = (f32[272,512]{1,0:T(8,128)S(1)}, f32[272,512]{1,0:T(8,128)S(1)}, u32[]{:S(2)}, u32[]{:S(2)}) collective-permute-start(f32[272,512]{1,0:T(8,128)S(1)} %shard_map.42._), channel_id=1, source_target_pairs={{0,1},{1,2},{2,3},{3,4},{4,5},{5,6},{6,7},{7,0},{8,9},{9,10},{10,1... | collective-permute-start | bytes 1671176 | tf_op jit(solution)/shard_map/ppermute | solution.py:456
  37.5 40.3 %collective-permute-start.8 = (f32[776,512]{1,0:T(8,128)S(1)}, f32[776,512]{1,0:T(8,128)S(1)}, u32[]{:S(2)}, u32[]{:S(2)}) collective-permute-start(f32[776,512]{1,0:T(8,128)S(1)} %get-tuple-element.54._), channel_id=1, source_target_pairs={{0,8},{8,16},{16,24},{24,0},{1,9},{9,17},{17,25},{25,1},{2,10},{10... | collective-permute-start | bytes 4767752 | tf_op jit(solution)/shard_map/ppermute | solution.py:456
  39.3 10.1 %collective-permute-start.7 = (f32[264,512]{1,0:T(8,128)S(1)}, f32[264,512]{1,0:T(8,128)S(1)}, u32[]{:S(2)}, u32[]{:S(2)}) collective-permute-start(f32[264,512]{1,0:T(8,128)S(1)} %get-tuple-element.58), channel_id=1, source_target_pairs={{0,7},{1,0},{2,1},{3,2},{4,3},{5,4},{6,5},{7,6},{8,15},{9,8},{10,9... | collective-permute-start | bytes 1622024 | tf_op jit(solution)/shard_map/ppermute | solution.py:456
  47.5 22.0 %collective-permute-start.10 = (f32[512,512]{1,0:T(8,128)S(1)}, f32[512,512]{1,0:T(8,128)S(1)}, u32[]{:S(2)}, u32[]{:S(2)}) collective-permute-start(f32[512,512]{1,0:T(8,128)S(1)} %get-tuple-element.56.__), channel_id=1, source_target_pairs={{0,1},{1,2},{2,3},{3,4},{4,5},{5,6},{6,7},{7,0},{8,9},{9,10},{10,1... | collective-permute-start | bytes 3145736 | tf_op jit(solution)/shard_map/ppermute | solution.py:456
  47.6 32.3 %collective-permute-start.13 = (f32[512,512]{1,0:T(8,128)S(1)}, f32[512,512]{1,0:T(8,128)S(1)}, u32[]{:S(2)}, u32[]{:S(2)}) collective-permute-start(f32[512,512]{1,0:T(8,128)S(1)} %shard_map.45._), channel_id=1, source_target_pairs={{0,1},{1,2},{2,3},{3,4},{4,5},{5,6},{6,7},{7,0},{8,9},{9,10},{10,1... | collective-permute-start | bytes 3145736 | tf_op jit(solution)/shard_map/ppermute | solution.py:456
  49.4 15.9 %collective-permute-start.9 = (f32[264,512]{1,0:T(8,128)S(1)}, f32[264,512]{1,0:T(8,128)S(1)}, u32[]{:S(2)}, u32[]{:S(2)}) collective-permute-start(f32[264,512]{1,0:T(8,128)S(1)} %shard_map.46._), channel_id=1, source_target_pairs={{0,7},{1,0},{2,1},{3,2},{4,3},{5,4},{6,5},{7,6},{8,15},{9,8},{10,9... | collective-permute-start | bytes 1622024 | tf_op jit(solution)/shard_map/ppermute | solution.py:456
  52.6 25.2 %collective-permute-start.12 = (f32[8,256]{1,0:T(8,128)S(1)}, f32[8,256]{1,0:T(8,128)S(1)}, u32[]{:S(2)}, u32[]{:S(2)}) collective-permute-start(f32[8,256]{1,0:T(8,128)S(1)} %get-tuple-element.66.sums_ref), channel_id=1, source_target_pairs={{0,16},{8,24},{16,0},{24,8},{1,17},{9,25},{17,1},{25,9},{2,18},{10... | collective-permute-start | bytes 24584 | tf_op jit(solution)/shard_map/ppermute | solution.py:456
  66.4 11.4 %collective-permute-start.11 = (f32[8,256]{1,0:T(8,128)S(1)}, f32[8,256]{1,0:T(8,128)S(1)}, u32[]{:S(2)}, u32[]{:S(2)}) collective-permute-start(f32[8,256]{1,0:T(8,128)S(1)} %get-tuple-element.69.sums_ref.rest_0_), channel_id=1, source_target_pairs={{0,24},{8,0},{16,8},{24,16},{1,25},{9,1},{17,9},{25,17},{2,26},{10... | collective-permute-start | bytes 24584 | tf_op jit(solution)/shard_map/ppermute | solution.py:456

commit v12 on v11

--- a/solution.py
+++ b/solution.py
@@ -336,12 +336,17 @@
     yd_ref[...] = yd0_ref[...] + dot3(n, eu, NN)
 
 
-def r_body(layers, size, _, r0_ref, below_ref, tx_ref, rs_ref, re_ref):
+def r_e_body(layers, size, _, r0_ref, below_ref, tx_ref, re_ref):
+    n = layers * size
+    su, nx = split(below_ref[:n, :]), split(tx_ref[:n, :])
+    re_ref[...] = r0_ref[n:, :] + dot3(su, nx, NN)
+
+
+def r_s_body(layers, size, _, r0_ref, below_ref, tx_ref, rs_ref):
     n = layers * size
     su, eu, nx = split(below_ref[:n, :]), split(below_ref[n:, :]), split(tx_ref[:n, :])
     cx = split(whole_sym(take_sym(tx_ref[n:, :], layers, size), layers))
     rs_ref[...] = r0_ref[:n, :] + dot3(su, cx, NN) + dot3(eu, nx, NT)
-    re_ref[...] = r0_ref[n:, :] + dot3(su, nx, NN)
 
 
 def hand_body(layers, size, _, __, tx_ref, cx_ref):
@@ -517,7 +522,8 @@
     own, g = go(g_body, outs=[total, (n + tall, n)], spaces=[hbm] + [vmem] * 5)(yc_up, own, more, g0, below, gc_in)
     g_in = passed_along(g, "row", 1)
     Cp_u = passed_along(Cp, "col", -1)
-    rs, re = go(r_body, outs=[panel, panel], spaces=[hbm] + [vmem] * 3)(g, r0, below, T_x)
+    (re,) = go(r_e_body, outs=[panel], spaces=[hbm] + [vmem] * 3)(g, r0, below, T_x)
+    (rs,) = go(r_s_body, outs=[panel], spaces=[hbm] + [vmem] * 3)(re, r0, below, T_x)
     (rs,) = go(copy_body, outs=[panel], spaces=[hbm] * 2 + [vmem])(yc_in, re, rs)
     rs_in, re_in = passed_along(rs, "col", 1), passed_along(re, "col", 1)
     (Cp_x,) = go(hand_body, outs=[packed], spaces=[hbm] * 2 + [vmem])(rs, Cp_u, T_x)

time: 81.3 us -> 81.3 us (level)
  starting transfers between devices: 25 us -> 23.5 us
  waiting for transfers between devices: 21.6 us -> 22.9 us
    ppermute x11, starting transfers between devices: 22.1 us -> 20.7 us  [passed_along(): lax.ppermute(value, axis, [(i, (i + by) % peers) for i in range(peers)])]
    ppermute x11, waiting for transfers between devices: 17.5 us -> 18.7 us  [passed_along(): lax.ppermute(value, axis, [(i, (i + by) % peers) for i in range(peers)])]
    pallas_call x1 -> x2, Pallas kernels: 2.72 us -> 2.89 us  [the longest x1 1.91 us: shards(): go(r_s_body, outs=[panel], spaces=[hbm] + [vmem] * 3)(re, r0, below, T_x)]
where the time goes in v12:
time: 81.3 us; the launch traced here: 81.1 us
  Pallas kernels  34.4 us (42%)
  starting transfers between devices  23.5 us (29%)
  waiting for transfers between devices  22.9 us (28%)
    ppermute x11, starting transfers between devices, passed_along(): lax.ppermute(value, axis, [(i, (i + by) % peers) for i in range(peers)])  20.7 us
    ppermute x11, waiting for transfers between devices, passed_along(): lax.ppermute(value, axis, [(i, (i + by) % peers) for i in range(peers)])  18.7 us
    pallas_call x1, Pallas kernels, shards(): go(local_y_body, outs=[sums, (layers, slots, size, size), packed] + [pane...  7.91 us
    pallas_call x1, Pallas kernels, shards(): go(early_body, outs=[panel] * 3, spaces=[hbm] + [vmem] * 8)  4.27 us
    ppermute x3, waiting for transfers between devices, swapped(): return lax.ppermute(value, axis, [(i, i ^ bit) for i in range(peers)])  4.16 us
    pallas_call x1, Pallas kernels, shards(): go(local_g_body, outs=[sums, (n + tall, n), (2 * n, n), packed], spaces=[...  3.88 us
    ppermute x3, starting transfers between devices, swapped(): return lax.ppermute(value, axis, [(i, i ^ bit) for i in range(peers)])  2.78 us
    pallas_call x1, Pallas kernels, shards(): go(middle_body, outs=[panel, panel], spaces=[hbm] + [vmem] * 5)  2.72 us
  transfers between devices with their start and end apart: 14, of which 7 were waited for; matrix products, arithmetic and copies ran while one was open for 0% of the time, Pallas kernels for 38%

profile of v12, /device:TPU:0, one launch (start us, length us, event | category | flops | bytes accessed | tf_op | source)
XLA Modules:
  0.0 81.1 jit_solution(1186006420674306329)
XLA Ops:
  0.0 2.5 %shard_map.37 = (f32[776,512]{1,0:T(8,128)S(1)}, f32[1024,512]{1,0:T(8,128)S(1)}) custom-call(s32[2,13]{1,0:T(2,128)} %bitcast.4, f32[2,14,256,256]{3,2,1,0:T(8,128)} %bitcast.7, f32[2,256]{1,0:T(2,128)} %bitcast.9), custom_call_target="tpu_custom_call" | custom-call | tf_op jit(solution)/shard_map/pallas_call | solution.py:491
  2.5 3.4 %collective-permute-start.2 = (f32[1024,512]{1,0:T(8,128)S(1)}, f32[1024,512]{1,0:T(8,128)S(1)}, u32[]{:S(2)}, u32[]{:S(2)}) collective-permute-start(f32[1024,512]{1,0:T(8,128)S(1)} %get-tuple-element.41.down_ref.e_ref), channel_id=1, source_target_pairs={{0,7},{1,0},{2,1},{3,2},{4,3},{5,4},{6,5},{7,6},{8,15},{9,8},{10,9... | collective-permute-start | bytes 6291464 | tf_op jit(solution)/shard_map/ppermute | solution.py:461
  6.0 3.6 %collective-permute-start.6 = (f32[776,512]{1,0:T(8,128)S(1)}, f32[776,512]{1,0:T(8,128)S(1)}, u32[]{:S(2)}, u32[]{:S(2)}) collective-permute-start(f32[776,512]{1,0:T(8,128)S(1)} %get-tuple-element.39._.t_ref), channel_id=1, source_target_pairs={{0,24},{8,0},{16,8},{24,16},{1,25},{9,1},{17,9},{25,17},{2,26},{10... | collective-permute-start | bytes 4767752 | tf_op jit(solution)/shard_map/ppermute | solution.py:461
  9.6 2.1 %shard_map.38 = (f32[512,512]{1,0:T(8,128)S(1)}, f32[264,512]{1,0:T(8,128)S(1)}) custom-call(s32[2,13]{1,0:T(2,128)} %bitcast.5, f32[2,14,256,256]{3,2,1,0:T(8,128)} %bitcast.8, f32[776,512]{1,0:T(8,128)S(1)} %get-tuple-element.39._.t_ref), custom_call_target="tpu_custom_call" | custom-call | tf_op jit(solution)/shard_map/pallas_call | solution.py:498
  11.7 1.1 %shard_map.39 = (f32[264,512]{1,0:T(8,128)S(1)}, f32[512,512]{1,0:T(8,128)S(1)}, f32[28,256]{1,0:T(8,128)S(1)}, f32[16,256]{1,0:T(8,128)S(1)}) custom-call(s32[2,13]{1,0:T(2,128)S(1)} %bitcast.6, f32[264,512]{1,0:T(8,128)S(1)} %get-tuple-element.40._, f32[1024,512]{1,0:T(8,128)S(1)} %get-tuple-element.41.down_ref.e_ref, ...), custom_call_target="tpu_custom_call" | custom-call | tf_op jit(solution)/shard_map/pallas_call | solution.py:502
  12.8 0.1 collective-permute-start
  12.9 1.2 %collective-permute-done.more_ref = f32[16,256]{1,0:T(8,128)S(1)} collective-permute-done((f32[16,256]{1,0:T(8,128)S(1)}, f32[16,256]{1,0:T(8,128)S(1)}, u32[]{:S(2)}, u32[]{:S(2)}) %collective-permute-start) | collective-permute-done | bytes 16416 | tf_op jit(solution)/shard_map/ppermute | solution.py:466
  14.1 3.9 %shard_map.40 = (f32[16,256]{1,0:T(8,128)S(1)}, f32[776,512]{1,0:T(8,128)S(1)}, f32[1024,512]{1,0:T(8,128)S(1)}, f32[264,512]{1,0:T(8,128)S(1)}) custom-call(f32[264,512]{1,0:T(8,128)S(1)} %get-tuple-element.40._, f32[16,256]{1,0:T(8,128)S(1)} %get-tuple-element.44.sums_ref, f32[16,256]{1,0:T(8,128)S(1)} %collective-permute-done.more_ref, ...), custom_call_target="tpu_custom_call" | custom-call | tf_op jit(solution)/shard_map/pallas_call | solution.py:511
  17.9 1.0 %collective-permute-start.1 = (f32[16,256]{1,0:T(8,128)S(1)}, f32[16,256]{1,0:T(8,128)S(1)}, u32[]{:S(2)}, u32[]{:S(2)}) collective-permute-start(f32[16,256]{1,0:T(8,128)S(1)} %get-tuple-element.46.sums_ref), channel_id=1, source_target_pairs={{0,4},{1,5},{2,6},{3,7},{4,0},{5,1},{6,2},{7,3},{8,12},{9,13},{10,... | collective-permute-start | bytes 49160 | tf_op jit(solution)/shard_map/ppermute | solution.py:466
  18.9 3.0 %collective-permute-done.1.more_ref = f32[16,256]{1,0:T(8,128)S(1)} collective-permute-done((f32[16,256]{1,0:T(8,128)S(1)}, f32[16,256]{1,0:T(8,128)S(1)}, u32[]{:S(2)}, u32[]{:S(2)}) %collective-permute-start.1) | collective-permute-done | bytes 16416 | tf_op jit(solution)/shard_map/ppermute | solution.py:466
  21.9 7.9 %shard_map.41 = (f32[16,256]{1,0:T(8,128)S(1)}, f32[2,14,256,256]{3,2,1,0:T(8,128)}, f32[264,512]{1,0:T(8,128)S(1)}, f32[512,512]{1,0:T(8,128)S(1)}, f32[512,512...) custom-call(f32[776,512]{1,0:T(8,128)S(1)} %get-tuple-element.45._.g0_ref, ...), custom_call_target="tpu_custom_call" | custom-call | tf_op jit(solution)/shard_map/pallas_call | solution.py:515
  29.8 1.7 %collective-permute-start.4 = (f32[16,256]{1,0:T(8,128)S(1)}, f32[16,256]{1,0:T(8,128)S(1)}, u32[]{:S(2)}, u32[]{:S(2)}) collective-permute-start(f32[16,256]{1,0:T(8,128)S(1)} %get-tuple-element.51.sums_ref), channel_id=1, source_target_pairs={{0,2},{1,3},{2,0},{3,1},{4,6},{5,7},{6,4},{7,5},{8,10},{9,11},{10,... | collective-permute-start | bytes 49160 | tf_op jit(solution)/shard_map/ppermute | solution.py:466
  31.5 3.9 %collective-permute-done.2.__.below_ref = f32[1024,512]{1,0:T(8,128)S(1)} collective-permute-done((f32[1024,512]{1,0:T(8,128)S(1)}, f32[1024,512]{1,0:T(8,128)S(1)}, u32[]{:S(2)}, u32[]{:S(2)}) %collective-permute-start.2) | collective-permute-done | bytes 2097184 | tf_op jit(solution)/shard_map/ppermute | solution.py:461
  35.5 0.2 collective-permute-start.3
  35.8 1.7 %shard_map.43 = (f32[8,256]{1,0:T(8,128)S(1)}, f32[776,512]{1,0:T(8,128)S(1)}) custom-call(f32[272,512]{1,0:T(8,128)S(1)} %shard_map.42._, f32[16,256]{1,0:T(8,128)S(1)} %get-tuple-element.51.sums_ref, f32[16,256]{1,0:T(8,128)S(1)} %collective-permute-done.4.more_ref, f32[776,512]{1,0:T(8,128)S(1)} %get-tuple-element.45._.g0_ref, ...), custom_call_target="tpu_custom_call" | custom-call | tf_op jit(solution)/shard_map/pallas_call | solution.py:522
  37.5 1.8 %collective-permute-start.8 = (f32[776,512]{1,0:T(8,128)S(1)}, f32[776,512]{1,0:T(8,128)S(1)}, u32[]{:S(2)}, u32[]{:S(2)}) collective-permute-start(f32[776,512]{1,0:T(8,128)S(1)} %get-tuple-element.52._), channel_id=1, source_target_pairs={{0,8},{8,16},{16,24},{24,0},{1,9},{9,17},{17,25},{25,1},{2,10},{10... | collective-permute-start | bytes 4767752 | tf_op jit(solution)/shard_map/ppermute | solution.py:461
  39.3 2.3 %collective-permute-start.7 = (f32[264,512]{1,0:T(8,128)S(1)}, f32[264,512]{1,0:T(8,128)S(1)}, u32[]{:S(2)}, u32[]{:S(2)}) collective-permute-start(f32[264,512]{1,0:T(8,128)S(1)} %get-tuple-element.54), channel_id=1, source_target_pairs={{0,7},{1,0},{2,1},{3,2},{4,3},{5,4},{6,5},{7,6},{8,15},{9,8},{10,9... | collective-permute-start | bytes 1622024 | tf_op jit(solution)/shard_map/ppermute | solution.py:461
  41.6 3.2 %collective-permute-done.6.tx_ref = f32[776,512]{1,0:T(8,128)S(1)} collective-permute-done((f32[776,512]{1,0:T(8,128)S(1)}, f32[776,512]{1,0:T(8,128)S(1)}, u32[]{:S(2)}, u32[]{:S(2)}) %collective-permute-start.6) | collective-permute-done | bytes 1589280 | tf_op jit(solution)/shard_map/ppermute | solution.py:461
  44.8 1.0 %shard_map.44._.__ = f32[512,512]{1,0:T(8,128)S(1)} custom-call(f32[776,512]{1,0:T(8,128)S(1)} %get-tuple-element.52._, f32[1024,512]{1,0:T(8,128)S(1)} %get-tuple-element.53.r0_ref, f32[1024,512]{1,0:T(8,128)S(1)} %collective-permute-done.2.__.below_ref, f32[776,512]{1,0:T(8,128)S(1)} %collective-permute-done.6.tx_ref), custom_call_target="tpu_custom_call" | custom-call | tf_op jit(solution)/shard_map/pallas_call | solution.py:525
  45.8 1.9 %shard_map.45.from_ref = f32[512,512]{1,0:T(8,128)S(1)} custom-call(f32[512,512]{1,0:T(8,128)S(1)} %shard_map.44._.__, f32[1024,512]{1,0:T(8,128)S(1)} %get-tuple-element.53.r0_ref, f32[1024,512]{1,0:T(8,128)S(1)} %collective-permute-done.2.__.below_ref, f32[776,512]{1,0:T(8,128)S(1)} %collective-permute-done.6.tx_ref), custom_call_target="tpu_custom_call" | custom-call | tf_op jit(solution)/shard_map/pallas_call | solution.py:526
  47.9 3.1 %collective-permute-done.7.__.cu_ref = f32[264,512]{1,0:T(8,128)S(1)} collective-permute-done((f32[264,512]{1,0:T(8,128)S(1)}, f32[264,512]{1,0:T(8,128)S(1)}, u32[]{:S(2)}, u32[]{:S(2)}) %collective-permute-start.7) | collective-permute-done | bytes 540704 | tf_op jit(solution)/shard_map/ppermute | solution.py:461
  51.1 3.2 %collective-permute-start.9 = (f32[264,512]{1,0:T(8,128)S(1)}, f32[264,512]{1,0:T(8,128)S(1)}, u32[]{:S(2)}, u32[]{:S(2)}) collective-permute-start(f32[264,512]{1,0:T(8,128)S(1)} %shard_map.47._), channel_id=1, source_target_pairs={{0,7},{1,0},{2,1},{3,2},{4,3},{5,4},{6,5},{7,6},{8,15},{9,8},{10,9... | collective-permute-start | bytes 1622024 | tf_op jit(solution)/shard_map/ppermute | solution.py:461
  54.2 4.4 %collective-permute-start.12 = (f32[8,256]{1,0:T(8,128)S(1)}, f32[8,256]{1,0:T(8,128)S(1)}, u32[]{:S(2)}, u32[]{:S(2)}) collective-permute-start(f32[8,256]{1,0:T(8,128)S(1)} %get-tuple-element.62.sums_ref), channel_id=1, source_target_pairs={{0,16},{8,24},{16,0},{24,8},{1,17},{9,25},{17,1},{25,9},{2,18},{10... | collective-permute-start | bytes 24584 | tf_op jit(solution)/shard_map/ppermute | solution.py:461
  58.7 4.3 %shard_map.48 = (f32[512,512]{1,0:T(8,128)S(1)}, f32[512,512]{1,0:T(8,128)S(1)}, f32[512,512]{1,0:T(8,128)S(1)}) custom-call(f32[264,512]{1,0:T(8,128)S(1)} %shard_map.47._, f32[776,512]{1,0:T(8,128)S(1)} %get-tuple-element.39._.t_ref, f32[1024,512]{1,0:T(8,128)S(1)} %get-tuple-element.41.down_ref.e_ref, f32[512,512]{1,0:T(8,128)S(1)} %get-tuple-element.42.d_ref, ...), custom_call_target="tpu_custom_call" | custom-call | tf_op jit(solution)/shard_map/pallas_call | solution.py:531
  62.9 2.7 %shard_map.49 = (f32[512,512]{1,0:T(8,128)S(1)}, f32[512,512]{1,0:T(8,128)S(1)}) custom-call(f32[512,512]{1,0:T(8,128)S(1)} %get-tuple-element.58._.yn_ref, f32[1024,512]{1,0:T(8,128)S(1)} %get-tuple-element.41.down_ref.e_ref, f32[512,512]{1,0:T(8,128)S(1)} %get-tuple-element.42.d_ref, f32[776,512]{1,0:T(8,128)S(1)} %collective-permute-done.6.tx_ref, ...), custom_call_target="tpu_custom_call" | custom-call | tf_op jit(solution)/shard_map/pallas_call | solution.py:532
  65.7 1.3 %collective-permute-done.9.cxu_ref = f32[264,512]{1,0:T(8,128)S(1)} collective-permute-done((f32[264,512]{1,0:T(8,128)S(1)}, f32[264,512]{1,0:T(8,128)S(1)}, u32[]{:S(2)}, u32[]{:S(2)}) %collective-permute-start.9) | collective-permute-done | bytes 540704 | tf_op jit(solution)/shard_map/ppermute | solution.py:461
  67.0 1.1 %shard_map.50 = (f32[8,256]{1,0:T(8,128)S(1)}, f32[512,512]{1,0:T(8,128)S(1)}) custom-call(f32[512,512]{1,0:T(8,128)S(1)} %get-tuple-element.61._.ye_ref, f32[8,256]{1,0:T(8,128)S(1)} %get-tuple-element.62.sums_ref, f32[512,512]{1,0:T(8,128)S(1)} %get-tuple-element.42.d_ref, f32[264,512]{1,0:T(8,128)S(1)} %collective-permute-done.9.cxu_ref, ...), custom_call_target="tpu_custom_call" | custom-call | tf_op jit(solution)/shard_map/pallas_call | solution.py:534
  68.1 1.5 %collective-permute-start.11 = (f32[8,256]{1,0:T(8,128)S(1)}, f32[8,256]{1,0:T(8,128)S(1)}, u32[]{:S(2)}, u32[]{:S(2)}) collective-permute-start(f32[8,256]{1,0:T(8,128)S(1)} %get-tuple-element.65.sums_ref.rest_0_), channel_id=1, source_target_pairs={{0,24},{8,0},{16,8},{24,16},{1,25},{9,1},{17,9},{25,17},{2,26},{10... | collective-permute-start | bytes 24584 | tf_op jit(solution)/shard_map/ppermute | solution.py:461
  69.6 1.0 %shard_map.51 = (f32[8,256]{1,0:T(8,128)}, f32[512,512]{1,0:T(8,128)S(1)}, f32[512,512]{1,0:T(8,128)S(1)}, f32[512,512]{1,0:T(8,128)S(1)}, f32[512,512]{1,0:T(8,128)S(1)}) custom-call(f32[28,256]{1,0:T(8,128)S(1)} %get-tuple-element.43.keep_ref, f32[512,512]{1,0:T(8,128)S(1)} %get-tuple-element.64._.yd_ref, f32[8,256]{1,0:T(8,128)S(1)} %get-tuple-element.65.sums_ref.rest_0_, ...), custom_call_target="tpu_custom_call" | custom-call | tf_op jit(solution)/shard_map/pallas_call | solution.py:536
  70.5 7.2 %collective-permute-done.12.rest_2_ = f32[8,256]{1,0:T(8,128)S(1)} collective-permute-done((f32[8,256]{1,0:T(8,128)S(1)}, f32[8,256]{1,0:T(8,128)S(1)}, u32[]{:S(2)}, u32[]{:S(2)}) %collective-permute-start.12) | collective-permute-done | bytes 8224 | tf_op jit(solution)/shard_map/ppermute | solution.py:461
  77.8 2.1 %shard_map.52 = (f32[2,14,256,256]{3,2,1,0:T(8,128)}, f32[8,256]{1,0:T(8,128)S(1)}) custom-call(f32[28,256]{1,0:T(8,128)S(1)} %get-tuple-element.43.keep_ref, f32[2,14,256,256]{3,2,1,0:T(8,128)} %get-tuple-element.48._, f32[512,512]{1,0:T(8,128)S(1)} %get-tuple-element.47.c_ref, ...), custom_call_target="tpu_custom_call", output_to_operand_aliasing={{0}: (1, {})} | custom-call | tf_op jit(solution)/shard_map/pallas_call | solution.py:541
  79.9 1.1 %shard_map.53 = f32[2,14,256,256]{3,2,1,0:T(8,128)} custom-call(f32[28,256]{1,0:T(8,128)S(1)} %get-tuple-element.43.keep_ref, f32[2,14,256,256]{3,2,1,0:T(8,128)} %get-tuple-element.70._, f32[8,256]{1,0:T(8,128)S(1)} %get-tuple-element.71.twice_ref, f32[1024,512]{1,0:T(8,128)S(1)} %get-tuple-element.41.down_ref.e_ref, ...), custom_call_target="tpu_custom_call", output_to_operand_aliasing={{}: (1, {})} | custom-call | tf_op jit(solution)/shard_map/pallas_call | solution.py:545
  (15 shorter events, 0.3 us)
Async XLA Ops:
  2.5 33.0 %collective-permute-start.2 = (f32[1024,512]{1,0:T(8,128)S(1)}, f32[1024,512]{1,0:T(8,128)S(1)}, u32[]{:S(2)}, u32[]{:S(2)}) collective-permute-start(f32[1024,512]{1,0:T(8,128)S(1)} %get-tuple-element.41.down_ref.e_ref), channel_id=1, source_target_pairs={{0,7},{1,0},{2,1},{3,2},{4,3},{5,4},{6,5},{7,6},{8,15},{9,8},{10,9... | collective-permute-start | bytes 6291464 | tf_op jit(solution)/shard_map/ppermute | solution.py:461
  6.0 5.8 %copy-start = (s32[1,1,2,13]{3,2,1,0:T(2,128)S(1)}, s32[1,1,2,13]{3,2,1,0:T(2,128)}, u32[]{:S(2)}) copy-start(s32[1,1,2,13]{3,2,1,0:T(2,128)} %param.5) | copy-start | bytes 316
  6.0 38.8 %collective-permute-start.6 = (f32[776,512]{1,0:T(8,128)S(1)}, f32[776,512]{1,0:T(8,128)S(1)}, u32[]{:S(2)}, u32[]{:S(2)}) collective-permute-start(f32[776,512]{1,0:T(8,128)S(1)} %get-tuple-element.39._.t_ref), channel_id=1, source_target_pairs={{0,24},{8,0},{16,8},{24,16},{1,25},{9,1},{17,9},{25,17},{2,26},{10... | collective-permute-start | bytes 4767752 | tf_op jit(solution)/shard_map/ppermute | solution.py:461
  11.6 24.1 %collective-permute-start.5 = (f32[264,512]{1,0:T(8,128)S(1)}, f32[264,512]{1,0:T(8,128)S(1)}, u32[]{:S(2)}, u32[]{:S(2)}) collective-permute-start(f32[264,512]{1,0:T(8,128)S(1)} %get-tuple-element.40._), channel_id=1, source_target_pairs={{0,1},{1,2},{2,3},{3,4},{4,5},{5,6},{6,7},{7,0},{8,9},{9,10},{10,1... | collective-permute-start | bytes 1622024 | tf_op jit(solution)/shard_map/ppermute | solution.py:461
  12.8 1.2 %collective-permute-start = (f32[16,256]{1,0:T(8,128)S(1)}, f32[16,256]{1,0:T(8,128)S(1)}, u32[]{:S(2)}, u32[]{:S(2)}) collective-permute-start(f32[16,256]{1,0:T(8,128)S(1)} %get-tuple-element.44.sums_ref), channel_id=1, source_target_pairs={{0,1},{1,0},{2,3},{3,2},{4,5},{5,4},{6,7},{7,6},{8,9},{9,8},{10,11... | collective-permute-start | bytes 49160 | tf_op jit(solution)/shard_map/ppermute | solution.py:466
  17.9 4.0 %collective-permute-start.1 = (f32[16,256]{1,0:T(8,128)S(1)}, f32[16,256]{1,0:T(8,128)S(1)}, u32[]{:S(2)}, u32[]{:S(2)}) collective-permute-start(f32[16,256]{1,0:T(8,128)S(1)} %get-tuple-element.46.sums_ref), channel_id=1, source_target_pairs={{0,4},{1,5},{2,6},{3,7},{4,0},{5,1},{6,2},{7,3},{8,12},{9,13},{10,... | collective-permute-start | bytes 49160 | tf_op jit(solution)/shard_map/ppermute | solution.py:466
  29.8 5.9 %collective-permute-start.4 = (f32[16,256]{1,0:T(8,128)S(1)}, f32[16,256]{1,0:T(8,128)S(1)}, u32[]{:S(2)}, u32[]{:S(2)}) collective-permute-start(f32[16,256]{1,0:T(8,128)S(1)} %get-tuple-element.51.sums_ref), channel_id=1, source_target_pairs={{0,2},{1,3},{2,0},{3,1},{4,6},{5,7},{6,4},{7,5},{8,10},{9,11},{10,... | collective-permute-start | bytes 49160 | tf_op jit(solution)/shard_map/ppermute | solution.py:466
  35.5 12.2 %collective-permute-start.3 = (f32[272,512]{1,0:T(8,128)S(1)}, f32[272,512]{1,0:T(8,128)S(1)}, u32[]{:S(2)}, u32[]{:S(2)}) collective-permute-start(f32[272,512]{1,0:T(8,128)S(1)} %shard_map.42._), channel_id=1, source_target_pairs={{0,1},{1,2},{2,3},{3,4},{4,5},{5,6},{6,7},{7,0},{8,9},{9,10},{10,1... | collective-permute-start | bytes 1671176 | tf_op jit(solution)/shard_map/ppermute | solution.py:461
  37.5 40.3 %collective-permute-start.8 = (f32[776,512]{1,0:T(8,128)S(1)}, f32[776,512]{1,0:T(8,128)S(1)}, u32[]{:S(2)}, u32[]{:S(2)}) collective-permute-start(f32[776,512]{1,0:T(8,128)S(1)} %get-tuple-element.52._), channel_id=1, source_target_pairs={{0,8},{8,16},{16,24},{24,0},{1,9},{9,17},{17,25},{25,1},{2,10},{10... | collective-permute-start | bytes 4767752 | tf_op jit(solution)/shard_map/ppermute | solution.py:461
  39.3 11.8 %collective-permute-start.7 = (f32[264,512]{1,0:T(8,128)S(1)}, f32[264,512]{1,0:T(8,128)S(1)}, u32[]{:S(2)}, u32[]{:S(2)}) collective-permute-start(f32[264,512]{1,0:T(8,128)S(1)} %get-tuple-element.54), channel_id=1, source_target_pairs={{0,7},{1,0},{2,1},{3,2},{4,3},{5,4},{6,5},{7,6},{8,15},{9,8},{10,9... | collective-permute-start | bytes 1622024 | tf_op jit(solution)/shard_map/ppermute | solution.py:461
  45.8 23.8 %collective-permute-start.10 = (f32[512,512]{1,0:T(8,128)S(1)}, f32[512,512]{1,0:T(8,128)S(1)}, u32[]{:S(2)}, u32[]{:S(2)}) collective-permute-start(f32[512,512]{1,0:T(8,128)S(1)} %shard_map.44._.__), channel_id=1, source_target_pairs={{0,1},{1,2},{2,3},{3,4},{4,5},{5,6},{6,7},{7,0},{8,9},{9,10},{10,1... | collective-permute-start | bytes 3145736 | tf_op jit(solution)/shard_map/ppermute | solution.py:461
  47.8 32.0 %collective-permute-start.13 = (f32[512,512]{1,0:T(8,128)S(1)}, f32[512,512]{1,0:T(8,128)S(1)}, u32[]{:S(2)}, u32[]{:S(2)}) collective-permute-start(f32[512,512]{1,0:T(8,128)S(1)} %shard_map.46._), channel_id=1, source_target_pairs={{0,1},{1,2},{2,3},{3,4},{4,5},{5,6},{6,7},{7,0},{8,9},{9,10},{10,1... | collective-permute-start | bytes 3145736 | tf_op jit(solution)/shard_map/ppermute | solution.py:461
  51.1 15.9 %collective-permute-start.9 = (f32[264,512]{1,0:T(8,128)S(1)}, f32[264,512]{1,0:T(8,128)S(1)}, u32[]{:S(2)}, u32[]{:S(2)}) collective-permute-start(f32[264,512]{1,0:T(8,128)S(1)} %shard_map.47._), channel_id=1, source_target_pairs={{0,7},{1,0},{2,1},{3,2},{4,3},{5,4},{6,5},{7,6},{8,15},{9,8},{10,9... | collective-permute-start | bytes 1622024 | tf_op jit(solution)/shard_map/ppermute | solution.py:461
  54.2 23.5 %collective-permute-start.12 = (f32[8,256]{1,0:T(8,128)S(1)}, f32[8,256]{1,0:T(8,128)S(1)}, u32[]{:S(2)}, u32[]{:S(2)}) collective-permute-start(f32[8,256]{1,0:T(8,128)S(1)} %get-tuple-element.62.sums_ref), channel_id=1, source_target_pairs={{0,16},{8,24},{16,0},{24,8},{1,17},{9,25},{17,1},{25,9},{2,18},{10... | collective-permute-start | bytes 24584 | tf_op jit(solution)/shard_map/ppermute | solution.py:461
  68.1 9.7 %collective-permute-start.11 = (f32[8,256]{1,0:T(8,128)S(1)}, f32[8,256]{1,0:T(8,128)S(1)}, u32[]{:S(2)}, u32[]{:S(2)}) collective-permute-start(f32[8,256]{1,0:T(8,128)S(1)} %get-tuple-element.65.sums_ref.rest_0_), channel_id=1, source_target_pairs={{0,24},{8,0},{16,8},{24,16},{1,25},{9,1},{17,9},{25,17},{2,26},{10... | collective-permute-start | bytes 24584 | tf_op jit(solution)/shard_map/ppermute | solution.py:461
